TPU v7x, 512 devices: a whole 4x8x8 slice. The times are simulated.
512 devices in a mesh: segment: 16 (over z_lo, x), shard: 32 (over y, z_hi, core).
Axes of the slice: x: 4, y: 8, z: 8 (z_hi: 2, z_lo: 4; z = z_hi * 4 + z_lo), core: 2. Of those that a mesh axis runs over, the one named last changes fastest.
Arguments:
- value_weight: bfloat16 [16, 8192, 4096], P('segment', 'shard'), as said below
- output_weight: bfloat16 [16, 4096, 8192], P('segment', None, 'shard'), as said below
- norm_gain: float32 [16, 8192], P('segment', 'shard'), may hold values from 0.1 to 1.9
- arriving: bfloat16 [16, 128, 8192], P('segment', None, 'shard'), may hold values from -6 to 6
- fresh_inputs: bfloat16 [1, 128, 8192], P(None, None, 'shard'), may hold values from -6 to 6
- returning: bfloat16 [16, 128, 8192], P('segment', None, 'shard'), may hold values from -8 to 8
- cotangents: bfloat16 [1, 128, 8192], P(None, None, 'shard'), may hold values from -8 to 8
- saved_inputs: bfloat16 [16, 2, 128, 8192], P('segment', None, None, 'shard'), may hold values from -8 to 8
- forward_base: bfloat16 [16, 8, 64, 8192], P('segment', None, None, 'shard'), may hold values from -6 to 6
- backward_base: bfloat16 [16, 8, 64, 8192], P('segment', None, None, 'shard'), may hold values from -8 to 8
- sample_ids: int32 [17, 2], replicated, may hold values from 0 to 7
- forward_exponents: int32 [16, 2, 64], P('segment', None, 'shard'), may hold values from -7 to -3
- backward_exponents: int32 [16, 2, 64], P('segment', None, 'shard'), may hold values from -7 to -3
Outputs:
- segment_outputs: bfloat16 [16, 128, 8192], P('segment', None, 'shard')
- input_grads: bfloat16 [16, 128, 8192], P('segment', None, 'shard')
- gain_grads: float32 [16, 8192], P('segment', 'shard')
Inputs may be any that keep to these rules, and one draw needn't show every extreme that they name: `value_weight`: entries of order the inverse square root of 8192. `output_weight`: entries of order the inverse square root of 4096.
All inputs are finite; a program needn't handle non-finite values.
Results may differ from a plain program's by a relative error of at most 0.025.
Values may be sent and summed in bfloat16 or wider, within the bound.
No kernel may reach another device: no remote copies, remote signals or barrier semaphores. Data moves between devices by JAX's collectives and lax.ppermute only.
A program may use at most 64 MiB of HBM per device.

v0:
```python
import jax
import jax.numpy as jnp
from jax import lax
from jax.sharding import PartitionSpec as P

D = 8192
BLOCK = 128


norm_epsilon = 1e-05


def shifted(value, axis, steps):
    count = lax.axis_size(axis)
    leading, last = (max(0, -steps), min(count, count - steps))
    return lax.ppermute(value, axis, [(source, source + steps) for source in range(leading, last)])


def power_two(exponent):
    magnitude = jnp.abs(exponent)
    factor = jnp.ones(exponent.shape, jnp.float32)
    for bit_number in range(4):
        bit_set = magnitude // 2**bit_number % 2 == 1
        factor = jnp.where(bit_set, factor * 2.0**2**bit_number, factor)
    return jnp.where(exponent < 0, 1.0 / factor, factor)


def decode_message(message, base_rows, exponents):
    leading = message.shape[:-1]
    features = message.shape[-1]
    shaped = leading + (features // BLOCK, BLOCK)
    block_scale = power_two(exponents)[..., None]
    block_inverse = power_two(-exponents)[..., None]
    base_float = base_rows.astype(jnp.float32).reshape(shaped)
    change = message.astype(jnp.float32).reshape(shaped) - base_float
    coded_delta = jnp.clip(change * block_inverse, -127.0, 127.0).astype(jnp.bfloat16)
    rebuilt = base_float + coded_delta.astype(jnp.float32) * block_scale
    return rebuilt.reshape(message.shape).astype(jnp.bfloat16)


def stored_rows(table, identifiers):
    slot_count = table.shape[0]
    selector = (identifiers[:, None] == jnp.arange(slot_count, dtype=jnp.int32)[None, :]).astype(
        table.dtype
    )
    picked = jnp.einsum("js,sqc->jqc", selector, table, preferred_element_type=jnp.float32)
    return picked.astype(table.dtype).reshape(-1, table.shape[-1])


def shards(
    value_weight,
    output_weight,
    norm_gain,
    arriving,
    fresh_inputs,
    returning,
    cotangents,
    saved_inputs,
    forward_base,
    backward_base,
    sample_ids,
    forward_exponents,
    backward_exponents,
):
    segment_index = lax.axis_index("segment")
    segment_count = lax.axis_size("segment")
    value_local = value_weight[0]
    output_local = output_weight[0]
    gain_local = norm_gain[0]
    tick_count = saved_inputs.shape[1]
    saved_float = saved_inputs[0].astype(jnp.float32)
    gain_total = jnp.zeros(gain_local.shape, jnp.float32)
    segment_out = arriving[0]
    grad_out = returning[0]
    for tick_index in range(tick_count):
        if tick_index == 0:
            forward_in = arriving[0]
            backward_in = returning[0]
        else:
            passed_on = shifted(segment_out, "segment", 1)
            forward_in = jnp.where(segment_index == 0, fresh_inputs[tick_index - 1], passed_on)
            passed_back = shifted(grad_out, "segment", -1)
            backward_in = jnp.where(
                segment_index == segment_count - 1, cotangents[tick_index - 1], passed_back
            )
        forward_micro = tick_index - segment_index + segment_count - 1
        forward_ids = lax.dynamic_index_in_dim(sample_ids, forward_micro, 0, keepdims=False)
        inputs_now = decode_message(
            forward_in, stored_rows(forward_base[0], forward_ids), forward_exponents[0, tick_index]
        )
        inputs_float = inputs_now.astype(jnp.float32)
        scaled = (inputs_float * gain_local).astype(jnp.bfloat16)
        row_squares = lax.psum(jnp.sum(inputs_float * inputs_float, axis=-1), "shard")
        factor = lax.rsqrt(row_squares / D + norm_epsilon)[:, None]
        partial_value = jnp.dot(scaled, value_local, preferred_element_type=jnp.float32)
        share = lax.psum_scatter(
            partial_value.astype(jnp.bfloat16), "shard", scatter_dimension=1, tiled=True
        ).astype(jnp.float32)
        pre_share = (factor * share).astype(jnp.bfloat16)
        branch = jnp.dot(
            lax.all_gather(pre_share, "shard", axis=1, tiled=True),
            output_local,
            preferred_element_type=jnp.float32,
        )
        segment_out = (inputs_float + branch).astype(jnp.bfloat16)
        backward_micro = tick_index + segment_index
        backward_ids = lax.dynamic_index_in_dim(sample_ids, backward_micro, 0, keepdims=False)
        grad_now = decode_message(
            backward_in,
            stored_rows(backward_base[0], backward_ids),
            backward_exponents[0, tick_index],
        )
        saved_now = saved_float[tick_index]
        saved_total = lax.psum(jnp.sum(saved_now * saved_now, axis=-1), "shard")
        saved_factor = lax.rsqrt(saved_total / D + norm_epsilon)[:, None]
        partial_grad = lax.dot_general(
            grad_now, output_local, (((1,), (1,)), ((), ())), preferred_element_type=jnp.float32
        )
        value_grad = lax.psum(partial_grad.astype(jnp.bfloat16), "shard")
        scaled_grad = lax.dot_general(
            value_grad, value_local, (((1,), (1,)), ((), ())), preferred_element_type=jnp.float32
        )
        weighted = saved_now * gain_local
        row_dot = lax.psum(jnp.sum(weighted * scaled_grad, axis=-1), "shard")[:, None]
        grad_float = grad_now.astype(jnp.float32)
        grad_out = (
            grad_float
            + saved_factor * gain_local * scaled_grad
            - saved_now * saved_factor**3 * row_dot / D
        ).astype(jnp.bfloat16)
        gain_total = gain_total + jnp.sum(scaled_grad * saved_now * saved_factor, axis=0)
    return (segment_out[None], grad_out[None], gain_total[None])


def solution(mesh):
    return jax.shard_map(
        shards,
        mesh=mesh,
        in_specs=(
            P("segment", "shard", None),
            P("segment", None, "shard"),
            P("segment", "shard"),
            P("segment", None, "shard"),
            P(None, None, "shard"),
            P("segment", None, "shard"),
            P(None, None, "shard"),
            P("segment", None, None, "shard"),
            P("segment", None, None, "shard"),
            P("segment", None, None, "shard"),
            P(),
            P("segment", None, "shard"),
            P("segment", None, "shard"),
        ),
        out_specs=(P("segment", None, "shard"), P("segment", None, "shard"), P("segment", "shard")),
        check_vma=False,
    )
```

profile of v0, /device:TPU:7, one launch (start us, length us, event | category | flops | bytes accessed | tf_op | source)
XLA Modules:
  0.0 1156.2 jit_solution(3910010279435550996)
XLA Ops:
  7.2 1.6 bitcast_select_fusion.3
  8.9 0.8 convert.9
  9.8 1.1 dynamic-slice_reduce_fusion
  10.8 2.0 add_convert_fusion
  12.8 3.4 convolution_convert_fusion.1
  16.3 0.1 broadcast_bitcast_fusion.6
  16.4 0.1 broadcast_bitcast_fusion.7
  16.5 1.0 fusion.35
  17.6 0.4 convolution_convert_fusion.3
  18.0 1.3 copy.46
  19.5 1.0 convert_element_type.269
  20.4 0.1 copy.38
  20.5 0.1 reduce_sum.75
  20.6 0.1 multiply_reduce_fusion.5
  20.7 89.0 %psum.58 = f32[128]{0:T(128)S(1)} all-reduce(f32[128]{0:T(128)S(1)} %multiply_reduce_fusion.5), channel_id=1, replica_groups=mesh['segment'=16,'shard'=32] {'shard'}, use_global_device_ids=true, to_apply=%region_7.8 | all-reduce | flops 128 | bytes 1024 | tf_op jit(solution)/shard_map/psum | solution.py:114
  109.8 257.6 %all-reduce.5.cloned.1.call-done = bf16[128,4096]{1,0:T(8,128)(2,1)} async-done(((bf16[128,4096]{1,0:T(8,128)(2,1)}), bf16[128,4096]{1,0:T(8,128)(2,1)}) %all-reduce.5.cloned.1.call-update) | async-done | bytes 1048592 | tf_op jit(solution)/shard_map/psum | solution.py:119
  367.4 2.2 multiply_reduce_fusion.1
  369.6 84.8 %all-reduce.1 = (f32[128]{0:T(128)S(1)}, f32[128]{0:T(128)S(1)}, f32[128]{0:T(128)}) all-reduce(f32[128]{0:T(128)S(1)} %reduce_sum.75, f32[128]{0:T(128)S(1)} %get-tuple-element.6, f32[128]{0:T(128)S(1)} %get-tuple-element.7), channel_id=1, replica_groups=mesh['segment'=16,'shard'=32] {'shard'}, use_global_device_ids=true, to_apply=%region_1.2 | all-reduce | flops 384 | bytes 3072 | tf_op jit(solution)/shard_map/psum | solution.py:93
  454.4 40.7 %reduce-scatter.7.cloned.1.call-done = bf16[128,128]{1,0:T(8,128)(2,1)} async-done(((bf16[4096,128]{1,0:T(8,128)(2,1)}), bf16[128,128]{1,0:T(8,128)(2,1)}) %reduce-scatter.7.cloned.1.call-update) | async-done | bytes 32784
  495.1 0.9 copy.47
  496.0 0.7 multiply_convert_fusion.1
  496.8 0.1 broadcast_bitcast_fusion
  496.9 0.1 broadcast_bitcast_fusion.1
  497.0 0.3 fusion.25
  497.3 0.3 fusion.27
  497.6 0.1 subtract_convert_fusion.1
  497.7 2.6 collective-permute-start.1
  500.4 0.1 broadcast_bitcast_fusion.4
  500.5 4.4 collective-permute-done.1
  504.9 0.9 fusion.46
  505.8 3.4 convolution_convert_fusion
  509.2 77.2 %all-gather.3.cloned.1.call-done = bf16[128,4096]{1,0:T(8,128)(2,1)} async-done(((bf16[128,128]{1,0:T(8,128)(2,1)}), bf16[128,4096]{1,0:T(8,128)(2,1)}) %all-gather.3.cloned.1.call-update) | async-done | bytes 1048592 | tf_op jit(solution)/shard_map/all_gather | solution.py:101
  586.5 2.4 fusion.21
  588.8 2.3 collective-permute-start
  591.2 2.6 collective-permute-done
  593.8 0.1 fusion.37
  594.0 0.4 convolution_convert_fusion.2
  594.4 1.3 copy.48
  595.8 333.0 %all-reduce.7.cloned.1.call-done = bf16[128,4096]{1,0:T(8,128)(2,1)} async-done(((bf16[128,4096]{1,0:T(8,128)(2,1)}), bf16[128,4096]{1,0:T(8,128)(2,1)}) %all-reduce.7.cloned.1.call-update) | async-done | bytes 1048592 | tf_op jit(solution)/shard_map/psum | solution.py:119
  928.8 2.1 multiply_reduce_fusion
  931.0 84.3 %all-reduce = (f32[128]{0:T(128)S(1)}, f32[128]{0:T(128)S(1)}) all-reduce(f32[128]{0:T(128)S(1)} %get-tuple-element.17, f32[128]{0:T(128)S(1)} %get-tuple-element.4), channel_id=1, replica_groups=mesh['segment'=16,'shard'=32] {'shard'}, use_global_device_ids=true, to_apply=%region_4.5 | all-reduce | flops 256 | bytes 2048 | tf_op jit(solution)/shard_map/psum | solution.py:93
  1015.3 40.5 %reduce-scatter.9.cloned.1.call-done = bf16[128,128]{1,0:T(8,128)(2,1)} async-done(((bf16[4096,128]{1,0:T(8,128)(2,1)}), bf16[128,128]{1,0:T(8,128)(2,1)}) %reduce-scatter.9.cloned.1.call-update) | async-done | bytes 32784
  1055.7 0.9 copy.49
  1056.6 0.7 multiply_convert_fusion
  1057.3 0.6 add.553
  1057.9 0.8 fusion.61
  1058.7 87.7 %all-gather.5.cloned.1.call-done = bf16[128,4096]{1,0:T(8,128)(2,1)} async-done(((bf16[128,128]{1,0:T(8,128)(2,1)}), bf16[128,4096]{1,0:T(8,128)(2,1)}) %all-gather.5.cloned.1.call-update) | async-done | bytes 1048592 | tf_op jit(solution)/shard_map/all_gather | solution.py:101
  1146.4 3.0 fusion.28
  (54 shorter events, 0.8 us)
Async XLA Ops:
  7.2 10.4 copy-start
  7.2 360.2 %all-reduce.5.cloned.1.call-start = ((), (), s32[]{:S(2)}) async-start(), calls=%async_computation.4 | async-start | bytes 2097152 | tf_op jit(solution)/shard_map/psum | solution.py:119
  12.8 3.6 copy-start.4
  12.8 3.7 copy-start.3
  12.8 4.7 copy-start.8
  16.3 478.8 %reduce-scatter.7.cloned.1.call-start = ((), (), s32[]{:S(2)}) async-start(), calls=%async_computation.6 | async-start | bytes 1081344
  19.4 477.4 %copy-start.5 = (f32[2,64,256]{2,0,1:T(2,128)S(1)}, f32[2,64,256]{2,0,1:T(2,128)}, u32[]{:S(2)}) copy-start(f32[2,64,256]{2,0,1:T(2,128)} %get-tuple-element.35) | copy-start | bytes 393220
  19.4 567.0 %all-gather.3.cloned.1.call-start = ((), (), s32[]{:S(2)}) async-start(), calls=%async_computation.2 | async-start | bytes 1081344 | tf_op jit(solution)/shard_map/all_gather | solution.py:101
  20.4 476.4 %copy-start.6 = (f32[2,64,256]{2,0,1:T(2,128)S(1)}, f32[2,64,256]{2,0,1:T(2,128)}, u32[]{:S(2)}) copy-start(f32[2,64,256]{2,0,1:T(2,128)} %get-tuple-element.33) | copy-start | bytes 393220
  20.7 476.2 %copy-start.11 = (f32[2]{0:T(128)S(1)}, f32[2]{0:T(128)}, u32[]{:S(2)}) copy-start(f32[2]{0:T(128)} %get-tuple-element.21) | copy-start | bytes 28
  367.4 129.6 %copy-start.2 = (bf16[1,8,64,256]{3,2,1,0:T(8,128)(2,1)S(1)}, bf16[1,8,64,256]{3,2,1,0:T(8,128)(2,1)}, u32[]{:S(2)}) copy-start(bf16[1,8,64,256]{3,2,1,0:T(8,128)(2,1)} %param.22) | copy-start | bytes 786436
  367.4 130.2 %copy-start.1 = (bf16[1,128,256]{2,1,0:T(8,128)(2,1)S(1)}, bf16[1,128,256]{2,1,0:T(8,128)(2,1)}, u32[]{:S(2)}) copy-start(bf16[1,128,256]{2,1,0:T(8,128)(2,1)} %param.18) | copy-start | bytes 196612
  367.4 133.0 %copy-start.10 = (f32[2]{0:T(128)S(1)}, f32[2]{0:T(128)}, u32[]{:S(2)}) copy-start(f32[2]{0:T(128)} %get-tuple-element.39) | copy-start | bytes 28
  496.7 432.1 %all-reduce.7.cloned.1.call-start = ((), (), s32[]{:S(2)}) async-start(), calls=%async_computation.5 | async-start | bytes 2097152 | tf_op jit(solution)/shard_map/psum | solution.py:119
  497.7 7.1 collective-permute-start.1
  509.1 82.0 %copy-start.9 = (f32[2]{0:T(128)S(1)}, f32[2]{0:T(128)}, u32[]{:S(2)}) copy-start(f32[2]{0:T(128)} %get-tuple-element.38) | copy-start | bytes 28
  509.1 84.7 %copy-start.7 = (bf16[1,128,256]{2,1,0:T(8,128)(2,1)S(1)}, bf16[1,128,256]{2,1,0:T(8,128)(2,1)}, u32[]{:S(2)}) copy-start(bf16[1,128,256]{2,1,0:T(8,128)(2,1)} %param.17) | copy-start | bytes 196612
  509.2 546.6 %reduce-scatter.9.cloned.1.call-start = ((), (), s32[]{:S(2)}) async-start(), calls=%async_computation.7 | async-start | bytes 1081344
  588.8 5.0 collective-permute-start
  594.4 1.4 copy-start.12
  595.8 550.6 %all-gather.5.cloned.1.call-start = ((), (), s32[]{:S(2)}) async-start(), calls=%async_computation.3 | async-start | bytes 1081344 | tf_op jit(solution)/shard_map/all_gather | solution.py:101
Sparse Core Ops, SparseCore 0:
  16.4 350.9 all-reduce.4
  372.7 122.3 reduce-scatter.6
  499.3 87.0 all-gather.2
  589.5 339.3 all-reduce.6
  933.3 122.4 reduce-scatter.8
  1059.3 87.0 all-gather.4
where the time goes:
time: 1160 us
  waiting for transfers between devices  844 us (73%)
  blocking collectives  258 us (22%)
  matrix products  20.9 us (2%)
  between operations  14.4 us (1%)
    psum x2, waiting for transfers between devices, shards(): value_grad = lax.psum(partial_grad.astype(jnp.bfloat16), 'shard')  591 us
    psum x2, blocking collectives, shards(): lax.psum(jnp.sum(inputs_float * inputs_float, axis=-1), 'shard')  169 us
    all_gather x2, waiting for transfers between devices, shards(): lax.all_gather(pre_share, 'shard', axis=1, tiled=True)  165 us
    psum x1, blocking collectives, shards(): saved_total = lax.psum(jnp.sum(saved_now * saved_now, axis=-1), 'shard')  89 us
    unnamed x8, waiting for transfers between devices  81.3 us
  transfers between devices with their start and end apart: 8, of which 8 were waited for; matrix products, arithmetic and copies ran while one was open for 2% of the time, Pallas kernels for 0%

commit v1 on v0

v1 whole, which is shorter than its diff:
```python
import functools

import jax
import jax.numpy as jnp
from jax import lax
from jax.experimental import pallas as pl
from jax.experimental.pallas import tpu as pltpu
from jax.sharding import PartitionSpec as P

D = 8192
BLOCK = 128
ROWS = 128
WIDTH = 256
SEQ = 64
STATS = 16
RING = 8
HALF = RING * WIDTH
EPSILON = 1e-05
F32 = jnp.float32
BF16 = jnp.bfloat16
VMEM_LIMIT = 20 * 1024 * 1024


def core_pairs():
    return [(index, index ^ 1) for index in range(4 * RING)]


def z_pairs():
    return [(index, index ^ 2) for index in range(4 * RING)]


def rings():
    return [[4 * y + rest for y in range(RING)] for rest in range(4)]


def swapped(value, groups=None):
    return lax.all_to_all(value, "shard", 0, 0, axis_index_groups=groups, tiled=True)


def shifted(value, axis, steps):
    count = lax.axis_size(axis)
    leading, last = (max(0, -steps), min(count, count - steps))
    return lax.ppermute(value, axis, [(source, source + steps) for source in range(leading, last)])


def call(kernel, name, outs, *, prefetch=(), blocks=None, flops=0, operands=()):
    blocks = blocks or {}

    def spec(position, operand):
        if position in blocks:
            shape, index_map = blocks[position]
            return pl.BlockSpec(shape, index_map)
        rank = len(operand.shape)
        return pl.BlockSpec(operand.shape, lambda *_: (0,) * rank)

    moved = 0
    for position, operand in enumerate(operands):
        shape = blocks[position][0] if position in blocks else operand.shape
        size = 1
        for length in shape:
            size *= length
        moved += size * operand.dtype.itemsize
    for out in outs:
        moved += out.size * out.dtype.itemsize
    return pl.pallas_call(
        kernel,
        out_shape=outs,
        grid_spec=pltpu.PrefetchScalarGridSpec(
            num_scalar_prefetch=len(prefetch),
            grid=(1,),
            in_specs=[spec(position, operand) for position, operand in enumerate(operands)],
            out_specs=[pl.BlockSpec(out.shape, lambda *_, rank=len(out.shape): (0,) * rank) for out in outs],
        ),
        compiler_params=pltpu.CompilerParams(vmem_limit_bytes=VMEM_LIMIT),
        cost_estimate=pl.CostEstimate(flops=flops, bytes_accessed=moved, transcendentals=0),
        name=name,
    )(*prefetch, *operands)


def shape_of(*dims, dtype=BF16):
    return jax.ShapeDtypeStruct(dims, dtype)


def across(column):
    return jnp.broadcast_to(column, (ROWS, ROWS)).T[0:1]


def down(row):
    square = jnp.broadcast_to(row, (ROWS, ROWS)).T
    return jnp.concatenate([square, square], axis=1)


def split_stats(total):
    high = total.astype(BF16).astype(F32)
    return jnp.concatenate([high, total - high], axis=1).astype(BF16)


def joined_stats(coded):
    value = coded.astype(F32)
    return value[:, :ROWS] + value[:, ROWS:]


def power_row(low, high, sign):
    lane = lax.broadcasted_iota(jnp.int32, (1, WIDTH), 1)
    exponent = sign * jnp.where(lane < BLOCK, low, high)
    magnitude = jnp.abs(exponent)
    grown = jnp.ones((1, WIDTH), F32)
    shrunk = jnp.ones((1, WIDTH), F32)
    for bit in range(4):
        bit_set = (magnitude >> bit) & 1 == 1
        grown = jnp.where(bit_set, grown * 2.0 ** (2**bit), grown)
        shrunk = jnp.where(bit_set, shrunk * 0.5 ** (2**bit), shrunk)
    return jnp.where(exponent < 0, shrunk, grown)


def decoded(message, first_ref, second_ref, exponents, tick):
    low, high = exponents[tick, 0], exponents[tick, 1]
    scale = power_row(low, high, 1)
    inverse = power_row(low, high, -1)
    base = jnp.concatenate([first_ref[0], second_ref[0]], axis=0).astype(F32)
    delta = jnp.clip((message.astype(F32) - base) * inverse, -127.0, 127.0).astype(BF16)
    return (base + delta.astype(F32) * scale).astype(BF16)


def chosen(meta, edge, refs):
    if len(refs) == 1:
        return refs[0][...]
    return jnp.where(meta[0] == edge, refs[1][0].astype(F32), refs[0][...].astype(F32))


def forward_start(tick, messages, ids, meta, exponents, *refs):
    given, refs = refs[:messages], refs[messages:]
    first, second, gain, weight, x_out, keep, send = refs
    x = decoded(chosen(meta, 0, given), first, second, exponents, tick)
    x_out[...] = x
    x = x.astype(F32)
    scaled = (x * gain[...]).astype(BF16)
    total = across(jnp.sum(x * x, axis=1, keepdims=True))
    stats = split_stats(jnp.broadcast_to(total, (STATS, ROWS)))
    core = meta[3]
    for out, half in ((send, 1 - core), (keep, core)):
        for j in range(RING):
            at = pl.multiple_of((half * RING + j) * WIDTH, WIDTH)
            part = jnp.dot(scaled, weight[:, pl.ds(at, WIDTH)], preferred_element_type=F32)
            out[j, :ROWS] = part.astype(BF16)
            out[j, ROWS:] = stats


def backward_start(tick, messages, last, ids, meta, exponents, *refs):
    given, refs = refs[:messages], refs[messages:]
    if tick == 0:
        first, second, weight, saved, g_out, keep, send = refs
        rows = []
        for k in range(2):
            value = saved[k].astype(F32)
            rows.append(jnp.broadcast_to(across(jnp.sum(value * value, axis=1, keepdims=True)), (STATS // 2, ROWS)))
        stats = split_stats(jnp.concatenate(rows, axis=0))
    else:
        first, second, weight, g_out, keep, send = refs
        stats = None
    g = decoded(chosen(meta, last, given), first, second, exponents, tick).astype(BF16)
    g_out[...] = g
    core = meta[3]
    for out, half in ((send, 1 - core), (keep, core)):
        for j in range(RING):
            at = pl.multiple_of((half * RING + j) * WIDTH, WIDTH)
            part = lax.dot_general(
                g, weight[pl.ds(at, WIDTH), :], (((1,), (1,)), ((), ())), preferred_element_type=F32
            )
            out[j, :ROWS] = part.astype(BF16)
            if stats is not None:
                out[j, ROWS:] = stats


def core_sum(keep, other, out):
    extra = keep.shape[1] > ROWS
    if extra:
        stats = split_stats(joined_stats(keep[0, ROWS:]) + joined_stats(other[0, ROWS:]))
    for j in range(RING):
        out[j, :ROWS] = (keep[j, :ROWS].astype(F32) + other[j, :ROWS].astype(F32)).astype(BF16)
        if extra:
            out[j, ROWS:] = stats


def ring_sum(pieces, out):
    total = pieces[0, :ROWS].astype(F32)
    for j in range(1, RING):
        total = total + pieces[j, :ROWS].astype(F32)
    out[:ROWS] = total.astype(BF16)
    if out.shape[0] > ROWS:
        stats = joined_stats(pieces[0, ROWS:])
        for j in range(1, RING):
            stats = stats + joined_stats(pieces[j, ROWS:])
        out[ROWS:] = split_stats(stats)


def forward_share(own, other, out):
    total = joined_stats(own[ROWS:]) + joined_stats(other[ROWS:])
    factor = lax.rsqrt(total[0:1] / D + EPSILON)
    value = own[:ROWS].astype(F32) + other[:ROWS].astype(F32)
    out[...] = jnp.broadcast_to((down(factor) * value).astype(BF16)[None], out.shape)


def backward_share(own, other, out, *stats):
    value = (own[:ROWS].astype(F32) + other[:ROWS].astype(F32)).astype(BF16)
    out[...] = jnp.broadcast_to(value[None], out.shape)
    if stats:
        stats[0][...] = joined_stats(own[ROWS:]) + joined_stats(other[ROWS:])


def forward_product(meta, blocks, own_weight, other_weight, mine, others):
    for weight, out in ((other_weight, others), (own_weight, mine)):
        total = jnp.zeros((ROWS, WIDTH), F32)
        for j in range(RING):
            at = j * WIDTH
            total = total + jnp.dot(blocks[j], weight[pl.ds(at, WIDTH), :], preferred_element_type=F32)
        out[...] = total


def backward_product(meta, blocks, own_weight, other_weight, mine, others):
    for weight, out in ((other_weight, others), (own_weight, mine)):
        total = jnp.zeros((ROWS, WIDTH), F32)
        for j in range(RING):
            at = j * WIDTH
            total = total + lax.dot_general(
                blocks[j], weight[:, pl.ds(at, WIDTH)], (((1,), (1,)), ((), ())), preferred_element_type=F32
            )
        out[...] = total


def forward_end(x, mine, other, out):
    out[...] = (x[...].astype(F32) + (mine[...] + other[...])).astype(BF16)


def saved_scale(stats, tick):
    at = tick * (STATS // 2)
    return down(lax.rsqrt(stats[at : at + 1] / D + EPSILON))


def backward_middle(tick, mine, other, saved, gain, stats, *refs):
    before, (scaled_grad, row_dot, gain_out) = refs[:-3], refs[-3:]
    value = mine[...] + other[...]
    scaled_grad[...] = value
    kept = saved[0].astype(F32)
    dots = jnp.sum(kept * gain[...] * value, axis=1, keepdims=True)
    row_dot[...] = jnp.broadcast_to(across(dots), row_dot.shape)
    total = jnp.sum(value * kept * saved_scale(stats, tick), axis=0, keepdims=True)
    gain_out[...] = total + before[0][...] if before else total


def backward_end(tick, g, scaled_grad, saved, gain, stats, *refs):
    dots, out = refs
    total = dots[0, 0:1]
    for j in range(1, dots.shape[0]):
        total = total + dots[j, 0:1]
    factor = saved_scale(stats, tick)
    value = g[...].astype(F32) + factor * gain[...] * scaled_grad[...]
    out[...] = (value - saved[0].astype(F32) * (factor * factor * factor) * down(total) / D).astype(BF16)


def scattered(keep, send):
    rows = keep.shape[1]
    other = lax.ppermute(send, "shard", core_pairs())
    (pieces,) = call(core_sum, "core_sum", [shape_of(RING, rows, WIDTH)], operands=(keep, other))
    (own,) = call(ring_sum, "ring_sum", [shape_of(rows, WIDTH)], operands=(swapped(pieces, rings()),))
    return own, lax.ppermute(own, "shard", z_pairs())


def shards(
    value_weight,
    output_weight,
    norm_gain,
    arriving,
    fresh_inputs,
    returning,
    cotangents,
    saved_inputs,
    forward_base,
    backward_base,
    sample_ids,
    forward_exponents,
    backward_exponents,
):
    segment = lax.axis_index("segment")
    segments = lax.axis_size("segment")
    position = lax.axis_index("shard")
    core = position % 2
    meta = jnp.stack([segment, position // 4, position // 2 % 2, core]).astype(jnp.int32)
    value_local, output_local = value_weight[0], output_weight[0]
    saved, ticks = saved_inputs[0], saved_inputs.shape[1]
    half = (1 - core) * HALF
    value_other = lax.ppermute(
        lax.dynamic_slice(value_local, (0, half), (WIDTH, HALF)), "shard", core_pairs()
    )
    output_other = lax.ppermute(
        lax.dynamic_slice(output_local, (half, 0), (HALF, WIDTH)), "shard", core_pairs()
    )
    piece = shape_of(ROWS, WIDTH)
    wide = shape_of(ROWS, WIDTH, dtype=F32)
    start_flops = 2 * ROWS * WIDTH * 2 * HALF

    def base_blocks(first, micro):
        return {
            first + sample: (
                (1, SEQ, WIDTH),
                lambda i, ids, meta, exps, sample=sample: (ids[micro(meta), sample], 0, 0),
            )
            for sample in range(2)
        }

    forward_message, backward_message = [arriving[0]], [returning[0]]
    stats = gain_total = None
    for tick in range(ticks):
        tall = shape_of(RING, ROWS + STATS, WIDTH)
        count = len(forward_message)
        x, keep, send = call(
            functools.partial(forward_start, tick, count),
            "forward_start",
            [piece, tall, tall],
            prefetch=(sample_ids, meta, forward_exponents[0]),
            operands=(*forward_message, forward_base[0], forward_base[0], norm_gain, value_local),
            blocks=base_blocks(count, lambda meta: tick - meta[0] + segments - 1),
            flops=start_flops,
        )
        low = tall if tick == 0 else shape_of(RING, ROWS, WIDTH)
        operands = (*backward_message, backward_base[0], backward_base[0], output_local)
        g, back_keep, back_send = call(
            functools.partial(backward_start, tick, count, segments - 1),
            "backward_start",
            [piece, low, low],
            prefetch=(sample_ids, meta, backward_exponents[0]),
            operands=operands + ((saved,) if tick == 0 else ()),
            blocks=base_blocks(count, lambda meta: tick + meta[0]),
            flops=start_flops,
        )
        own, other = scattered(keep, send)
        back_own, back_other = scattered(back_keep, back_send)

        copies = shape_of(RING, ROWS, WIDTH)
        (pre,) = call(forward_share, "forward_share", [copies], operands=(own, other))
        gathered = swapped(pre, rings())
        share_outs = [copies] + ([shape_of(STATS, ROWS, dtype=F32)] if tick == 0 else [])
        value_grad, *given = call(
            backward_share, "backward_share", share_outs, operands=(back_own, back_other)
        )
        stats = given[0] if given else stats
        back_gathered = swapped(value_grad, rings())

        mine, others = call(
            forward_product,
            "forward_product",
            [wide, wide],
            prefetch=(meta,),
            operands=(gathered, output_local, output_other),
            blocks={1: ((HALF, WIDTH), lambda i, meta: (meta[3], 0))},
            flops=start_flops,
        )
        (segment_out,) = call(
            forward_end,
            "forward_end",
            [piece],
            operands=(x, mine, lax.ppermute(others, "shard", core_pairs())),
        )
        if tick + 1 < ticks:
            forward_message = [shifted(segment_out, "segment", 1), fresh_inputs[tick : tick + 1]]

        mine, others = call(
            backward_product,
            "backward_product",
            [wide, wide],
            prefetch=(meta,),
            operands=(back_gathered, value_local, value_other),
            blocks={1: ((WIDTH, HALF), lambda i, meta: (0, meta[3]))},
            flops=start_flops,
        )
        saved_block = {2: ((1, ROWS, WIDTH), lambda i, tick=tick: (tick, 0, 0))}
        before = () if gain_total is None else (gain_total,)
        small = shape_of(4 * RING, 8, ROWS, dtype=F32)
        scaled_grad, dots, gain_total = call(
            functools.partial(backward_middle, tick),
            "backward_middle",
            [wide, small, shape_of(1, WIDTH, dtype=F32)],
            operands=(mine, lax.ppermute(others, "shard", core_pairs()), saved, norm_gain, stats) + before,
            blocks=saved_block,
        )
        (input_grad,) = call(
            functools.partial(backward_end, tick),
            "backward_end",
            [piece],
            operands=(g, scaled_grad, saved, norm_gain, stats, swapped(dots)),
            blocks=saved_block,
        )
        if tick + 1 < ticks:
            backward_message = [shifted(input_grad, "segment", -1), cotangents[tick : tick + 1]]
    return (segment_out[None], input_grad[None], gain_total)


def solution(mesh):
    return jax.shard_map(
        shards,
        mesh=mesh,
        in_specs=(
            P("segment", "shard", None),
            P("segment", None, "shard"),
            P("segment", "shard"),
            P("segment", None, "shard"),
            P(None, None, "shard"),
            P("segment", None, "shard"),
            P(None, None, "shard"),
            P("segment", None, None, "shard"),
            P("segment", None, None, "shard"),
            P("segment", None, None, "shard"),
            P(),
            P("segment", None, "shard"),
            P("segment", None, "shard"),
        ),
        out_specs=(P("segment", None, "shard"), P("segment", None, "shard"), P("segment", "shard")),
        check_vma=False,
    )
```

time: 1160 us -> 269 us (0.23)
  waiting for transfers between devices: 844 us -> 79.1 us
  blocking collectives: 258 us -> 25.1 us
  starting transfers between devices: 5.19 us -> 106 us
  Pallas kernels: 0 us -> 28.7 us
  local copies, waits for them, and re-layouts: 6.27 us -> 27.3 us
  matrix products: 20.9 us -> 0 us
  between operations: 14.4 us -> 1.25 us
    psum x2 -> x0, waiting for transfers between devices: 591 us -> none  [shards(): value_grad = lax.psum(partial_grad.astype(jnp.bfloat16), 'shard')]
    psum x3 -> x0, blocking collectives: 258 us -> none  [the longest x2 169 us: shards(): lax.psum(jnp.sum(inputs_float * inputs_float, axis=-1), 'shard')]
    all_gather x2 -> x0, waiting for transfers between devices: 165 us -> none  [shards(): lax.all_gather(pre_share, 'shard', axis=1, tiled=True)]
    unnamed x8 -> x0, waiting for transfers between devices: 81.3 us -> none
    ppermute x0 -> x14, starting transfers between devices: none -> 54.6 us  [the longest x4 25.7 us: scattered(): return (own, lax.ppermute(own, 'shard', z_pairs()))]
    all_to_all x0 -> x9, waiting for transfers between devices: none -> 49.7 us  [swapped(): lax.all_to_all(value, 'shard', 0, 0, axis_index_groups=groups, tiled=True)]
    all_to_all x0 -> x9, starting transfers between devices: none -> 46.8 us  [swapped(): lax.all_to_all(value, 'shard', 0, 0, axis_index_groups=groups, tiled=True)]
    pallas_call x0 -> x26, Pallas kernels: none -> 28.7 us  [call(): pl.pallas_call(kernel, out_shape=outs, grid_spec=pltpu.PrefetchScalarGrid...]
  transfers between devices with their start and end apart: 8 -> 25, of which waited for: 8 -> 18; matrix products, arithmetic and copies ran while one was open for 2% -> 1% of each run, Pallas kernels for 0% -> 9%
where the time goes in v1:
time: 269 us; the launch traced here: 267 us
  starting transfers between devices  106 us (39%)
  waiting for transfers between devices  79.1 us (29%)
  Pallas kernels  28.7 us (11%)
  local copies, waits for them, and re-layouts  27.3 us (10%)
  blocking collectives  25.1 us (9%)
    all_to_all x9, waiting for transfers between devices, swapped(): lax.all_to_all(value, 'shard', 0, 0, axis_index_groups=groups, tiled=True)  49.7 us
    all_to_all x9, starting transfers between devices, swapped(): lax.all_to_all(value, 'shard', 0, 0, axis_index_groups=groups, tiled=True)  46.8 us
    pallas_call x26, Pallas kernels, call(): pl.pallas_call(kernel, out_shape=outs, grid_spec=pltpu.PrefetchScalarGrid...  28.7 us
    ppermute x4, starting transfers between devices, scattered(): return (own, lax.ppermute(own, 'shard', z_pairs()))  25.7 us
    all_to_all x1, blocking collectives, swapped(): lax.all_to_all(value, 'shard', 0, 0, axis_index_groups=groups, tiled=True)  25.1 us
    unnamed x91, local copies, waits for them, and re-layouts  23.8 us
    ppermute x4, waiting for transfers between devices, scattered(): return (own, lax.ppermute(own, 'shard', z_pairs()))  13 us
    ppermute x4, starting transfers between devices, scattered(): other = lax.ppermute(send, 'shard', core_pairs())  12.7 us
  transfers between devices with their start and end apart: 25, of which 18 were waited for; matrix products, arithmetic and copies ran while one was open for 1% of the time, Pallas kernels for 9%

profile of v1, /device:TPU:7, one launch (start us, length us, event | category | flops | bytes accessed | tf_op | source)
XLA Modules:
  0.0 267.2 jit_solution(2147589376411657773)
XLA Ops:
  1.5 1.6 copy-done.1
  8.1 2.6 collective-permute-start.8
  10.7 1.6 collective-permute-done.8.other
  12.4 25.1 %all_to_all.50.pieces = bf16[8,144,256]{2,1,0:T(8,128)(2,1)S(1)} all-to-all(bf16[8,144,256]{2,1,0:T(8,128)(2,1)S(1)} %core_sum.6), channel_id=1, replica_groups={{0,4,8,12,16,20,24,28},{1,5,9,13,17,21,25,29},{2,6,10,14,18,22,26,30},{..., dimensions={0} | all-to-all | bytes 1179648 | tf_op jit(solution)/shard_map/all_to_all | solution.py:37
  37.6 10.6 %collective-permute-start.9 = (bf16[144,256]{1,0:T(8,128)(2,1)S(1)}, bf16[144,256]{1,0:T(8,128)(2,1)S(1)}, u32[]{:S(2)}, u32[]{:S(2)}) collective-permute-start(bf16[144,256]{1,0:T(8,128)(2,1)S(1)} %ring_sum.6.own), channel_id=1, source_target_pairs={{0,2},{1,3},{2,0},{3,1},{4,6},{5,7},{6,4},{7,5},{8,10},{9,11},{10,... | collective-permute-start | bytes 221192 | tf_op jit(solution)/shard_map/ppermute | solution.py:266
  48.3 1.8 collective-permute-done.9.other
  50.9 4.1 %all-to-all-start.5 = ((bf16[8,128,256]{2,1,0:T(8,128)(2,1)}), bf16[8,128,256]{2,1,0:T(8,128)(2,1)}, u32[]{:S(2)}, u32[]{:S(2)}) async-start(bf16[8,128,256]{2,1,0:T(8,128)(2,1)} %get-tuple-element.44), calls=%async_computation.5 | async-start | bytes 1048576 | tf_op jit(solution)/shard_map/all_to_all | solution.py:37
  55.1 2.1 forward_start.2
  58.6 4.5 %collective-permute-start = (bf16[8,144,256]{2,1,0:T(8,128)(2,1)}, bf16[8,144,256]{2,1,0:T(8,128)(2,1)}, u32[]{:S(2)}, u32[]{:S(2)}) collective-permute-start(bf16[8,144,256]{2,1,0:T(8,128)(2,1)} %get-tuple-element.33), channel_id=1, source_target_pairs={{0,1},{1,0},{2,3},{3,2},{4,5},{5,4},{6,7},{7,6},{8,9},{9,8},{10,11... | collective-permute-start | bytes 1769480 | tf_op jit(solution)/shard_map/ppermute | solution.py:263
  64.2 1.9 collective-permute-start.10
  68.2 1.8 all-to-all-done.5.blocks
  70.0 4.9 %all-to-all-start = ((bf16[8,144,256]{2,1,0:T(8,128)(2,1)}), bf16[8,144,256]{2,1,0:T(8,128)(2,1)}, u32[]{:S(2)}, u32[]{:S(2)}) async-start(bf16[8,144,256]{2,1,0:T(8,128)(2,1)} %copy-done.11), calls=%async_computation | async-start | bytes 1179648 | tf_op jit(solution)/shard_map/all_to_all | solution.py:37
  74.9 3.0 %backward_product.2 = (f32[128,256]{1,0:T(8,128)S(1)}, f32[128,256]{1,0:T(8,128)}) custom-call(s32[4]{0:T(128)S(1)} %pad_add_fusion.meta, bf16[8,128,256]{2,1,0:T(8,128)(2,1)} %all-to-all-done.5.blocks, bf16[256,4096]{1,0:T(8,128)(2,1)S(1)} %bitcast.20, bf16[256,2048]{1,0:T(8,128)(2,1)S(1)} %collective-permute-done.10.other_weight), custom_call_target="tpu_custom_call" | custom-call | flops 268435456 | bytes 2883584 | tf_op jit(solution)/shard_map/backward_product/pallas_call | solution.py:65
  78.0 4.7 %collective-permute-start.11 = (f32[128,256]{1,0:T(8,128)}, f32[128,256]{1,0:T(8,128)}, u32[]{:S(2)}, u32[]{:S(2)}) collective-permute-start(f32[128,256]{1,0:T(8,128)} %get-tuple-element.46), channel_id=1, source_target_pairs={{0,1},{1,0},{2,3},{3,2},{4,5},{5,4},{6,7},{7,6},{8,9},{9,8},{10,11... | collective-permute-start | bytes 393224 | tf_op jit(solution)/shard_map/ppermute | solution.py:383
  82.7 8.8 %all-to-all-done.pieces = bf16[8,144,256]{2,1,0:T(8,128)(2,1)} async-done(((bf16[8,144,256]{2,1,0:T(8,128)(2,1)}), bf16[8,144,256]{2,1,0:T(8,128)(2,1)}, u32[]{:S(2)}, u32[]{:S(2)}) %all-to-all-start) | async-done | bytes 589856 | tf_op jit(solution)/shard_map/all_to_all | solution.py:37
  91.5 1.8 ring_sum.4.own
  93.3 8.1 %collective-permute-start.1 = (bf16[144,256]{1,0:T(8,128)(2,1)}, bf16[144,256]{1,0:T(8,128)(2,1)}, u32[]{:S(2)}, u32[]{:S(2)}) collective-permute-start(bf16[144,256]{1,0:T(8,128)(2,1)} %ring_sum.4.own), channel_id=1, source_target_pairs={{0,2},{1,3},{2,0},{3,1},{4,6},{5,7},{6,4},{7,5},{8,10},{9,11},{10,... | collective-permute-start | bytes 221192 | tf_op jit(solution)/shard_map/ppermute | solution.py:266
  104.3 7.7 %all-to-all-start.6 = ((f32[32,8,128]{2,1,0:T(8,128)}), f32[32,8,128]{2,1,0:T(8,128)}, u32[]{:S(2)}, u32[]{:S(2)}) async-start(f32[32,8,128]{2,1,0:T(8,128)} %copy-done.22), calls=%async_computation.6 | async-start | bytes 262144 | tf_op jit(solution)/shard_map/all_to_all | solution.py:37
  112.1 2.3 dynamic-slice_bitcast_fusion.1
  114.4 2.3 collective-permute-start.2
  118.6 6.9 %all-to-all-done.6.refs_0_ = f32[32,8,128]{2,1,0:T(8,128)} async-done(((f32[32,8,128]{2,1,0:T(8,128)}), f32[32,8,128]{2,1,0:T(8,128)}, u32[]{:S(2)}, u32[]{:S(2)}) %all-to-all-start.6) | async-done | bytes 131104 | tf_op jit(solution)/shard_map/all_to_all | solution.py:37
  125.5 4.1 %all-to-all-start.1 = ((bf16[8,128,256]{2,1,0:T(8,128)(2,1)}), bf16[8,128,256]{2,1,0:T(8,128)(2,1)}, u32[]{:S(2)}, u32[]{:S(2)}) async-start(bf16[8,128,256]{2,1,0:T(8,128)(2,1)} %copy-done.15), calls=%async_computation.1 | async-start | bytes 1048576 | tf_op jit(solution)/shard_map/all_to_all | solution.py:37
  133.8 2.5 collective-permute-start.12
  136.3 5.3 %collective-permute-done.12.refs_0_ = bf16[128,256]{1,0:T(8,128)(2,1)S(1)} collective-permute-done((bf16[128,256]{1,0:T(8,128)(2,1)S(1)}, bf16[128,256]{1,0:T(8,128)(2,1)S(1)}, u32[]{:S(2)}, u32[]{:S(2)}) %collective-permute-start.12) | collective-permute-done | bytes 65568 | tf_op jit(solution)/shard_map/ppermute | solution.py:43
  146.9 2.7 collective-permute-start.13
  152.0 6.6 %all-to-all-start.7 = ((bf16[8,128,256]{2,1,0:T(8,128)(2,1)}), bf16[8,128,256]{2,1,0:T(8,128)(2,1)}, u32[]{:S(2)}, u32[]{:S(2)}) async-start(bf16[8,128,256]{2,1,0:T(8,128)(2,1)} %copy-done.13), calls=%async_computation.7 | async-start | bytes 1048576 | tf_op jit(solution)/shard_map/all_to_all | solution.py:37
  160.3 2.4 forward_product.2
  162.6 2.6 collective-permute-start.3
  166.2 1.9 collective-permute-start.4
  168.1 3.5 %collective-permute-done.4.refs_0_ = bf16[128,256]{1,0:T(8,128)(2,1)S(1)} collective-permute-done((bf16[128,256]{1,0:T(8,128)(2,1)S(1)}, bf16[128,256]{1,0:T(8,128)(2,1)S(1)}, u32[]{:S(2)}, u32[]{:S(2)}) %collective-permute-start.4) | collective-permute-done | bytes 65568 | tf_op jit(solution)/shard_map/ppermute | solution.py:43
  172.9 3.0 %collective-permute-start.5 = (bf16[8,144,256]{2,1,0:T(8,128)(2,1)S(1)}, bf16[8,144,256]{2,1,0:T(8,128)(2,1)S(1)}, u32[]{:S(2)}, u32[]{:S(2)}) collective-permute-start(bf16[8,144,256]{2,1,0:T(8,128)(2,1)S(1)} %get-tuple-element.38), channel_id=1, source_target_pairs={{0,1},{1,0},{2,3},{3,2},{4,5},{5,4},{6,7},{7,6},{8,9},{9,8},{10,11... | collective-permute-start | bytes 1769480 | tf_op jit(solution)/shard_map/ppermute | solution.py:263
  175.9 1.6 collective-permute-done.5.other
  178.5 6.9 %all-to-all-start.2 = ((bf16[8,144,256]{2,1,0:T(8,128)(2,1)}), bf16[8,144,256]{2,1,0:T(8,128)(2,1)}, u32[]{:S(2)}, u32[]{:S(2)}) async-start(bf16[8,144,256]{2,1,0:T(8,128)(2,1)} %copy-done.12), calls=%async_computation.2 | async-start | bytes 1179648 | tf_op jit(solution)/shard_map/all_to_all | solution.py:37
  186.5 3.5 %collective-permute-start.14 = (bf16[128,256]{1,0:T(8,128)(2,1)S(1)}, bf16[128,256]{1,0:T(8,128)(2,1)S(1)}, u32[]{:S(2)}, u32[]{:S(2)}) collective-permute-start(bf16[128,256]{1,0:T(8,128)(2,1)S(1)} %ring_sum.7.own), channel_id=1, source_target_pairs={{0,2},{1,3},{2,0},{3,1},{4,6},{5,7},{6,4},{7,5},{8,10},{9,11},{10,... | collective-permute-start | bytes 196616 | tf_op jit(solution)/shard_map/ppermute | solution.py:266
  190.0 5.5 %collective-permute-done.14.other = bf16[128,256]{1,0:T(8,128)(2,1)S(1)} collective-permute-done((bf16[128,256]{1,0:T(8,128)(2,1)S(1)}, bf16[128,256]{1,0:T(8,128)(2,1)S(1)}, u32[]{:S(2)}, u32[]{:S(2)}) %collective-permute-start.14) | collective-permute-done | bytes 65568 | tf_op jit(solution)/shard_map/ppermute | solution.py:266
  196.4 8.5 %all-to-all-done.2.pieces = bf16[8,144,256]{2,1,0:T(8,128)(2,1)} async-done(((bf16[8,144,256]{2,1,0:T(8,128)(2,1)}), bf16[8,144,256]{2,1,0:T(8,128)(2,1)}, u32[]{:S(2)}, u32[]{:S(2)}) %all-to-all-start.2) | async-done | bytes 589856 | tf_op jit(solution)/shard_map/all_to_all | solution.py:37
  204.9 4.1 %all-to-all-start.8 = ((bf16[8,128,256]{2,1,0:T(8,128)(2,1)}), bf16[8,128,256]{2,1,0:T(8,128)(2,1)}, u32[]{:S(2)}, u32[]{:S(2)}) async-start(bf16[8,128,256]{2,1,0:T(8,128)(2,1)} %copy-done.14), calls=%async_computation.8 | async-start | bytes 1048576 | tf_op jit(solution)/shard_map/all_to_all | solution.py:37
  210.2 3.5 %collective-permute-start.6 = (bf16[144,256]{1,0:T(8,128)(2,1)S(1)}, bf16[144,256]{1,0:T(8,128)(2,1)S(1)}, u32[]{:S(2)}, u32[]{:S(2)}) collective-permute-start(bf16[144,256]{1,0:T(8,128)(2,1)S(1)} %ring_sum.5.own), channel_id=1, source_target_pairs={{0,2},{1,3},{2,0},{3,1},{4,6},{5,7},{6,4},{7,5},{8,10},{9,11},{10,... | collective-permute-start | bytes 221192 | tf_op jit(solution)/shard_map/ppermute | solution.py:266
  213.6 5.6 %collective-permute-done.6.other = bf16[144,256]{1,0:T(8,128)(2,1)S(1)} collective-permute-done((bf16[144,256]{1,0:T(8,128)(2,1)S(1)}, bf16[144,256]{1,0:T(8,128)(2,1)S(1)}, u32[]{:S(2)}, u32[]{:S(2)}) %collective-permute-start.6) | collective-permute-done | bytes 73760 | tf_op jit(solution)/shard_map/ppermute | solution.py:266
  220.2 6.8 %all-to-all-done.8.blocks = bf16[8,128,256]{2,1,0:T(8,128)(2,1)} async-done(((bf16[8,128,256]{2,1,0:T(8,128)(2,1)}), bf16[8,128,256]{2,1,0:T(8,128)(2,1)}, u32[]{:S(2)}, u32[]{:S(2)}) %all-to-all-start.8) | async-done | bytes 524320 | tf_op jit(solution)/shard_map/all_to_all | solution.py:37
  227.0 4.1 %all-to-all-start.3 = ((bf16[8,128,256]{2,1,0:T(8,128)(2,1)}), bf16[8,128,256]{2,1,0:T(8,128)(2,1)}, u32[]{:S(2)}, u32[]{:S(2)}) async-start(bf16[8,128,256]{2,1,0:T(8,128)(2,1)} %copy-done.16), calls=%async_computation.3 | async-start | bytes 1048576 | tf_op jit(solution)/shard_map/all_to_all | solution.py:37
  231.2 2.4 backward_product.3
  233.6 2.4 collective-permute-start.15
  237.7 11.3 %all-to-all-done.3.blocks = bf16[8,128,256]{2,1,0:T(8,128)(2,1)} async-done(((bf16[8,128,256]{2,1,0:T(8,128)(2,1)}), bf16[8,128,256]{2,1,0:T(8,128)(2,1)}, u32[]{:S(2)}, u32[]{:S(2)}) %all-to-all-start.3) | async-done | bytes 524320 | tf_op jit(solution)/shard_map/all_to_all | solution.py:37
  249.1 4.0 %all-to-all-start.9 = ((f32[32,8,128]{2,1,0:T(8,128)}), f32[32,8,128]{2,1,0:T(8,128)S(1)}, u32[]{:S(2)}, u32[]{:S(2)}) async-start(f32[32,8,128]{2,1,0:T(8,128)} %get-tuple-element.57), calls=%async_computation.9 | async-start | bytes 262144 | tf_op jit(solution)/shard_map/all_to_all | solution.py:37
  254.7 2.4 forward_product.3
  257.1 2.3 collective-permute-start.7
  261.0 5.5 %all-to-all-done.9.refs_0_ = f32[32,8,128]{2,1,0:T(8,128)S(1)} async-done(((f32[32,8,128]{2,1,0:T(8,128)}), f32[32,8,128]{2,1,0:T(8,128)S(1)}, u32[]{:S(2)}, u32[]{:S(2)}) %all-to-all-start.9) | async-done | bytes 131104 | tf_op jit(solution)/shard_map/all_to_all | solution.py:37
  (123 shorter events, 42.5 us)
Async XLA Ops:
  1.5 1.6 copy-start.1
  8.1 42.9 %copy-start.32 = (bf16[128,256]{1,0:T(8,128)(2,1)}, bf16[128,256]{1,0:T(8,128)(2,1)S(1)}, u32[]{:S(2)}) copy-start(bf16[128,256]{1,0:T(8,128)(2,1)S(1)} %get-tuple-element.41.g) | copy-start | bytes 196612
  8.1 4.2 %collective-permute-start.8 = (bf16[8,144,256]{2,1,0:T(8,128)(2,1)S(1)}, bf16[8,144,256]{2,1,0:T(8,128)(2,1)S(1)}, u32[]{:S(2)}, u32[]{:S(2)}) collective-permute-start(bf16[8,144,256]{2,1,0:T(8,128)(2,1)S(1)} %get-tuple-element.43), channel_id=1, source_target_pairs={{0,1},{1,0},{2,3},{3,2},{4,5},{5,4},{6,7},{7,6},{8,9},{9,8},{10,11... | collective-permute-start | bytes 1769480 | tf_op jit(solution)/shard_map/ppermute | solution.py:263
  12.3 42.8 %copy-start = (bf16[1,256,4096]{2,1,0:T(8,128)(2,1)S(1)}, bf16[1,256,4096]{2,1,0:T(8,128)(2,1)}, u32[]{:S(2)}) copy-start(bf16[1,256,4096]{2,1,0:T(8,128)(2,1)} %param.13) | copy-start | bytes 6291460
  12.3 42.8 %copy-start.7 = (bf16[1,8,64,256]{3,2,1,0:T(8,128)(2,1)S(1)}, bf16[1,8,64,256]{3,2,1,0:T(8,128)(2,1)}, u32[]{:S(2)}) copy-start(bf16[1,8,64,256]{3,2,1,0:T(8,128)(2,1)} %param.21) | copy-start | bytes 786436
  12.3 42.8 %copy-start.26 = (bf16[1,128,256]{2,1,0:T(8,128)(2,1)S(1)}, bf16[1,128,256]{2,1,0:T(8,128)(2,1)}, u32[]{:S(2)}) copy-start(bf16[1,128,256]{2,1,0:T(8,128)(2,1)} %param.16) | copy-start | bytes 196612
  12.3 42.8 %copy-start.35 = (f32[1,256]{1,0:T(1,128)S(1)}, f32[1,256]{1,0:T(1,128)}, u32[]{:S(2)}) copy-start(f32[1,256]{1,0:T(1,128)} %gain.7) | copy-start | bytes 3076
  12.3 42.9 %copy-start.39 = (s32[1,2,2]{2,1,0:T(2,128)S(1)}, s32[1,2,2]{2,1,0:T(2,128)}, u32[]{:S(2)}) copy-start(s32[1,2,2]{2,1,0:T(2,128)} %param.24) | copy-start | bytes 52
  37.6 12.5 %collective-permute-start.9 = (bf16[144,256]{1,0:T(8,128)(2,1)S(1)}, bf16[144,256]{1,0:T(8,128)(2,1)S(1)}, u32[]{:S(2)}, u32[]{:S(2)}) collective-permute-start(bf16[144,256]{1,0:T(8,128)(2,1)S(1)} %ring_sum.6.own), channel_id=1, source_target_pairs={{0,2},{1,3},{2,0},{3,1},{4,6},{5,7},{6,4},{7,5},{8,10},{9,11},{10,... | collective-permute-start | bytes 221192 | tf_op jit(solution)/shard_map/ppermute | solution.py:266
  50.9 50.4 %copy-start.19 = (f32[16,128]{1,0:T(8,128)}, f32[16,128]{1,0:T(8,128)S(1)}, u32[]{:S(2)}) copy-start(f32[16,128]{1,0:T(8,128)S(1)} %get-tuple-element.47.stats) | copy-start | bytes 24580
  50.9 19.1 %all-to-all-start.5 = ((bf16[8,128,256]{2,1,0:T(8,128)(2,1)}), bf16[8,128,256]{2,1,0:T(8,128)(2,1)}, u32[]{:S(2)}, u32[]{:S(2)}) async-start(bf16[8,128,256]{2,1,0:T(8,128)(2,1)} %get-tuple-element.44), calls=%async_computation.5 | async-start | bytes 1048576 | tf_op jit(solution)/shard_map/all_to_all | solution.py:37
  58.6 7.5 %collective-permute-start = (bf16[8,144,256]{2,1,0:T(8,128)(2,1)}, bf16[8,144,256]{2,1,0:T(8,128)(2,1)}, u32[]{:S(2)}, u32[]{:S(2)}) collective-permute-start(bf16[8,144,256]{2,1,0:T(8,128)(2,1)} %get-tuple-element.33), channel_id=1, source_target_pairs={{0,1},{1,0},{2,3},{3,2},{4,5},{5,4},{6,7},{7,6},{8,9},{9,8},{10,11... | collective-permute-start | bytes 1769480 | tf_op jit(solution)/shard_map/ppermute | solution.py:263
  63.1 3.0 %copy-start.18 = (bf16[8,144,256]{2,1,0:T(8,128)(2,1)S(1)}, bf16[8,144,256]{2,1,0:T(8,128)(2,1)}, u32[]{:S(2)}) copy-start(bf16[8,144,256]{2,1,0:T(8,128)(2,1)} %copy-done.17) | copy-start | bytes 1769476
  64.2 10.7 %collective-permute-start.10 = (bf16[256,2048]{1,0:T(8,128)(2,1)}, bf16[256,2048]{1,0:T(8,128)(2,1)S(1)}, u32[]{:S(2)}, u32[]{:S(2)}) collective-permute-start(bf16[256,2048]{1,0:T(8,128)(2,1)} %dynamic-slice_bitcast_fusion), channel_id=1, source_target_pairs={{0,1},{1,0},{2,3},{3,2},{4,5},{5,4},{6,7},{7,6},{8,9},{9,8},{10,11... | collective-permute-start | bytes 3145736 | tf_op jit(solution)/shard_map/ppermute | solution.py:292
  70.0 21.5 %all-to-all-start = ((bf16[8,144,256]{2,1,0:T(8,128)(2,1)}), bf16[8,144,256]{2,1,0:T(8,128)(2,1)}, u32[]{:S(2)}, u32[]{:S(2)}) async-start(bf16[8,144,256]{2,1,0:T(8,128)(2,1)} %copy-done.11), calls=%async_computation | async-start | bytes 1179648 | tf_op jit(solution)/shard_map/all_to_all | solution.py:37
  74.9 26.5 %copy-start.10 = (bf16[1,2,128,256]{3,2,1,0:T(8,128)(2,1)S(1)}, bf16[1,2,128,256]{3,2,1,0:T(8,128)(2,1)}, u32[]{:S(2)}) copy-start(bf16[1,2,128,256]{3,2,1,0:T(8,128)(2,1)} %param.20) | copy-start | bytes 393220
  78.0 23.4 %collective-permute-start.11 = (f32[128,256]{1,0:T(8,128)}, f32[128,256]{1,0:T(8,128)}, u32[]{:S(2)}, u32[]{:S(2)}) collective-permute-start(f32[128,256]{1,0:T(8,128)} %get-tuple-element.46), channel_id=1, source_target_pairs={{0,1},{1,0},{2,3},{3,2},{4,5},{5,4},{6,7},{7,6},{8,9},{9,8},{10,11... | collective-permute-start | bytes 393224 | tf_op jit(solution)/shard_map/ppermute | solution.py:383
  93.3 23.5 %collective-permute-start.1 = (bf16[144,256]{1,0:T(8,128)(2,1)}, bf16[144,256]{1,0:T(8,128)(2,1)}, u32[]{:S(2)}, u32[]{:S(2)}) collective-permute-start(bf16[144,256]{1,0:T(8,128)(2,1)} %ring_sum.4.own), channel_id=1, source_target_pairs={{0,2},{1,3},{2,0},{3,1},{4,6},{5,7},{6,4},{7,5},{8,10},{9,11},{10,... | collective-permute-start | bytes 221192 | tf_op jit(solution)/shard_map/ppermute | solution.py:266
  104.3 21.2 %all-to-all-start.6 = ((f32[32,8,128]{2,1,0:T(8,128)}), f32[32,8,128]{2,1,0:T(8,128)}, u32[]{:S(2)}, u32[]{:S(2)}) async-start(f32[32,8,128]{2,1,0:T(8,128)} %copy-done.22), calls=%async_computation.6 | async-start | bytes 262144 | tf_op jit(solution)/shard_map/all_to_all | solution.py:37
  112.1 29.5 %copy-start.6 = (bf16[1,8,64,256]{3,2,1,0:T(8,128)(2,1)S(1)}, bf16[1,8,64,256]{3,2,1,0:T(8,128)(2,1)}, u32[]{:S(2)}) copy-start(bf16[1,8,64,256]{3,2,1,0:T(8,128)(2,1)} %param.22) | copy-start | bytes 786436
  114.4 44.2 %collective-permute-start.2 = (bf16[2048,256]{1,0:T(8,128)(2,1)}, bf16[2048,256]{1,0:T(8,128)(2,1)}, u32[]{:S(2)}, u32[]{:S(2)}) collective-permute-start(bf16[2048,256]{1,0:T(8,128)(2,1)} %dynamic-slice_bitcast_fusion.1), channel_id=1, source_target_pairs={{0,1},{1,0},{2,3},{3,2},{4,5},{5,4},{6,7},{7,6},{8,9},{9,8},{10,11... | collective-permute-start | bytes 3145736 | tf_op jit(solution)/shard_map/ppermute | solution.py:295
  125.5 26.5 %all-to-all-start.1 = ((bf16[8,128,256]{2,1,0:T(8,128)(2,1)}), bf16[8,128,256]{2,1,0:T(8,128)(2,1)}, u32[]{:S(2)}, u32[]{:S(2)}) async-start(bf16[8,128,256]{2,1,0:T(8,128)(2,1)} %copy-done.15), calls=%async_computation.1 | async-start | bytes 1048576 | tf_op jit(solution)/shard_map/all_to_all | solution.py:37
  133.8 7.7 %collective-permute-start.12 = (bf16[128,256]{1,0:T(8,128)(2,1)S(1)}, bf16[128,256]{1,0:T(8,128)(2,1)S(1)}, u32[]{:S(2)}, u32[]{:S(2)}) collective-permute-start(bf16[128,256]{1,0:T(8,128)(2,1)S(1)} %backward_end.2), channel_id=1, source_target_pairs={{32,0},{64,32},{96,64},{128,96},{160,128},{192,160},{224,192},{256... | collective-permute-start | bytes 196616 | tf_op jit(solution)/shard_map/ppermute | solution.py:43
  141.6 1.6 copy-start.2
  146.9 4.2 %collective-permute-start.13 = (bf16[8,128,256]{2,1,0:T(8,128)(2,1)S(1)}, bf16[8,128,256]{2,1,0:T(8,128)(2,1)S(1)}, u32[]{:S(2)}, u32[]{:S(2)}) collective-permute-start(bf16[8,128,256]{2,1,0:T(8,128)(2,1)S(1)} %get-tuple-element.52), channel_id=1, source_target_pairs={{0,1},{1,0},{2,3},{3,2},{4,5},{5,4},{6,7},{7,6},{8,9},{9,8},{10,11... | collective-permute-start | bytes 1572872 | tf_op jit(solution)/shard_map/ppermute | solution.py:263
  152.0 26.5 %all-to-all-start.7 = ((bf16[8,128,256]{2,1,0:T(8,128)(2,1)}), bf16[8,128,256]{2,1,0:T(8,128)(2,1)}, u32[]{:S(2)}, u32[]{:S(2)}) async-start(bf16[8,128,256]{2,1,0:T(8,128)(2,1)} %copy-done.13), calls=%async_computation.7 | async-start | bytes 1048576 | tf_op jit(solution)/shard_map/all_to_all | solution.py:37
  158.6 1.6 copy-start.3
  160.2 5.9 %copy-start.29 = (bf16[128,256]{1,0:T(8,128)(2,1)S(1)}, bf16[128,256]{1,0:T(8,128)(2,1)}, u32[]{:S(2)}) copy-start(bf16[128,256]{1,0:T(8,128)(2,1)} %copy-done.28) | copy-start | bytes 196612
  160.2 11.4 %copy-start.8 = (bf16[1,8,64,256]{3,2,1,0:T(8,128)(2,1)S(1)}, bf16[1,8,64,256]{3,2,1,0:T(8,128)(2,1)}, u32[]{:S(2)}) copy-start(bf16[1,8,64,256]{3,2,1,0:T(8,128)(2,1)} %param.21) | copy-start | bytes 786436
  160.2 11.4 %copy-start.34 = (bf16[1,128,256]{2,1,0:T(8,128)(2,1)S(1)}, bf16[1,128,256]{2,1,0:T(8,128)(2,1)}, u32[]{:S(2)}) copy-start(bf16[1,128,256]{2,1,0:T(8,128)(2,1)} %refs_1_.2) | copy-start | bytes 196612
  160.2 11.4 %copy-start.37 = (f32[1,256]{1,0:T(1,128)S(1)}, f32[1,256]{1,0:T(1,128)}, u32[]{:S(2)}) copy-start(f32[1,256]{1,0:T(1,128)} %gain.7) | copy-start | bytes 3076
  160.2 11.4 %copy-start.40 = (s32[1,2,2]{2,1,0:T(2,128)S(1)}, s32[1,2,2]{2,1,0:T(2,128)}, u32[]{:S(2)}) copy-start(s32[1,2,2]{2,1,0:T(2,128)} %param.24) | copy-start | bytes 52
  162.6 3.5 %collective-permute-start.3 = (f32[128,256]{1,0:T(8,128)S(1)}, f32[128,256]{1,0:T(8,128)S(1)}, u32[]{:S(2)}, u32[]{:S(2)}) collective-permute-start(f32[128,256]{1,0:T(8,128)S(1)} %get-tuple-element.35), channel_id=1, source_target_pairs={{0,1},{1,0},{2,3},{3,2},{4,5},{5,4},{6,7},{7,6},{8,9},{9,8},{10,11... | collective-permute-start | bytes 393224 | tf_op jit(solution)/shard_map/ppermute | solution.py:362
  166.2 5.4 %collective-permute-start.4 = (bf16[128,256]{1,0:T(8,128)(2,1)S(1)}, bf16[128,256]{1,0:T(8,128)(2,1)S(1)}, u32[]{:S(2)}, u32[]{:S(2)}) collective-permute-start(bf16[128,256]{1,0:T(8,128)(2,1)S(1)} %forward_end.2), channel_id=1, source_target_pairs={{0,32},{32,64},{64,96},{96,128},{128,160},{160,192},{192,224},{224... | collective-permute-start | bytes 196616 | tf_op jit(solution)/shard_map/ppermute | solution.py:43
  172.9 4.6 %collective-permute-start.5 = (bf16[8,144,256]{2,1,0:T(8,128)(2,1)S(1)}, bf16[8,144,256]{2,1,0:T(8,128)(2,1)S(1)}, u32[]{:S(2)}, u32[]{:S(2)}) collective-permute-start(bf16[8,144,256]{2,1,0:T(8,128)(2,1)S(1)} %get-tuple-element.38), channel_id=1, source_target_pairs={{0,1},{1,0},{2,3},{3,2},{4,5},{5,4},{6,7},{7,6},{8,9},{9,8},{10,11... | collective-permute-start | bytes 1769480 | tf_op jit(solution)/shard_map/ppermute | solution.py:263
  178.5 26.4 %all-to-all-start.2 = ((bf16[8,144,256]{2,1,0:T(8,128)(2,1)}), bf16[8,144,256]{2,1,0:T(8,128)(2,1)}, u32[]{:S(2)}, u32[]{:S(2)}) async-start(bf16[8,144,256]{2,1,0:T(8,128)(2,1)} %copy-done.12), calls=%async_computation.2 | async-start | bytes 1179648 | tf_op jit(solution)/shard_map/all_to_all | solution.py:37
  186.5 9.0 %collective-permute-start.14 = (bf16[128,256]{1,0:T(8,128)(2,1)S(1)}, bf16[128,256]{1,0:T(8,128)(2,1)S(1)}, u32[]{:S(2)}, u32[]{:S(2)}) collective-permute-start(bf16[128,256]{1,0:T(8,128)(2,1)S(1)} %ring_sum.7.own), channel_id=1, source_target_pairs={{0,2},{1,3},{2,0},{3,1},{4,6},{5,7},{6,4},{7,5},{8,10},{9,11},{10,... | collective-permute-start | bytes 196616 | tf_op jit(solution)/shard_map/ppermute | solution.py:266
  204.9 22.1 %all-to-all-start.8 = ((bf16[8,128,256]{2,1,0:T(8,128)(2,1)}), bf16[8,128,256]{2,1,0:T(8,128)(2,1)}, u32[]{:S(2)}, u32[]{:S(2)}) async-start(bf16[8,128,256]{2,1,0:T(8,128)(2,1)} %copy-done.14), calls=%async_computation.8 | async-start | bytes 1048576 | tf_op jit(solution)/shard_map/all_to_all | solution.py:37
  210.2 9.1 %collective-permute-start.6 = (bf16[144,256]{1,0:T(8,128)(2,1)S(1)}, bf16[144,256]{1,0:T(8,128)(2,1)S(1)}, u32[]{:S(2)}, u32[]{:S(2)}) collective-permute-start(bf16[144,256]{1,0:T(8,128)(2,1)S(1)} %ring_sum.5.own), channel_id=1, source_target_pairs={{0,2},{1,3},{2,0},{3,1},{4,6},{5,7},{6,4},{7,5},{8,10},{9,11},{10,... | collective-permute-start | bytes 221192 | tf_op jit(solution)/shard_map/ppermute | solution.py:266
  227.0 22.1 %all-to-all-start.3 = ((bf16[8,128,256]{2,1,0:T(8,128)(2,1)}), bf16[8,128,256]{2,1,0:T(8,128)(2,1)}, u32[]{:S(2)}, u32[]{:S(2)}) async-start(bf16[8,128,256]{2,1,0:T(8,128)(2,1)} %copy-done.16), calls=%async_computation.3 | async-start | bytes 1048576 | tf_op jit(solution)/shard_map/all_to_all | solution.py:37
  231.1 5.8 %copy-start.21 = (f32[16,128]{1,0:T(8,128)S(1)}, f32[16,128]{1,0:T(8,128)}, u32[]{:S(2)}) copy-start(f32[16,128]{1,0:T(8,128)} %copy-done.19) | copy-start | bytes 24580
  231.1 5.8 %copy-start.38 = (f32[1,256]{1,0:T(1,128)S(1)}, f32[1,256]{1,0:T(1,128)}, u32[]{:S(2)}) copy-start(f32[1,256]{1,0:T(1,128)} %gain.7) | copy-start | bytes 3076
  231.2 5.8 %copy-start.44 = (f32[1,256]{1,0:T(1,128)S(1)}, f32[1,256]{1,0:T(1,128)}, u32[]{:S(2)}) copy-start(f32[1,256]{1,0:T(1,128)} %copy-done.43) | copy-start | bytes 3076
  233.6 3.4 %collective-permute-start.15 = (f32[128,256]{1,0:T(8,128)S(1)}, f32[128,256]{1,0:T(8,128)S(1)}, u32[]{:S(2)}, u32[]{:S(2)}) collective-permute-start(f32[128,256]{1,0:T(8,128)S(1)} %get-tuple-element.54), channel_id=1, source_target_pairs={{0,1},{1,0},{2,3},{3,2},{4,5},{5,4},{6,7},{7,6},{8,9},{9,8},{10,11... | collective-permute-start | bytes 393224 | tf_op jit(solution)/shard_map/ppermute | solution.py:383
  249.1 17.4 %all-to-all-start.9 = ((f32[32,8,128]{2,1,0:T(8,128)}), f32[32,8,128]{2,1,0:T(8,128)S(1)}, u32[]{:S(2)}, u32[]{:S(2)}) async-start(f32[32,8,128]{2,1,0:T(8,128)} %get-tuple-element.57), calls=%async_computation.9 | async-start | bytes 262144 | tf_op jit(solution)/shard_map/all_to_all | solution.py:37
  253.1 1.6 copy-start.4
  254.7 11.8 %copy-start.31 = (bf16[128,256]{1,0:T(8,128)(2,1)S(1)}, bf16[128,256]{1,0:T(8,128)(2,1)}, u32[]{:S(2)}) copy-start(bf16[128,256]{1,0:T(8,128)(2,1)} %copy-done.30) | copy-start | bytes 196612
  257.1 3.2 %collective-permute-start.7 = (f32[128,256]{1,0:T(8,128)S(1)}, f32[128,256]{1,0:T(8,128)S(1)}, u32[]{:S(2)}, u32[]{:S(2)}) collective-permute-start(f32[128,256]{1,0:T(8,128)S(1)} %get-tuple-element.40), channel_id=1, source_target_pairs={{0,1},{1,0},{2,3},{3,2},{4,5},{5,4},{6,7},{7,6},{8,9},{9,8},{10,11... | collective-permute-start | bytes 393224 | tf_op jit(solution)/shard_map/ppermute | solution.py:362
  (22 other events, 16.7 us)

commit v2 on v1

--- a/solution.py
+++ b/solution.py
@@ -29,8 +29,16 @@
     return [(index, index ^ 2) for index in range(4 * RING)]
 
 
+def near_pairs():
+    return [(index, index ^ 4) for index in range(4 * RING)]
+
+
 def rings():
     return [[4 * y + rest for y in range(RING)] for rest in range(4)]
+
+
+def half_rings():
+    return [[4 * y + rest for y in range(odd, RING, 2)] for odd in range(2) for rest in range(4)]
 
 
 def swapped(value, groups=None):
@@ -48,6 +56,8 @@
 
     def spec(position, operand):
         if position in blocks:
+            if blocks[position] is None:
+                return pl.BlockSpec(memory_space=pl.ANY)
             shape, index_map = blocks[position]
             return pl.BlockSpec(shape, index_map)
         rank = len(operand.shape)
@@ -55,7 +65,7 @@
 
     moved = 0
     for position, operand in enumerate(operands):
-        shape = blocks[position][0] if position in blocks else operand.shape
+        shape = (blocks[position] or ((0,),))[0] if position in blocks else operand.shape
         size = 1
         for length in shape:
             size *= length
@@ -128,6 +138,10 @@
     return jnp.where(meta[0] == edge, refs[1][0].astype(F32), refs[0][...].astype(F32))
 
 
+def paired(j, odd):
+    return 2 * (j % (RING // 2)) + (odd if j < RING // 2 else 1 - odd)
+
+
 def forward_start(tick, messages, ids, meta, exponents, *refs):
     given, refs = refs[:messages], refs[messages:]
     first, second, gain, weight, x_out, keep, send = refs
@@ -137,28 +151,18 @@
     scaled = (x * gain[...]).astype(BF16)
     total = across(jnp.sum(x * x, axis=1, keepdims=True))
     stats = split_stats(jnp.broadcast_to(total, (STATS, ROWS)))
-    core = meta[3]
+    odd, core = meta[1] % 2, meta[3]
     for out, half in ((send, 1 - core), (keep, core)):
         for j in range(RING):
-            at = pl.multiple_of((half * RING + j) * WIDTH, WIDTH)
+            at = pl.multiple_of((half * RING + paired(j, odd)) * WIDTH, WIDTH)
             part = jnp.dot(scaled, weight[:, pl.ds(at, WIDTH)], preferred_element_type=F32)
             out[j, :ROWS] = part.astype(BF16)
             out[j, ROWS:] = stats
 
 
 def backward_start(tick, messages, last, ids, meta, exponents, *refs):
-    given, refs = refs[:messages], refs[messages:]
-    if tick == 0:
-        first, second, weight, saved, g_out, keep, send = refs
-        rows = []
-        for k in range(2):
-            value = saved[k].astype(F32)
-            rows.append(jnp.broadcast_to(across(jnp.sum(value * value, axis=1, keepdims=True)), (STATS // 2, ROWS)))
-        stats = split_stats(jnp.concatenate(rows, axis=0))
-    else:
-        first, second, weight, g_out, keep, send = refs
-        stats = None
-    g = decoded(chosen(meta, last, given), first, second, exponents, tick).astype(BF16)
+    given, (first, second, weight, g_out, keep, send) = refs[:messages], refs[messages:]
+    g = decoded(chosen(meta, last, given), first, second, exponents, tick)
     g_out[...] = g
     core = meta[3]
     for out, half in ((send, 1 - core), (keep, core)):
@@ -167,29 +171,31 @@
             part = lax.dot_general(
                 g, weight[pl.ds(at, WIDTH), :], (((1,), (1,)), ((), ())), preferred_element_type=F32
             )
-            out[j, :ROWS] = part.astype(BF16)
-            if stats is not None:
-                out[j, ROWS:] = stats
-
-
-def core_sum(keep, other, out):
-    extra = keep.shape[1] > ROWS
-    if extra:
-        stats = split_stats(joined_stats(keep[0, ROWS:]) + joined_stats(other[0, ROWS:]))
+            out[j] = part.astype(BF16)
+
+
+def tall_sum(mine, other, _, *outs):
+    stats = split_stats(joined_stats(mine[0, ROWS:]) + joined_stats(other[0, ROWS:]))
+    each = outs[0].shape[0]
+    for j in range(mine.shape[0]):
+        out, at = outs[j // each], j % each
+        out[at, :ROWS] = (mine[j, :ROWS].astype(F32) + other[j, :ROWS].astype(F32)).astype(BF16)
+        out[at, ROWS:] = stats
+
+
+def low_sum(mine, other, _, out):
     for j in range(RING):
-        out[j, :ROWS] = (keep[j, :ROWS].astype(F32) + other[j, :ROWS].astype(F32)).astype(BF16)
-        if extra:
-            out[j, ROWS:] = stats
+        out[j] = (mine[j].astype(F32) + other[j].astype(F32)).astype(BF16)
 
 
 def ring_sum(pieces, out):
     total = pieces[0, :ROWS].astype(F32)
-    for j in range(1, RING):
+    for j in range(1, pieces.shape[0]):
         total = total + pieces[j, :ROWS].astype(F32)
     out[:ROWS] = total.astype(BF16)
     if out.shape[0] > ROWS:
         stats = joined_stats(pieces[0, ROWS:])
-        for j in range(1, RING):
+        for j in range(1, pieces.shape[0]):
             stats = stats + joined_stats(pieces[j, ROWS:])
         out[ROWS:] = split_stats(stats)
 
@@ -201,19 +207,19 @@
     out[...] = jnp.broadcast_to((down(factor) * value).astype(BF16)[None], out.shape)
 
 
-def backward_share(own, other, out, *stats):
-    value = (own[:ROWS].astype(F32) + other[:ROWS].astype(F32)).astype(BF16)
+def backward_share(own, other, out):
+    value = (own[...].astype(F32) + other[...].astype(F32)).astype(BF16)
     out[...] = jnp.broadcast_to(value[None], out.shape)
-    if stats:
-        stats[0][...] = joined_stats(own[ROWS:]) + joined_stats(other[ROWS:])
-
-
-def forward_product(meta, blocks, own_weight, other_weight, mine, others):
+
+
+def forward_product(meta, near, far, own_weight, other_weight, mine, others):
+    odd, half = meta[1] % 2, RING // 2
     for weight, out in ((other_weight, others), (own_weight, mine)):
         total = jnp.zeros((ROWS, WIDTH), F32)
         for j in range(RING):
-            at = j * WIDTH
-            total = total + jnp.dot(blocks[j], weight[pl.ds(at, WIDTH), :], preferred_element_type=F32)
+            at = pl.multiple_of(paired(j, odd) * WIDTH, WIDTH)
+            block = near[j] if j < half else far[j - half]
+            total = total + jnp.dot(block, weight[pl.ds(at, WIDTH), :], preferred_element_type=F32)
         out[...] = total
 
 
@@ -232,38 +238,59 @@
     out[...] = (x[...].astype(F32) + (mine[...] + other[...])).astype(BF16)
 
 
-def saved_scale(stats, tick):
-    at = tick * (STATS // 2)
-    return down(lax.rsqrt(stats[at : at + 1] / D + EPSILON))
-
-
-def backward_middle(tick, mine, other, saved, gain, stats, *refs):
-    before, (scaled_grad, row_dot, gain_out) = refs[:-3], refs[-3:]
+def backward_middle(tick, mine, other, saved, gain, scaled_grad, dots):
     value = mine[...] + other[...]
     scaled_grad[...] = value
-    kept = saved[0].astype(F32)
-    dots = jnp.sum(kept * gain[...] * value, axis=1, keepdims=True)
-    row_dot[...] = jnp.broadcast_to(across(dots), row_dot.shape)
-    total = jnp.sum(value * kept * saved_scale(stats, tick), axis=0, keepdims=True)
-    gain_out[...] = total + before[0][...] if before else total
-
-
-def backward_end(tick, g, scaled_grad, saved, gain, stats, *refs):
-    dots, out = refs
-    total = dots[0, 0:1]
+    terms = [saved[tick].astype(F32) * gain[...] * value]
+    if tick == 0:
+        for k in range(2):
+            kept = saved[k].astype(F32)
+            terms.append(kept * kept)
+    rows = [across(jnp.sum(term, axis=1, keepdims=True)) for term in terms]
+    rows.append(jnp.zeros((8 - len(rows), ROWS), F32))
+    dots[...] = jnp.broadcast_to(jnp.concatenate(rows, axis=0)[None], dots.shape)
+
+
+def backward_end(tick, g, scaled_grad, saved, gain, dots, *refs):
+    before, (out, gain_out, *left) = refs[: 2 if tick else 0], refs[2 if tick else 0 :]
+    total = dots[0]
     for j in range(1, dots.shape[0]):
-        total = total + dots[j, 0:1]
-    factor = saved_scale(stats, tick)
+        total = total + dots[j]
+    if tick == 0:
+        squares = total[1:2]
+        left[0][...] = jnp.broadcast_to(total[2:3], left[0].shape)
+    else:
+        squares = before[0][0:1]
+    factor = down(lax.rsqrt(squares / D + EPSILON))
+    kept = saved[tick].astype(F32)
+    sums = jnp.sum(scaled_grad[...] * kept * factor, axis=0, keepdims=True)
+    gain_out[...] = sums + before[1][...] if tick else sums
     value = g[...].astype(F32) + factor * gain[...] * scaled_grad[...]
-    out[...] = (value - saved[0].astype(F32) * (factor * factor * factor) * down(total) / D).astype(BF16)
-
-
-def scattered(keep, send):
-    rows = keep.shape[1]
+    out[...] = (value - kept * (factor * factor * factor) * down(total[0:1]) / D).astype(BF16)
+
+
+def forward_scattered(keep, send, after):
+    half = shape_of(RING // 2, ROWS + STATS, WIDTH)
     other = lax.ppermute(send, "shard", core_pairs())
-    (pieces,) = call(core_sum, "core_sum", [shape_of(RING, rows, WIDTH)], operands=(keep, other))
-    (own,) = call(ring_sum, "ring_sum", [shape_of(rows, WIDTH)], operands=(swapped(pieces, rings()),))
-    return own, lax.ppermute(own, "shard", z_pairs())
+    mine, theirs = call(tall_sum, "core_sum", [half, half], operands=(keep, other, after), blocks={2: None})
+    other = lax.ppermute(theirs, "shard", near_pairs())
+    (pieces,) = call(tall_sum, "near_sum", [half], operands=(mine, other, after), blocks={2: None})
+    pieces = swapped(pieces, half_rings())
+    (own,) = call(ring_sum, "ring_sum", [shape_of(ROWS + STATS, WIDTH)], operands=(pieces,))
+    return own
+
+
+def backward_scattered(keep, send, after):
+    other = lax.ppermute(send, "shard", core_pairs())
+    (pieces,) = call(
+        low_sum, "low_sum", [shape_of(RING, ROWS, WIDTH)], operands=(keep, other, after), blocks={2: None}
+    )
+    (own,) = call(ring_sum, "low_ring_sum", [shape_of(ROWS, WIDTH)], operands=(swapped(pieces, rings()),))
+    return own, pieces
+
+
+def over_z(own):
+    return lax.ppermute(own, "shard", z_pairs())
 
 
 def shards(
@@ -309,7 +336,7 @@
         }
 
     forward_message, backward_message = [arriving[0]], [returning[0]]
-    stats = gain_total = None
+    left = ()
     for tick in range(ticks):
         tall = shape_of(RING, ROWS + STATS, WIDTH)
         count = len(forward_message)
@@ -322,28 +349,27 @@
             blocks=base_blocks(count, lambda meta: tick - meta[0] + segments - 1),
             flops=start_flops,
         )
-        low = tall if tick == 0 else shape_of(RING, ROWS, WIDTH)
-        operands = (*backward_message, backward_base[0], backward_base[0], output_local)
+        low = shape_of(RING, ROWS, WIDTH)
         g, back_keep, back_send = call(
             functools.partial(backward_start, tick, count, segments - 1),
             "backward_start",
             [piece, low, low],
             prefetch=(sample_ids, meta, backward_exponents[0]),
-            operands=operands + ((saved,) if tick == 0 else ()),
+            operands=(*backward_message, backward_base[0], backward_base[0], output_local),
             blocks=base_blocks(count, lambda meta: tick + meta[0]),
             flops=start_flops,
         )
-        own, other = scattered(keep, send)
-        back_own, back_other = scattered(back_keep, back_send)
-
+        back_own, pieces = backward_scattered(back_keep, back_send, x if tick == 0 else g)
+        own = forward_scattered(keep, send, pieces if tick == 0 else x)
+
+        copies = shape_of(RING // 2, ROWS, WIDTH)
+        (pre,) = call(forward_share, "forward_share", [copies], operands=(own, over_z(own)))
+        near = swapped(pre, half_rings())
+        far = lax.ppermute(near, "shard", near_pairs())
         copies = shape_of(RING, ROWS, WIDTH)
-        (pre,) = call(forward_share, "forward_share", [copies], operands=(own, other))
-        gathered = swapped(pre, rings())
-        share_outs = [copies] + ([shape_of(STATS, ROWS, dtype=F32)] if tick == 0 else [])
-        value_grad, *given = call(
-            backward_share, "backward_share", share_outs, operands=(back_own, back_other)
-        )
-        stats = given[0] if given else stats
+        (value_grad,) = call(
+            backward_share, "backward_share", [copies], operands=(back_own, over_z(back_own))
+        )
         back_gathered = swapped(value_grad, rings())
 
         mine, others = call(
@@ -351,8 +377,8 @@
             "forward_product",
             [wide, wide],
             prefetch=(meta,),
-            operands=(gathered, output_local, output_other),
-            blocks={1: ((HALF, WIDTH), lambda i, meta: (meta[3], 0))},
+            operands=(near, far, output_local, output_other),
+            blocks={2: ((HALF, WIDTH), lambda i, meta: (meta[3], 0))},
             flops=start_flops,
         )
         (segment_out,) = call(
@@ -373,23 +399,20 @@
             blocks={1: ((WIDTH, HALF), lambda i, meta: (0, meta[3]))},
             flops=start_flops,
         )
-        saved_block = {2: ((1, ROWS, WIDTH), lambda i, tick=tick: (tick, 0, 0))}
-        before = () if gain_total is None else (gain_total,)
-        small = shape_of(4 * RING, 8, ROWS, dtype=F32)
-        scaled_grad, dots, gain_total = call(
+        scaled_grad, dots = call(
             functools.partial(backward_middle, tick),
             "backward_middle",
-            [wide, small, shape_of(1, WIDTH, dtype=F32)],
-            operands=(mine, lax.ppermute(others, "shard", core_pairs()), saved, norm_gain, stats) + before,
-            blocks=saved_block,
-        )
-        (input_grad,) = call(
+            [wide, shape_of(4 * RING, 8, ROWS, dtype=F32)],
+            operands=(mine, lax.ppermute(others, "shard", core_pairs()), saved, norm_gain),
+        )
+        outs = [piece, shape_of(1, WIDTH, dtype=F32)]
+        input_grad, gain_total, *rest = call(
             functools.partial(backward_end, tick),
             "backward_end",
-            [piece],
-            operands=(g, scaled_grad, saved, norm_gain, stats, swapped(dots)),
-            blocks=saved_block,
-        )
+            outs + ([shape_of(8, ROWS, dtype=F32)] if tick == 0 else []),
+            operands=(g, scaled_grad, saved, norm_gain, swapped(dots), *left),
+        )
+        left = (*rest, gain_total)
         if tick + 1 < ticks:
             backward_message = [shifted(input_grad, "segment", -1), cotangents[tick : tick + 1]]
     return (segment_out[None], input_grad[None], gain_total)

time: 269 us -> 304 us (1.13)
  starting transfers between devices: 106 us -> 131 us
  blocking collectives: 25.1 us -> 15.7 us
  local copies, waits for them, and re-layouts: 27.3 us -> 35.5 us
  waiting for transfers between devices: 79.1 us -> 86.8 us
    ppermute x8 -> x12, waiting for transfers between devices: 17.7 us -> 41.9 us  [the longest x4 18 us: over_z(): return lax.ppermute(own, 'shard', z_pairs())]
    all_to_all x9, waiting for transfers between devices: 49.7 us -> 32.6 us  [swapped(): lax.all_to_all(value, 'shard', 0, 0, axis_index_groups=groups, tiled=True)]
    ppermute x8 -> x12, starting transfers between devices: 38.4 us -> 48.7 us  [the longest x4 24.4 us: over_z(): return lax.ppermute(own, 'shard', z_pairs())]
    all_to_all x1, blocking collectives: 25.1 us -> 15.7 us  [swapped(): lax.all_to_all(value, 'shard', 0, 0, axis_index_groups=groups, tiled=True)]
    unnamed x91 -> x109, local copies, waits for them, and re-layouts: 23.8 us -> 32.2 us
    all_to_all x9, starting transfers between devices: 46.8 us -> 54.7 us  [swapped(): lax.all_to_all(value, 'shard', 0, 0, axis_index_groups=groups, tiled=True)]
    ppermute x4, starting transfers between devices: 11.9 us -> 16 us  [shards(): lax.ppermute(others, 'shard', core_pairs())]
    pallas_call x26 -> x28, Pallas kernels: 28.7 us -> 31 us  [call(): pl.pallas_call(kernel, out_shape=outs, grid_spec=pltpu.PrefetchScalarGrid...]
  transfers between devices with their start and end apart: 25 -> 29, of which waited for: 18 -> 18; matrix products, arithmetic and copies ran while one was open for 1% -> 1% of each run, Pallas kernels for 9% -> 9%
where the time goes in v2:
time: 304 us; the launch traced here: 301 us
  starting transfers between devices  131 us (43%)
  waiting for transfers between devices  86.8 us (29%)
  local copies, waits for them, and re-layouts  35.5 us (12%)
  Pallas kernels  31 us (10%)
  blocking collectives  15.7 us (5%)
    all_to_all x9, starting transfers between devices, swapped(): lax.all_to_all(value, 'shard', 0, 0, axis_index_groups=groups, tiled=True)  54.7 us
    all_to_all x9, waiting for transfers between devices, swapped(): lax.all_to_all(value, 'shard', 0, 0, axis_index_groups=groups, tiled=True)  32.6 us
    unnamed x109, local copies, waits for them, and re-layouts  32.2 us
    pallas_call x28, Pallas kernels, call(): pl.pallas_call(kernel, out_shape=outs, grid_spec=pltpu.PrefetchScalarGrid...  31 us
    ppermute x4, starting transfers between devices, over_z(): return lax.ppermute(own, 'shard', z_pairs())  24.4 us
    ppermute x4, waiting for transfers between devices, over_z(): return lax.ppermute(own, 'shard', z_pairs())  18 us
    ppermute x4, starting transfers between devices, shards(): lax.ppermute(others, 'shard', core_pairs())  16 us
    all_to_all x1, blocking collectives, swapped(): lax.all_to_all(value, 'shard', 0, 0, axis_index_groups=groups, tiled=True)  15.7 us
  transfers between devices with their start and end apart: 29, of which 18 were waited for; matrix products, arithmetic and copies ran while one was open for 1% of the time, Pallas kernels for 9%

profile of v2, /device:TPU:7, one launch (start us, length us, event | category | flops | bytes accessed | tf_op | source)
XLA Modules:
  0.0 301.4 jit_solution(7710593699017452248)
XLA Ops:
  7.5 2.6 collective-permute-start
  16.6 3.2 %collective-permute-start.2 = (bf16[4,144,256]{2,1,0:T(8,128)(2,1)S(1)}, bf16[4,144,256]{2,1,0:T(8,128)(2,1)S(1)}, u32[]{:S(2)}, u32[]{:S(2)}) collective-permute-start(bf16[4,144,256]{2,1,0:T(8,128)(2,1)S(1)} %get-tuple-element.42), channel_id=1, source_target_pairs={{0,4},{1,5},{2,6},{3,7},{4,0},{5,1},{6,2},{7,3},{8,12},{9,13},{10,... | collective-permute-start | bytes 884744 | tf_op jit(solution)/shard_map/ppermute | solution.py:276
  19.8 7.1 %collective-permute-done.2.other = bf16[4,144,256]{2,1,0:T(8,128)(2,1)S(1)} collective-permute-done((bf16[4,144,256]{2,1,0:T(8,128)(2,1)S(1)}, bf16[4,144,256]{2,1,0:T(8,128)(2,1)S(1)}, u32[]{:S(2)}, u32[]{:S(2)}) %collective-permute-start.2) | collective-permute-done | bytes 294944 | tf_op jit(solution)/shard_map/ppermute | solution.py:276
  27.1 15.7 %all_to_all.50.pieces = bf16[4,144,256]{2,1,0:T(8,128)(2,1)S(1)} all-to-all(bf16[4,144,256]{2,1,0:T(8,128)(2,1)S(1)} %near_sum.2), channel_id=1, replica_groups={{0,8,16,24},{1,9,17,25},{2,10,18,26},{3,11,19,27},{4,12,20,28},{5,13,21..., dimensions={0} | all-to-all | bytes 589824 | tf_op jit(solution)/shard_map/all_to_all | solution.py:45
  42.7 5.4 %all-to-all-start.4 = ((bf16[8,128,256]{2,1,0:T(8,128)(2,1)}), bf16[8,128,256]{2,1,0:T(8,128)(2,1)}, u32[]{:S(2)}, u32[]{:S(2)}) async-start(bf16[8,128,256]{2,1,0:T(8,128)(2,1)} %low_sum.2._), calls=%async_computation.4 | async-start | bytes 1048576 | tf_op jit(solution)/shard_map/all_to_all | solution.py:45
  48.1 2.3 dynamic-slice_bitcast_fusion.1
  50.4 4.5 %collective-permute-start.5 = (bf16[2048,256]{1,0:T(8,128)(2,1)}, bf16[2048,256]{1,0:T(8,128)(2,1)S(1)}, u32[]{:S(2)}, u32[]{:S(2)}) collective-permute-start(bf16[2048,256]{1,0:T(8,128)(2,1)} %dynamic-slice_bitcast_fusion.1), channel_id=1, source_target_pairs={{0,1},{1,0},{2,3},{3,2},{4,5},{5,4},{6,7},{7,6},{8,9},{9,8},{10,11... | collective-permute-start | bytes 3145736 | tf_op jit(solution)/shard_map/ppermute | solution.py:322
  54.9 10.6 %collective-permute-start.3 = (bf16[144,256]{1,0:T(8,128)(2,1)S(1)}, bf16[144,256]{1,0:T(8,128)(2,1)S(1)}, u32[]{:S(2)}, u32[]{:S(2)}) collective-permute-start(bf16[144,256]{1,0:T(8,128)(2,1)S(1)} %ring_sum.2.own), channel_id=1, source_target_pairs={{0,2},{1,3},{2,0},{3,1},{4,6},{5,7},{6,4},{7,5},{8,10},{9,11},{10,... | collective-permute-start | bytes 221192 | tf_op jit(solution)/shard_map/ppermute | solution.py:293
  65.5 2.6 collective-permute-done.3.other
  69.0 6.8 %all-to-all-start.1 = ((bf16[4,128,256]{2,1,0:T(8,128)(2,1)}), bf16[4,128,256]{2,1,0:T(8,128)(2,1)}, u32[]{:S(2)}, u32[]{:S(2)}) async-start(bf16[4,128,256]{2,1,0:T(8,128)(2,1)} %forward_share.2), calls=%async_computation.1 | async-start | bytes 524288 | tf_op jit(solution)/shard_map/all_to_all | solution.py:45
  76.8 2.9 collective-permute-start.14
  80.8 8.8 %collective-permute-start.13 = (bf16[128,256]{1,0:T(8,128)(2,1)S(1)}, bf16[128,256]{1,0:T(8,128)(2,1)S(1)}, u32[]{:S(2)}, u32[]{:S(2)}) collective-permute-start(bf16[128,256]{1,0:T(8,128)(2,1)S(1)} %low_ring_sum.2.own), channel_id=1, source_target_pairs={{0,2},{1,3},{2,0},{3,1},{4,6},{5,7},{6,4},{7,5},{8,10},{9,11},{10,... | collective-permute-start | bytes 196616 | tf_op jit(solution)/shard_map/ppermute | solution.py:293
  89.6 2.4 collective-permute-done.13.other
  92.9 7.1 %all-to-all-start.5 = ((bf16[8,128,256]{2,1,0:T(8,128)(2,1)}), bf16[8,128,256]{2,1,0:T(8,128)(2,1)}, u32[]{:S(2)}, u32[]{:S(2)}) async-start(bf16[8,128,256]{2,1,0:T(8,128)(2,1)} %copy-done.12), calls=%async_computation.5 | async-start | bytes 1048576 | tf_op jit(solution)/shard_map/all_to_all | solution.py:45
  99.9 3.4 %collective-permute-start.4 = (bf16[4,128,256]{2,1,0:T(8,128)(2,1)}, bf16[4,128,256]{2,1,0:T(8,128)(2,1)S(1)}, u32[]{:S(2)}, u32[]{:S(2)}) collective-permute-start(bf16[4,128,256]{2,1,0:T(8,128)(2,1)} %all-to-all-done.1.near), channel_id=1, source_target_pairs={{0,4},{1,5},{2,6},{3,7},{4,0},{5,1},{6,2},{7,3},{8,12},{9,13},{10,... | collective-permute-start | bytes 786440 | tf_op jit(solution)/shard_map/ppermute | solution.py:368
  103.3 14.9 %collective-permute-done.4.far = bf16[4,128,256]{2,1,0:T(8,128)(2,1)S(1)} collective-permute-done((bf16[4,128,256]{2,1,0:T(8,128)(2,1)}, bf16[4,128,256]{2,1,0:T(8,128)(2,1)S(1)}, u32[]{:S(2)}, u32[]{:S(2)}) %collective-permute-start.4) | collective-permute-done | bytes 262176 | tf_op jit(solution)/shard_map/ppermute | solution.py:368
  119.8 1.9 forward_product.2
  121.7 3.8 %collective-permute-start.6 = (f32[128,256]{1,0:T(8,128)S(1)}, f32[128,256]{1,0:T(8,128)S(1)}, u32[]{:S(2)}, u32[]{:S(2)}) collective-permute-start(f32[128,256]{1,0:T(8,128)S(1)} %get-tuple-element.44), channel_id=1, source_target_pairs={{0,1},{1,0},{2,3},{3,2},{4,5},{5,4},{6,7},{7,6},{8,9},{9,8},{10,11... | collective-permute-start | bytes 393224 | tf_op jit(solution)/shard_map/ppermute | solution.py:388
  128.5 3.1 %collective-permute-done.7.refs_0_ = bf16[128,256]{1,0:T(8,128)(2,1)S(1)} collective-permute-done((bf16[128,256]{1,0:T(8,128)(2,1)S(1)}, bf16[128,256]{1,0:T(8,128)(2,1)S(1)}, u32[]{:S(2)}, u32[]{:S(2)}) %collective-permute-start.7) | collective-permute-done | bytes 65568 | tf_op jit(solution)/shard_map/ppermute | solution.py:51
  133.7 2.0 forward_start.3
  137.2 3.5 %collective-permute-start.8 = (bf16[8,144,256]{2,1,0:T(8,128)(2,1)}, bf16[8,144,256]{2,1,0:T(8,128)(2,1)}, u32[]{:S(2)}, u32[]{:S(2)}) collective-permute-start(bf16[8,144,256]{2,1,0:T(8,128)(2,1)} %get-tuple-element.47), channel_id=1, source_target_pairs={{0,1},{1,0},{2,3},{3,2},{4,5},{5,4},{6,7},{7,6},{8,9},{9,8},{10,11... | collective-permute-start | bytes 1769480 | tf_op jit(solution)/shard_map/ppermute | solution.py:274
  140.8 2.7 backward_product.2
  143.6 2.1 collective-permute-start.15
  149.2 11.1 %all-to-all-start.6 = ((f32[32,8,128]{2,1,0:T(8,128)}), f32[32,8,128]{2,1,0:T(8,128)}, u32[]{:S(2)}, u32[]{:S(2)}) async-start(f32[32,8,128]{2,1,0:T(8,128)} %copy-done.34), calls=%async_computation.6 | async-start | bytes 262144 | tf_op jit(solution)/shard_map/all_to_all | solution.py:45
  164.8 3.3 %collective-permute-start.9 = (bf16[4,144,256]{2,1,0:T(8,128)(2,1)}, bf16[4,144,256]{2,1,0:T(8,128)(2,1)}, u32[]{:S(2)}, u32[]{:S(2)}) collective-permute-start(bf16[4,144,256]{2,1,0:T(8,128)(2,1)} %get-tuple-element.49), channel_id=1, source_target_pairs={{0,4},{1,5},{2,6},{3,7},{4,0},{5,1},{6,2},{7,3},{8,12},{9,13},{10,... | collective-permute-start | bytes 884744 | tf_op jit(solution)/shard_map/ppermute | solution.py:276
  168.1 5.4 %all-to-all-done.6.dots = f32[32,8,128]{2,1,0:T(8,128)} async-done(((f32[32,8,128]{2,1,0:T(8,128)}), f32[32,8,128]{2,1,0:T(8,128)}, u32[]{:S(2)}, u32[]{:S(2)}) %all-to-all-start.6) | async-done | bytes 131104 | tf_op jit(solution)/shard_map/all_to_all | solution.py:45
  177.7 2.4 collective-permute-start.16
  180.2 5.0 %collective-permute-done.16.refs_0_ = bf16[128,256]{1,0:T(8,128)(2,1)S(1)} collective-permute-done((bf16[128,256]{1,0:T(8,128)(2,1)S(1)}, bf16[128,256]{1,0:T(8,128)(2,1)S(1)}, u32[]{:S(2)}, u32[]{:S(2)}) %collective-permute-start.16) | collective-permute-done | bytes 65568 | tf_op jit(solution)/shard_map/ppermute | solution.py:51
  188.3 2.2 backward_start.3
  191.9 2.9 collective-permute-start.17
  196.7 4.1 %all-to-all-start.2 = ((bf16[4,144,256]{2,1,0:T(8,128)(2,1)}), bf16[4,144,256]{2,1,0:T(8,128)(2,1)}, u32[]{:S(2)}, u32[]{:S(2)}) async-start(bf16[4,144,256]{2,1,0:T(8,128)(2,1)} %copy-done.14), calls=%async_computation.2 | async-start | bytes 589824 | tf_op jit(solution)/shard_map/all_to_all | solution.py:45
  204.6 6.0 %all-to-all-done.2.pieces = bf16[4,144,256]{2,1,0:T(8,128)(2,1)} async-done(((bf16[4,144,256]{2,1,0:T(8,128)(2,1)}), bf16[4,144,256]{2,1,0:T(8,128)(2,1)}, u32[]{:S(2)}, u32[]{:S(2)}) %all-to-all-start.2) | async-done | bytes 294944 | tf_op jit(solution)/shard_map/all_to_all | solution.py:45
  210.6 4.5 %all-to-all-start.7 = ((bf16[8,128,256]{2,1,0:T(8,128)(2,1)}), bf16[8,128,256]{2,1,0:T(8,128)(2,1)}, u32[]{:S(2)}, u32[]{:S(2)}) async-start(bf16[8,128,256]{2,1,0:T(8,128)(2,1)} %copy-done.11), calls=%async_computation.7 | async-start | bytes 1048576 | tf_op jit(solution)/shard_map/all_to_all | solution.py:45
  216.1 3.0 %collective-permute-start.10 = (bf16[144,256]{1,0:T(8,128)(2,1)S(1)}, bf16[144,256]{1,0:T(8,128)(2,1)S(1)}, u32[]{:S(2)}, u32[]{:S(2)}) collective-permute-start(bf16[144,256]{1,0:T(8,128)(2,1)S(1)} %ring_sum.3.own), channel_id=1, source_target_pairs={{0,2},{1,3},{2,0},{3,1},{4,6},{5,7},{6,4},{7,5},{8,10},{9,11},{10,... | collective-permute-start | bytes 221192 | tf_op jit(solution)/shard_map/ppermute | solution.py:293
  219.2 6.0 %collective-permute-done.10.other = bf16[144,256]{1,0:T(8,128)(2,1)S(1)} collective-permute-done((bf16[144,256]{1,0:T(8,128)(2,1)S(1)}, bf16[144,256]{1,0:T(8,128)(2,1)S(1)}, u32[]{:S(2)}, u32[]{:S(2)}) %collective-permute-start.10) | collective-permute-done | bytes 73760 | tf_op jit(solution)/shard_map/ppermute | solution.py:293
  226.0 5.0 %all-to-all-done.7.pieces = bf16[8,128,256]{2,1,0:T(8,128)(2,1)} async-done(((bf16[8,128,256]{2,1,0:T(8,128)(2,1)}), bf16[8,128,256]{2,1,0:T(8,128)(2,1)}, u32[]{:S(2)}, u32[]{:S(2)}) %all-to-all-start.7) | async-done | bytes 524320 | tf_op jit(solution)/shard_map/all_to_all | solution.py:45
  231.0 3.4 %all-to-all-start.3 = ((bf16[4,128,256]{2,1,0:T(8,128)(2,1)}), bf16[4,128,256]{2,1,0:T(8,128)(2,1)S(1)}, u32[]{:S(2)}, u32[]{:S(2)}) async-start(bf16[4,128,256]{2,1,0:T(8,128)(2,1)} %forward_share.3), calls=%async_computation.3 | async-start | bytes 524288 | tf_op jit(solution)/shard_map/all_to_all | solution.py:45
  235.5 1.9 collective-permute-start.18
  237.4 7.0 %collective-permute-done.18.other = bf16[128,256]{1,0:T(8,128)(2,1)S(1)} collective-permute-done((bf16[128,256]{1,0:T(8,128)(2,1)S(1)}, bf16[128,256]{1,0:T(8,128)(2,1)S(1)}, u32[]{:S(2)}, u32[]{:S(2)}) %collective-permute-start.18) | collective-permute-done | bytes 65568 | tf_op jit(solution)/shard_map/ppermute | solution.py:293
  245.3 7.9 %all-to-all-start.8 = ((bf16[8,128,256]{2,1,0:T(8,128)(2,1)}), bf16[8,128,256]{2,1,0:T(8,128)(2,1)}, u32[]{:S(2)}, u32[]{:S(2)}) async-start(bf16[8,128,256]{2,1,0:T(8,128)(2,1)} %copy-done.13), calls=%async_computation.8 | async-start | bytes 1048576 | tf_op jit(solution)/shard_map/all_to_all | solution.py:45
  253.1 3.5 %collective-permute-start.11 = (bf16[4,128,256]{2,1,0:T(8,128)(2,1)S(1)}, bf16[4,128,256]{2,1,0:T(8,128)(2,1)}, u32[]{:S(2)}, u32[]{:S(2)}) collective-permute-start(bf16[4,128,256]{2,1,0:T(8,128)(2,1)S(1)} %all-to-all-done.3.near), channel_id=1, source_target_pairs={{0,4},{1,5},{2,6},{3,7},{4,0},{5,1},{6,2},{7,3},{8,12},{9,13},{10,... | collective-permute-start | bytes 786440 | tf_op jit(solution)/shard_map/ppermute | solution.py:368
  256.6 11.1 %all-to-all-done.8.blocks = bf16[8,128,256]{2,1,0:T(8,128)(2,1)} async-done(((bf16[8,128,256]{2,1,0:T(8,128)(2,1)}), bf16[8,128,256]{2,1,0:T(8,128)(2,1)}, u32[]{:S(2)}, u32[]{:S(2)}) %all-to-all-start.8) | async-done | bytes 524320 | tf_op jit(solution)/shard_map/all_to_all | solution.py:45
  267.7 2.7 backward_product.3
  270.4 7.9 %collective-permute-start.19 = (f32[128,256]{1,0:T(8,128)S(1)}, f32[128,256]{1,0:T(8,128)S(1)}, u32[]{:S(2)}, u32[]{:S(2)}) collective-permute-start(f32[128,256]{1,0:T(8,128)S(1)} %get-tuple-element.62), channel_id=1, source_target_pairs={{0,1},{1,0},{2,3},{3,2},{4,5},{5,4},{6,7},{7,6},{8,9},{9,8},{10,11... | collective-permute-start | bytes 393224 | tf_op jit(solution)/shard_map/ppermute | solution.py:406
  280.1 4.5 %all-to-all-start.9 = ((f32[32,8,128]{2,1,0:T(8,128)}), f32[32,8,128]{2,1,0:T(8,128)}, u32[]{:S(2)}, u32[]{:S(2)}) async-start(f32[32,8,128]{2,1,0:T(8,128)} %get-tuple-element.64), calls=%async_computation.9 | async-start | bytes 262144 | tf_op jit(solution)/shard_map/all_to_all | solution.py:45
  286.2 1.9 forward_product.3
  288.1 2.3 collective-permute-start.12
  292.9 5.1 %all-to-all-done.9.dots = f32[32,8,128]{2,1,0:T(8,128)} async-done(((f32[32,8,128]{2,1,0:T(8,128)}), f32[32,8,128]{2,1,0:T(8,128)}, u32[]{:S(2)}, u32[]{:S(2)}) %all-to-all-start.9) | async-done | bytes 131104 | tf_op jit(solution)/shard_map/all_to_all | solution.py:45
  (151 shorter events, 60.7 us)
Async XLA Ops:
  0.6 9.5 %copy-start.50 = (s32[1,2,2]{2,1,0:T(2,128)S(1)}, s32[1,2,2]{2,1,0:T(2,128)}, u32[]{:S(2)}) copy-start(s32[1,2,2]{2,1,0:T(2,128)} %param.25) | copy-start | bytes 52
  0.6 9.5 %copy-start.36 = (bf16[1,128,256]{2,1,0:T(8,128)(2,1)S(1)}, bf16[1,128,256]{2,1,0:T(8,128)(2,1)}, u32[]{:S(2)}) copy-start(bf16[1,128,256]{2,1,0:T(8,128)(2,1)} %param.18) | copy-start | bytes 196612
  6.3 3.9 %copy-start.2 = (bf16[1,4096,256]{2,1,0:T(8,128)(2,1)S(1)}, bf16[1,4096,256]{2,1,0:T(8,128)(2,1)}, u32[]{:S(2)}) copy-start(bf16[1,4096,256]{2,1,0:T(8,128)(2,1)} %param.14) | copy-start | bytes 6291460
  6.3 3.9 %copy-start.8 = (bf16[1,8,64,256]{3,2,1,0:T(8,128)(2,1)S(1)}, bf16[1,8,64,256]{3,2,1,0:T(8,128)(2,1)}, u32[]{:S(2)}) copy-start(bf16[1,8,64,256]{3,2,1,0:T(8,128)(2,1)} %param.22) | copy-start | bytes 786436
  7.5 9.0 %copy-start.28 = (bf16[128,256]{1,0:T(8,128)(2,1)}, bf16[128,256]{1,0:T(8,128)(2,1)S(1)}, u32[]{:S(2)}) copy-start(bf16[128,256]{1,0:T(8,128)(2,1)S(1)} %get-tuple-element.36._.x) | copy-start | bytes 196612
  7.5 8.9 %collective-permute-start = (bf16[8,144,256]{2,1,0:T(8,128)(2,1)S(1)}, bf16[8,144,256]{2,1,0:T(8,128)(2,1)S(1)}, u32[]{:S(2)}, u32[]{:S(2)}) collective-permute-start(bf16[8,144,256]{2,1,0:T(8,128)(2,1)S(1)} %get-tuple-element.38), channel_id=1, source_target_pairs={{0,1},{1,0},{2,3},{3,2},{4,5},{5,4},{6,7},{7,6},{8,9},{9,8},{10,11... | collective-permute-start | bytes 1769480 | tf_op jit(solution)/shard_map/ppermute | solution.py:274
  11.8 15.3 %copy-start.38 = (bf16[128,256]{1,0:T(8,128)(2,1)}, bf16[128,256]{1,0:T(8,128)(2,1)S(1)}, u32[]{:S(2)}) copy-start(bf16[128,256]{1,0:T(8,128)(2,1)S(1)} %get-tuple-element.52.g) | copy-start | bytes 196612
  11.8 3.8 %collective-permute-start.1 = (bf16[8,128,256]{2,1,0:T(8,128)(2,1)S(1)}, bf16[8,128,256]{2,1,0:T(8,128)(2,1)S(1)}, u32[]{:S(2)}, u32[]{:S(2)}) collective-permute-start(bf16[8,128,256]{2,1,0:T(8,128)(2,1)S(1)} %get-tuple-element.40), channel_id=1, source_target_pairs={{0,1},{1,0},{2,3},{3,2},{4,5},{5,4},{6,7},{7,6},{8,9},{9,8},{10,11... | collective-permute-start | bytes 1572872 | tf_op jit(solution)/shard_map/ppermute | solution.py:284
  16.6 10.4 %collective-permute-start.2 = (bf16[4,144,256]{2,1,0:T(8,128)(2,1)S(1)}, bf16[4,144,256]{2,1,0:T(8,128)(2,1)S(1)}, u32[]{:S(2)}, u32[]{:S(2)}) collective-permute-start(bf16[4,144,256]{2,1,0:T(8,128)(2,1)S(1)} %get-tuple-element.42), channel_id=1, source_target_pairs={{0,4},{1,5},{2,6},{3,7},{4,0},{5,1},{6,2},{7,3},{8,12},{9,13},{10,... | collective-permute-start | bytes 884744 | tf_op jit(solution)/shard_map/ppermute | solution.py:276
  42.7 33.0 %copy-start.1 = (bf16[1,256,4096]{2,1,0:T(8,128)(2,1)S(1)}, bf16[1,256,4096]{2,1,0:T(8,128)(2,1)}, u32[]{:S(2)}) copy-start(bf16[1,256,4096]{2,1,0:T(8,128)(2,1)} %param.13) | copy-start | bytes 6291460
  42.7 26.2 %all-to-all-start.4 = ((bf16[8,128,256]{2,1,0:T(8,128)(2,1)}), bf16[8,128,256]{2,1,0:T(8,128)(2,1)}, u32[]{:S(2)}, u32[]{:S(2)}) async-start(bf16[8,128,256]{2,1,0:T(8,128)(2,1)} %low_sum.2._), calls=%async_computation.4 | async-start | bytes 1048576 | tf_op jit(solution)/shard_map/all_to_all | solution.py:45
  50.4 52.9 %collective-permute-start.5 = (bf16[2048,256]{1,0:T(8,128)(2,1)}, bf16[2048,256]{1,0:T(8,128)(2,1)S(1)}, u32[]{:S(2)}, u32[]{:S(2)}) collective-permute-start(bf16[2048,256]{1,0:T(8,128)(2,1)} %dynamic-slice_bitcast_fusion.1), channel_id=1, source_target_pairs={{0,1},{1,0},{2,3},{3,2},{4,5},{5,4},{6,7},{7,6},{8,9},{9,8},{10,11... | collective-permute-start | bytes 3145736 | tf_op jit(solution)/shard_map/ppermute | solution.py:322
  54.9 13.3 %collective-permute-start.3 = (bf16[144,256]{1,0:T(8,128)(2,1)S(1)}, bf16[144,256]{1,0:T(8,128)(2,1)S(1)}, u32[]{:S(2)}, u32[]{:S(2)}) collective-permute-start(bf16[144,256]{1,0:T(8,128)(2,1)S(1)} %ring_sum.2.own), channel_id=1, source_target_pairs={{0,2},{1,3},{2,0},{3,1},{4,6},{5,7},{6,4},{7,5},{8,10},{9,11},{10,... | collective-permute-start | bytes 221192 | tf_op jit(solution)/shard_map/ppermute | solution.py:293
  69.0 23.9 %all-to-all-start.1 = ((bf16[4,128,256]{2,1,0:T(8,128)(2,1)}), bf16[4,128,256]{2,1,0:T(8,128)(2,1)}, u32[]{:S(2)}, u32[]{:S(2)}) async-start(bf16[4,128,256]{2,1,0:T(8,128)(2,1)} %forward_share.2), calls=%async_computation.1 | async-start | bytes 524288 | tf_op jit(solution)/shard_map/all_to_all | solution.py:45
  76.8 64.0 %collective-permute-start.14 = (bf16[256,2048]{1,0:T(8,128)(2,1)}, bf16[256,2048]{1,0:T(8,128)(2,1)}, u32[]{:S(2)}, u32[]{:S(2)}) collective-permute-start(bf16[256,2048]{1,0:T(8,128)(2,1)} %dynamic-slice_bitcast_fusion), channel_id=1, source_target_pairs={{0,1},{1,0},{2,3},{3,2},{4,5},{5,4},{6,7},{7,6},{8,9},{9,8},{10,11... | collective-permute-start | bytes 3145736 | tf_op jit(solution)/shard_map/ppermute | solution.py:319
  80.8 11.2 %collective-permute-start.13 = (bf16[128,256]{1,0:T(8,128)(2,1)S(1)}, bf16[128,256]{1,0:T(8,128)(2,1)S(1)}, u32[]{:S(2)}, u32[]{:S(2)}) collective-permute-start(bf16[128,256]{1,0:T(8,128)(2,1)S(1)} %low_ring_sum.2.own), channel_id=1, source_target_pairs={{0,2},{1,3},{2,0},{3,1},{4,6},{5,7},{6,4},{7,5},{8,10},{9,11},{10,... | collective-permute-start | bytes 196616 | tf_op jit(solution)/shard_map/ppermute | solution.py:293
  92.9 33.6 %copy-start.29 = (bf16[128,256]{1,0:T(8,128)(2,1)S(1)}, bf16[128,256]{1,0:T(8,128)(2,1)}, u32[]{:S(2)}) copy-start(bf16[128,256]{1,0:T(8,128)(2,1)} %copy-done.28) | copy-start | bytes 196612
  92.9 38.7 %copy-start.7 = (bf16[1,8,64,256]{3,2,1,0:T(8,128)(2,1)S(1)}, bf16[1,8,64,256]{3,2,1,0:T(8,128)(2,1)}, u32[]{:S(2)}) copy-start(bf16[1,8,64,256]{3,2,1,0:T(8,128)(2,1)} %param.21) | copy-start | bytes 786436
  92.9 47.9 %all-to-all-start.5 = ((bf16[8,128,256]{2,1,0:T(8,128)(2,1)}), bf16[8,128,256]{2,1,0:T(8,128)(2,1)}, u32[]{:S(2)}, u32[]{:S(2)}) async-start(bf16[8,128,256]{2,1,0:T(8,128)(2,1)} %copy-done.12), calls=%async_computation.5 | async-start | bytes 1048576 | tf_op jit(solution)/shard_map/all_to_all | solution.py:45
  99.9 18.3 %collective-permute-start.4 = (bf16[4,128,256]{2,1,0:T(8,128)(2,1)}, bf16[4,128,256]{2,1,0:T(8,128)(2,1)S(1)}, u32[]{:S(2)}, u32[]{:S(2)}) collective-permute-start(bf16[4,128,256]{2,1,0:T(8,128)(2,1)} %all-to-all-done.1.near), channel_id=1, source_target_pairs={{0,4},{1,5},{2,6},{3,7},{4,0},{5,1},{6,2},{7,3},{8,12},{9,13},{10,... | collective-permute-start | bytes 786440 | tf_op jit(solution)/shard_map/ppermute | solution.py:368
  121.7 4.8 %collective-permute-start.6 = (f32[128,256]{1,0:T(8,128)S(1)}, f32[128,256]{1,0:T(8,128)S(1)}, u32[]{:S(2)}, u32[]{:S(2)}) collective-permute-start(f32[128,256]{1,0:T(8,128)S(1)} %get-tuple-element.44), channel_id=1, source_target_pairs={{0,1},{1,0},{2,3},{3,2},{4,5},{5,4},{6,7},{7,6},{8,9},{9,8},{10,11... | collective-permute-start | bytes 393224 | tf_op jit(solution)/shard_map/ppermute | solution.py:388
  126.5 5.0 %collective-permute-start.7 = (bf16[128,256]{1,0:T(8,128)(2,1)S(1)}, bf16[128,256]{1,0:T(8,128)(2,1)S(1)}, u32[]{:S(2)}, u32[]{:S(2)}) collective-permute-start(bf16[128,256]{1,0:T(8,128)(2,1)S(1)} %forward_end.2), channel_id=1, source_target_pairs={{0,32},{32,64},{64,96},{96,128},{128,160},{160,192},{192,224},{224... | collective-permute-start | bytes 196616 | tf_op jit(solution)/shard_map/ppermute | solution.py:51
  137.2 9.7 %copy-start.10 = (bf16[1,2,128,256]{3,2,1,0:T(8,128)(2,1)S(1)}, bf16[1,2,128,256]{3,2,1,0:T(8,128)(2,1)}, u32[]{:S(2)}) copy-start(bf16[1,2,128,256]{3,2,1,0:T(8,128)(2,1)} %param.20) | copy-start | bytes 393220
  137.2 23.1 %collective-permute-start.8 = (bf16[8,144,256]{2,1,0:T(8,128)(2,1)}, bf16[8,144,256]{2,1,0:T(8,128)(2,1)}, u32[]{:S(2)}, u32[]{:S(2)}) collective-permute-start(bf16[8,144,256]{2,1,0:T(8,128)(2,1)} %get-tuple-element.47), channel_id=1, source_target_pairs={{0,1},{1,0},{2,3},{3,2},{4,5},{5,4},{6,7},{7,6},{8,9},{9,8},{10,11... | collective-permute-start | bytes 1769480 | tf_op jit(solution)/shard_map/ppermute | solution.py:274
  143.5 41.6 %copy-start.9 = (bf16[1,8,64,256]{3,2,1,0:T(8,128)(2,1)S(1)}, bf16[1,8,64,256]{3,2,1,0:T(8,128)(2,1)}, u32[]{:S(2)}) copy-start(bf16[1,8,64,256]{3,2,1,0:T(8,128)(2,1)} %param.22) | copy-start | bytes 786436
  143.6 3.4 %collective-permute-start.15 = (f32[128,256]{1,0:T(8,128)S(1)}, f32[128,256]{1,0:T(8,128)S(1)}, u32[]{:S(2)}, u32[]{:S(2)}) collective-permute-start(f32[128,256]{1,0:T(8,128)S(1)} %get-tuple-element.54), channel_id=1, source_target_pairs={{0,1},{1,0},{2,3},{3,2},{4,5},{5,4},{6,7},{7,6},{8,9},{9,8},{10,11... | collective-permute-start | bytes 393224 | tf_op jit(solution)/shard_map/ppermute | solution.py:406
  149.2 24.4 %all-to-all-start.6 = ((f32[32,8,128]{2,1,0:T(8,128)}), f32[32,8,128]{2,1,0:T(8,128)}, u32[]{:S(2)}, u32[]{:S(2)}) async-start(f32[32,8,128]{2,1,0:T(8,128)} %copy-done.34), calls=%async_computation.6 | async-start | bytes 262144 | tf_op jit(solution)/shard_map/all_to_all | solution.py:45
  164.8 30.0 %collective-permute-start.9 = (bf16[4,144,256]{2,1,0:T(8,128)(2,1)}, bf16[4,144,256]{2,1,0:T(8,128)(2,1)}, u32[]{:S(2)}, u32[]{:S(2)}) collective-permute-start(bf16[4,144,256]{2,1,0:T(8,128)(2,1)} %get-tuple-element.49), channel_id=1, source_target_pairs={{0,4},{1,5},{2,6},{3,7},{4,0},{5,1},{6,2},{7,3},{8,12},{9,13},{10,... | collective-permute-start | bytes 884744 | tf_op jit(solution)/shard_map/ppermute | solution.py:276
  173.6 21.3 %copy-start.19 = (bf16[128,256]{1,0:T(8,128)(2,1)S(1)}, bf16[128,256]{1,0:T(8,128)(2,1)}, u32[]{:S(2)}) copy-start(bf16[128,256]{1,0:T(8,128)(2,1)} %copy-done.17) | copy-start | bytes 196612
  173.6 21.3 %copy-start.24 = (bf16[4,144,256]{2,1,0:T(8,128)(2,1)S(1)}, bf16[4,144,256]{2,1,0:T(8,128)(2,1)}, u32[]{:S(2)}) copy-start(bf16[4,144,256]{2,1,0:T(8,128)(2,1)} %copy-done.23) | copy-start | bytes 884740
  177.7 2.5 copy-start.52
  177.7 7.5 %collective-permute-start.16 = (bf16[128,256]{1,0:T(8,128)(2,1)S(1)}, bf16[128,256]{1,0:T(8,128)(2,1)S(1)}, u32[]{:S(2)}, u32[]{:S(2)}) collective-permute-start(bf16[128,256]{1,0:T(8,128)(2,1)S(1)} %get-tuple-element.57), channel_id=1, source_target_pairs={{32,0},{64,32},{96,64},{128,96},{160,128},{192,160},{224,192},{256... | collective-permute-start | bytes 196616 | tf_op jit(solution)/shard_map/ppermute | solution.py:51
  191.9 8.8 %collective-permute-start.17 = (bf16[8,128,256]{2,1,0:T(8,128)(2,1)}, bf16[8,128,256]{2,1,0:T(8,128)(2,1)}, u32[]{:S(2)}, u32[]{:S(2)}) collective-permute-start(bf16[8,128,256]{2,1,0:T(8,128)(2,1)} %get-tuple-element.60), channel_id=1, source_target_pairs={{0,1},{1,0},{2,3},{3,2},{4,5},{5,4},{6,7},{7,6},{8,9},{9,8},{10,11... | collective-permute-start | bytes 1572872 | tf_op jit(solution)/shard_map/ppermute | solution.py:284
  196.7 14.0 %all-to-all-start.2 = ((bf16[4,144,256]{2,1,0:T(8,128)(2,1)}), bf16[4,144,256]{2,1,0:T(8,128)(2,1)}, u32[]{:S(2)}, u32[]{:S(2)}) async-start(bf16[4,144,256]{2,1,0:T(8,128)(2,1)} %copy-done.14), calls=%async_computation.2 | async-start | bytes 589824 | tf_op jit(solution)/shard_map/all_to_all | solution.py:45
  210.6 20.3 %all-to-all-start.7 = ((bf16[8,128,256]{2,1,0:T(8,128)(2,1)}), bf16[8,128,256]{2,1,0:T(8,128)(2,1)}, u32[]{:S(2)}, u32[]{:S(2)}) async-start(bf16[8,128,256]{2,1,0:T(8,128)(2,1)} %copy-done.11), calls=%async_computation.7 | async-start | bytes 1048576 | tf_op jit(solution)/shard_map/all_to_all | solution.py:45
  216.1 9.0 %collective-permute-start.10 = (bf16[144,256]{1,0:T(8,128)(2,1)S(1)}, bf16[144,256]{1,0:T(8,128)(2,1)S(1)}, u32[]{:S(2)}, u32[]{:S(2)}) collective-permute-start(bf16[144,256]{1,0:T(8,128)(2,1)S(1)} %ring_sum.3.own), channel_id=1, source_target_pairs={{0,2},{1,3},{2,0},{3,1},{4,6},{5,7},{6,4},{7,5},{8,10},{9,11},{10,... | collective-permute-start | bytes 221192 | tf_op jit(solution)/shard_map/ppermute | solution.py:293
  231.0 14.3 %all-to-all-start.3 = ((bf16[4,128,256]{2,1,0:T(8,128)(2,1)}), bf16[4,128,256]{2,1,0:T(8,128)(2,1)S(1)}, u32[]{:S(2)}, u32[]{:S(2)}) async-start(bf16[4,128,256]{2,1,0:T(8,128)(2,1)} %forward_share.3), calls=%async_computation.3 | async-start | bytes 524288 | tf_op jit(solution)/shard_map/all_to_all | solution.py:45
  235.5 8.9 %collective-permute-start.18 = (bf16[128,256]{1,0:T(8,128)(2,1)S(1)}, bf16[128,256]{1,0:T(8,128)(2,1)S(1)}, u32[]{:S(2)}, u32[]{:S(2)}) collective-permute-start(bf16[128,256]{1,0:T(8,128)(2,1)S(1)} %low_ring_sum.3.own), channel_id=1, source_target_pairs={{0,2},{1,3},{2,0},{3,1},{4,6},{5,7},{6,4},{7,5},{8,10},{9,11},{10,... | collective-permute-start | bytes 196616 | tf_op jit(solution)/shard_map/ppermute | solution.py:293
  245.3 22.4 %all-to-all-start.8 = ((bf16[8,128,256]{2,1,0:T(8,128)(2,1)}), bf16[8,128,256]{2,1,0:T(8,128)(2,1)}, u32[]{:S(2)}, u32[]{:S(2)}) async-start(bf16[8,128,256]{2,1,0:T(8,128)(2,1)} %copy-done.13), calls=%async_computation.8 | async-start | bytes 1048576 | tf_op jit(solution)/shard_map/all_to_all | solution.py:45
  253.1 26.1 %copy-start.45 = (f32[1,256]{1,0:T(1,128)S(1)}, f32[1,256]{1,0:T(1,128)}, u32[]{:S(2)}) copy-start(f32[1,256]{1,0:T(1,128)} %gain.7) | copy-start | bytes 3076
  253.1 31.5 %collective-permute-start.11 = (bf16[4,128,256]{2,1,0:T(8,128)(2,1)S(1)}, bf16[4,128,256]{2,1,0:T(8,128)(2,1)}, u32[]{:S(2)}, u32[]{:S(2)}) collective-permute-start(bf16[4,128,256]{2,1,0:T(8,128)(2,1)S(1)} %all-to-all-done.3.near), channel_id=1, source_target_pairs={{0,4},{1,5},{2,6},{3,7},{4,0},{5,1},{6,2},{7,3},{8,12},{9,13},{10,... | collective-permute-start | bytes 786440 | tf_op jit(solution)/shard_map/ppermute | solution.py:368
  270.4 8.8 %collective-permute-start.19 = (f32[128,256]{1,0:T(8,128)S(1)}, f32[128,256]{1,0:T(8,128)S(1)}, u32[]{:S(2)}, u32[]{:S(2)}) collective-permute-start(f32[128,256]{1,0:T(8,128)S(1)} %get-tuple-element.62), channel_id=1, source_target_pairs={{0,1},{1,0},{2,3},{3,2},{4,5},{5,4},{6,7},{7,6},{8,9},{9,8},{10,11... | collective-permute-start | bytes 393224 | tf_op jit(solution)/shard_map/ppermute | solution.py:406
  280.1 4.5 %copy-start.30 = (f32[128,256]{1,0:T(8,128)}, f32[128,256]{1,0:T(8,128)S(1)}, u32[]{:S(2)}) copy-start(f32[128,256]{1,0:T(8,128)S(1)} %get-tuple-element.63.scaled_grad) | copy-start | bytes 393220
  280.1 17.9 %all-to-all-start.9 = ((f32[32,8,128]{2,1,0:T(8,128)}), f32[32,8,128]{2,1,0:T(8,128)}, u32[]{:S(2)}, u32[]{:S(2)}) async-start(f32[32,8,128]{2,1,0:T(8,128)} %get-tuple-element.64), calls=%async_computation.9 | async-start | bytes 262144 | tf_op jit(solution)/shard_map/all_to_all | solution.py:45
  284.6 1.6 copy-start.5
  286.2 11.8 %copy-start.49 = (f32[8,128]{1,0:T(8,128)S(1)}, f32[8,128]{1,0:T(8,128)}, u32[]{:S(2)}) copy-start(f32[8,128]{1,0:T(8,128)} %copy-done.48) | copy-start | bytes 12292
  286.2 11.8 %copy-start.53 = (f32[1,256]{1,0:T(1,128)S(1)}, f32[1,256]{1,0:T(1,128)}, u32[]{:S(2)}) copy-start(f32[1,256]{1,0:T(1,128)} %copy-done.52) | copy-start | bytes 3076
  288.1 3.3 %collective-permute-start.12 = (f32[128,256]{1,0:T(8,128)S(1)}, f32[128,256]{1,0:T(8,128)S(1)}, u32[]{:S(2)}, u32[]{:S(2)}) collective-permute-start(f32[128,256]{1,0:T(8,128)S(1)} %get-tuple-element.51), channel_id=1, source_target_pairs={{0,1},{1,0},{2,3},{3,2},{4,5},{5,4},{6,7},{7,6},{8,9},{9,8},{10,11... | collective-permute-start | bytes 393224 | tf_op jit(solution)/shard_map/ppermute | solution.py:388
  (35 other events, 29.8 us)

commit v3 on v2

v3 whole, which is shorter than its diff:
```python
import functools

import jax
import jax.numpy as jnp
from jax import lax
from jax.experimental import pallas as pl
from jax.experimental.pallas import tpu as pltpu
from jax.sharding import PartitionSpec as P

D = 8192
BLOCK = 128
ROWS = 128
WIDTH = 256
SEQ = 64
STATS = 16
RING = 8
HALF = RING * WIDTH
EPSILON = 1e-05
F32 = jnp.float32
BF16 = jnp.bfloat16
VMEM_LIMIT = 20 * 1024 * 1024


def core_pairs():
    return [(index, index ^ 1) for index in range(4 * RING)]


def z_pairs():
    return [(index, index ^ 2) for index in range(4 * RING)]


def rings():
    return [[4 * y + rest for y in range(RING)] for rest in range(4)]


def swapped(value, groups=None):
    return lax.all_to_all(value, "shard", 0, 0, axis_index_groups=groups, tiled=True)


def gate(value, *after):
    return lax.optimization_barrier((value, *after))[0]


def shifted(value, axis, steps):
    count = lax.axis_size(axis)
    leading, last = (max(0, -steps), min(count, count - steps))
    return lax.ppermute(value, axis, [(source, source + steps) for source in range(leading, last)])


def call(kernel, name, outs, *, prefetch=(), blocks=None, operands=(), after=()):
    blocks = blocks or {}
    first, last = len(prefetch) + len(operands), len(prefetch) + len(operands) + len(after)

    def body(*refs):
        kernel(*refs[:first], *refs[last:])

    def spec(position, operand):
        if position in blocks:
            shape, index_map = blocks[position]
            return pl.BlockSpec(shape, index_map)
        rank = len(operand.shape)
        return pl.BlockSpec(operand.shape, lambda *_: (0,) * rank)

    in_specs = [spec(position, operand) for position, operand in enumerate(operands)]
    return pl.pallas_call(
        body,
        out_shape=outs,
        grid_spec=pltpu.PrefetchScalarGridSpec(
            num_scalar_prefetch=len(prefetch),
            grid=(1,),
            in_specs=in_specs + [pl.BlockSpec(memory_space=pl.ANY)] * len(after),
            out_specs=[pl.BlockSpec(out.shape, lambda *_, rank=len(out.shape): (0,) * rank) for out in outs],
        ),
        compiler_params=pltpu.CompilerParams(vmem_limit_bytes=VMEM_LIMIT),
        cost_estimate=pl.CostEstimate(flops=0, bytes_accessed=0, transcendentals=0),
        name=name,
    )(*prefetch, *operands, *after)


def shape_of(*dims, dtype=BF16):
    return jax.ShapeDtypeStruct(dims, dtype)


def across(column):
    return jnp.broadcast_to(column, (ROWS, ROWS)).T[0:1]


def down(row):
    square = jnp.broadcast_to(row, (ROWS, ROWS)).T
    return jnp.concatenate([square, square], axis=1)


def split_stats(total):
    high = total.astype(BF16).astype(F32)
    return jnp.concatenate([high, total - high], axis=1).astype(BF16)


def joined_stats(coded):
    value = coded.astype(F32)
    return value[:, :ROWS] + value[:, ROWS:]


def power_row(low, high, sign):
    lane = lax.broadcasted_iota(jnp.int32, (1, WIDTH), 1)
    exponent = sign * jnp.where(lane < BLOCK, low, high)
    magnitude = jnp.abs(exponent)
    grown = jnp.ones((1, WIDTH), F32)
    shrunk = jnp.ones((1, WIDTH), F32)
    for bit in range(4):
        bit_set = (magnitude >> bit) & 1 == 1
        grown = jnp.where(bit_set, grown * 2.0 ** (2**bit), grown)
        shrunk = jnp.where(bit_set, shrunk * 0.5 ** (2**bit), shrunk)
    return jnp.where(exponent < 0, shrunk, grown)


def decoded(message, first_ref, second_ref, exponents, tick):
    low, high = exponents[tick, 0], exponents[tick, 1]
    scale = power_row(low, high, 1)
    inverse = power_row(low, high, -1)
    base = jnp.concatenate([first_ref[0], second_ref[0]], axis=0).astype(F32)
    delta = jnp.clip((message.astype(F32) - base) * inverse, -127.0, 127.0).astype(BF16)
    return (base + delta.astype(F32) * scale).astype(BF16)


def chosen(meta, edge, refs):
    if len(refs) == 1:
        return refs[0][...]
    return jnp.where(meta[0] == edge, refs[1][0].astype(F32), refs[0][...].astype(F32))


def forward_start(tick, messages, ids, meta, exponents, *refs):
    given, refs = refs[:messages], refs[messages:]
    first, second, gain, weight, x_out, keep, send = refs
    x = decoded(chosen(meta, 0, given), first, second, exponents, tick)
    x_out[...] = x
    x = x.astype(F32)
    scaled = (x * gain[...]).astype(BF16)
    total = across(jnp.sum(x * x, axis=1, keepdims=True))
    stats = split_stats(jnp.broadcast_to(total, (STATS, ROWS)))
    core = meta[3]
    for out, half in ((send, 1 - core), (keep, core)):
        for j in range(RING):
            at = pl.multiple_of((half * RING + j) * WIDTH, WIDTH)
            part = jnp.dot(scaled, weight[:, pl.ds(at, WIDTH)], preferred_element_type=F32)
            out[j, :ROWS] = part.astype(BF16)
            out[j, ROWS:] = stats


def backward_start(tick, messages, last, ids, meta, exponents, *refs):
    given, (first, second, weight, g_out, keep, send) = refs[:messages], refs[messages:]
    g = decoded(chosen(meta, last, given), first, second, exponents, tick)
    g_out[...] = g
    core = meta[3]
    for out, half in ((send, 1 - core), (keep, core)):
        for j in range(RING):
            at = pl.multiple_of((half * RING + j) * WIDTH, WIDTH)
            part = lax.dot_general(
                g, weight[pl.ds(at, WIDTH), :], (((1,), (1,)), ((), ())), preferred_element_type=F32
            )
            out[j] = part.astype(BF16)


def core_sum(mine, other, out):
    for j in range(RING):
        out[j, :ROWS] = (mine[j, :ROWS].astype(F32) + other[j, :ROWS].astype(F32)).astype(BF16)
    if out.shape[1] > ROWS:
        stats = split_stats(joined_stats(mine[0, ROWS:]) + joined_stats(other[0, ROWS:]))
        for j in range(RING):
            out[j, ROWS:] = stats


def ring_sum(pieces, out):
    total = pieces[0, :ROWS].astype(F32)
    for j in range(1, pieces.shape[0]):
        total = total + pieces[j, :ROWS].astype(F32)
    out[:ROWS] = total.astype(BF16)
    if out.shape[0] > ROWS:
        stats = joined_stats(pieces[0, ROWS:])
        for j in range(1, pieces.shape[0]):
            stats = stats + joined_stats(pieces[j, ROWS:])
        out[ROWS:] = split_stats(stats)


def forward_share(own, other, out):
    total = joined_stats(own[ROWS:]) + joined_stats(other[ROWS:])
    factor = lax.rsqrt(total[0:1] / D + EPSILON)
    value = own[:ROWS].astype(F32) + other[:ROWS].astype(F32)
    out[...] = jnp.broadcast_to((down(factor) * value).astype(BF16)[None], out.shape)


def backward_share(own, other, out):
    value = (own[...].astype(F32) + other[...].astype(F32)).astype(BF16)
    out[...] = jnp.broadcast_to(value[None], out.shape)


def halves(value, output, value_out, output_out):
    value_out[...] = value[...]
    output_out[...] = output[...]


def forward_product(blocks, own_weight, other_weight, mine, others):
    for weight, out in ((other_weight, others), (own_weight, mine)):
        total = jnp.zeros((ROWS, WIDTH), F32)
        for j in range(RING):
            rows = weight[j * WIDTH : (j + 1) * WIDTH, :]
            total = total + jnp.dot(blocks[j], rows, preferred_element_type=F32)
        out[...] = total


def backward_product(blocks, own_weight, other_weight, mine, others):
    for weight, out in ((other_weight, others), (own_weight, mine)):
        total = jnp.zeros((ROWS, WIDTH), F32)
        for j in range(RING):
            columns = weight[:, j * WIDTH : (j + 1) * WIDTH]
            total = total + lax.dot_general(
                blocks[j], columns, (((1,), (1,)), ((), ())), preferred_element_type=F32
            )
        out[...] = total


def forward_end(x, mine, other, out):
    out[...] = (x[...].astype(F32) + (mine[...] + other[...])).astype(BF16)


def backward_middle(tick, mine, other, saved, gain, scaled_grad, dots):
    value = mine[...] + other[...]
    scaled_grad[...] = value
    terms = [saved[tick].astype(F32) * gain[...] * value]
    if tick == 0:
        for k in range(2):
            kept = saved[k].astype(F32)
            terms.append(kept * kept)
    rows = [across(jnp.sum(term, axis=1, keepdims=True)) for term in terms]
    rows.append(jnp.zeros((8 - len(rows), ROWS), F32))
    dots[...] = jnp.broadcast_to(jnp.concatenate(rows, axis=0)[None], dots.shape)


def backward_end(tick, g, scaled_grad, saved, gain, dots, *refs):
    before, (out, gain_out, *left) = refs[: 2 if tick else 0], refs[2 if tick else 0 :]
    total = dots[0]
    for j in range(1, dots.shape[0]):
        total = total + dots[j]
    if tick == 0:
        squares = total[1:2]
        left[0][...] = jnp.broadcast_to(total[2:3], left[0].shape)
    else:
        squares = before[0][0:1]
    factor = down(lax.rsqrt(squares / D + EPSILON))
    kept = saved[tick].astype(F32)
    sums = jnp.sum(scaled_grad[...] * kept * factor, axis=0, keepdims=True)
    gain_out[...] = sums + before[1][...] if tick else sums
    value = g[...].astype(F32) + factor * gain[...] * scaled_grad[...]
    out[...] = (value - kept * (factor * factor * factor) * down(total[0:1]) / D).astype(BF16)


def over(value, pairs):
    return lax.ppermute(value, "shard", pairs)


def shards(
    value_weight,
    output_weight,
    norm_gain,
    arriving,
    fresh_inputs,
    returning,
    cotangents,
    saved_inputs,
    forward_base,
    backward_base,
    sample_ids,
    forward_exponents,
    backward_exponents,
):
    segment = lax.axis_index("segment")
    segments = lax.axis_size("segment")
    position = lax.axis_index("shard")
    core = position % 2
    meta = jnp.stack([segment, position // 4, position // 2 % 2, core]).astype(jnp.int32)
    value_local, output_local = value_weight[0], output_weight[0]
    saved = saved_inputs[0]
    low = shape_of(ROWS, WIDTH)
    wide = shape_of(ROWS, WIDTH, dtype=F32)
    tall = shape_of(ROWS + STATS, WIDTH)
    eight = shape_of(RING, ROWS, WIDTH)
    eight_tall = shape_of(RING, ROWS + STATS, WIDTH)
    row = shape_of(1, WIDTH, dtype=F32)
    own_half = {1: ((HALF, WIDTH), lambda i, meta: (meta[3], 0))}
    own_columns = {1: ((WIDTH, HALF), lambda i, meta: (0, meta[3]))}

    def base_blocks(first, micro):
        return {
            first + sample: (
                (1, SEQ, WIDTH),
                lambda i, ids, meta, exps, sample=sample: (ids[micro(meta), sample], 0, 0),
            )
            for sample in range(2)
        }

    def forward_begin(tick, messages, *after):
        count = len(messages)
        x, keep, send = call(
            functools.partial(forward_start, tick, count),
            "forward_start",
            [low, eight_tall, eight_tall],
            prefetch=(sample_ids, meta, forward_exponents[0]),
            operands=(*messages, forward_base[0], forward_base[0], norm_gain, value_local),
            blocks=base_blocks(count, lambda meta: tick - meta[0] + segments - 1),
            after=after,
        )
        operands = (keep, over(send, core_pairs()))
        return x, *call(core_sum, "forward_core_sum", [eight_tall], operands=operands)

    def backward_begin(tick, messages, *after):
        count = len(messages)
        g, keep, send = call(
            functools.partial(backward_start, tick, count, segments - 1),
            "backward_start",
            [low, eight, eight],
            prefetch=(sample_ids, meta, backward_exponents[0]),
            operands=(*messages, backward_base[0], backward_base[0], output_local),
            blocks=base_blocks(count, lambda meta: tick + meta[0]),
            after=after,
        )
        operands = (keep, over(send, core_pairs()))
        return g, *call(core_sum, "backward_core_sum", [eight], operands=operands)

    def forward_turn(pieces, *after):
        (own,) = call(ring_sum, "forward_ring_sum", [tall], operands=(pieces,), after=after)
        return call(forward_share, "forward_share", [eight], operands=(own, over(own, z_pairs())))[0]

    def backward_turn(pieces, *after):
        (own,) = call(ring_sum, "backward_ring_sum", [low], operands=(pieces,), after=after)
        return call(backward_share, "backward_share", [eight], operands=(own, over(own, z_pairs())))[0]

    def with_meta(kernel):
        return lambda _, *refs: kernel(*refs)

    def forward_finish(x, gathered, *after):
        mine, others = call(
            with_meta(forward_product),
            "forward_product",
            [wide, wide],
            prefetch=(meta,),
            operands=(gathered, output_local, output_other),
            blocks=own_half,
            after=after,
        )
        operands = (x, mine, over(others, core_pairs()))
        return call(forward_end, "forward_end", [low], operands=operands)[0]

    def backward_dots(tick, gathered, *after):
        mine, others = call(
            with_meta(backward_product),
            "backward_product",
            [wide, wide],
            prefetch=(meta,),
            operands=(gathered, value_local, value_other),
            blocks=own_columns,
            after=after,
        )
        return call(
            functools.partial(backward_middle, tick),
            "backward_middle",
            [wide, shape_of(4 * RING, 8, ROWS, dtype=F32)],
            operands=(mine, over(others, core_pairs()), saved, norm_gain),
        )

    def backward_finish(tick, g, scaled_grad, dots, left, *after):
        return call(
            functools.partial(backward_end, tick),
            "backward_end",
            [low, row] + ([shape_of(8, ROWS, dtype=F32)] if tick == 0 else []),
            operands=(g, scaled_grad, saved, norm_gain, dots, *left),
            after=after,
        )

    g, back_pieces = backward_begin(0, [returning[0]])
    gated = gate(back_pieces)
    back_landed = swapped(gated, rings())

    x, pieces = forward_begin(0, [arriving[0]], gated)
    value_half, output_half = call(
        with_meta(halves),
        "halves",
        [shape_of(WIDTH, HALF), shape_of(HALF, WIDTH)],
        prefetch=(meta,),
        operands=(value_local, output_local),
        blocks={
            0: ((WIDTH, HALF), lambda i, meta: (0, 1 - meta[3])),
            1: ((HALF, WIDTH), lambda i, meta: (1 - meta[3], 0)),
        },
        after=(gated,),
    )
    value_other, output_other = over(value_half, core_pairs()), over(output_half, core_pairs())
    gated = gate(pieces, back_landed, value_other, output_other)
    landed = swapped(gated, rings())

    copies = backward_turn(back_landed, gated)
    gated = gate(copies, landed)
    back_gathered = swapped(gated, rings())

    copies = forward_turn(landed, gated)
    gated = gate(copies, back_gathered)
    gathered = swapped(gated, rings())

    scaled_grad, dots = backward_dots(0, back_gathered, gated)
    gated = gate(dots, gathered)
    all_dots = swapped(gated)

    segment_out = forward_finish(x, gathered, gated)
    x, pieces = forward_begin(1, [shifted(segment_out, "segment", 1), fresh_inputs])
    gated = gate(pieces, all_dots)
    landed = swapped(gated, rings())

    input_grad, gain_total, squares = backward_finish(0, g, scaled_grad, all_dots, (), gated)
    g, back_pieces = backward_begin(1, [shifted(input_grad, "segment", -1), cotangents])
    gated = gate(back_pieces, landed)
    back_landed = swapped(gated, rings())

    copies = forward_turn(landed, gated)
    gated = gate(copies, back_landed)
    gathered = swapped(gated, rings())

    copies = backward_turn(back_landed, gated)
    gated = gate(copies, gathered)
    back_gathered = swapped(gated, rings())

    segment_out = forward_finish(x, gathered, gated)
    scaled_grad, dots = backward_dots(1, back_gathered, segment_out)
    all_dots = swapped(dots)
    input_grad, gain_total = backward_finish(1, g, scaled_grad, all_dots, (squares, gain_total))
    return (segment_out[None], input_grad[None], gain_total)


def solution(mesh):
    return jax.shard_map(
        shards,
        mesh=mesh,
        in_specs=(
            P("segment", "shard", None),
            P("segment", None, "shard"),
            P("segment", "shard"),
            P("segment", None, "shard"),
            P(None, None, "shard"),
            P("segment", None, "shard"),
            P(None, None, "shard"),
            P("segment", None, None, "shard"),
            P("segment", None, None, "shard"),
            P("segment", None, None, "shard"),
            P(),
            P("segment", None, "shard"),
            P("segment", None, "shard"),
        ),
        out_specs=(P("segment", None, "shard"), P("segment", None, "shard"), P("segment", "shard")),
        check_vma=False,
    )
```

time: 304 us -> 276 us (0.908)
  starting transfers between devices: 131 us -> 112 us
  local copies, waits for them, and re-layouts: 35.5 us -> 21.7 us
    all_to_all x9, waiting for transfers between devices: 32.6 us -> 57.8 us  [swapped(): lax.all_to_all(value, 'shard', 0, 0, axis_index_groups=groups, tiled=True)]
    ppermute x18 -> x14, waiting for transfers between devices: 46.1 us -> 23.9 us  [over(): return lax.ppermute(value, 'shard', pairs)]
    ppermute x18 -> x14, starting transfers between devices: 72 us -> 56.7 us  [over(): return lax.ppermute(value, 'shard', pairs)]
    unnamed x109 -> x87, local copies, waits for them, and re-layouts: 32.2 us -> 21.7 us
    all_to_all x9, starting transfers between devices: 54.7 us -> 49.3 us  [swapped(): lax.all_to_all(value, 'shard', 0, 0, axis_index_groups=groups, tiled=True)]
    dynamic_slice x2 -> x0, local copies, waits for them, and re-layouts: 3.35 us -> none  [the longest x1 2.29 us: shards(): lax.dynamic_slice(output_local, (half, 0), (HALF, WIDTH))]
    pallas_call x28 -> x27, Pallas kernels: 31 us -> 33.8 us  [call(): pl.pallas_call(body, out_shape=outs, grid_spec=pltpu.PrefetchScalarGridSp...]
  transfers between devices with their start and end apart: 29 -> 25, of which waited for: 18 -> 21; matrix products, arithmetic and copies ran while one was open for 1% -> 0% of each run, Pallas kernels for 9% -> 8%
where the time goes in v3:
time: 276 us; the launch traced here: 274 us
  starting transfers between devices  112 us (41%)
  waiting for transfers between devices  88.1 us (32%)
  Pallas kernels  33.8 us (12%)
  local copies, waits for them, and re-layouts  21.7 us (8%)
  blocking collectives  16.6 us (6%)
    all_to_all x9, waiting for transfers between devices, swapped(): lax.all_to_all(value, 'shard', 0, 0, axis_index_groups=groups, tiled=True)  57.8 us
    ppermute x14, starting transfers between devices, over(): return lax.ppermute(value, 'shard', pairs)  56.7 us
    all_to_all x9, starting transfers between devices, swapped(): lax.all_to_all(value, 'shard', 0, 0, axis_index_groups=groups, tiled=True)  49.3 us
    pallas_call x27, Pallas kernels, call(): pl.pallas_call(body, out_shape=outs, grid_spec=pltpu.PrefetchScalarGridSp...  33.8 us
    ppermute x14, waiting for transfers between devices, over(): return lax.ppermute(value, 'shard', pairs)  23.9 us
    unnamed x87, local copies, waits for them, and re-layouts  21.7 us
    all_to_all x1, blocking collectives, swapped(): lax.all_to_all(value, 'shard', 0, 0, axis_index_groups=groups, tiled=True)  16.6 us
    ppermute x2, waiting for transfers between devices, shifted(): lax.ppermute(value, axis, [(source, source + steps) for source in range(l...  6.45 us
  transfers between devices with their start and end apart: 25, of which 21 were waited for; matrix products, arithmetic and copies ran while one was open for 0% of the time, Pallas kernels for 8%

profile of v3, /device:TPU:7, one launch (start us, length us, event | category | flops | bytes accessed | tf_op | source)
XLA Modules:
  0.0 273.7 jit_solution(5737973357694863854)
XLA Ops:
  1.5 1.6 copy-done
  7.2 2.6 collective-permute-start
  12.2 2.0 halves.1
  14.2 2.3 collective-permute-start.2
  16.5 2.0 collective-permute-start.3
  18.5 6.8 %all-to-all-start = ((bf16[8,128,256]{2,1,0:T(8,128)(2,1)}), bf16[8,128,256]{2,1,0:T(8,128)(2,1)}, u32[]{:S(2)}, u32[]{:S(2)}) async-start(bf16[8,128,256]{2,1,0:T(8,128)(2,1)} %backward_core_sum.2.refs_8_.refs_3_), calls=%async_computation | async-start | bytes 1048576 | tf_op jit(solution)/shard_map/all_to_all | solution.py:37
  29.6 2.6 collective-permute-start.1
  32.2 1.6 collective-permute-done.1.refs_1_
  34.7 8.7 %all-to-all-done.refs_0_ = bf16[8,128,256]{2,1,0:T(8,128)(2,1)} async-done(((bf16[8,128,256]{2,1,0:T(8,128)(2,1)}), bf16[8,128,256]{2,1,0:T(8,128)(2,1)}, u32[]{:S(2)}, u32[]{:S(2)}) %all-to-all-start) | async-done | bytes 524320 | tf_op jit(solution)/shard_map/all_to_all | solution.py:37
  43.4 4.2 %all-to-all-start.1 = ((bf16[8,144,256]{2,1,0:T(8,128)(2,1)}), bf16[8,144,256]{2,1,0:T(8,128)(2,1)}, u32[]{:S(2)}, u32[]{:S(2)}) async-start(bf16[8,144,256]{2,1,0:T(8,128)(2,1)} %forward_core_sum.2.refs_1_), calls=%async_computation.1 | async-start | bytes 1179648 | tf_op jit(solution)/shard_map/all_to_all | solution.py:37
  48.8 10.6 %collective-permute-start.4 = (bf16[128,256]{1,0:T(8,128)(2,1)S(1)}, bf16[128,256]{1,0:T(8,128)(2,1)S(1)}, u32[]{:S(2)}, u32[]{:S(2)}) collective-permute-start(bf16[128,256]{1,0:T(8,128)(2,1)S(1)} %backward_ring_sum.2.refs_0_), channel_id=1, source_target_pairs={{0,2},{1,3},{2,0},{3,1},{4,6},{5,7},{6,4},{7,5},{8,10},{9,11},{10,... | collective-permute-start | bytes 196616 | tf_op jit(solution)/shard_map/ppermute | solution.py:257
  59.4 2.0 collective-permute-done.4.refs_1_
  62.3 4.8 %all-to-all-done.1.refs_0_ = bf16[8,144,256]{2,1,0:T(8,128)(2,1)} async-done(((bf16[8,144,256]{2,1,0:T(8,128)(2,1)}), bf16[8,144,256]{2,1,0:T(8,128)(2,1)}, u32[]{:S(2)}, u32[]{:S(2)}) %all-to-all-start.1) | async-done | bytes 589856 | tf_op jit(solution)/shard_map/all_to_all | solution.py:37
  67.0 4.1 %all-to-all-start.2 = ((bf16[8,128,256]{2,1,0:T(8,128)(2,1)}), bf16[8,128,256]{2,1,0:T(8,128)(2,1)}, u32[]{:S(2)}, u32[]{:S(2)}) async-start(bf16[8,128,256]{2,1,0:T(8,128)(2,1)} %backward_share.2.refs_1_), calls=%async_computation.2 | async-start | bytes 1048576 | tf_op jit(solution)/shard_map/all_to_all | solution.py:37
  72.3 10.6 %collective-permute-start.5 = (bf16[144,256]{1,0:T(8,128)(2,1)S(1)}, bf16[144,256]{1,0:T(8,128)(2,1)S(1)}, u32[]{:S(2)}, u32[]{:S(2)}) collective-permute-start(bf16[144,256]{1,0:T(8,128)(2,1)S(1)} %forward_ring_sum.2.refs_0_), channel_id=1, source_target_pairs={{0,2},{1,3},{2,0},{3,1},{4,6},{5,7},{6,4},{7,5},{8,10},{9,11},{10,... | collective-permute-start | bytes 221192 | tf_op jit(solution)/shard_map/ppermute | solution.py:257
  83.0 2.2 collective-permute-done.5.refs_1_
  86.1 3.1 %all-to-all-done.2.refs_1_ = bf16[8,128,256]{2,1,0:T(8,128)(2,1)} async-done(((bf16[8,128,256]{2,1,0:T(8,128)(2,1)}), bf16[8,128,256]{2,1,0:T(8,128)(2,1)}, u32[]{:S(2)}, u32[]{:S(2)}) %all-to-all-start.2) | async-done | bytes 524320 | tf_op jit(solution)/shard_map/all_to_all | solution.py:37
  89.1 4.1 %all-to-all-start.3 = ((bf16[8,128,256]{2,1,0:T(8,128)(2,1)}), bf16[8,128,256]{2,1,0:T(8,128)(2,1)}, u32[]{:S(2)}, u32[]{:S(2)}) async-start(bf16[8,128,256]{2,1,0:T(8,128)(2,1)} %forward_share.2.refs_4_), calls=%async_computation.3 | async-start | bytes 1048576 | tf_op jit(solution)/shard_map/all_to_all | solution.py:37
  94.9 2.4 backward_product.2
  97.3 3.7 %collective-permute-start.6 = (f32[128,256]{1,0:T(8,128)S(1)}, f32[128,256]{1,0:T(8,128)S(1)}, u32[]{:S(2)}, u32[]{:S(2)}) collective-permute-start(f32[128,256]{1,0:T(8,128)S(1)} %get-tuple-element.53), channel_id=1, source_target_pairs={{0,1},{1,0},{2,3},{3,2},{4,5},{5,4},{6,7},{7,6},{8,9},{9,8},{10,11... | collective-permute-start | bytes 393224 | tf_op jit(solution)/shard_map/ppermute | solution.py:257
  103.5 5.7 %all-to-all-done.3.refs_1_ = bf16[8,128,256]{2,1,0:T(8,128)(2,1)} async-done(((bf16[8,128,256]{2,1,0:T(8,128)(2,1)}), bf16[8,128,256]{2,1,0:T(8,128)(2,1)}, u32[]{:S(2)}, u32[]{:S(2)}) %all-to-all-start.3) | async-done | bytes 524320 | tf_op jit(solution)/shard_map/all_to_all | solution.py:37
  110.1 2.5 forward_product.2
  112.6 4.5 %collective-permute-start.7 = (f32[128,256]{1,0:T(8,128)S(1)}, f32[128,256]{1,0:T(8,128)S(1)}, u32[]{:S(2)}, u32[]{:S(2)}) collective-permute-start(f32[128,256]{1,0:T(8,128)S(1)} %get-tuple-element.57), channel_id=1, source_target_pairs={{0,1},{1,0},{2,3},{3,2},{4,5},{5,4},{6,7},{7,6},{8,9},{9,8},{10,11... | collective-permute-start | bytes 393224 | tf_op jit(solution)/shard_map/ppermute | solution.py:257
  118.1 3.9 %collective-permute-start.8 = (bf16[128,256]{1,0:T(8,128)(2,1)S(1)}, bf16[128,256]{1,0:T(8,128)(2,1)S(1)}, u32[]{:S(2)}, u32[]{:S(2)}) collective-permute-start(bf16[128,256]{1,0:T(8,128)(2,1)S(1)} %forward_end.2), channel_id=1, source_target_pairs={{0,32},{32,64},{64,96},{96,128},{128,160},{160,192},{192,224},{224... | collective-permute-start | bytes 196616 | tf_op jit(solution)/shard_map/ppermute | solution.py:47
  123.3 2.0 forward_start.3
  126.8 3.3 %collective-permute-start.9 = (bf16[8,144,256]{2,1,0:T(8,128)(2,1)}, bf16[8,144,256]{2,1,0:T(8,128)(2,1)}, u32[]{:S(2)}, u32[]{:S(2)}) collective-permute-start(bf16[8,144,256]{2,1,0:T(8,128)(2,1)} %get-tuple-element.60), channel_id=1, source_target_pairs={{0,1},{1,0},{2,3},{3,2},{4,5},{5,4},{6,7},{7,6},{8,9},{9,8},{10,11... | collective-permute-start | bytes 1769480 | tf_op jit(solution)/shard_map/ppermute | solution.py:257
  130.2 10.7 %all-to-all-start.4 = ((f32[32,8,128]{2,1,0:T(8,128)}), f32[32,8,128]{2,1,0:T(8,128)}, u32[]{:S(2)}, u32[]{:S(2)}) async-start(f32[32,8,128]{2,1,0:T(8,128)} %copy-done.13), calls=%async_computation.4 | async-start | bytes 262144 | tf_op jit(solution)/shard_map/all_to_all | solution.py:37
  141.9 2.0 forward_core_sum.3.refs_5_
  143.9 10.1 %all-to-all-done.4.refs_4_ = f32[32,8,128]{2,1,0:T(8,128)} async-done(((f32[32,8,128]{2,1,0:T(8,128)}), f32[32,8,128]{2,1,0:T(8,128)}, u32[]{:S(2)}, u32[]{:S(2)}) %all-to-all-start.4) | async-done | bytes 131104 | tf_op jit(solution)/shard_map/all_to_all | solution.py:37
  154.0 4.2 %all-to-all-start.5 = ((bf16[8,144,256]{2,1,0:T(8,128)(2,1)}), bf16[8,144,256]{2,1,0:T(8,128)(2,1)}, u32[]{:S(2)}, u32[]{:S(2)}) async-start(bf16[8,144,256]{2,1,0:T(8,128)(2,1)} %forward_core_sum.3.refs_5_), calls=%async_computation.5 | async-start | bytes 1179648 | tf_op jit(solution)/shard_map/all_to_all | solution.py:37
  162.3 2.4 collective-permute-start.10
  164.8 5.1 %collective-permute-done.10.refs_3_ = bf16[128,256]{1,0:T(8,128)(2,1)S(1)} collective-permute-done((bf16[128,256]{1,0:T(8,128)(2,1)S(1)}, bf16[128,256]{1,0:T(8,128)(2,1)S(1)}, u32[]{:S(2)}, u32[]{:S(2)}) %collective-permute-start.10) | collective-permute-done | bytes 65568 | tf_op jit(solution)/shard_map/ppermute | solution.py:47
  173.6 2.8 %collective-permute-start.11 = (bf16[8,128,256]{2,1,0:T(8,128)(2,1)S(1)}, bf16[8,128,256]{2,1,0:T(8,128)(2,1)S(1)}, u32[]{:S(2)}, u32[]{:S(2)}) collective-permute-start(bf16[8,128,256]{2,1,0:T(8,128)(2,1)S(1)} %get-tuple-element.66), channel_id=1, source_target_pairs={{0,1},{1,0},{2,3},{3,2},{4,5},{5,4},{6,7},{7,6},{8,9},{9,8},{10,11... | collective-permute-start | bytes 1572872 | tf_op jit(solution)/shard_map/ppermute | solution.py:257
  178.9 6.8 %all-to-all-start.6 = ((bf16[8,128,256]{2,1,0:T(8,128)(2,1)}), bf16[8,128,256]{2,1,0:T(8,128)(2,1)}, u32[]{:S(2)}, u32[]{:S(2)}) async-start(bf16[8,128,256]{2,1,0:T(8,128)(2,1)} %backward_core_sum.3.refs_1_), calls=%async_computation.6 | async-start | bytes 1048576 | tf_op jit(solution)/shard_map/all_to_all | solution.py:37
  186.8 3.4 %collective-permute-start.12 = (bf16[144,256]{1,0:T(8,128)(2,1)S(1)}, bf16[144,256]{1,0:T(8,128)(2,1)S(1)}, u32[]{:S(2)}, u32[]{:S(2)}) collective-permute-start(bf16[144,256]{1,0:T(8,128)(2,1)S(1)} %forward_ring_sum.3.refs_0_), channel_id=1, source_target_pairs={{0,2},{1,3},{2,0},{3,1},{4,6},{5,7},{6,4},{7,5},{8,10},{9,11},{10,... | collective-permute-start | bytes 221192 | tf_op jit(solution)/shard_map/ppermute | solution.py:257
  190.3 5.6 %collective-permute-done.12.refs_1_ = bf16[144,256]{1,0:T(8,128)(2,1)S(1)} collective-permute-done((bf16[144,256]{1,0:T(8,128)(2,1)S(1)}, bf16[144,256]{1,0:T(8,128)(2,1)S(1)}, u32[]{:S(2)}, u32[]{:S(2)}) %collective-permute-start.12) | collective-permute-done | bytes 73760 | tf_op jit(solution)/shard_map/ppermute | solution.py:257
  196.8 6.9 %all-to-all-done.6.refs_0_ = bf16[8,128,256]{2,1,0:T(8,128)(2,1)} async-done(((bf16[8,128,256]{2,1,0:T(8,128)(2,1)}), bf16[8,128,256]{2,1,0:T(8,128)(2,1)}, u32[]{:S(2)}, u32[]{:S(2)}) %all-to-all-start.6) | async-done | bytes 524320 | tf_op jit(solution)/shard_map/all_to_all | solution.py:37
  203.8 4.1 %all-to-all-start.7 = ((bf16[8,128,256]{2,1,0:T(8,128)(2,1)}), bf16[8,128,256]{2,1,0:T(8,128)(2,1)}, u32[]{:S(2)}, u32[]{:S(2)}) async-start(bf16[8,128,256]{2,1,0:T(8,128)(2,1)} %forward_share.3.refs_1_), calls=%async_computation.7 | async-start | bytes 1048576 | tf_op jit(solution)/shard_map/all_to_all | solution.py:37
  209.0 3.4 %collective-permute-start.13 = (bf16[128,256]{1,0:T(8,128)(2,1)S(1)}, bf16[128,256]{1,0:T(8,128)(2,1)S(1)}, u32[]{:S(2)}, u32[]{:S(2)}) collective-permute-start(bf16[128,256]{1,0:T(8,128)(2,1)S(1)} %backward_ring_sum.3.refs_0_), channel_id=1, source_target_pairs={{0,2},{1,3},{2,0},{3,1},{4,6},{5,7},{6,4},{7,5},{8,10},{9,11},{10,... | collective-permute-start | bytes 196616 | tf_op jit(solution)/shard_map/ppermute | solution.py:257
  212.5 5.5 %collective-permute-done.13.refs_1_ = bf16[128,256]{1,0:T(8,128)(2,1)S(1)} collective-permute-done((bf16[128,256]{1,0:T(8,128)(2,1)S(1)}, bf16[128,256]{1,0:T(8,128)(2,1)S(1)}, u32[]{:S(2)}, u32[]{:S(2)}) %collective-permute-start.13) | collective-permute-done | bytes 65568 | tf_op jit(solution)/shard_map/ppermute | solution.py:257
  218.9 7.0 %all-to-all-done.7.refs_1_ = bf16[8,128,256]{2,1,0:T(8,128)(2,1)} async-done(((bf16[8,128,256]{2,1,0:T(8,128)(2,1)}), bf16[8,128,256]{2,1,0:T(8,128)(2,1)}, u32[]{:S(2)}, u32[]{:S(2)}) %all-to-all-start.7) | async-done | bytes 524320 | tf_op jit(solution)/shard_map/all_to_all | solution.py:37
  225.9 4.1 %all-to-all-start.8 = ((bf16[8,128,256]{2,1,0:T(8,128)(2,1)}), bf16[8,128,256]{2,1,0:T(8,128)(2,1)}, u32[]{:S(2)}, u32[]{:S(2)}) async-start(bf16[8,128,256]{2,1,0:T(8,128)(2,1)} %backward_share.3.refs_4_), calls=%async_computation.8 | async-start | bytes 1048576 | tf_op jit(solution)/shard_map/all_to_all | solution.py:37
  230.0 2.4 forward_product.3
  232.4 2.4 collective-permute-start.14
  236.5 11.5 %all-to-all-done.8.refs_1_ = bf16[8,128,256]{2,1,0:T(8,128)(2,1)} async-done(((bf16[8,128,256]{2,1,0:T(8,128)(2,1)}), bf16[8,128,256]{2,1,0:T(8,128)(2,1)}, u32[]{:S(2)}, u32[]{:S(2)}) %all-to-all-start.8) | async-done | bytes 524320 | tf_op jit(solution)/shard_map/all_to_all | solution.py:37
  250.4 2.4 backward_product.3
  252.8 2.4 collective-permute-start.15
  256.3 16.6 %all_to_all.50.refs_4_ = f32[32,8,128]{2,1,0:T(8,128)S(1)} all-to-all(f32[32,8,128]{2,1,0:T(8,128)S(1)} %get-tuple-element.76), channel_id=1, replica_groups=mesh['segment'=16,'shard'=32] {'shard'}, dimensions={0} | all-to-all | bytes 262144 | tf_op jit(solution)/shard_map/all_to_all | solution.py:37
  (118 shorter events, 46.5 us)
Async XLA Ops:
  1.5 1.6 copy-start
  5.6 6.6 %copy-start.1 = (bf16[1,4096,256]{2,1,0:T(8,128)(2,1)S(1)}, bf16[1,4096,256]{2,1,0:T(8,128)(2,1)}, u32[]{:S(2)}) copy-start(bf16[1,4096,256]{2,1,0:T(8,128)(2,1)} %param.14) | copy-start | bytes 6291460
  5.6 6.6 %copy-start.2 = (bf16[1,256,4096]{2,1,0:T(8,128)(2,1)S(1)}, bf16[1,256,4096]{2,1,0:T(8,128)(2,1)}, u32[]{:S(2)}) copy-start(bf16[1,256,4096]{2,1,0:T(8,128)(2,1)} %param.13) | copy-start | bytes 6291460
  7.2 7.0 %copy-start.21 = (bf16[128,256]{1,0:T(8,128)(2,1)}, bf16[128,256]{1,0:T(8,128)(2,1)S(1)}, u32[]{:S(2)}) copy-start(bf16[128,256]{1,0:T(8,128)(2,1)S(1)} %get-tuple-element.62.refs_0_) | copy-start | bytes 196612
  7.2 4.1 %collective-permute-start = (bf16[8,128,256]{2,1,0:T(8,128)(2,1)S(1)}, bf16[8,128,256]{2,1,0:T(8,128)(2,1)S(1)}, u32[]{:S(2)}, u32[]{:S(2)}) collective-permute-start(bf16[8,128,256]{2,1,0:T(8,128)(2,1)S(1)} %get-tuple-element.43), channel_id=1, source_target_pairs={{0,1},{1,0},{2,3},{3,2},{4,5},{5,4},{6,7},{7,6},{8,9},{9,8},{10,11... | collective-permute-start | bytes 1572872 | tf_op jit(solution)/shard_map/ppermute | solution.py:257
  12.2 13.2 %copy-start.7 = (bf16[1,8,64,256]{3,2,1,0:T(8,128)(2,1)S(1)}, bf16[1,8,64,256]{3,2,1,0:T(8,128)(2,1)}, u32[]{:S(2)}) copy-start(bf16[1,8,64,256]{3,2,1,0:T(8,128)(2,1)} %param.21) | copy-start | bytes 786436
  12.2 13.2 %copy-start.19 = (bf16[1,128,256]{2,1,0:T(8,128)(2,1)S(1)}, bf16[1,128,256]{2,1,0:T(8,128)(2,1)}, u32[]{:S(2)}) copy-start(bf16[1,128,256]{2,1,0:T(8,128)(2,1)} %param.16) | copy-start | bytes 196612
  14.2 29.2 %collective-permute-start.2 = (bf16[256,2048]{1,0:T(8,128)(2,1)}, bf16[256,2048]{1,0:T(8,128)(2,1)S(1)}, u32[]{:S(2)}, u32[]{:S(2)}) collective-permute-start(bf16[256,2048]{1,0:T(8,128)(2,1)} %get-tuple-element.47), channel_id=1, source_target_pairs={{0,1},{1,0},{2,3},{3,2},{4,5},{5,4},{6,7},{7,6},{8,9},{9,8},{10,11... | collective-permute-start | bytes 3145736 | tf_op jit(solution)/shard_map/ppermute | solution.py:257
  16.5 27.0 %collective-permute-start.3 = (bf16[2048,256]{1,0:T(8,128)(2,1)}, bf16[2048,256]{1,0:T(8,128)(2,1)}, u32[]{:S(2)}, u32[]{:S(2)}) collective-permute-start(bf16[2048,256]{1,0:T(8,128)(2,1)} %get-tuple-element.48), channel_id=1, source_target_pairs={{0,1},{1,0},{2,3},{3,2},{4,5},{5,4},{6,7},{7,6},{8,9},{9,8},{10,11... | collective-permute-start | bytes 3145736 | tf_op jit(solution)/shard_map/ppermute | solution.py:257
  18.5 24.9 %all-to-all-start = ((bf16[8,128,256]{2,1,0:T(8,128)(2,1)}), bf16[8,128,256]{2,1,0:T(8,128)(2,1)}, u32[]{:S(2)}, u32[]{:S(2)}) async-start(bf16[8,128,256]{2,1,0:T(8,128)(2,1)} %backward_core_sum.2.refs_8_.refs_3_), calls=%async_computation | async-start | bytes 1048576 | tf_op jit(solution)/shard_map/all_to_all | solution.py:37
  25.4 1.6 copy-start.3
  29.6 32.7 %copy-start.27 = (bf16[128,256]{1,0:T(8,128)(2,1)}, bf16[128,256]{1,0:T(8,128)(2,1)S(1)}, u32[]{:S(2)}) copy-start(bf16[128,256]{1,0:T(8,128)(2,1)S(1)} %get-tuple-element.44.refs_0_) | copy-start | bytes 196612
  29.6 4.2 %collective-permute-start.1 = (bf16[8,144,256]{2,1,0:T(8,128)(2,1)S(1)}, bf16[8,144,256]{2,1,0:T(8,128)(2,1)S(1)}, u32[]{:S(2)}, u32[]{:S(2)}) collective-permute-start(bf16[8,144,256]{2,1,0:T(8,128)(2,1)S(1)} %get-tuple-element.46), channel_id=1, source_target_pairs={{0,1},{1,0},{2,3},{3,2},{4,5},{5,4},{6,7},{7,6},{8,9},{9,8},{10,11... | collective-permute-start | bytes 1769480 | tf_op jit(solution)/shard_map/ppermute | solution.py:257
  43.4 23.6 %all-to-all-start.1 = ((bf16[8,144,256]{2,1,0:T(8,128)(2,1)}), bf16[8,144,256]{2,1,0:T(8,128)(2,1)}, u32[]{:S(2)}, u32[]{:S(2)}) async-start(bf16[8,144,256]{2,1,0:T(8,128)(2,1)} %forward_core_sum.2.refs_1_), calls=%async_computation.1 | async-start | bytes 1179648 | tf_op jit(solution)/shard_map/all_to_all | solution.py:37
  48.8 12.7 %collective-permute-start.4 = (bf16[128,256]{1,0:T(8,128)(2,1)S(1)}, bf16[128,256]{1,0:T(8,128)(2,1)S(1)}, u32[]{:S(2)}, u32[]{:S(2)}) collective-permute-start(bf16[128,256]{1,0:T(8,128)(2,1)S(1)} %backward_ring_sum.2.refs_0_), channel_id=1, source_target_pairs={{0,2},{1,3},{2,0},{3,1},{4,6},{5,7},{6,4},{7,5},{8,10},{9,11},{10,... | collective-permute-start | bytes 196616 | tf_op jit(solution)/shard_map/ppermute | solution.py:257
  67.0 22.1 %all-to-all-start.2 = ((bf16[8,128,256]{2,1,0:T(8,128)(2,1)}), bf16[8,128,256]{2,1,0:T(8,128)(2,1)}, u32[]{:S(2)}, u32[]{:S(2)}) async-start(bf16[8,128,256]{2,1,0:T(8,128)(2,1)} %backward_share.2.refs_1_), calls=%async_computation.2 | async-start | bytes 1048576 | tf_op jit(solution)/shard_map/all_to_all | solution.py:37
  72.3 12.8 %collective-permute-start.5 = (bf16[144,256]{1,0:T(8,128)(2,1)S(1)}, bf16[144,256]{1,0:T(8,128)(2,1)S(1)}, u32[]{:S(2)}, u32[]{:S(2)}) collective-permute-start(bf16[144,256]{1,0:T(8,128)(2,1)S(1)} %forward_ring_sum.2.refs_0_), channel_id=1, source_target_pairs={{0,2},{1,3},{2,0},{3,1},{4,6},{5,7},{6,4},{7,5},{8,10},{9,11},{10,... | collective-permute-start | bytes 221192 | tf_op jit(solution)/shard_map/ppermute | solution.py:257
  89.1 20.0 %all-to-all-start.3 = ((bf16[8,128,256]{2,1,0:T(8,128)(2,1)}), bf16[8,128,256]{2,1,0:T(8,128)(2,1)}, u32[]{:S(2)}, u32[]{:S(2)}) async-start(bf16[8,128,256]{2,1,0:T(8,128)(2,1)} %forward_share.2.refs_4_), calls=%async_computation.3 | async-start | bytes 1048576 | tf_op jit(solution)/shard_map/all_to_all | solution.py:37
  93.3 1.6 copy-start.4
  94.9 7.1 %copy-start.10 = (bf16[1,2,128,256]{3,2,1,0:T(8,128)(2,1)S(1)}, bf16[1,2,128,256]{3,2,1,0:T(8,128)(2,1)}, u32[]{:S(2)}) copy-start(bf16[1,2,128,256]{3,2,1,0:T(8,128)(2,1)} %param.20) | copy-start | bytes 393220
  94.9 7.1 %copy-start.31 = (f32[1,256]{1,0:T(1,128)S(1)}, f32[1,256]{1,0:T(1,128)}, u32[]{:S(2)}) copy-start(f32[1,256]{1,0:T(1,128)} %refs_3_.7) | copy-start | bytes 3076
  97.3 4.7 %collective-permute-start.6 = (f32[128,256]{1,0:T(8,128)S(1)}, f32[128,256]{1,0:T(8,128)S(1)}, u32[]{:S(2)}, u32[]{:S(2)}) collective-permute-start(f32[128,256]{1,0:T(8,128)S(1)} %get-tuple-element.53), channel_id=1, source_target_pairs={{0,1},{1,0},{2,3},{3,2},{4,5},{5,4},{6,7},{7,6},{8,9},{9,8},{10,11... | collective-permute-start | bytes 393224 | tf_op jit(solution)/shard_map/ppermute | solution.py:257
  110.1 8.0 %copy-start.28 = (bf16[128,256]{1,0:T(8,128)(2,1)S(1)}, bf16[128,256]{1,0:T(8,128)(2,1)}, u32[]{:S(2)}) copy-start(bf16[128,256]{1,0:T(8,128)(2,1)} %copy-done.27) | copy-start | bytes 196612
  110.1 13.2 %copy-start.5 = (bf16[1,256,4096]{2,1,0:T(8,128)(2,1)S(1)}, bf16[1,256,4096]{2,1,0:T(8,128)(2,1)}, u32[]{:S(2)}) copy-start(bf16[1,256,4096]{2,1,0:T(8,128)(2,1)} %param.13) | copy-start | bytes 6291460
  110.1 13.2 %copy-start.29 = (bf16[1,128,256]{2,1,0:T(8,128)(2,1)S(1)}, bf16[1,128,256]{2,1,0:T(8,128)(2,1)}, u32[]{:S(2)}) copy-start(bf16[1,128,256]{2,1,0:T(8,128)(2,1)} %refs_4_.2) | copy-start | bytes 196612
  110.1 13.2 %copy-start.32 = (f32[1,256]{1,0:T(1,128)S(1)}, f32[1,256]{1,0:T(1,128)}, u32[]{:S(2)}) copy-start(f32[1,256]{1,0:T(1,128)} %refs_3_.7) | copy-start | bytes 3076
  110.1 13.2 %copy-start.38 = (s32[1,2,2]{2,1,0:T(2,128)S(1)}, s32[1,2,2]{2,1,0:T(2,128)}, u32[]{:S(2)}) copy-start(s32[1,2,2]{2,1,0:T(2,128)} %param.24) | copy-start | bytes 52
  112.6 5.4 %collective-permute-start.7 = (f32[128,256]{1,0:T(8,128)S(1)}, f32[128,256]{1,0:T(8,128)S(1)}, u32[]{:S(2)}, u32[]{:S(2)}) collective-permute-start(f32[128,256]{1,0:T(8,128)S(1)} %get-tuple-element.57), channel_id=1, source_target_pairs={{0,1},{1,0},{2,3},{3,2},{4,5},{5,4},{6,7},{7,6},{8,9},{9,8},{10,11... | collective-permute-start | bytes 393224 | tf_op jit(solution)/shard_map/ppermute | solution.py:257
  118.1 5.2 %collective-permute-start.8 = (bf16[128,256]{1,0:T(8,128)(2,1)S(1)}, bf16[128,256]{1,0:T(8,128)(2,1)S(1)}, u32[]{:S(2)}, u32[]{:S(2)}) collective-permute-start(bf16[128,256]{1,0:T(8,128)(2,1)S(1)} %forward_end.2), channel_id=1, source_target_pairs={{0,32},{32,64},{64,96},{96,128},{128,160},{160,192},{192,224},{224... | collective-permute-start | bytes 196616 | tf_op jit(solution)/shard_map/ppermute | solution.py:47
  126.8 43.1 %copy-start.9 = (bf16[1,8,64,256]{3,2,1,0:T(8,128)(2,1)S(1)}, bf16[1,8,64,256]{3,2,1,0:T(8,128)(2,1)}, u32[]{:S(2)}) copy-start(bf16[1,8,64,256]{3,2,1,0:T(8,128)(2,1)} %param.22) | copy-start | bytes 786436
  126.8 14.0 %collective-permute-start.9 = (bf16[8,144,256]{2,1,0:T(8,128)(2,1)}, bf16[8,144,256]{2,1,0:T(8,128)(2,1)}, u32[]{:S(2)}, u32[]{:S(2)}) collective-permute-start(bf16[8,144,256]{2,1,0:T(8,128)(2,1)} %get-tuple-element.60), channel_id=1, source_target_pairs={{0,1},{1,0},{2,3},{3,2},{4,5},{5,4},{6,7},{7,6},{8,9},{9,8},{10,11... | collective-permute-start | bytes 1769480 | tf_op jit(solution)/shard_map/ppermute | solution.py:257
  130.2 23.9 %all-to-all-start.4 = ((f32[32,8,128]{2,1,0:T(8,128)}), f32[32,8,128]{2,1,0:T(8,128)}, u32[]{:S(2)}, u32[]{:S(2)}) async-start(f32[32,8,128]{2,1,0:T(8,128)} %copy-done.13), calls=%async_computation.4 | async-start | bytes 262144 | tf_op jit(solution)/shard_map/all_to_all | solution.py:37
  154.0 24.9 %all-to-all-start.5 = ((bf16[8,144,256]{2,1,0:T(8,128)(2,1)}), bf16[8,144,256]{2,1,0:T(8,128)(2,1)}, u32[]{:S(2)}, u32[]{:S(2)}) async-start(bf16[8,144,256]{2,1,0:T(8,128)(2,1)} %forward_core_sum.3.refs_5_), calls=%async_computation.5 | async-start | bytes 1179648 | tf_op jit(solution)/shard_map/all_to_all | solution.py:37
  162.3 2.4 copy-start.41
  162.3 7.6 %collective-permute-start.10 = (bf16[128,256]{1,0:T(8,128)(2,1)S(1)}, bf16[128,256]{1,0:T(8,128)(2,1)S(1)}, u32[]{:S(2)}, u32[]{:S(2)}) collective-permute-start(bf16[128,256]{1,0:T(8,128)(2,1)S(1)} %get-tuple-element.64), channel_id=1, source_target_pairs={{32,0},{64,32},{96,64},{128,96},{160,128},{192,160},{224,192},{256... | collective-permute-start | bytes 196616 | tf_op jit(solution)/shard_map/ppermute | solution.py:47
  173.6 4.3 %collective-permute-start.11 = (bf16[8,128,256]{2,1,0:T(8,128)(2,1)S(1)}, bf16[8,128,256]{2,1,0:T(8,128)(2,1)S(1)}, u32[]{:S(2)}, u32[]{:S(2)}) collective-permute-start(bf16[8,128,256]{2,1,0:T(8,128)(2,1)S(1)} %get-tuple-element.66), channel_id=1, source_target_pairs={{0,1},{1,0},{2,3},{3,2},{4,5},{5,4},{6,7},{7,6},{8,9},{9,8},{10,11... | collective-permute-start | bytes 1572872 | tf_op jit(solution)/shard_map/ppermute | solution.py:257
  178.9 24.9 %all-to-all-start.6 = ((bf16[8,128,256]{2,1,0:T(8,128)(2,1)}), bf16[8,128,256]{2,1,0:T(8,128)(2,1)}, u32[]{:S(2)}, u32[]{:S(2)}) async-start(bf16[8,128,256]{2,1,0:T(8,128)(2,1)} %backward_core_sum.3.refs_1_), calls=%async_computation.6 | async-start | bytes 1048576 | tf_op jit(solution)/shard_map/all_to_all | solution.py:37
  186.8 9.1 %collective-permute-start.12 = (bf16[144,256]{1,0:T(8,128)(2,1)S(1)}, bf16[144,256]{1,0:T(8,128)(2,1)S(1)}, u32[]{:S(2)}, u32[]{:S(2)}) collective-permute-start(bf16[144,256]{1,0:T(8,128)(2,1)S(1)} %forward_ring_sum.3.refs_0_), channel_id=1, source_target_pairs={{0,2},{1,3},{2,0},{3,1},{4,6},{5,7},{6,4},{7,5},{8,10},{9,11},{10,... | collective-permute-start | bytes 221192 | tf_op jit(solution)/shard_map/ppermute | solution.py:257
  203.8 22.1 %all-to-all-start.7 = ((bf16[8,128,256]{2,1,0:T(8,128)(2,1)}), bf16[8,128,256]{2,1,0:T(8,128)(2,1)}, u32[]{:S(2)}, u32[]{:S(2)}) async-start(bf16[8,128,256]{2,1,0:T(8,128)(2,1)} %forward_share.3.refs_1_), calls=%async_computation.7 | async-start | bytes 1048576 | tf_op jit(solution)/shard_map/all_to_all | solution.py:37
  209.0 9.0 %collective-permute-start.13 = (bf16[128,256]{1,0:T(8,128)(2,1)S(1)}, bf16[128,256]{1,0:T(8,128)(2,1)S(1)}, u32[]{:S(2)}, u32[]{:S(2)}) collective-permute-start(bf16[128,256]{1,0:T(8,128)(2,1)S(1)} %backward_ring_sum.3.refs_0_), channel_id=1, source_target_pairs={{0,2},{1,3},{2,0},{3,1},{4,6},{5,7},{6,4},{7,5},{8,10},{9,11},{10,... | collective-permute-start | bytes 196616 | tf_op jit(solution)/shard_map/ppermute | solution.py:257
  225.9 22.1 %all-to-all-start.8 = ((bf16[8,128,256]{2,1,0:T(8,128)(2,1)}), bf16[8,128,256]{2,1,0:T(8,128)(2,1)}, u32[]{:S(2)}, u32[]{:S(2)}) async-start(bf16[8,128,256]{2,1,0:T(8,128)(2,1)} %backward_share.3.refs_4_), calls=%async_computation.8 | async-start | bytes 1048576 | tf_op jit(solution)/shard_map/all_to_all | solution.py:37
  230.0 5.8 %copy-start.26 = (bf16[128,256]{1,0:T(8,128)(2,1)S(1)}, bf16[128,256]{1,0:T(8,128)(2,1)}, u32[]{:S(2)}) copy-start(bf16[128,256]{1,0:T(8,128)(2,1)} %copy-done.25) | copy-start | bytes 196612
  232.4 23.8 %copy-start.34 = (f32[1,256]{1,0:T(1,128)S(1)}, f32[1,256]{1,0:T(1,128)}, u32[]{:S(2)}) copy-start(f32[1,256]{1,0:T(1,128)} %refs_3_.7) | copy-start | bytes 3076
  232.4 3.4 %collective-permute-start.14 = (f32[128,256]{1,0:T(8,128)S(1)}, f32[128,256]{1,0:T(8,128)S(1)}, u32[]{:S(2)}, u32[]{:S(2)}) collective-permute-start(f32[128,256]{1,0:T(8,128)S(1)} %get-tuple-element.71), channel_id=1, source_target_pairs={{0,1},{1,0},{2,3},{3,2},{4,5},{5,4},{6,7},{7,6},{8,9},{9,8},{10,11... | collective-permute-start | bytes 393224 | tf_op jit(solution)/shard_map/ppermute | solution.py:257
  250.4 22.5 %copy-start.24 = (bf16[128,256]{1,0:T(8,128)(2,1)S(1)}, bf16[128,256]{1,0:T(8,128)(2,1)}, u32[]{:S(2)}) copy-start(bf16[128,256]{1,0:T(8,128)(2,1)} %copy-done.23) | copy-start | bytes 196612
  250.4 22.5 %copy-start.36 = (f32[8,128]{1,0:T(8,128)S(1)}, f32[8,128]{1,0:T(8,128)}, u32[]{:S(2)}) copy-start(f32[8,128]{1,0:T(8,128)} %copy-done.35) | copy-start | bytes 12292
  250.4 22.5 %copy-start.42 = (f32[1,256]{1,0:T(1,128)S(1)}, f32[1,256]{1,0:T(1,128)}, u32[]{:S(2)}) copy-start(f32[1,256]{1,0:T(1,128)} %copy-done.41) | copy-start | bytes 3076
  252.8 3.4 %collective-permute-start.15 = (f32[128,256]{1,0:T(8,128)S(1)}, f32[128,256]{1,0:T(8,128)S(1)}, u32[]{:S(2)}, u32[]{:S(2)}) collective-permute-start(f32[128,256]{1,0:T(8,128)S(1)} %get-tuple-element.74), channel_id=1, source_target_pairs={{0,1},{1,0},{2,3},{3,2},{4,5},{5,4},{6,7},{7,6},{8,9},{9,8},{10,11... | collective-permute-start | bytes 393224 | tf_op jit(solution)/shard_map/ppermute | solution.py:257
  (20 other events, 16.1 us)

commit v4 on v3

--- a/solution.py
+++ b/solution.py
@@ -19,6 +19,8 @@
 F32 = jnp.float32
 BF16 = jnp.bfloat16
 VMEM_LIMIT = 20 * 1024 * 1024
+WIDE_LIMIT = 56 * 1024 * 1024
+DOT_ROWS = 16
 
 
 def core_pairs():
@@ -47,7 +49,7 @@
     return lax.ppermute(value, axis, [(source, source + steps) for source in range(leading, last)])
 
 
-def call(kernel, name, outs, *, prefetch=(), blocks=None, operands=(), after=()):
+def call(kernel, name, outs, *, prefetch=(), blocks=None, operands=(), after=(), limit=VMEM_LIMIT):
     blocks = blocks or {}
     first, last = len(prefetch) + len(operands), len(prefetch) + len(operands) + len(after)
 
@@ -71,7 +73,7 @@
             in_specs=in_specs + [pl.BlockSpec(memory_space=pl.ANY)] * len(after),
             out_specs=[pl.BlockSpec(out.shape, lambda *_, rank=len(out.shape): (0,) * rank) for out in outs],
         ),
-        compiler_params=pltpu.CompilerParams(vmem_limit_bytes=VMEM_LIMIT),
+        compiler_params=pltpu.CompilerParams(vmem_limit_bytes=limit),
         cost_estimate=pl.CostEstimate(flops=0, bytes_accessed=0, transcendentals=0),
         name=name,
     )(*prefetch, *operands, *after)
@@ -193,9 +195,8 @@
     out[...] = jnp.broadcast_to(value[None], out.shape)
 
 
-def halves(value, output, value_out, output_out):
-    value_out[...] = value[...]
-    output_out[...] = output[...]
+def half(weight, out):
+    out[...] = weight[...]
 
 
 def forward_product(blocks, own_weight, other_weight, mine, others):
@@ -231,15 +232,15 @@
             kept = saved[k].astype(F32)
             terms.append(kept * kept)
     rows = [across(jnp.sum(term, axis=1, keepdims=True)) for term in terms]
-    rows.append(jnp.zeros((8 - len(rows), ROWS), F32))
+    rows.append(jnp.zeros((DOT_ROWS - len(rows), ROWS), F32))
     dots[...] = jnp.broadcast_to(jnp.concatenate(rows, axis=0)[None], dots.shape)
 
 
 def backward_end(tick, g, scaled_grad, saved, gain, dots, *refs):
     before, (out, gain_out, *left) = refs[: 2 if tick else 0], refs[2 if tick else 0 :]
-    total = dots[0]
+    total = dots[0, :8]
     for j in range(1, dots.shape[0]):
-        total = total + dots[j]
+        total = total + dots[j, :8]
     if tick == 0:
         squares = total[1:2]
         left[0][...] = jnp.broadcast_to(total[2:3], left[0].shape)
@@ -321,6 +322,7 @@
             operands=(*messages, backward_base[0], backward_base[0], output_local),
             blocks=base_blocks(count, lambda meta: tick + meta[0]),
             after=after,
+            limit=VMEM_LIMIT if tick else WIDE_LIMIT,
         )
         operands = (keep, over(send, core_pairs()))
         return g, *call(core_sum, "backward_core_sum", [eight], operands=operands)
@@ -335,6 +337,18 @@
 
     def with_meta(kernel):
         return lambda _, *refs: kernel(*refs)
+
+    def exchanged_half(weight, block, index_map, *after):
+        (own,) = call(
+            with_meta(half),
+            "half",
+            [shape_of(*block)],
+            prefetch=(meta,),
+            operands=(weight,),
+            blocks={0: (block, index_map)},
+            after=after,
+        )
+        return over(own, core_pairs())
 
     def forward_finish(x, gathered, *after):
         mine, others = call(
@@ -358,11 +372,12 @@
             operands=(gathered, value_local, value_other),
             blocks=own_columns,
             after=after,
+            limit=WIDE_LIMIT if tick else VMEM_LIMIT,
         )
         return call(
             functools.partial(backward_middle, tick),
             "backward_middle",
-            [wide, shape_of(4 * RING, 8, ROWS, dtype=F32)],
+            [wide, shape_of(4 * RING, DOT_ROWS, ROWS, dtype=F32)],
             operands=(mine, over(others, core_pairs()), saved, norm_gain),
         )
 
@@ -380,28 +395,17 @@
     back_landed = swapped(gated, rings())
 
     x, pieces = forward_begin(0, [arriving[0]], gated)
-    value_half, output_half = call(
-        with_meta(halves),
-        "halves",
-        [shape_of(WIDTH, HALF), shape_of(HALF, WIDTH)],
-        prefetch=(meta,),
-        operands=(value_local, output_local),
-        blocks={
-            0: ((WIDTH, HALF), lambda i, meta: (0, 1 - meta[3])),
-            1: ((HALF, WIDTH), lambda i, meta: (1 - meta[3], 0)),
-        },
-        after=(gated,),
-    )
-    value_other, output_other = over(value_half, core_pairs()), over(output_half, core_pairs())
-    gated = gate(pieces, back_landed, value_other, output_other)
+    gated = gate(pieces, back_landed)
     landed = swapped(gated, rings())
 
+    value_other = exchanged_half(value_local, (WIDTH, HALF), lambda i, meta: (0, 1 - meta[3]), gated)
     copies = backward_turn(back_landed, gated)
-    gated = gate(copies, landed)
+    gated = gate(copies, landed, value_other)
     back_gathered = swapped(gated, rings())
 
+    output_other = exchanged_half(output_local, (HALF, WIDTH), lambda i, meta: (1 - meta[3], 0), gated)
     copies = forward_turn(landed, gated)
-    gated = gate(copies, back_gathered)
+    gated = gate(copies, back_gathered, output_other)
     gathered = swapped(gated, rings())
 
     scaled_grad, dots = backward_dots(0, back_gathered, gated)

time: 276 us -> 277 us (level)
  waiting for transfers between devices: 88.1 us -> 101 us
  local copies, waits for them, and re-layouts: 21.7 us -> 11.1 us
  starting transfers between devices: 112 us -> 107 us
    all_to_all x9, waiting for transfers between devices: 57.8 us -> 70.3 us  [swapped(): lax.all_to_all(value, 'shard', 0, 0, axis_index_groups=groups, tiled=True)]
    unnamed x87 -> x77, local copies, waits for them, and re-layouts: 21.7 us -> 11.1 us
    all_to_all x9, starting transfers between devices: 49.3 us -> 45 us  [swapped(): lax.all_to_all(value, 'shard', 0, 0, axis_index_groups=groups, tiled=True)]
    pallas_call x27 -> x28, Pallas kernels: 33.8 us -> 36 us  [call(): pl.pallas_call(body, out_shape=outs, grid_spec=pltpu.PrefetchScalarGridSp...]
  transfers between devices with their start and end apart: 25 -> 25, of which waited for: 21 -> 22; matrix products, arithmetic and copies ran while one was open for 0% -> 0% of each run, Pallas kernels for 8% -> 7%
where the time goes in v4:
time: 277 us; the launch traced here: 276 us
  starting transfers between devices  107 us (39%)
  waiting for transfers between devices  101 us (36%)
  Pallas kernels  36 us (13%)
  blocking collectives  19.2 us (7%)
  local copies, waits for them, and re-layouts  11.1 us (4%)
    all_to_all x9, waiting for transfers between devices, swapped(): lax.all_to_all(value, 'shard', 0, 0, axis_index_groups=groups, tiled=True)  70.3 us
    ppermute x14, starting transfers between devices, over(): return lax.ppermute(value, 'shard', pairs)  55.3 us
    all_to_all x9, starting transfers between devices, swapped(): lax.all_to_all(value, 'shard', 0, 0, axis_index_groups=groups, tiled=True)  45 us
    pallas_call x28, Pallas kernels, call(): pl.pallas_call(body, out_shape=outs, grid_spec=pltpu.PrefetchScalarGridSp...  36 us
    ppermute x14, waiting for transfers between devices, over(): return lax.ppermute(value, 'shard', pairs)  24.3 us
    all_to_all x1, blocking collectives, swapped(): lax.all_to_all(value, 'shard', 0, 0, axis_index_groups=groups, tiled=True)  19.2 us
    unnamed x77, local copies, waits for them, and re-layouts  11.1 us
    ppermute x2, starting transfers between devices, shifted(): lax.ppermute(value, axis, [(source, source + steps) for source in range(l...  6.38 us
  transfers between devices with their start and end apart: 25, of which 22 were waited for; matrix products, arithmetic and copies ran while one was open for 0% of the time, Pallas kernels for 7%

profile of v4, /device:TPU:7, one launch (start us, length us, event | category | flops | bytes accessed | tf_op | source)
XLA Modules:
  0.0 275.6 jit_solution(6170237766941160934)
XLA Ops:
  2.7 4.5 %backward_start.2 = (bf16[128,256]{1,0:T(8,128)(2,1)}, bf16[8,128,256]{2,1,0:T(8,128)(2,1)}, bf16[8,128,256]{2,1,0:T(8,128)(2,1)}) custom-call(s32[17,2]{1,0:T(8,128)} %copy.18.refs_0_, s32[4]{0:T(128)} %pad_add_fusion.refs_1_.refs_0_, s32[2,2]{1,0:T(2,128)} %bitcast.40, bf16[128,256]{1,0:T(8,128)(2,1)} %bitcast.43, bf16[8,64,256]{2,1,0:T(8,128)(2,1)} %bitcast.29, ...), custom_call_target="tpu_custom_call" | custom-call | tf_op jit(solution)/shard_map/backward_start/pallas_call | solution.py:67
  7.2 2.6 collective-permute-start
  9.7 1.7 collective-permute-done.refs_1_
  13.4 6.8 %all-to-all-start = ((bf16[8,128,256]{2,1,0:T(8,128)(2,1)}), bf16[8,128,256]{2,1,0:T(8,128)(2,1)S(1)}, u32[]{:S(2)}, u32[]{:S(2)}) async-start(bf16[8,128,256]{2,1,0:T(8,128)(2,1)} %backward_core_sum.2.refs_8_), calls=%async_computation | async-start | bytes 1048576 | tf_op jit(solution)/shard_map/all_to_all | solution.py:39
  21.6 2.6 collective-permute-start.1
  26.7 11.5 %all-to-all-done.refs_0_ = bf16[8,128,256]{2,1,0:T(8,128)(2,1)S(1)} async-done(((bf16[8,128,256]{2,1,0:T(8,128)(2,1)}), bf16[8,128,256]{2,1,0:T(8,128)(2,1)S(1)}, u32[]{:S(2)}, u32[]{:S(2)}) %all-to-all-start) | async-done | bytes 524320 | tf_op jit(solution)/shard_map/all_to_all | solution.py:39
  40.6 2.5 collective-permute-start.3
  43.1 4.2 %all-to-all-start.1 = ((bf16[8,144,256]{2,1,0:T(8,128)(2,1)}), bf16[8,144,256]{2,1,0:T(8,128)(2,1)}, u32[]{:S(2)}, u32[]{:S(2)}) async-start(bf16[8,144,256]{2,1,0:T(8,128)(2,1)} %forward_core_sum.2.refs_1_.refs_2_), calls=%async_computation.1 | async-start | bytes 1179648 | tf_op jit(solution)/shard_map/all_to_all | solution.py:39
  48.4 10.6 %collective-permute-start.2 = (bf16[128,256]{1,0:T(8,128)(2,1)S(1)}, bf16[128,256]{1,0:T(8,128)(2,1)S(1)}, u32[]{:S(2)}, u32[]{:S(2)}) collective-permute-start(bf16[128,256]{1,0:T(8,128)(2,1)S(1)} %backward_ring_sum.2.refs_0_), channel_id=1, source_target_pairs={{0,2},{1,3},{2,0},{3,1},{4,6},{5,7},{6,4},{7,5},{8,10},{9,11},{10,... | collective-permute-start | bytes 196616 | tf_op jit(solution)/shard_map/ppermute | solution.py:258
  59.1 2.4 collective-permute-done.2.refs_1_
  62.4 4.4 %all-to-all-done.1.refs_0_ = bf16[8,144,256]{2,1,0:T(8,128)(2,1)} async-done(((bf16[8,144,256]{2,1,0:T(8,128)(2,1)}), bf16[8,144,256]{2,1,0:T(8,128)(2,1)}, u32[]{:S(2)}, u32[]{:S(2)}) %all-to-all-start.1) | async-done | bytes 589856 | tf_op jit(solution)/shard_map/all_to_all | solution.py:39
  68.4 2.3 collective-permute-start.5
  70.7 4.2 %all-to-all-start.2 = ((bf16[8,128,256]{2,1,0:T(8,128)(2,1)}), bf16[8,128,256]{2,1,0:T(8,128)(2,1)}, u32[]{:S(2)}, u32[]{:S(2)}) async-start(bf16[8,128,256]{2,1,0:T(8,128)(2,1)} %backward_share.2.refs_1_.refs_2_), calls=%async_computation.2 | async-start | bytes 1048576 | tf_op jit(solution)/shard_map/all_to_all | solution.py:39
  76.1 10.6 %collective-permute-start.4 = (bf16[144,256]{1,0:T(8,128)(2,1)S(1)}, bf16[144,256]{1,0:T(8,128)(2,1)S(1)}, u32[]{:S(2)}, u32[]{:S(2)}) collective-permute-start(bf16[144,256]{1,0:T(8,128)(2,1)S(1)} %forward_ring_sum.2.refs_0_), channel_id=1, source_target_pairs={{0,2},{1,3},{2,0},{3,1},{4,6},{5,7},{6,4},{7,5},{8,10},{9,11},{10,... | collective-permute-start | bytes 221192 | tf_op jit(solution)/shard_map/ppermute | solution.py:258
  86.7 2.6 collective-permute-done.4.refs_1_
  90.2 2.8 %all-to-all-done.2.refs_1_ = bf16[8,128,256]{2,1,0:T(8,128)(2,1)} async-done(((bf16[8,128,256]{2,1,0:T(8,128)(2,1)}), bf16[8,128,256]{2,1,0:T(8,128)(2,1)}, u32[]{:S(2)}, u32[]{:S(2)}) %all-to-all-start.2) | async-done | bytes 524320 | tf_op jit(solution)/shard_map/all_to_all | solution.py:39
  93.0 4.1 %all-to-all-start.3 = ((bf16[8,128,256]{2,1,0:T(8,128)(2,1)}), bf16[8,128,256]{2,1,0:T(8,128)(2,1)}, u32[]{:S(2)}, u32[]{:S(2)}) async-start(bf16[8,128,256]{2,1,0:T(8,128)(2,1)} %forward_share.2.refs_4_), calls=%async_computation.3 | async-start | bytes 1048576 | tf_op jit(solution)/shard_map/all_to_all | solution.py:39
  98.7 2.4 backward_product.2
  101.1 2.5 collective-permute-start.6
  106.3 8.8 %all-to-all-done.3.refs_1_ = bf16[8,128,256]{2,1,0:T(8,128)(2,1)} async-done(((bf16[8,128,256]{2,1,0:T(8,128)(2,1)}), bf16[8,128,256]{2,1,0:T(8,128)(2,1)}, u32[]{:S(2)}, u32[]{:S(2)}) %all-to-all-start.3) | async-done | bytes 524320 | tf_op jit(solution)/shard_map/all_to_all | solution.py:39
  115.1 2.5 forward_product.2
  117.6 2.4 collective-permute-start.7
  121.0 3.9 %collective-permute-start.8 = (bf16[128,256]{1,0:T(8,128)(2,1)S(1)}, bf16[128,256]{1,0:T(8,128)(2,1)S(1)}, u32[]{:S(2)}, u32[]{:S(2)}) collective-permute-start(bf16[128,256]{1,0:T(8,128)(2,1)S(1)} %forward_end.2), channel_id=1, source_target_pairs={{0,32},{32,64},{64,96},{96,128},{128,160},{160,192},{192,224},{224... | collective-permute-start | bytes 196616 | tf_op jit(solution)/shard_map/ppermute | solution.py:49
  126.2 2.0 forward_start.3
  128.9 3.3 %collective-permute-start.9 = (bf16[8,144,256]{2,1,0:T(8,128)(2,1)}, bf16[8,144,256]{2,1,0:T(8,128)(2,1)}, u32[]{:S(2)}, u32[]{:S(2)}) collective-permute-start(bf16[8,144,256]{2,1,0:T(8,128)(2,1)} %get-tuple-element.56), channel_id=1, source_target_pairs={{0,1},{1,0},{2,3},{3,2},{4,5},{5,4},{6,7},{7,6},{8,9},{9,8},{10,11... | collective-permute-start | bytes 1769480 | tf_op jit(solution)/shard_map/ppermute | solution.py:258
  132.2 10.6 %all-to-all-start.4 = ((f32[32,16,128]{2,1,0:T(8,128)}), f32[32,16,128]{2,1,0:T(8,128)S(1)}, u32[]{:S(2)}, u32[]{:S(2)}) async-start(f32[32,16,128]{2,1,0:T(8,128)} %get-tuple-element.51.refs_4_), calls=%async_computation.4 | async-start | bytes 524288 | tf_op jit(solution)/shard_map/all_to_all | solution.py:39
  142.8 2.0 forward_core_sum.3.refs_5_
  144.9 13.3 %all-to-all-done.4.refs_4_ = f32[32,16,128]{2,1,0:T(8,128)S(1)} async-done(((f32[32,16,128]{2,1,0:T(8,128)}), f32[32,16,128]{2,1,0:T(8,128)S(1)}, u32[]{:S(2)}, u32[]{:S(2)}) %all-to-all-start.4) | async-done | bytes 262176 | tf_op jit(solution)/shard_map/all_to_all | solution.py:39
  158.1 3.5 %all-to-all-start.5 = ((bf16[8,144,256]{2,1,0:T(8,128)(2,1)}), bf16[8,144,256]{2,1,0:T(8,128)(2,1)S(1)}, u32[]{:S(2)}, u32[]{:S(2)}) async-start(bf16[8,144,256]{2,1,0:T(8,128)(2,1)} %forward_core_sum.3.refs_5_), calls=%async_computation.5 | async-start | bytes 1179648 | tf_op jit(solution)/shard_map/all_to_all | solution.py:39
  163.4 2.5 collective-permute-start.10
  165.9 4.9 %collective-permute-done.10.refs_3_ = bf16[128,256]{1,0:T(8,128)(2,1)S(1)} collective-permute-done((bf16[128,256]{1,0:T(8,128)(2,1)S(1)}, bf16[128,256]{1,0:T(8,128)(2,1)S(1)}, u32[]{:S(2)}, u32[]{:S(2)}) %collective-permute-start.10) | collective-permute-done | bytes 65568 | tf_op jit(solution)/shard_map/ppermute | solution.py:49
  173.1 3.2 %collective-permute-start.11 = (bf16[8,128,256]{2,1,0:T(8,128)(2,1)S(1)}, bf16[8,128,256]{2,1,0:T(8,128)(2,1)S(1)}, u32[]{:S(2)}, u32[]{:S(2)}) collective-permute-start(bf16[8,128,256]{2,1,0:T(8,128)(2,1)S(1)} %get-tuple-element.62), channel_id=1, source_target_pairs={{0,1},{1,0},{2,3},{3,2},{4,5},{5,4},{6,7},{7,6},{8,9},{9,8},{10,11... | collective-permute-start | bytes 1572872 | tf_op jit(solution)/shard_map/ppermute | solution.py:258
  178.7 2.3 all-to-all-done.5.refs_0_
  181.0 4.6 %all-to-all-start.6 = ((bf16[8,128,256]{2,1,0:T(8,128)(2,1)}), bf16[8,128,256]{2,1,0:T(8,128)(2,1)S(1)}, u32[]{:S(2)}, u32[]{:S(2)}) async-start(bf16[8,128,256]{2,1,0:T(8,128)(2,1)} %backward_core_sum.3.refs_1_), calls=%async_computation.6 | async-start | bytes 1048576 | tf_op jit(solution)/shard_map/all_to_all | solution.py:39
  185.6 3.9 %collective-permute-start.12 = (bf16[144,256]{1,0:T(8,128)(2,1)S(1)}, bf16[144,256]{1,0:T(8,128)(2,1)S(1)}, u32[]{:S(2)}, u32[]{:S(2)}) collective-permute-start(bf16[144,256]{1,0:T(8,128)(2,1)S(1)} %forward_ring_sum.3.refs_0_), channel_id=1, source_target_pairs={{0,2},{1,3},{2,0},{3,1},{4,6},{5,7},{6,4},{7,5},{8,10},{9,11},{10,... | collective-permute-start | bytes 221192 | tf_op jit(solution)/shard_map/ppermute | solution.py:258
  189.5 5.2 %collective-permute-done.12.refs_1_ = bf16[144,256]{1,0:T(8,128)(2,1)S(1)} collective-permute-done((bf16[144,256]{1,0:T(8,128)(2,1)S(1)}, bf16[144,256]{1,0:T(8,128)(2,1)S(1)}, u32[]{:S(2)}, u32[]{:S(2)}) %collective-permute-start.12) | collective-permute-done | bytes 73760 | tf_op jit(solution)/shard_map/ppermute | solution.py:258
  195.6 7.9 %all-to-all-done.6.refs_0_ = bf16[8,128,256]{2,1,0:T(8,128)(2,1)S(1)} async-done(((bf16[8,128,256]{2,1,0:T(8,128)(2,1)}), bf16[8,128,256]{2,1,0:T(8,128)(2,1)S(1)}, u32[]{:S(2)}, u32[]{:S(2)}) %all-to-all-start.6) | async-done | bytes 524320 | tf_op jit(solution)/shard_map/all_to_all | solution.py:39
  203.5 3.5 %all-to-all-start.7 = ((bf16[8,128,256]{2,1,0:T(8,128)(2,1)}), bf16[8,128,256]{2,1,0:T(8,128)(2,1)S(1)}, u32[]{:S(2)}, u32[]{:S(2)}) async-start(bf16[8,128,256]{2,1,0:T(8,128)(2,1)} %forward_share.3.refs_1_), calls=%async_computation.7 | async-start | bytes 1048576 | tf_op jit(solution)/shard_map/all_to_all | solution.py:39
  207.1 3.9 %collective-permute-start.13 = (bf16[128,256]{1,0:T(8,128)(2,1)S(1)}, bf16[128,256]{1,0:T(8,128)(2,1)S(1)}, u32[]{:S(2)}, u32[]{:S(2)}) collective-permute-start(bf16[128,256]{1,0:T(8,128)(2,1)S(1)} %backward_ring_sum.3.refs_0_), channel_id=1, source_target_pairs={{0,2},{1,3},{2,0},{3,1},{4,6},{5,7},{6,4},{7,5},{8,10},{9,11},{10,... | collective-permute-start | bytes 196616 | tf_op jit(solution)/shard_map/ppermute | solution.py:258
  211.0 5.1 %collective-permute-done.13.refs_1_ = bf16[128,256]{1,0:T(8,128)(2,1)S(1)} collective-permute-done((bf16[128,256]{1,0:T(8,128)(2,1)S(1)}, bf16[128,256]{1,0:T(8,128)(2,1)S(1)}, u32[]{:S(2)}, u32[]{:S(2)}) %collective-permute-start.13) | collective-permute-done | bytes 65568 | tf_op jit(solution)/shard_map/ppermute | solution.py:258
  216.9 7.9 %all-to-all-done.7.refs_1_ = bf16[8,128,256]{2,1,0:T(8,128)(2,1)S(1)} async-done(((bf16[8,128,256]{2,1,0:T(8,128)(2,1)}), bf16[8,128,256]{2,1,0:T(8,128)(2,1)S(1)}, u32[]{:S(2)}, u32[]{:S(2)}) %all-to-all-start.7) | async-done | bytes 524320 | tf_op jit(solution)/shard_map/all_to_all | solution.py:39
  224.9 3.5 %all-to-all-start.8 = ((bf16[8,128,256]{2,1,0:T(8,128)(2,1)}), bf16[8,128,256]{2,1,0:T(8,128)(2,1)S(1)}, u32[]{:S(2)}, u32[]{:S(2)}) async-start(bf16[8,128,256]{2,1,0:T(8,128)(2,1)} %backward_share.3.refs_4_), calls=%async_computation.8 | async-start | bytes 1048576 | tf_op jit(solution)/shard_map/all_to_all | solution.py:39
  228.4 2.2 forward_product.3
  230.6 2.5 collective-permute-start.14
  234.8 11.5 %all-to-all-done.8.refs_1_ = bf16[8,128,256]{2,1,0:T(8,128)(2,1)S(1)} async-done(((bf16[8,128,256]{2,1,0:T(8,128)(2,1)}), bf16[8,128,256]{2,1,0:T(8,128)(2,1)S(1)}, u32[]{:S(2)}, u32[]{:S(2)}) %all-to-all-start.8) | async-done | bytes 524320 | tf_op jit(solution)/shard_map/all_to_all | solution.py:39
  247.0 3.9 %backward_product.3 = (f32[128,256]{1,0:T(8,128)}, f32[128,256]{1,0:T(8,128)}) custom-call(s32[4]{0:T(128)} %pad_add_fusion.refs_1_.refs_0_, bf16[8,128,256]{2,1,0:T(8,128)(2,1)} %copy-done.37, bf16[256,4096]{1,0:T(8,128)(2,1)} %bitcast.20, bf16[256,2048]{1,0:T(8,128)(2,1)} %copy-done.4, bf16[128,256]{1,0:T(8,128)(2,1)} %forward_end.3.refs_4_), custom_call_target="tpu_custom_call" | custom-call | tf_op jit(solution)/shard_map/backward_product/pallas_call | solution.py:67
  250.9 2.4 collective-permute-start.15
  255.6 19.2 %all_to_all.50.refs_4_ = f32[32,16,128]{2,1,0:T(8,128)S(1)} all-to-all(f32[32,16,128]{2,1,0:T(8,128)S(1)} %get-tuple-element.72), channel_id=1, replica_groups=mesh['segment'=16,'shard'=32] {'shard'}, dimensions={0} | all-to-all | bytes 524288 | tf_op jit(solution)/shard_map/all_to_all | solution.py:39
  (109 shorter events, 36.6 us)
Async XLA Ops:
  2.6 17.6 %copy-start.1 = (bf16[1,256,4096]{2,1,0:T(8,128)(2,1)S(1)}, bf16[1,256,4096]{2,1,0:T(8,128)(2,1)}, u32[]{:S(2)}) copy-start(bf16[1,256,4096]{2,1,0:T(8,128)(2,1)} %param.13) | copy-start | bytes 6291460
  2.6 17.6 %copy-start.5 = (bf16[1,8,64,256]{3,2,1,0:T(8,128)(2,1)S(1)}, bf16[1,8,64,256]{3,2,1,0:T(8,128)(2,1)}, u32[]{:S(2)}) copy-start(bf16[1,8,64,256]{3,2,1,0:T(8,128)(2,1)} %param.21) | copy-start | bytes 786436
  2.6 17.7 %copy-start.12 = (s32[17,2]{1,0:T(8,128)S(1)}, s32[17,2]{1,0:T(8,128)}, u32[]{:S(2)}) copy-start(s32[17,2]{1,0:T(8,128)} %copy.18.refs_0_) | copy-start | bytes 412
  2.6 17.7 %copy-start.16 = (bf16[1,128,256]{2,1,0:T(8,128)(2,1)S(1)}, bf16[1,128,256]{2,1,0:T(8,128)(2,1)}, u32[]{:S(2)}) copy-start(bf16[1,128,256]{2,1,0:T(8,128)(2,1)} %param.16) | copy-start | bytes 196612
  2.6 17.7 %copy-start.24 = (s32[4]{0:T(128)S(1)}, s32[4]{0:T(128)}, u32[]{:S(2)}) copy-start(s32[4]{0:T(128)} %pad_add_fusion.refs_1_.refs_0_) | copy-start | bytes 52
  2.6 17.7 %copy-start.25 = (f32[1,256]{1,0:T(1,128)S(1)}, f32[1,256]{1,0:T(1,128)}, u32[]{:S(2)}) copy-start(f32[1,256]{1,0:T(1,128)} %refs_3_.7) | copy-start | bytes 3076
  2.6 17.7 %copy-start.32 = (s32[1,2,2]{2,1,0:T(2,128)S(1)}, s32[1,2,2]{2,1,0:T(2,128)}, u32[]{:S(2)}) copy-start(s32[1,2,2]{2,1,0:T(2,128)} %param.24) | copy-start | bytes 52
  7.2 4.3 %collective-permute-start = (bf16[8,128,256]{2,1,0:T(8,128)(2,1)}, bf16[8,128,256]{2,1,0:T(8,128)(2,1)S(1)}, u32[]{:S(2)}, u32[]{:S(2)}) collective-permute-start(bf16[8,128,256]{2,1,0:T(8,128)(2,1)} %get-tuple-element.41), channel_id=1, source_target_pairs={{0,1},{1,0},{2,3},{3,2},{4,5},{5,4},{6,7},{7,6},{8,9},{9,8},{10,11... | collective-permute-start | bytes 1572872 | tf_op jit(solution)/shard_map/ppermute | solution.py:258
  13.4 24.8 %all-to-all-start = ((bf16[8,128,256]{2,1,0:T(8,128)(2,1)}), bf16[8,128,256]{2,1,0:T(8,128)(2,1)S(1)}, u32[]{:S(2)}, u32[]{:S(2)}) async-start(bf16[8,128,256]{2,1,0:T(8,128)(2,1)} %backward_core_sum.2.refs_8_), calls=%async_computation | async-start | bytes 1048576 | tf_op jit(solution)/shard_map/all_to_all | solution.py:39
  21.6 19.0 %copy-start.20 = (bf16[128,256]{1,0:T(8,128)(2,1)}, bf16[128,256]{1,0:T(8,128)(2,1)S(1)}, u32[]{:S(2)}) copy-start(bf16[128,256]{1,0:T(8,128)(2,1)S(1)} %get-tuple-element.42.refs_0_) | copy-start | bytes 196612
  21.6 4.2 %collective-permute-start.1 = (bf16[8,144,256]{2,1,0:T(8,128)(2,1)S(1)}, bf16[8,144,256]{2,1,0:T(8,128)(2,1)S(1)}, u32[]{:S(2)}, u32[]{:S(2)}) collective-permute-start(bf16[8,144,256]{2,1,0:T(8,128)(2,1)S(1)} %get-tuple-element.44), channel_id=1, source_target_pairs={{0,1},{1,0},{2,3},{3,2},{4,5},{5,4},{6,7},{7,6},{8,9},{9,8},{10,11... | collective-permute-start | bytes 1769480 | tf_op jit(solution)/shard_map/ppermute | solution.py:258
  40.6 26.2 %copy-start = (bf16[1,4096,256]{2,1,0:T(8,128)(2,1)S(1)}, bf16[1,4096,256]{2,1,0:T(8,128)(2,1)}, u32[]{:S(2)}) copy-start(bf16[1,4096,256]{2,1,0:T(8,128)(2,1)} %param.14) | copy-start | bytes 6291460
  40.6 26.2 %collective-permute-start.3 = (bf16[256,2048]{1,0:T(8,128)(2,1)}, bf16[256,2048]{1,0:T(8,128)(2,1)S(1)}, u32[]{:S(2)}, u32[]{:S(2)}) collective-permute-start(bf16[256,2048]{1,0:T(8,128)(2,1)} %half.2), channel_id=1, source_target_pairs={{0,1},{1,0},{2,3},{3,2},{4,5},{5,4},{6,7},{7,6},{8,9},{9,8},{10,11... | collective-permute-start | bytes 3145736 | tf_op jit(solution)/shard_map/ppermute | solution.py:258
  43.1 23.7 %all-to-all-start.1 = ((bf16[8,144,256]{2,1,0:T(8,128)(2,1)}), bf16[8,144,256]{2,1,0:T(8,128)(2,1)}, u32[]{:S(2)}, u32[]{:S(2)}) async-start(bf16[8,144,256]{2,1,0:T(8,128)(2,1)} %forward_core_sum.2.refs_1_.refs_2_), calls=%async_computation.1 | async-start | bytes 1179648 | tf_op jit(solution)/shard_map/all_to_all | solution.py:39
  48.4 13.1 %collective-permute-start.2 = (bf16[128,256]{1,0:T(8,128)(2,1)S(1)}, bf16[128,256]{1,0:T(8,128)(2,1)S(1)}, u32[]{:S(2)}, u32[]{:S(2)}) collective-permute-start(bf16[128,256]{1,0:T(8,128)(2,1)S(1)} %backward_ring_sum.2.refs_0_), channel_id=1, source_target_pairs={{0,2},{1,3},{2,0},{3,1},{4,6},{5,7},{6,4},{7,5},{8,10},{9,11},{10,... | collective-permute-start | bytes 196616 | tf_op jit(solution)/shard_map/ppermute | solution.py:258
  66.8 30.3 %copy-start.4 = (bf16[256,2048]{1,0:T(8,128)(2,1)}, bf16[256,2048]{1,0:T(8,128)(2,1)S(1)}, u32[]{:S(2)}) copy-start(bf16[256,2048]{1,0:T(8,128)(2,1)S(1)} %collective-permute-done.3.refs_3_) | copy-start | bytes 3145732
  68.4 24.5 %collective-permute-start.5 = (bf16[2048,256]{1,0:T(8,128)(2,1)}, bf16[2048,256]{1,0:T(8,128)(2,1)}, u32[]{:S(2)}, u32[]{:S(2)}) collective-permute-start(bf16[2048,256]{1,0:T(8,128)(2,1)} %half.3), channel_id=1, source_target_pairs={{0,1},{1,0},{2,3},{3,2},{4,5},{5,4},{6,7},{7,6},{8,9},{9,8},{10,11... | collective-permute-start | bytes 3145736 | tf_op jit(solution)/shard_map/ppermute | solution.py:258
  70.7 22.2 %all-to-all-start.2 = ((bf16[8,128,256]{2,1,0:T(8,128)(2,1)}), bf16[8,128,256]{2,1,0:T(8,128)(2,1)}, u32[]{:S(2)}, u32[]{:S(2)}) async-start(bf16[8,128,256]{2,1,0:T(8,128)(2,1)} %backward_share.2.refs_1_.refs_2_), calls=%async_computation.2 | async-start | bytes 1048576 | tf_op jit(solution)/shard_map/all_to_all | solution.py:39
  76.1 13.2 %collective-permute-start.4 = (bf16[144,256]{1,0:T(8,128)(2,1)S(1)}, bf16[144,256]{1,0:T(8,128)(2,1)S(1)}, u32[]{:S(2)}, u32[]{:S(2)}) collective-permute-start(bf16[144,256]{1,0:T(8,128)(2,1)S(1)} %forward_ring_sum.2.refs_0_), channel_id=1, source_target_pairs={{0,2},{1,3},{2,0},{3,1},{4,6},{5,7},{6,4},{7,5},{8,10},{9,11},{10,... | collective-permute-start | bytes 221192 | tf_op jit(solution)/shard_map/ppermute | solution.py:258
  93.0 22.1 %all-to-all-start.3 = ((bf16[8,128,256]{2,1,0:T(8,128)(2,1)}), bf16[8,128,256]{2,1,0:T(8,128)(2,1)}, u32[]{:S(2)}, u32[]{:S(2)}) async-start(bf16[8,128,256]{2,1,0:T(8,128)(2,1)} %forward_share.2.refs_4_), calls=%async_computation.3 | async-start | bytes 1048576 | tf_op jit(solution)/shard_map/all_to_all | solution.py:39
  101.1 3.5 %collective-permute-start.6 = (f32[128,256]{1,0:T(8,128)S(1)}, f32[128,256]{1,0:T(8,128)S(1)}, u32[]{:S(2)}, u32[]{:S(2)}) collective-permute-start(f32[128,256]{1,0:T(8,128)S(1)} %get-tuple-element.49), channel_id=1, source_target_pairs={{0,1},{1,0},{2,3},{3,2},{4,5},{5,4},{6,7},{7,6},{8,9},{9,8},{10,11... | collective-permute-start | bytes 393224 | tf_op jit(solution)/shard_map/ppermute | solution.py:258
  104.6 16.3 %copy-start.21 = (bf16[128,256]{1,0:T(8,128)(2,1)S(1)}, bf16[128,256]{1,0:T(8,128)(2,1)}, u32[]{:S(2)}) copy-start(bf16[128,256]{1,0:T(8,128)(2,1)} %copy-done.20) | copy-start | bytes 196612
  115.0 11.2 %copy-start.23 = (bf16[1,128,256]{2,1,0:T(8,128)(2,1)S(1)}, bf16[1,128,256]{2,1,0:T(8,128)(2,1)}, u32[]{:S(2)}) copy-start(bf16[1,128,256]{2,1,0:T(8,128)(2,1)} %refs_4_.2) | copy-start | bytes 196612
  115.1 11.2 %copy-start.27 = (f32[1,256]{1,0:T(1,128)S(1)}, f32[1,256]{1,0:T(1,128)}, u32[]{:S(2)}) copy-start(f32[1,256]{1,0:T(1,128)} %refs_3_.7) | copy-start | bytes 3076
  115.1 11.2 %copy-start.33 = (s32[1,2,2]{2,1,0:T(2,128)S(1)}, s32[1,2,2]{2,1,0:T(2,128)}, u32[]{:S(2)}) copy-start(s32[1,2,2]{2,1,0:T(2,128)} %param.24) | copy-start | bytes 52
  117.6 3.4 %collective-permute-start.7 = (f32[128,256]{1,0:T(8,128)S(1)}, f32[128,256]{1,0:T(8,128)S(1)}, u32[]{:S(2)}, u32[]{:S(2)}) collective-permute-start(f32[128,256]{1,0:T(8,128)S(1)} %get-tuple-element.53), channel_id=1, source_target_pairs={{0,1},{1,0},{2,3},{3,2},{4,5},{5,4},{6,7},{7,6},{8,9},{9,8},{10,11... | collective-permute-start | bytes 393224 | tf_op jit(solution)/shard_map/ppermute | solution.py:258
  121.0 5.2 %collective-permute-start.8 = (bf16[128,256]{1,0:T(8,128)(2,1)S(1)}, bf16[128,256]{1,0:T(8,128)(2,1)S(1)}, u32[]{:S(2)}, u32[]{:S(2)}) collective-permute-start(bf16[128,256]{1,0:T(8,128)(2,1)S(1)} %forward_end.2), channel_id=1, source_target_pairs={{0,32},{32,64},{64,96},{96,128},{128,160},{160,192},{192,224},{224... | collective-permute-start | bytes 196616 | tf_op jit(solution)/shard_map/ppermute | solution.py:49
  128.9 32.8 %copy-start.15 = (f32[128,256]{1,0:T(8,128)S(1)}, f32[128,256]{1,0:T(8,128)}, u32[]{:S(2)}) copy-start(f32[128,256]{1,0:T(8,128)} %copy-done.14) | copy-start | bytes 393220
  128.9 13.9 %collective-permute-start.9 = (bf16[8,144,256]{2,1,0:T(8,128)(2,1)}, bf16[8,144,256]{2,1,0:T(8,128)(2,1)}, u32[]{:S(2)}, u32[]{:S(2)}) collective-permute-start(bf16[8,144,256]{2,1,0:T(8,128)(2,1)} %get-tuple-element.56), channel_id=1, source_target_pairs={{0,1},{1,0},{2,3},{3,2},{4,5},{5,4},{6,7},{7,6},{8,9},{9,8},{10,11... | collective-permute-start | bytes 1769480 | tf_op jit(solution)/shard_map/ppermute | solution.py:258
  132.2 25.9 %all-to-all-start.4 = ((f32[32,16,128]{2,1,0:T(8,128)}), f32[32,16,128]{2,1,0:T(8,128)S(1)}, u32[]{:S(2)}, u32[]{:S(2)}) async-start(f32[32,16,128]{2,1,0:T(8,128)} %get-tuple-element.51.refs_4_), calls=%async_computation.4 | async-start | bytes 524288 | tf_op jit(solution)/shard_map/all_to_all | solution.py:39
  142.8 28.0 %copy-start.6 = (bf16[1,8,64,256]{3,2,1,0:T(8,128)(2,1)S(1)}, bf16[1,8,64,256]{3,2,1,0:T(8,128)(2,1)}, u32[]{:S(2)}) copy-start(bf16[1,8,64,256]{3,2,1,0:T(8,128)(2,1)} %param.22) | copy-start | bytes 786436
  142.8 28.0 %copy-start.17 = (bf16[1,128,256]{2,1,0:T(8,128)(2,1)S(1)}, bf16[1,128,256]{2,1,0:T(8,128)(2,1)}, u32[]{:S(2)}) copy-start(bf16[1,128,256]{2,1,0:T(8,128)(2,1)} %refs_4_.3) | copy-start | bytes 196612
  158.1 22.9 %all-to-all-start.5 = ((bf16[8,144,256]{2,1,0:T(8,128)(2,1)}), bf16[8,144,256]{2,1,0:T(8,128)(2,1)S(1)}, u32[]{:S(2)}, u32[]{:S(2)}) async-start(bf16[8,144,256]{2,1,0:T(8,128)(2,1)} %forward_core_sum.3.refs_5_), calls=%async_computation.5 | async-start | bytes 1179648 | tf_op jit(solution)/shard_map/all_to_all | solution.py:39
  163.4 14.4 %copy-start.30 = (f32[8,128]{1,0:T(8,128)}, f32[8,128]{1,0:T(8,128)S(1)}, u32[]{:S(2)}) copy-start(f32[8,128]{1,0:T(8,128)S(1)} %get-tuple-element.73.refs_5_) | copy-start | bytes 12292
  163.4 14.4 %copy-start.35 = (f32[1,256]{1,0:T(1,128)}, f32[1,256]{1,0:T(1,128)S(1)}, u32[]{:S(2)}) copy-start(f32[1,256]{1,0:T(1,128)S(1)} %get-tuple-element.74.refs_6_) | copy-start | bytes 3076
  163.4 7.4 %collective-permute-start.10 = (bf16[128,256]{1,0:T(8,128)(2,1)S(1)}, bf16[128,256]{1,0:T(8,128)(2,1)S(1)}, u32[]{:S(2)}, u32[]{:S(2)}) collective-permute-start(bf16[128,256]{1,0:T(8,128)(2,1)S(1)} %get-tuple-element.60), channel_id=1, source_target_pairs={{32,0},{64,32},{96,64},{128,96},{160,128},{192,160},{224,192},{256... | collective-permute-start | bytes 196616 | tf_op jit(solution)/shard_map/ppermute | solution.py:49
  173.1 4.7 %collective-permute-start.11 = (bf16[8,128,256]{2,1,0:T(8,128)(2,1)S(1)}, bf16[8,128,256]{2,1,0:T(8,128)(2,1)S(1)}, u32[]{:S(2)}, u32[]{:S(2)}) collective-permute-start(bf16[8,128,256]{2,1,0:T(8,128)(2,1)S(1)} %get-tuple-element.62), channel_id=1, source_target_pairs={{0,1},{1,0},{2,3},{3,2},{4,5},{5,4},{6,7},{7,6},{8,9},{9,8},{10,11... | collective-permute-start | bytes 1572872 | tf_op jit(solution)/shard_map/ppermute | solution.py:258
  181.0 22.5 %all-to-all-start.6 = ((bf16[8,128,256]{2,1,0:T(8,128)(2,1)}), bf16[8,128,256]{2,1,0:T(8,128)(2,1)S(1)}, u32[]{:S(2)}, u32[]{:S(2)}) async-start(bf16[8,128,256]{2,1,0:T(8,128)(2,1)} %backward_core_sum.3.refs_1_), calls=%async_computation.6 | async-start | bytes 1048576 | tf_op jit(solution)/shard_map/all_to_all | solution.py:39
  185.6 9.1 %collective-permute-start.12 = (bf16[144,256]{1,0:T(8,128)(2,1)S(1)}, bf16[144,256]{1,0:T(8,128)(2,1)S(1)}, u32[]{:S(2)}, u32[]{:S(2)}) collective-permute-start(bf16[144,256]{1,0:T(8,128)(2,1)S(1)} %forward_ring_sum.3.refs_0_), channel_id=1, source_target_pairs={{0,2},{1,3},{2,0},{3,1},{4,6},{5,7},{6,4},{7,5},{8,10},{9,11},{10,... | collective-permute-start | bytes 221192 | tf_op jit(solution)/shard_map/ppermute | solution.py:258
  203.5 21.4 %all-to-all-start.7 = ((bf16[8,128,256]{2,1,0:T(8,128)(2,1)}), bf16[8,128,256]{2,1,0:T(8,128)(2,1)S(1)}, u32[]{:S(2)}, u32[]{:S(2)}) async-start(bf16[8,128,256]{2,1,0:T(8,128)(2,1)} %forward_share.3.refs_1_), calls=%async_computation.7 | async-start | bytes 1048576 | tf_op jit(solution)/shard_map/all_to_all | solution.py:39
  207.1 9.0 %collective-permute-start.13 = (bf16[128,256]{1,0:T(8,128)(2,1)S(1)}, bf16[128,256]{1,0:T(8,128)(2,1)S(1)}, u32[]{:S(2)}, u32[]{:S(2)}) collective-permute-start(bf16[128,256]{1,0:T(8,128)(2,1)S(1)} %backward_ring_sum.3.refs_0_), channel_id=1, source_target_pairs={{0,2},{1,3},{2,0},{3,1},{4,6},{5,7},{6,4},{7,5},{8,10},{9,11},{10,... | collective-permute-start | bytes 196616 | tf_op jit(solution)/shard_map/ppermute | solution.py:258
  224.9 21.4 %all-to-all-start.8 = ((bf16[8,128,256]{2,1,0:T(8,128)(2,1)}), bf16[8,128,256]{2,1,0:T(8,128)(2,1)S(1)}, u32[]{:S(2)}, u32[]{:S(2)}) async-start(bf16[8,128,256]{2,1,0:T(8,128)(2,1)} %backward_share.3.refs_4_), calls=%async_computation.8 | async-start | bytes 1048576 | tf_op jit(solution)/shard_map/all_to_all | solution.py:39
  230.6 23.9 %copy-start.10 = (bf16[1,2,128,256]{3,2,1,0:T(8,128)(2,1)S(1)}, bf16[1,2,128,256]{3,2,1,0:T(8,128)(2,1)}, u32[]{:S(2)}) copy-start(bf16[1,2,128,256]{3,2,1,0:T(8,128)(2,1)} %param.20) | copy-start | bytes 393220
  230.6 23.9 %copy-start.29 = (f32[1,256]{1,0:T(1,128)S(1)}, f32[1,256]{1,0:T(1,128)}, u32[]{:S(2)}) copy-start(f32[1,256]{1,0:T(1,128)} %refs_3_.7) | copy-start | bytes 3076
  230.6 3.5 %collective-permute-start.14 = (f32[128,256]{1,0:T(8,128)S(1)}, f32[128,256]{1,0:T(8,128)S(1)}, u32[]{:S(2)}, u32[]{:S(2)}) collective-permute-start(f32[128,256]{1,0:T(8,128)S(1)} %get-tuple-element.67), channel_id=1, source_target_pairs={{0,1},{1,0},{2,3},{3,2},{4,5},{5,4},{6,7},{7,6},{8,9},{9,8},{10,11... | collective-permute-start | bytes 393224 | tf_op jit(solution)/shard_map/ppermute | solution.py:258
  234.8 40.0 %copy-start.31 = (f32[8,128]{1,0:T(8,128)S(1)}, f32[8,128]{1,0:T(8,128)}, u32[]{:S(2)}) copy-start(f32[8,128]{1,0:T(8,128)} %copy-done.30) | copy-start | bytes 12292
  234.8 40.0 %copy-start.36 = (f32[1,256]{1,0:T(1,128)S(1)}, f32[1,256]{1,0:T(1,128)}, u32[]{:S(2)}) copy-start(f32[1,256]{1,0:T(1,128)} %copy-done.35) | copy-start | bytes 3076
  250.9 3.6 %collective-permute-start.15 = (f32[128,256]{1,0:T(8,128)}, f32[128,256]{1,0:T(8,128)S(1)}, u32[]{:S(2)}, u32[]{:S(2)}) collective-permute-start(f32[128,256]{1,0:T(8,128)} %get-tuple-element.70), channel_id=1, source_target_pairs={{0,1},{1,0},{2,3},{3,2},{4,5},{5,4},{6,7},{7,6},{8,9},{9,8},{10,11... | collective-permute-start | bytes 393224 | tf_op jit(solution)/shard_map/ppermute | solution.py:258
  (15 other events, 38.4 us)

commit v5 on v4

--- a/solution.py
+++ b/solution.py
@@ -19,8 +19,7 @@
 F32 = jnp.float32
 BF16 = jnp.bfloat16
 VMEM_LIMIT = 20 * 1024 * 1024
-WIDE_LIMIT = 56 * 1024 * 1024
-DOT_ROWS = 16
+DOT_ROWS = 8
 
 
 def core_pairs():
@@ -49,7 +48,7 @@
     return lax.ppermute(value, axis, [(source, source + steps) for source in range(leading, last)])
 
 
-def call(kernel, name, outs, *, prefetch=(), blocks=None, operands=(), after=(), limit=VMEM_LIMIT):
+def call(kernel, name, outs, *, prefetch=(), blocks=None, operands=(), after=()):
     blocks = blocks or {}
     first, last = len(prefetch) + len(operands), len(prefetch) + len(operands) + len(after)
 
@@ -73,7 +72,7 @@
             in_specs=in_specs + [pl.BlockSpec(memory_space=pl.ANY)] * len(after),
             out_specs=[pl.BlockSpec(out.shape, lambda *_, rank=len(out.shape): (0,) * rank) for out in outs],
         ),
-        compiler_params=pltpu.CompilerParams(vmem_limit_bytes=limit),
+        compiler_params=pltpu.CompilerParams(vmem_limit_bytes=VMEM_LIMIT),
         cost_estimate=pl.CostEstimate(flops=0, bytes_accessed=0, transcendentals=0),
         name=name,
     )(*prefetch, *operands, *after)
@@ -322,18 +321,17 @@
             operands=(*messages, backward_base[0], backward_base[0], output_local),
             blocks=base_blocks(count, lambda meta: tick + meta[0]),
             after=after,
-            limit=VMEM_LIMIT if tick else WIDE_LIMIT,
         )
         operands = (keep, over(send, core_pairs()))
         return g, *call(core_sum, "backward_core_sum", [eight], operands=operands)
 
     def forward_turn(pieces, *after):
         (own,) = call(ring_sum, "forward_ring_sum", [tall], operands=(pieces,), after=after)
-        return call(forward_share, "forward_share", [eight], operands=(own, over(own, z_pairs())))[0]
+        return own, *call(forward_share, "forward_share", [eight], operands=(own, over(own, z_pairs())))
 
     def backward_turn(pieces, *after):
         (own,) = call(ring_sum, "backward_ring_sum", [low], operands=(pieces,), after=after)
-        return call(backward_share, "backward_share", [eight], operands=(own, over(own, z_pairs())))[0]
+        return own, *call(backward_share, "backward_share", [eight], operands=(own, over(own, z_pairs())))
 
     def with_meta(kernel):
         return lambda _, *refs: kernel(*refs)
@@ -372,7 +370,6 @@
             operands=(gathered, value_local, value_other),
             blocks=own_columns,
             after=after,
-            limit=WIDE_LIMIT if tick else VMEM_LIMIT,
         )
         return call(
             functools.partial(backward_middle, tick),
@@ -390,30 +387,29 @@
             after=after,
         )
 
-    g, back_pieces = backward_begin(0, [returning[0]])
-    gated = gate(back_pieces)
+    x, pieces = forward_begin(0, [arriving[0]])
+    gated = gate(pieces)
+    landed = swapped(gated, rings())
+
+    g, back_pieces = backward_begin(0, [returning[0]], gated)
+    gated = gate(back_pieces, landed)
     back_landed = swapped(gated, rings())
 
-    x, pieces = forward_begin(0, [arriving[0]], gated)
-    gated = gate(pieces, back_landed)
-    landed = swapped(gated, rings())
-
-    value_other = exchanged_half(value_local, (WIDTH, HALF), lambda i, meta: (0, 1 - meta[3]), gated)
-    copies = backward_turn(back_landed, gated)
-    gated = gate(copies, landed, value_other)
+    own, copies = forward_turn(landed, gated)
+    output_other = exchanged_half(output_local, (HALF, WIDTH), lambda i, meta: (1 - meta[3], 0), own)
+    gated = gate(copies, back_landed, output_other)
+    gathered = swapped(gated, rings())
+
+    own, copies = backward_turn(back_landed, gated)
+    value_other = exchanged_half(value_local, (WIDTH, HALF), lambda i, meta: (0, 1 - meta[3]), own)
+    gated = gate(copies, gathered, value_other)
     back_gathered = swapped(gated, rings())
-
-    output_other = exchanged_half(output_local, (HALF, WIDTH), lambda i, meta: (1 - meta[3], 0), gated)
-    copies = forward_turn(landed, gated)
-    gated = gate(copies, back_gathered, output_other)
-    gathered = swapped(gated, rings())
-
-    scaled_grad, dots = backward_dots(0, back_gathered, gated)
-    gated = gate(dots, gathered)
-    all_dots = swapped(gated)
 
     segment_out = forward_finish(x, gathered, gated)
     x, pieces = forward_begin(1, [shifted(segment_out, "segment", 1), fresh_inputs])
+    scaled_grad, dots = backward_dots(0, back_gathered)
+    all_dots = swapped(dots)
+
     gated = gate(pieces, all_dots)
     landed = swapped(gated, rings())
 
@@ -422,11 +418,11 @@
     gated = gate(back_pieces, landed)
     back_landed = swapped(gated, rings())
 
-    copies = forward_turn(landed, gated)
+    _, copies = forward_turn(landed, gated)
     gated = gate(copies, back_landed)
     gathered = swapped(gated, rings())
 
-    copies = backward_turn(back_landed, gated)
+    _, copies = backward_turn(back_landed, gated)
     gated = gate(copies, gathered)
     back_gathered = swapped(gated, rings())
 

time: 277 us -> 278 us (level)
  waiting for transfers between devices: 101 us -> 88.3 us
  local copies, waits for them, and re-layouts: 11.1 us -> 21.4 us
  starting transfers between devices: 107 us -> 114 us
    all_to_all x9, waiting for transfers between devices: 70.3 us -> 57 us  [swapped(): lax.all_to_all(value, 'shard', 0, 0, axis_index_groups=groups, tiled=True)]
    unnamed x77 -> x83, local copies, waits for them, and re-layouts: 11.1 us -> 21.4 us
    all_to_all x9, starting transfers between devices: 45 us -> 54 us  [swapped(): lax.all_to_all(value, 'shard', 0, 0, axis_index_groups=groups, tiled=True)]
  transfers between devices with their start and end apart: 25 -> 25, of which waited for: 22 -> 21; matrix products, arithmetic and copies ran while one was open for 0% -> 0% of each run, Pallas kernels for 7% -> 9%
where the time goes in v5:
time: 278 us; the launch traced here: 276 us
  starting transfers between devices  114 us (41%)
  waiting for transfers between devices  88.3 us (32%)
  Pallas kernels  34.1 us (12%)
  local copies, waits for them, and re-layouts  21.4 us (8%)
  blocking collectives  16.6 us (6%)
    all_to_all x9, waiting for transfers between devices, swapped(): lax.all_to_all(value, 'shard', 0, 0, axis_index_groups=groups, tiled=True)  57 us
    all_to_all x9, starting transfers between devices, swapped(): lax.all_to_all(value, 'shard', 0, 0, axis_index_groups=groups, tiled=True)  54 us
    ppermute x14, starting transfers between devices, over(): return lax.ppermute(value, 'shard', pairs)  53.6 us
    pallas_call x28, Pallas kernels, call(): pl.pallas_call(body, out_shape=outs, grid_spec=pltpu.PrefetchScalarGridSp...  34.1 us
    ppermute x14, waiting for transfers between devices, over(): return lax.ppermute(value, 'shard', pairs)  24.7 us
    unnamed x83, local copies, waits for them, and re-layouts  21.4 us
    all_to_all x1, blocking collectives, swapped(): lax.all_to_all(value, 'shard', 0, 0, axis_index_groups=groups, tiled=True)  16.6 us
    ppermute x2, waiting for transfers between devices, shifted(): lax.ppermute(value, axis, [(source, source + steps) for source in range(l...  6.62 us
  transfers between devices with their start and end apart: 25, of which 21 were waited for; matrix products, arithmetic and copies ran while one was open for 0% of the time, Pallas kernels for 9%

profile of v5, /device:TPU:7, one launch (start us, length us, event | category | flops | bytes accessed | tf_op | source)
XLA Modules:
  0.0 275.7 jit_solution(5403844783386664213)
XLA Ops:
  1.5 1.6 copy-done.1
  8.2 2.7 collective-permute-start
  10.9 1.6 collective-permute-done.refs_1_
  13.5 6.8 %all-to-all-start = ((bf16[8,144,256]{2,1,0:T(8,128)(2,1)}), bf16[8,144,256]{2,1,0:T(8,128)(2,1)S(1)}, u32[]{:S(2)}, u32[]{:S(2)}) async-start(bf16[8,144,256]{2,1,0:T(8,128)(2,1)} %forward_core_sum.2.refs_7_), calls=%async_computation | async-start | bytes 1179648 | tf_op jit(solution)/shard_map/all_to_all | solution.py:38
  21.9 2.6 collective-permute-start.1
  26.9 12.7 %all-to-all-done.refs_0_ = bf16[8,144,256]{2,1,0:T(8,128)(2,1)S(1)} async-done(((bf16[8,144,256]{2,1,0:T(8,128)(2,1)}), bf16[8,144,256]{2,1,0:T(8,128)(2,1)S(1)}, u32[]{:S(2)}, u32[]{:S(2)}) %all-to-all-start) | async-done | bytes 589856 | tf_op jit(solution)/shard_map/all_to_all | solution.py:38
  41.3 2.4 collective-permute-start.3
  43.7 4.2 %all-to-all-start.1 = ((bf16[8,128,256]{2,1,0:T(8,128)(2,1)}), bf16[8,128,256]{2,1,0:T(8,128)(2,1)}, u32[]{:S(2)}, u32[]{:S(2)}) async-start(bf16[8,128,256]{2,1,0:T(8,128)(2,1)} %backward_core_sum.2.refs_1_), calls=%async_computation.1 | async-start | bytes 1048576 | tf_op jit(solution)/shard_map/all_to_all | solution.py:38
  47.9 10.7 %collective-permute-start.2 = (bf16[144,256]{1,0:T(8,128)(2,1)S(1)}, bf16[144,256]{1,0:T(8,128)(2,1)S(1)}, u32[]{:S(2)}, u32[]{:S(2)}) collective-permute-start(bf16[144,256]{1,0:T(8,128)(2,1)S(1)} %forward_ring_sum.2.refs_0_.refs_2_), channel_id=1, source_target_pairs={{0,2},{1,3},{2,0},{3,1},{4,6},{5,7},{6,4},{7,5},{8,10},{9,11},{10,... | collective-permute-start | bytes 221192 | tf_op jit(solution)/shard_map/ppermute | solution.py:257
  58.6 2.6 collective-permute-done.2.refs_1_
  62.1 3.9 %all-to-all-done.1.refs_0_ = bf16[8,128,256]{2,1,0:T(8,128)(2,1)} async-done(((bf16[8,128,256]{2,1,0:T(8,128)(2,1)}), bf16[8,128,256]{2,1,0:T(8,128)(2,1)}, u32[]{:S(2)}, u32[]{:S(2)}) %all-to-all-start.1) | async-done | bytes 524320 | tf_op jit(solution)/shard_map/all_to_all | solution.py:38
  68.7 1.6 half.3
  70.3 2.3 collective-permute-start.5
  72.6 4.2 %all-to-all-start.2 = ((bf16[8,128,256]{2,1,0:T(8,128)(2,1)}), bf16[8,128,256]{2,1,0:T(8,128)(2,1)}, u32[]{:S(2)}, u32[]{:S(2)}) async-start(bf16[8,128,256]{2,1,0:T(8,128)(2,1)} %forward_share.2.refs_1_), calls=%async_computation.2 | async-start | bytes 1048576 | tf_op jit(solution)/shard_map/all_to_all | solution.py:38
  76.8 10.7 %collective-permute-start.4 = (bf16[128,256]{1,0:T(8,128)(2,1)S(1)}, bf16[128,256]{1,0:T(8,128)(2,1)S(1)}, u32[]{:S(2)}, u32[]{:S(2)}) collective-permute-start(bf16[128,256]{1,0:T(8,128)(2,1)S(1)} %backward_ring_sum.2.refs_0_.refs_2_), channel_id=1, source_target_pairs={{0,2},{1,3},{2,0},{3,1},{4,6},{5,7},{6,4},{7,5},{8,10},{9,11},{10,... | collective-permute-start | bytes 196616 | tf_op jit(solution)/shard_map/ppermute | solution.py:257
  87.4 2.4 collective-permute-done.4.refs_1_
  90.7 4.2 %all-to-all-done.2.refs_1_ = bf16[8,128,256]{2,1,0:T(8,128)(2,1)} async-done(((bf16[8,128,256]{2,1,0:T(8,128)(2,1)}), bf16[8,128,256]{2,1,0:T(8,128)(2,1)}, u32[]{:S(2)}, u32[]{:S(2)}) %all-to-all-start.2) | async-done | bytes 524320 | tf_op jit(solution)/shard_map/all_to_all | solution.py:38
  94.8 4.1 %all-to-all-start.3 = ((bf16[8,128,256]{2,1,0:T(8,128)(2,1)}), bf16[8,128,256]{2,1,0:T(8,128)(2,1)}, u32[]{:S(2)}, u32[]{:S(2)}) async-start(bf16[8,128,256]{2,1,0:T(8,128)(2,1)} %backward_share.2.refs_4_), calls=%async_computation.3 | async-start | bytes 1048576 | tf_op jit(solution)/shard_map/all_to_all | solution.py:38
  99.0 2.2 forward_product.2
  101.3 2.4 collective-permute-start.6
  104.6 3.9 %collective-permute-start.7 = (bf16[128,256]{1,0:T(8,128)(2,1)S(1)}, bf16[128,256]{1,0:T(8,128)(2,1)S(1)}, u32[]{:S(2)}, u32[]{:S(2)}) collective-permute-start(bf16[128,256]{1,0:T(8,128)(2,1)S(1)} %forward_end.2), channel_id=1, source_target_pairs={{0,32},{32,64},{64,96},{96,128},{128,160},{160,192},{192,224},{224... | collective-permute-start | bytes 196616 | tf_op jit(solution)/shard_map/ppermute | solution.py:48
  110.1 2.0 forward_start.3
  113.5 3.0 %collective-permute-start.8 = (bf16[8,144,256]{2,1,0:T(8,128)(2,1)}, bf16[8,144,256]{2,1,0:T(8,128)(2,1)}, u32[]{:S(2)}, u32[]{:S(2)}) collective-permute-start(bf16[8,144,256]{2,1,0:T(8,128)(2,1)} %get-tuple-element.51), channel_id=1, source_target_pairs={{0,1},{1,0},{2,3},{3,2},{4,5},{5,4},{6,7},{7,6},{8,9},{9,8},{10,11... | collective-permute-start | bytes 1769480 | tf_op jit(solution)/shard_map/ppermute | solution.py:257
  116.9 1.6 copy-done.4
  118.5 2.7 backward_product.2
  121.3 2.4 collective-permute-start.9
  126.9 15.5 %all-to-all-start.4 = ((f32[32,8,128]{2,1,0:T(8,128)}), f32[32,8,128]{2,1,0:T(8,128)}, u32[]{:S(2)}, u32[]{:S(2)}) async-start(f32[32,8,128]{2,1,0:T(8,128)} %copy-done.15), calls=%async_computation.4 | async-start | bytes 262144 | tf_op jit(solution)/shard_map/all_to_all | solution.py:38
  143.5 2.0 forward_core_sum.3.refs_5_
  145.5 10.1 %all-to-all-done.4.refs_4_ = f32[32,8,128]{2,1,0:T(8,128)} async-done(((f32[32,8,128]{2,1,0:T(8,128)}), f32[32,8,128]{2,1,0:T(8,128)}, u32[]{:S(2)}, u32[]{:S(2)}) %all-to-all-start.4) | async-done | bytes 131104 | tf_op jit(solution)/shard_map/all_to_all | solution.py:38
  155.6 4.2 %all-to-all-start.5 = ((bf16[8,144,256]{2,1,0:T(8,128)(2,1)}), bf16[8,144,256]{2,1,0:T(8,128)(2,1)}, u32[]{:S(2)}, u32[]{:S(2)}) async-start(bf16[8,144,256]{2,1,0:T(8,128)(2,1)} %forward_core_sum.3.refs_5_), calls=%async_computation.5 | async-start | bytes 1179648 | tf_op jit(solution)/shard_map/all_to_all | solution.py:38
  163.9 2.4 collective-permute-start.10
  166.3 5.1 %collective-permute-done.10.refs_3_ = bf16[128,256]{1,0:T(8,128)(2,1)S(1)} collective-permute-done((bf16[128,256]{1,0:T(8,128)(2,1)S(1)}, bf16[128,256]{1,0:T(8,128)(2,1)S(1)}, u32[]{:S(2)}, u32[]{:S(2)}) %collective-permute-start.10) | collective-permute-done | bytes 65568 | tf_op jit(solution)/shard_map/ppermute | solution.py:48
  175.2 2.8 %collective-permute-start.11 = (bf16[8,128,256]{2,1,0:T(8,128)(2,1)S(1)}, bf16[8,128,256]{2,1,0:T(8,128)(2,1)S(1)}, u32[]{:S(2)}, u32[]{:S(2)}) collective-permute-start(bf16[8,128,256]{2,1,0:T(8,128)(2,1)S(1)} %get-tuple-element.60), channel_id=1, source_target_pairs={{0,1},{1,0},{2,3},{3,2},{4,5},{5,4},{6,7},{7,6},{8,9},{9,8},{10,11... | collective-permute-start | bytes 1572872 | tf_op jit(solution)/shard_map/ppermute | solution.py:257
  180.5 6.8 %all-to-all-start.6 = ((bf16[8,128,256]{2,1,0:T(8,128)(2,1)}), bf16[8,128,256]{2,1,0:T(8,128)(2,1)}, u32[]{:S(2)}, u32[]{:S(2)}) async-start(bf16[8,128,256]{2,1,0:T(8,128)(2,1)} %backward_core_sum.3.refs_1_), calls=%async_computation.6 | async-start | bytes 1048576 | tf_op jit(solution)/shard_map/all_to_all | solution.py:38
  188.4 3.4 %collective-permute-start.12 = (bf16[144,256]{1,0:T(8,128)(2,1)S(1)}, bf16[144,256]{1,0:T(8,128)(2,1)S(1)}, u32[]{:S(2)}, u32[]{:S(2)}) collective-permute-start(bf16[144,256]{1,0:T(8,128)(2,1)S(1)} %forward_ring_sum.3.refs_0_), channel_id=1, source_target_pairs={{0,2},{1,3},{2,0},{3,1},{4,6},{5,7},{6,4},{7,5},{8,10},{9,11},{10,... | collective-permute-start | bytes 221192 | tf_op jit(solution)/shard_map/ppermute | solution.py:257
  191.9 5.7 %collective-permute-done.12.refs_1_ = bf16[144,256]{1,0:T(8,128)(2,1)S(1)} collective-permute-done((bf16[144,256]{1,0:T(8,128)(2,1)S(1)}, bf16[144,256]{1,0:T(8,128)(2,1)S(1)}, u32[]{:S(2)}, u32[]{:S(2)}) %collective-permute-start.12) | collective-permute-done | bytes 73760 | tf_op jit(solution)/shard_map/ppermute | solution.py:257
  198.5 6.9 %all-to-all-done.6.refs_0_ = bf16[8,128,256]{2,1,0:T(8,128)(2,1)} async-done(((bf16[8,128,256]{2,1,0:T(8,128)(2,1)}), bf16[8,128,256]{2,1,0:T(8,128)(2,1)}, u32[]{:S(2)}, u32[]{:S(2)}) %all-to-all-start.6) | async-done | bytes 524320 | tf_op jit(solution)/shard_map/all_to_all | solution.py:38
  205.3 4.1 %all-to-all-start.7 = ((bf16[8,128,256]{2,1,0:T(8,128)(2,1)}), bf16[8,128,256]{2,1,0:T(8,128)(2,1)}, u32[]{:S(2)}, u32[]{:S(2)}) async-start(bf16[8,128,256]{2,1,0:T(8,128)(2,1)} %forward_share.3.refs_1_), calls=%async_computation.7 | async-start | bytes 1048576 | tf_op jit(solution)/shard_map/all_to_all | solution.py:38
  210.6 3.4 %collective-permute-start.13 = (bf16[128,256]{1,0:T(8,128)(2,1)S(1)}, bf16[128,256]{1,0:T(8,128)(2,1)S(1)}, u32[]{:S(2)}, u32[]{:S(2)}) collective-permute-start(bf16[128,256]{1,0:T(8,128)(2,1)S(1)} %backward_ring_sum.3.refs_0_), channel_id=1, source_target_pairs={{0,2},{1,3},{2,0},{3,1},{4,6},{5,7},{6,4},{7,5},{8,10},{9,11},{10,... | collective-permute-start | bytes 196616 | tf_op jit(solution)/shard_map/ppermute | solution.py:257
  214.1 5.6 %collective-permute-done.13.refs_1_ = bf16[128,256]{1,0:T(8,128)(2,1)S(1)} collective-permute-done((bf16[128,256]{1,0:T(8,128)(2,1)S(1)}, bf16[128,256]{1,0:T(8,128)(2,1)S(1)}, u32[]{:S(2)}, u32[]{:S(2)}) %collective-permute-start.13) | collective-permute-done | bytes 65568 | tf_op jit(solution)/shard_map/ppermute | solution.py:257
  220.5 7.0 %all-to-all-done.7.refs_1_ = bf16[8,128,256]{2,1,0:T(8,128)(2,1)} async-done(((bf16[8,128,256]{2,1,0:T(8,128)(2,1)}), bf16[8,128,256]{2,1,0:T(8,128)(2,1)}, u32[]{:S(2)}, u32[]{:S(2)}) %all-to-all-start.7) | async-done | bytes 524320 | tf_op jit(solution)/shard_map/all_to_all | solution.py:38
  227.4 4.2 %all-to-all-start.8 = ((bf16[8,128,256]{2,1,0:T(8,128)(2,1)}), bf16[8,128,256]{2,1,0:T(8,128)(2,1)}, u32[]{:S(2)}, u32[]{:S(2)}) async-start(bf16[8,128,256]{2,1,0:T(8,128)(2,1)} %backward_share.3.refs_4_), calls=%async_computation.8 | async-start | bytes 1048576 | tf_op jit(solution)/shard_map/all_to_all | solution.py:38
  231.6 2.1 forward_product.3
  233.7 2.4 collective-permute-start.14
  237.7 11.8 %all-to-all-done.8.refs_1_ = bf16[8,128,256]{2,1,0:T(8,128)(2,1)} async-done(((bf16[8,128,256]{2,1,0:T(8,128)(2,1)}), bf16[8,128,256]{2,1,0:T(8,128)(2,1)}, u32[]{:S(2)}, u32[]{:S(2)}) %all-to-all-start.8) | async-done | bytes 524320 | tf_op jit(solution)/shard_map/all_to_all | solution.py:38
  252.0 2.7 backward_product.3
  254.7 2.4 collective-permute-start.15
  258.3 16.6 %all_to_all.50.refs_4_ = f32[32,8,128]{2,1,0:T(8,128)S(1)} all-to-all(f32[32,8,128]{2,1,0:T(8,128)S(1)} %get-tuple-element.70), channel_id=1, replica_groups=mesh['segment'=16,'shard'=32] {'shard'}, dimensions={0} | all-to-all | bytes 262144 | tf_op jit(solution)/shard_map/all_to_all | solution.py:38
  (115 shorter events, 45.8 us)
Async XLA Ops:
  1.5 1.6 copy-start.1
  8.2 12.2 %copy-start = (bf16[1,4096,256]{2,1,0:T(8,128)(2,1)S(1)}, bf16[1,4096,256]{2,1,0:T(8,128)(2,1)}, u32[]{:S(2)}) copy-start(bf16[1,4096,256]{2,1,0:T(8,128)(2,1)} %param.14) | copy-start | bytes 6291460
  8.2 12.2 %copy-start.8 = (bf16[1,8,64,256]{3,2,1,0:T(8,128)(2,1)S(1)}, bf16[1,8,64,256]{3,2,1,0:T(8,128)(2,1)}, u32[]{:S(2)}) copy-start(bf16[1,8,64,256]{3,2,1,0:T(8,128)(2,1)} %param.22) | copy-start | bytes 786436
  8.2 12.2 %copy-start.17 = (bf16[1,128,256]{2,1,0:T(8,128)(2,1)S(1)}, bf16[1,128,256]{2,1,0:T(8,128)(2,1)}, u32[]{:S(2)}) copy-start(bf16[1,128,256]{2,1,0:T(8,128)(2,1)} %param.18) | copy-start | bytes 196612
  8.2 12.2 %copy-start.35 = (s32[1,2,2]{2,1,0:T(2,128)S(1)}, s32[1,2,2]{2,1,0:T(2,128)}, u32[]{:S(2)}) copy-start(s32[1,2,2]{2,1,0:T(2,128)} %param.25) | copy-start | bytes 52
  8.2 4.3 %collective-permute-start = (bf16[8,144,256]{2,1,0:T(8,128)(2,1)S(1)}, bf16[8,144,256]{2,1,0:T(8,128)(2,1)S(1)}, u32[]{:S(2)}, u32[]{:S(2)}) collective-permute-start(bf16[8,144,256]{2,1,0:T(8,128)(2,1)S(1)} %get-tuple-element.41), channel_id=1, source_target_pairs={{0,1},{1,0},{2,3},{3,2},{4,5},{5,4},{6,7},{7,6},{8,9},{9,8},{10,11... | collective-permute-start | bytes 1769480 | tf_op jit(solution)/shard_map/ppermute | solution.py:257
  13.5 26.2 %all-to-all-start = ((bf16[8,144,256]{2,1,0:T(8,128)(2,1)}), bf16[8,144,256]{2,1,0:T(8,128)(2,1)S(1)}, u32[]{:S(2)}, u32[]{:S(2)}) async-start(bf16[8,144,256]{2,1,0:T(8,128)(2,1)} %forward_core_sum.2.refs_7_), calls=%async_computation | async-start | bytes 1179648 | tf_op jit(solution)/shard_map/all_to_all | solution.py:38
  21.9 17.8 %copy-start.19 = (bf16[128,256]{1,0:T(8,128)(2,1)}, bf16[128,256]{1,0:T(8,128)(2,1)S(1)}, u32[]{:S(2)}) copy-start(bf16[128,256]{1,0:T(8,128)(2,1)S(1)} %get-tuple-element.56.refs_0_) | copy-start | bytes 196612
  21.9 4.1 %collective-permute-start.1 = (bf16[8,128,256]{2,1,0:T(8,128)(2,1)S(1)}, bf16[8,128,256]{2,1,0:T(8,128)(2,1)S(1)}, u32[]{:S(2)}, u32[]{:S(2)}) collective-permute-start(bf16[8,128,256]{2,1,0:T(8,128)(2,1)S(1)} %get-tuple-element.43), channel_id=1, source_target_pairs={{0,1},{1,0},{2,3},{3,2},{4,5},{5,4},{6,7},{7,6},{8,9},{9,8},{10,11... | collective-permute-start | bytes 1572872 | tf_op jit(solution)/shard_map/ppermute | solution.py:257
  41.3 24.6 %collective-permute-start.3 = (bf16[2048,256]{1,0:T(8,128)(2,1)}, bf16[2048,256]{1,0:T(8,128)(2,1)S(1)}, u32[]{:S(2)}, u32[]{:S(2)}) collective-permute-start(bf16[2048,256]{1,0:T(8,128)(2,1)} %half.2), channel_id=1, source_target_pairs={{0,1},{1,0},{2,3},{3,2},{4,5},{5,4},{6,7},{7,6},{8,9},{9,8},{10,11... | collective-permute-start | bytes 3145736 | tf_op jit(solution)/shard_map/ppermute | solution.py:257
  43.7 22.2 %all-to-all-start.1 = ((bf16[8,128,256]{2,1,0:T(8,128)(2,1)}), bf16[8,128,256]{2,1,0:T(8,128)(2,1)}, u32[]{:S(2)}, u32[]{:S(2)}) async-start(bf16[8,128,256]{2,1,0:T(8,128)(2,1)} %backward_core_sum.2.refs_1_), calls=%async_computation.1 | async-start | bytes 1048576 | tf_op jit(solution)/shard_map/all_to_all | solution.py:38
  47.9 13.3 %collective-permute-start.2 = (bf16[144,256]{1,0:T(8,128)(2,1)S(1)}, bf16[144,256]{1,0:T(8,128)(2,1)S(1)}, u32[]{:S(2)}, u32[]{:S(2)}) collective-permute-start(bf16[144,256]{1,0:T(8,128)(2,1)S(1)} %forward_ring_sum.2.refs_0_.refs_2_), channel_id=1, source_target_pairs={{0,2},{1,3},{2,0},{3,1},{4,6},{5,7},{6,4},{7,5},{8,10},{9,11},{10,... | collective-permute-start | bytes 221192 | tf_op jit(solution)/shard_map/ppermute | solution.py:257
  67.1 1.6 copy-start.2
  70.3 24.6 %collective-permute-start.5 = (bf16[256,2048]{1,0:T(8,128)(2,1)}, bf16[256,2048]{1,0:T(8,128)(2,1)}, u32[]{:S(2)}, u32[]{:S(2)}) collective-permute-start(bf16[256,2048]{1,0:T(8,128)(2,1)} %half.3), channel_id=1, source_target_pairs={{0,1},{1,0},{2,3},{3,2},{4,5},{5,4},{6,7},{7,6},{8,9},{9,8},{10,11... | collective-permute-start | bytes 3145736 | tf_op jit(solution)/shard_map/ppermute | solution.py:257
  72.6 22.2 %all-to-all-start.2 = ((bf16[8,128,256]{2,1,0:T(8,128)(2,1)}), bf16[8,128,256]{2,1,0:T(8,128)(2,1)}, u32[]{:S(2)}, u32[]{:S(2)}) async-start(bf16[8,128,256]{2,1,0:T(8,128)(2,1)} %forward_share.2.refs_1_), calls=%async_computation.2 | async-start | bytes 1048576 | tf_op jit(solution)/shard_map/all_to_all | solution.py:38
  76.8 13.1 %collective-permute-start.4 = (bf16[128,256]{1,0:T(8,128)(2,1)S(1)}, bf16[128,256]{1,0:T(8,128)(2,1)S(1)}, u32[]{:S(2)}, u32[]{:S(2)}) collective-permute-start(bf16[128,256]{1,0:T(8,128)(2,1)S(1)} %backward_ring_sum.2.refs_0_.refs_2_), channel_id=1, source_target_pairs={{0,2},{1,3},{2,0},{3,1},{4,6},{5,7},{6,4},{7,5},{8,10},{9,11},{10,... | collective-permute-start | bytes 196616 | tf_op jit(solution)/shard_map/ppermute | solution.py:257
  94.8 22.1 %all-to-all-start.3 = ((bf16[8,128,256]{2,1,0:T(8,128)(2,1)}), bf16[8,128,256]{2,1,0:T(8,128)(2,1)}, u32[]{:S(2)}, u32[]{:S(2)}) async-start(bf16[8,128,256]{2,1,0:T(8,128)(2,1)} %backward_share.2.refs_4_), calls=%async_computation.3 | async-start | bytes 1048576 | tf_op jit(solution)/shard_map/all_to_all | solution.py:38
  99.0 5.6 %copy-start.26 = (bf16[128,256]{1,0:T(8,128)(2,1)S(1)}, bf16[128,256]{1,0:T(8,128)(2,1)}, u32[]{:S(2)}) copy-start(bf16[128,256]{1,0:T(8,128)(2,1)} %copy-done.25) | copy-start | bytes 196612
  99.0 11.1 %copy-start.3 = (bf16[1,256,4096]{2,1,0:T(8,128)(2,1)S(1)}, bf16[1,256,4096]{2,1,0:T(8,128)(2,1)}, u32[]{:S(2)}) copy-start(bf16[1,256,4096]{2,1,0:T(8,128)(2,1)} %param.13) | copy-start | bytes 6291460
  99.0 11.1 %copy-start.7 = (bf16[1,8,64,256]{3,2,1,0:T(8,128)(2,1)S(1)}, bf16[1,8,64,256]{3,2,1,0:T(8,128)(2,1)}, u32[]{:S(2)}) copy-start(bf16[1,8,64,256]{3,2,1,0:T(8,128)(2,1)} %param.21) | copy-start | bytes 786436
  99.0 11.0 %copy-start.27 = (bf16[1,128,256]{2,1,0:T(8,128)(2,1)S(1)}, bf16[1,128,256]{2,1,0:T(8,128)(2,1)}, u32[]{:S(2)}) copy-start(bf16[1,128,256]{2,1,0:T(8,128)(2,1)} %refs_4_.2) | copy-start | bytes 196612
  99.0 11.0 %copy-start.29 = (f32[1,256]{1,0:T(1,128)S(1)}, f32[1,256]{1,0:T(1,128)}, u32[]{:S(2)}) copy-start(f32[1,256]{1,0:T(1,128)} %refs_3_.7) | copy-start | bytes 3076
  99.0 11.0 %copy-start.34 = (s32[1,2,2]{2,1,0:T(2,128)S(1)}, s32[1,2,2]{2,1,0:T(2,128)}, u32[]{:S(2)}) copy-start(s32[1,2,2]{2,1,0:T(2,128)} %param.24) | copy-start | bytes 52
  101.3 3.3 %collective-permute-start.6 = (f32[128,256]{1,0:T(8,128)S(1)}, f32[128,256]{1,0:T(8,128)S(1)}, u32[]{:S(2)}, u32[]{:S(2)}) collective-permute-start(f32[128,256]{1,0:T(8,128)S(1)} %get-tuple-element.48), channel_id=1, source_target_pairs={{0,1},{1,0},{2,3},{3,2},{4,5},{5,4},{6,7},{7,6},{8,9},{9,8},{10,11... | collective-permute-start | bytes 393224 | tf_op jit(solution)/shard_map/ppermute | solution.py:257
  104.6 5.4 %collective-permute-start.7 = (bf16[128,256]{1,0:T(8,128)(2,1)S(1)}, bf16[128,256]{1,0:T(8,128)(2,1)S(1)}, u32[]{:S(2)}, u32[]{:S(2)}) collective-permute-start(bf16[128,256]{1,0:T(8,128)(2,1)S(1)} %forward_end.2), channel_id=1, source_target_pairs={{0,32},{32,64},{64,96},{96,128},{128,160},{160,192},{192,224},{224... | collective-permute-start | bytes 196616 | tf_op jit(solution)/shard_map/ppermute | solution.py:48
  110.1 14.6 %copy-start.9 = (bf16[1,2,128,256]{3,2,1,0:T(8,128)(2,1)S(1)}, bf16[1,2,128,256]{3,2,1,0:T(8,128)(2,1)}, u32[]{:S(2)}) copy-start(bf16[1,2,128,256]{3,2,1,0:T(8,128)(2,1)} %param.20) | copy-start | bytes 393220
  113.5 28.9 %collective-permute-start.8 = (bf16[8,144,256]{2,1,0:T(8,128)(2,1)}, bf16[8,144,256]{2,1,0:T(8,128)(2,1)}, u32[]{:S(2)}, u32[]{:S(2)}) collective-permute-start(bf16[8,144,256]{2,1,0:T(8,128)(2,1)} %get-tuple-element.51), channel_id=1, source_target_pairs={{0,1},{1,0},{2,3},{3,2},{4,5},{5,4},{6,7},{7,6},{8,9},{9,8},{10,11... | collective-permute-start | bytes 1769480 | tf_op jit(solution)/shard_map/ppermute | solution.py:257
  116.9 1.6 copy-start.4
  121.3 3.4 %collective-permute-start.9 = (f32[128,256]{1,0:T(8,128)S(1)}, f32[128,256]{1,0:T(8,128)S(1)}, u32[]{:S(2)}, u32[]{:S(2)}) collective-permute-start(f32[128,256]{1,0:T(8,128)S(1)} %get-tuple-element.53), channel_id=1, source_target_pairs={{0,1},{1,0},{2,3},{3,2},{4,5},{5,4},{6,7},{7,6},{8,9},{9,8},{10,11... | collective-permute-start | bytes 393224 | tf_op jit(solution)/shard_map/ppermute | solution.py:257
  126.9 28.7 %all-to-all-start.4 = ((f32[32,8,128]{2,1,0:T(8,128)}), f32[32,8,128]{2,1,0:T(8,128)}, u32[]{:S(2)}, u32[]{:S(2)}) async-start(f32[32,8,128]{2,1,0:T(8,128)} %copy-done.15), calls=%async_computation.4 | async-start | bytes 262144 | tf_op jit(solution)/shard_map/all_to_all | solution.py:38
  142.4 1.1 copy-start.11
  155.6 24.9 %all-to-all-start.5 = ((bf16[8,144,256]{2,1,0:T(8,128)(2,1)}), bf16[8,144,256]{2,1,0:T(8,128)(2,1)}, u32[]{:S(2)}, u32[]{:S(2)}) async-start(bf16[8,144,256]{2,1,0:T(8,128)(2,1)} %forward_core_sum.3.refs_5_), calls=%async_computation.5 | async-start | bytes 1179648 | tf_op jit(solution)/shard_map/all_to_all | solution.py:38
  163.9 2.4 copy-start.39
  163.9 7.6 %collective-permute-start.10 = (bf16[128,256]{1,0:T(8,128)(2,1)S(1)}, bf16[128,256]{1,0:T(8,128)(2,1)S(1)}, u32[]{:S(2)}, u32[]{:S(2)}) collective-permute-start(bf16[128,256]{1,0:T(8,128)(2,1)S(1)} %get-tuple-element.58), channel_id=1, source_target_pairs={{32,0},{64,32},{96,64},{128,96},{160,128},{192,160},{224,192},{256... | collective-permute-start | bytes 196616 | tf_op jit(solution)/shard_map/ppermute | solution.py:48
  175.2 4.4 %collective-permute-start.11 = (bf16[8,128,256]{2,1,0:T(8,128)(2,1)S(1)}, bf16[8,128,256]{2,1,0:T(8,128)(2,1)S(1)}, u32[]{:S(2)}, u32[]{:S(2)}) collective-permute-start(bf16[8,128,256]{2,1,0:T(8,128)(2,1)S(1)} %get-tuple-element.60), channel_id=1, source_target_pairs={{0,1},{1,0},{2,3},{3,2},{4,5},{5,4},{6,7},{7,6},{8,9},{9,8},{10,11... | collective-permute-start | bytes 1572872 | tf_op jit(solution)/shard_map/ppermute | solution.py:257
  180.5 24.9 %all-to-all-start.6 = ((bf16[8,128,256]{2,1,0:T(8,128)(2,1)}), bf16[8,128,256]{2,1,0:T(8,128)(2,1)}, u32[]{:S(2)}, u32[]{:S(2)}) async-start(bf16[8,128,256]{2,1,0:T(8,128)(2,1)} %backward_core_sum.3.refs_1_), calls=%async_computation.6 | async-start | bytes 1048576 | tf_op jit(solution)/shard_map/all_to_all | solution.py:38
  188.4 9.1 %collective-permute-start.12 = (bf16[144,256]{1,0:T(8,128)(2,1)S(1)}, bf16[144,256]{1,0:T(8,128)(2,1)S(1)}, u32[]{:S(2)}, u32[]{:S(2)}) collective-permute-start(bf16[144,256]{1,0:T(8,128)(2,1)S(1)} %forward_ring_sum.3.refs_0_), channel_id=1, source_target_pairs={{0,2},{1,3},{2,0},{3,1},{4,6},{5,7},{6,4},{7,5},{8,10},{9,11},{10,... | collective-permute-start | bytes 221192 | tf_op jit(solution)/shard_map/ppermute | solution.py:257
  205.3 22.1 %all-to-all-start.7 = ((bf16[8,128,256]{2,1,0:T(8,128)(2,1)}), bf16[8,128,256]{2,1,0:T(8,128)(2,1)}, u32[]{:S(2)}, u32[]{:S(2)}) async-start(bf16[8,128,256]{2,1,0:T(8,128)(2,1)} %forward_share.3.refs_1_), calls=%async_computation.7 | async-start | bytes 1048576 | tf_op jit(solution)/shard_map/all_to_all | solution.py:38
  210.6 9.0 %collective-permute-start.13 = (bf16[128,256]{1,0:T(8,128)(2,1)S(1)}, bf16[128,256]{1,0:T(8,128)(2,1)S(1)}, u32[]{:S(2)}, u32[]{:S(2)}) collective-permute-start(bf16[128,256]{1,0:T(8,128)(2,1)S(1)} %backward_ring_sum.3.refs_0_), channel_id=1, source_target_pairs={{0,2},{1,3},{2,0},{3,1},{4,6},{5,7},{6,4},{7,5},{8,10},{9,11},{10,... | collective-permute-start | bytes 196616 | tf_op jit(solution)/shard_map/ppermute | solution.py:257
  227.4 22.1 %all-to-all-start.8 = ((bf16[8,128,256]{2,1,0:T(8,128)(2,1)}), bf16[8,128,256]{2,1,0:T(8,128)(2,1)}, u32[]{:S(2)}, u32[]{:S(2)}) async-start(bf16[8,128,256]{2,1,0:T(8,128)(2,1)} %backward_share.3.refs_4_), calls=%async_computation.8 | async-start | bytes 1048576 | tf_op jit(solution)/shard_map/all_to_all | solution.py:38
  231.6 5.5 %copy-start.24 = (bf16[128,256]{1,0:T(8,128)(2,1)S(1)}, bf16[128,256]{1,0:T(8,128)(2,1)}, u32[]{:S(2)}) copy-start(bf16[128,256]{1,0:T(8,128)(2,1)} %copy-done.23) | copy-start | bytes 196612
  233.7 24.4 %copy-start.32 = (f32[1,256]{1,0:T(1,128)S(1)}, f32[1,256]{1,0:T(1,128)}, u32[]{:S(2)}) copy-start(f32[1,256]{1,0:T(1,128)} %refs_3_.7) | copy-start | bytes 3076
  233.7 3.4 %collective-permute-start.14 = (f32[128,256]{1,0:T(8,128)S(1)}, f32[128,256]{1,0:T(8,128)S(1)}, u32[]{:S(2)}, u32[]{:S(2)}) collective-permute-start(f32[128,256]{1,0:T(8,128)S(1)} %get-tuple-element.65), channel_id=1, source_target_pairs={{0,1},{1,0},{2,3},{3,2},{4,5},{5,4},{6,7},{7,6},{8,9},{9,8},{10,11... | collective-permute-start | bytes 393224 | tf_op jit(solution)/shard_map/ppermute | solution.py:257
  249.6 1.6 copy-start.5
  252.0 22.9 %copy-start.22 = (bf16[128,256]{1,0:T(8,128)(2,1)S(1)}, bf16[128,256]{1,0:T(8,128)(2,1)}, u32[]{:S(2)}) copy-start(bf16[128,256]{1,0:T(8,128)(2,1)} %copy-done.21) | copy-start | bytes 196612
  252.0 22.9 %copy-start.38 = (f32[8,128]{1,0:T(8,128)S(1)}, f32[8,128]{1,0:T(8,128)}, u32[]{:S(2)}) copy-start(f32[8,128]{1,0:T(8,128)} %copy-done.37) | copy-start | bytes 12292
  252.0 22.9 %copy-start.40 = (f32[1,256]{1,0:T(1,128)S(1)}, f32[1,256]{1,0:T(1,128)}, u32[]{:S(2)}) copy-start(f32[1,256]{1,0:T(1,128)} %copy-done.39) | copy-start | bytes 3076
  254.7 3.4 %collective-permute-start.15 = (f32[128,256]{1,0:T(8,128)S(1)}, f32[128,256]{1,0:T(8,128)S(1)}, u32[]{:S(2)}, u32[]{:S(2)}) collective-permute-start(f32[128,256]{1,0:T(8,128)S(1)} %get-tuple-element.68), channel_id=1, source_target_pairs={{0,1},{1,0},{2,3},{3,2},{4,5},{5,4},{6,7},{7,6},{8,9},{9,8},{10,11... | collective-permute-start | bytes 393224 | tf_op jit(solution)/shard_map/ppermute | solution.py:257
  (18 other events, 13.2 us)

commit v6 on v5

--- a/solution.py
+++ b/solution.py
@@ -19,7 +19,7 @@
 F32 = jnp.float32
 BF16 = jnp.bfloat16
 VMEM_LIMIT = 20 * 1024 * 1024
-DOT_ROWS = 8
+EXTRA = 8
 
 
 def core_pairs():
@@ -34,7 +34,11 @@
     return [[4 * y + rest for y in range(RING)] for rest in range(4)]
 
 
-def swapped(value, groups=None):
+def planes():
+    return [[2 * chip + core for chip in range(2 * RING)] for core in range(2)]
+
+
+def swapped(value, groups):
     return lax.all_to_all(value, "shard", 0, 0, axis_index_groups=groups, tiled=True)
 
 
@@ -48,7 +52,7 @@
     return lax.ppermute(value, axis, [(source, source + steps) for source in range(leading, last)])
 
 
-def call(kernel, name, outs, *, prefetch=(), blocks=None, operands=(), after=()):
+def call(kernel, name, outs, *, prefetch=(), blocks=None, operands=(), after=(), scratch=()):
     blocks = blocks or {}
     first, last = len(prefetch) + len(operands), len(prefetch) + len(operands) + len(after)
 
@@ -57,6 +61,8 @@
 
     def spec(position, operand):
         if position in blocks:
+            if blocks[position] is None:
+                return pl.BlockSpec(memory_space=pl.ANY)
             shape, index_map = blocks[position]
             return pl.BlockSpec(shape, index_map)
         rank = len(operand.shape)
@@ -71,6 +77,7 @@
             grid=(1,),
             in_specs=in_specs + [pl.BlockSpec(memory_space=pl.ANY)] * len(after),
             out_specs=[pl.BlockSpec(out.shape, lambda *_, rank=len(out.shape): (0,) * rank) for out in outs],
+            scratch_shapes=scratch,
         ),
         compiler_params=pltpu.CompilerParams(vmem_limit_bytes=VMEM_LIMIT),
         cost_estimate=pl.CostEstimate(flops=0, bytes_accessed=0, transcendentals=0),
@@ -148,7 +155,17 @@
 
 
 def backward_start(tick, messages, last, ids, meta, exponents, *refs):
-    given, (first, second, weight, g_out, keep, send) = refs[:messages], refs[messages:]
+    given, refs = refs[:messages], refs[messages:]
+    if tick == 0:
+        first, second, weight, saved, gain, g_out, keep, send, weighted, squares = refs
+        rows = [jnp.zeros((1, ROWS), F32)]
+        for k in range(2):
+            kept = saved[k].astype(F32)
+            weighted[k] = kept * gain[...]
+            rows.append(across(jnp.sum(kept * kept, axis=1, keepdims=True)))
+        squares[...] = jnp.concatenate(rows + [jnp.zeros((EXTRA - 3, ROWS), F32)], axis=0)
+    else:
+        first, second, weight, g_out, keep, send = refs
     g = decoded(chosen(meta, last, given), first, second, exponents, tick)
     g_out[...] = g
     core = meta[3]
@@ -182,64 +199,76 @@
         out[ROWS:] = split_stats(stats)
 
 
-def forward_share(own, other, out):
+def forward_share(own, other, *refs):
     total = joined_stats(own[ROWS:]) + joined_stats(other[ROWS:])
     factor = lax.rsqrt(total[0:1] / D + EPSILON)
     value = own[:ROWS].astype(F32) + other[:ROWS].astype(F32)
-    out[...] = jnp.broadcast_to((down(factor) * value).astype(BF16)[None], out.shape)
-
-
-def backward_share(own, other, out):
+    value = (down(factor) * value).astype(BF16)
+    out, *half = refs[len(refs) // 2 :]
+    out[...] = jnp.broadcast_to(value[None], out.shape)
+    if half:
+        half[0][...] = refs[0][...]
+
+
+def backward_share(own, other, *refs):
     value = (own[...].astype(F32) + other[...].astype(F32)).astype(BF16)
+    out, *half = refs[len(refs) // 2 :]
     out[...] = jnp.broadcast_to(value[None], out.shape)
-
-
-def half(weight, out):
-    out[...] = weight[...]
-
-
-def forward_product(blocks, own_weight, other_weight, mine, others):
-    for weight, out in ((other_weight, others), (own_weight, mine)):
+    if half:
+        half[0][...] = refs[0][...]
+
+
+def forward_product(meta, blocks, weight, other_weight, mine, others, own_weight, arrived):
+    at = pl.multiple_of(meta[3] * HALF, HALF)
+    copy = pltpu.make_async_copy(weight.at[pl.ds(at, HALF), :], own_weight, arrived)
+    copy.start()
+    for half, out in ((other_weight, others), (own_weight, mine)):
+        if half is own_weight:
+            copy.wait()
         total = jnp.zeros((ROWS, WIDTH), F32)
         for j in range(RING):
-            rows = weight[j * WIDTH : (j + 1) * WIDTH, :]
+            rows = half[j * WIDTH : (j + 1) * WIDTH, :]
             total = total + jnp.dot(blocks[j], rows, preferred_element_type=F32)
         out[...] = total
 
 
-def backward_product(blocks, own_weight, other_weight, mine, others):
-    for weight, out in ((other_weight, others), (own_weight, mine)):
+def backward_product(meta, blocks, weight, other_weight, weighted, other_weighted, squares, mine, others, own_weight, arrived):
+    at = pl.multiple_of(meta[3] * HALF, HALF)
+    copy = pltpu.make_async_copy(weight.at[:, pl.ds(at, HALF)], own_weight, arrived)
+    copy.start()
+    dots = jnp.zeros((ROWS, 1), F32)
+    for half, out, factors in ((other_weight, others, other_weighted), (own_weight, mine, weighted)):
+        if half is own_weight:
+            copy.wait()
         total = jnp.zeros((ROWS, WIDTH), F32)
         for j in range(RING):
-            columns = weight[:, j * WIDTH : (j + 1) * WIDTH]
+            columns = half[:, j * WIDTH : (j + 1) * WIDTH]
             total = total + lax.dot_general(
                 blocks[j], columns, (((1,), (1,)), ((), ())), preferred_element_type=F32
             )
-        out[...] = total
+        out[:ROWS] = total
+        dots = dots + jnp.sum(total * factors[0], axis=1, keepdims=True)
+    rows = jnp.concatenate([across(dots), squares[1:]], axis=0)
+    rows = jnp.concatenate([rows, jnp.zeros_like(rows)], axis=1)
+    mine[ROWS:] = rows
+    others[ROWS:] = rows
 
 
 def forward_end(x, mine, other, out):
     out[...] = (x[...].astype(F32) + (mine[...] + other[...])).astype(BF16)
 
 
-def backward_middle(tick, mine, other, saved, gain, scaled_grad, dots):
-    value = mine[...] + other[...]
-    scaled_grad[...] = value
-    terms = [saved[tick].astype(F32) * gain[...] * value]
-    if tick == 0:
-        for k in range(2):
-            kept = saved[k].astype(F32)
-            terms.append(kept * kept)
-    rows = [across(jnp.sum(term, axis=1, keepdims=True)) for term in terms]
-    rows.append(jnp.zeros((DOT_ROWS - len(rows), ROWS), F32))
-    dots[...] = jnp.broadcast_to(jnp.concatenate(rows, axis=0)[None], dots.shape)
+def backward_middle(mine, other, scaled_grad, dots):
+    scaled_grad[...] = mine[:ROWS] + other[:ROWS]
+    rows = mine[ROWS:, :ROWS] + other[ROWS:, :ROWS]
+    dots[...] = jnp.broadcast_to(rows[None], dots.shape)
 
 
 def backward_end(tick, g, scaled_grad, saved, gain, dots, *refs):
     before, (out, gain_out, *left) = refs[: 2 if tick else 0], refs[2 if tick else 0 :]
-    total = dots[0, :8]
+    total = dots[0]
     for j in range(1, dots.shape[0]):
-        total = total + dots[j, :8]
+        total = total + dots[j]
     if tick == 0:
         squares = total[1:2]
         left[0][...] = jnp.broadcast_to(total[2:3], left[0].shape)
@@ -285,8 +314,8 @@
     eight = shape_of(RING, ROWS, WIDTH)
     eight_tall = shape_of(RING, ROWS + STATS, WIDTH)
     row = shape_of(1, WIDTH, dtype=F32)
-    own_half = {1: ((HALF, WIDTH), lambda i, meta: (meta[3], 0))}
-    own_columns = {1: ((WIDTH, HALF), lambda i, meta: (0, meta[3]))}
+    product = shape_of(ROWS + EXTRA, WIDTH, dtype=F32)
+    fetched = pltpu.SemaphoreType.DMA
 
     def base_blocks(first, micro):
         return {
@@ -313,70 +342,62 @@
 
     def backward_begin(tick, messages, *after):
         count = len(messages)
-        g, keep, send = call(
+        outs, extra = [low, eight, eight], ()
+        if tick == 0:
+            outs += [shape_of(2, ROWS, WIDTH, dtype=F32), shape_of(EXTRA, ROWS, dtype=F32)]
+            extra = (saved, norm_gain)
+        g, keep, send, *rest = call(
             functools.partial(backward_start, tick, count, segments - 1),
             "backward_start",
-            [low, eight, eight],
+            outs,
             prefetch=(sample_ids, meta, backward_exponents[0]),
-            operands=(*messages, backward_base[0], backward_base[0], output_local),
+            operands=(*messages, backward_base[0], backward_base[0], output_local, *extra),
             blocks=base_blocks(count, lambda meta: tick + meta[0]),
             after=after,
         )
         operands = (keep, over(send, core_pairs()))
-        return g, *call(core_sum, "backward_core_sum", [eight], operands=operands)
-
-    def forward_turn(pieces, *after):
-        (own,) = call(ring_sum, "forward_ring_sum", [tall], operands=(pieces,), after=after)
-        return own, *call(forward_share, "forward_share", [eight], operands=(own, over(own, z_pairs())))
-
-    def backward_turn(pieces, *after):
-        (own,) = call(ring_sum, "backward_ring_sum", [low], operands=(pieces,), after=after)
-        return own, *call(backward_share, "backward_share", [eight], operands=(own, over(own, z_pairs())))
+        return g, *call(core_sum, "backward_core_sum", [eight], operands=operands), *rest
+
+    def turn(kernel, name, block, pieces, half, *after):
+        (own,) = call(ring_sum, name + "_ring_sum", [block], operands=(pieces,), after=after)
+        operands, outs, blocks = (own, over(own, z_pairs())), [eight], {}
+        if half:
+            weight, shape, index_map = half
+            operands, outs, blocks = (*operands, weight), [eight, shape_of(*shape)], {2: (shape, index_map)}
+        return call(with_meta(kernel), name + "_share", outs, prefetch=(meta,), operands=operands, blocks=blocks)
 
     def with_meta(kernel):
         return lambda _, *refs: kernel(*refs)
 
-    def exchanged_half(weight, block, index_map, *after):
-        (own,) = call(
-            with_meta(half),
-            "half",
-            [shape_of(*block)],
-            prefetch=(meta,),
-            operands=(weight,),
-            blocks={0: (block, index_map)},
-            after=after,
-        )
-        return over(own, core_pairs())
-
     def forward_finish(x, gathered, *after):
         mine, others = call(
-            with_meta(forward_product),
+            forward_product,
             "forward_product",
             [wide, wide],
             prefetch=(meta,),
             operands=(gathered, output_local, output_other),
-            blocks=own_half,
+            blocks={1: None},
             after=after,
+            scratch=(pltpu.VMEM((HALF, WIDTH), BF16), fetched),
         )
         operands = (x, mine, over(others, core_pairs()))
         return call(forward_end, "forward_end", [low], operands=operands)[0]
 
     def backward_dots(tick, gathered, *after):
+        one = ((1, ROWS, WIDTH), lambda i, meta: (tick, 0, 0))
         mine, others = call(
-            with_meta(backward_product),
+            backward_product,
             "backward_product",
-            [wide, wide],
+            [product, product],
             prefetch=(meta,),
-            operands=(gathered, value_local, value_other),
-            blocks=own_columns,
+            operands=(gathered, value_local, value_other, weighted, other_weighted, squares),
+            blocks={1: None, 3: one, 4: one},
             after=after,
+            scratch=(pltpu.VMEM((WIDTH, HALF), BF16), fetched),
         )
-        return call(
-            functools.partial(backward_middle, tick),
-            "backward_middle",
-            [wide, shape_of(4 * RING, DOT_ROWS, ROWS, dtype=F32)],
-            operands=(mine, over(others, core_pairs()), saved, norm_gain),
-        )
+        operands = (mine, over(others, core_pairs()))
+        outs = [wide, shape_of(2 * RING, EXTRA, ROWS, dtype=F32)]
+        return call(backward_middle, "backward_middle", outs, operands=operands)
 
     def backward_finish(tick, g, scaled_grad, dots, left, *after):
         return call(
@@ -391,45 +412,48 @@
     gated = gate(pieces)
     landed = swapped(gated, rings())
 
-    g, back_pieces = backward_begin(0, [returning[0]], gated)
+    g, back_pieces, weighted, squares = backward_begin(0, [returning[0]], gated)
+    other_weighted = over(weighted, core_pairs())
     gated = gate(back_pieces, landed)
     back_landed = swapped(gated, rings())
 
-    own, copies = forward_turn(landed, gated)
-    output_other = exchanged_half(output_local, (HALF, WIDTH), lambda i, meta: (1 - meta[3], 0), own)
-    gated = gate(copies, back_landed, output_other)
+    half = (output_local, (HALF, WIDTH), lambda i, meta: (1 - meta[3], 0))
+    copies, half = turn(forward_share, "forward", tall, landed, half, gated)
+    output_other = over(half, core_pairs())
+    gated = gate(copies, back_landed)
     gathered = swapped(gated, rings())
 
-    own, copies = backward_turn(back_landed, gated)
-    value_other = exchanged_half(value_local, (WIDTH, HALF), lambda i, meta: (0, 1 - meta[3]), own)
-    gated = gate(copies, gathered, value_other)
+    half = (value_local, (WIDTH, HALF), lambda i, meta: (0, 1 - meta[3]))
+    copies, half = turn(backward_share, "backward", low, back_landed, half, gated)
+    value_other = over(half, core_pairs())
+    gated = gate(copies, gathered)
     back_gathered = swapped(gated, rings())
 
     segment_out = forward_finish(x, gathered, gated)
     x, pieces = forward_begin(1, [shifted(segment_out, "segment", 1), fresh_inputs])
     scaled_grad, dots = backward_dots(0, back_gathered)
-    all_dots = swapped(dots)
+    all_dots = swapped(dots, planes())
 
     gated = gate(pieces, all_dots)
     landed = swapped(gated, rings())
 
-    input_grad, gain_total, squares = backward_finish(0, g, scaled_grad, all_dots, (), gated)
+    input_grad, gain_total, saved_squares = backward_finish(0, g, scaled_grad, all_dots, (), gated)
     g, back_pieces = backward_begin(1, [shifted(input_grad, "segment", -1), cotangents])
     gated = gate(back_pieces, landed)
     back_landed = swapped(gated, rings())
 
-    _, copies = forward_turn(landed, gated)
+    (copies,) = turn(forward_share, "forward", tall, landed, None, gated)
     gated = gate(copies, back_landed)
     gathered = swapped(gated, rings())
 
-    _, copies = backward_turn(back_landed, gated)
+    (copies,) = turn(backward_share, "backward", low, back_landed, None, gated)
     gated = gate(copies, gathered)
     back_gathered = swapped(gated, rings())
 
     segment_out = forward_finish(x, gathered, gated)
     scaled_grad, dots = backward_dots(1, back_gathered, segment_out)
-    all_dots = swapped(dots)
-    input_grad, gain_total = backward_finish(1, g, scaled_grad, all_dots, (squares, gain_total))
+    all_dots = swapped(dots, planes())
+    input_grad, gain_total = backward_finish(1, g, scaled_grad, all_dots, (saved_squares, gain_total))
     return (segment_out[None], input_grad[None], gain_total)
 
 

time: 278 us -> 280 us (level)
  local copies, waits for them, and re-layouts: 21.4 us -> 31 us
  waiting for transfers between devices: 88.3 us -> 82.4 us
    all_to_all x9, waiting for transfers between devices: 57 us -> 45.8 us  [swapped(): lax.all_to_all(value, 'shard', 0, 0, axis_index_groups=groups, tiled=True)]
    unnamed x83 -> x111, local copies, waits for them, and re-layouts: 21.4 us -> 31 us
    ppermute x14 -> x15, waiting for transfers between devices: 24.7 us -> 29 us  [over(): return lax.ppermute(value, 'shard', pairs)]
    ppermute x14 -> x15, starting transfers between devices: 53.6 us -> 54.4 us  [over(): return lax.ppermute(value, 'shard', pairs)]
    pallas_call x28 -> x26, Pallas kernels: 34.1 us -> 34.3 us  [call(): pl.pallas_call(body, out_shape=outs, grid_spec=pltpu.PrefetchScalarGridSp...]
  transfers between devices with their start and end apart: 25 -> 26, of which waited for: 21 -> 20; matrix products, arithmetic and copies ran while one was open for 0% -> 0% of each run, Pallas kernels for 9% -> 10%
where the time goes in v6:
time: 280 us; the launch traced here: 277 us
  starting transfers between devices  114 us (41%)
  waiting for transfers between devices  82.4 us (29%)
  Pallas kernels  34.3 us (12%)
  local copies, waits for them, and re-layouts  31 us (11%)
  blocking collectives  14.4 us (5%)
    ppermute x15, starting transfers between devices, over(): return lax.ppermute(value, 'shard', pairs)  54.4 us
    all_to_all x9, starting transfers between devices, swapped(): lax.all_to_all(value, 'shard', 0, 0, axis_index_groups=groups, tiled=True)  54 us
    all_to_all x9, waiting for transfers between devices, swapped(): lax.all_to_all(value, 'shard', 0, 0, axis_index_groups=groups, tiled=True)  45.8 us
    pallas_call x26, Pallas kernels, call(): pl.pallas_call(body, out_shape=outs, grid_spec=pltpu.PrefetchScalarGridSp...  34.3 us
    unnamed x111, local copies, waits for them, and re-layouts  31 us
    ppermute x15, waiting for transfers between devices, over(): return lax.ppermute(value, 'shard', pairs)  29 us
    all_to_all x1, blocking collectives, swapped(): lax.all_to_all(value, 'shard', 0, 0, axis_index_groups=groups, tiled=True)  14.4 us
    ppermute x2, waiting for transfers between devices, shifted(): lax.ppermute(value, axis, [(source, source + steps) for source in range(l...  7.55 us
  transfers between devices with their start and end apart: 26, of which 20 were waited for; matrix products, arithmetic and copies ran while one was open for 0% of the time, Pallas kernels for 10%

profile of v6, /device:TPU:7, one launch (start us, length us, event | category | flops | bytes accessed | tf_op | source)
XLA Modules:
  0.0 277.2 jit_solution(3493370320344328542)
XLA Ops:
  1.5 1.6 copy-done.1
  7.6 2.7 collective-permute-start
  10.3 1.6 collective-permute-done.refs_1_
  12.9 6.8 %all-to-all-start = ((bf16[8,144,256]{2,1,0:T(8,128)(2,1)}), bf16[8,144,256]{2,1,0:T(8,128)(2,1)S(1)}, u32[]{:S(2)}, u32[]{:S(2)}) async-start(bf16[8,144,256]{2,1,0:T(8,128)(2,1)} %forward_core_sum.2.refs_9_), calls=%async_computation | async-start | bytes 1179648 | tf_op jit(solution)/shard_map/all_to_all | solution.py:42
  23.3 2.6 collective-permute-start.1
  28.3 10.8 %all-to-all-done.refs_0_ = bf16[8,144,256]{2,1,0:T(8,128)(2,1)S(1)} async-done(((bf16[8,144,256]{2,1,0:T(8,128)(2,1)}), bf16[8,144,256]{2,1,0:T(8,128)(2,1)S(1)}, u32[]{:S(2)}, u32[]{:S(2)}) %all-to-all-start) | async-done | bytes 589856 | tf_op jit(solution)/shard_map/all_to_all | solution.py:42
  39.1 3.5 %all-to-all-start.1 = ((bf16[8,128,256]{2,1,0:T(8,128)(2,1)}), bf16[8,128,256]{2,1,0:T(8,128)(2,1)S(1)}, u32[]{:S(2)}, u32[]{:S(2)}) async-start(bf16[8,128,256]{2,1,0:T(8,128)(2,1)} %backward_core_sum.2.refs_1_), calls=%async_computation.1 | async-start | bytes 1048576 | tf_op jit(solution)/shard_map/all_to_all | solution.py:42
  42.6 10.6 %collective-permute-start.2 = (bf16[144,256]{1,0:T(8,128)(2,1)S(1)}, bf16[144,256]{1,0:T(8,128)(2,1)S(1)}, u32[]{:S(2)}, u32[]{:S(2)}) collective-permute-start(bf16[144,256]{1,0:T(8,128)(2,1)S(1)} %forward_ring_sum.2.refs_1_), channel_id=1, source_target_pairs={{0,2},{1,3},{2,0},{3,1},{4,6},{5,7},{6,4},{7,5},{8,10},{9,11},{10,... | collective-permute-start | bytes 221192 | tf_op jit(solution)/shard_map/ppermute | solution.py:286
  53.3 2.2 collective-permute-done.2.refs_2_
  57.9 2.5 all-to-all-done.1.refs_0_
  60.4 4.1 %all-to-all-start.2 = ((bf16[8,128,256]{2,1,0:T(8,128)(2,1)}), bf16[8,128,256]{2,1,0:T(8,128)(2,1)}, u32[]{:S(2)}, u32[]{:S(2)}) async-start(bf16[8,128,256]{2,1,0:T(8,128)(2,1)} %get-tuple-element.52.refs_1_), calls=%async_computation.2 | async-start | bytes 1048576 | tf_op jit(solution)/shard_map/all_to_all | solution.py:42
  64.6 4.3 %collective-permute-start.3 = (bf16[2048,256]{1,0:T(8,128)(2,1)}, bf16[2048,256]{1,0:T(8,128)(2,1)S(1)}, u32[]{:S(2)}, u32[]{:S(2)}) collective-permute-start(bf16[2048,256]{1,0:T(8,128)(2,1)} %copy-done.54), channel_id=1, source_target_pairs={{0,1},{1,0},{2,3},{3,2},{4,5},{5,4},{6,7},{7,6},{8,9},{9,8},{10,11... | collective-permute-start | bytes 3145736 | tf_op jit(solution)/shard_map/ppermute | solution.py:286
  70.0 8.8 %collective-permute-start.4 = (bf16[128,256]{1,0:T(8,128)(2,1)S(1)}, bf16[128,256]{1,0:T(8,128)(2,1)S(1)}, u32[]{:S(2)}, u32[]{:S(2)}) collective-permute-start(bf16[128,256]{1,0:T(8,128)(2,1)S(1)} %backward_ring_sum.2.refs_1_), channel_id=1, source_target_pairs={{0,2},{1,3},{2,0},{3,1},{4,6},{5,7},{6,4},{7,5},{8,10},{9,11},{10,... | collective-permute-start | bytes 196616 | tf_op jit(solution)/shard_map/ppermute | solution.py:286
  78.8 2.5 collective-permute-done.4.refs_2_
  82.9 1.6 backward_share.2
  85.4 2.5 collective-permute-start.8
  87.9 6.8 %all-to-all-start.3 = ((bf16[8,128,256]{2,1,0:T(8,128)(2,1)}), bf16[8,128,256]{2,1,0:T(8,128)(2,1)}, u32[]{:S(2)}, u32[]{:S(2)}) async-start(bf16[8,128,256]{2,1,0:T(8,128)(2,1)} %copy-done.9), calls=%async_computation.3 | async-start | bytes 1048576 | tf_op jit(solution)/shard_map/all_to_all | solution.py:42
  95.9 2.5 forward_product.2
  98.4 2.3 collective-permute-start.5
  101.8 2.9 %collective-permute-start.6 = (bf16[128,256]{1,0:T(8,128)(2,1)S(1)}, bf16[128,256]{1,0:T(8,128)(2,1)S(1)}, u32[]{:S(2)}, u32[]{:S(2)}) collective-permute-start(bf16[128,256]{1,0:T(8,128)(2,1)S(1)} %forward_end.2), channel_id=1, source_target_pairs={{0,32},{32,64},{64,96},{96,128},{128,160},{160,192},{192,224},{224... | collective-permute-start | bytes 196616 | tf_op jit(solution)/shard_map/ppermute | solution.py:52
  104.7 2.5 collective-permute-done.6.refs_3_
  107.3 2.0 forward_start.3
  110.7 2.9 %collective-permute-start.7 = (bf16[8,144,256]{2,1,0:T(8,128)(2,1)}, bf16[8,144,256]{2,1,0:T(8,128)(2,1)}, u32[]{:S(2)}, u32[]{:S(2)}) collective-permute-start(bf16[8,144,256]{2,1,0:T(8,128)(2,1)} %get-tuple-element.60), channel_id=1, source_target_pairs={{0,1},{1,0},{2,3},{3,2},{4,5},{5,4},{6,7},{7,6},{8,9},{9,8},{10,11... | collective-permute-start | bytes 1769480 | tf_op jit(solution)/shard_map/ppermute | solution.py:286
  113.7 1.9 collective-permute-start.9
  122.0 3.6 %backward_product.2 = (f32[136,256]{1,0:T(8,128)S(1)}, f32[136,256]{1,0:T(8,128)S(1)}) custom-call(s32[4]{0:T(128)S(1)} %pad_add_fusion.refs_1_.refs_0_, bf16[8,128,256]{2,1,0:T(8,128)(2,1)} %all-to-all-done.3.refs_1_, bf16[256,4096]{1,0:T(8,128)(2,1)S(1)} %bitcast.23, bf16[256,2048]{1,0:T(8,128)(2,1)} %collective-permute-done.8.refs_3_, ...), custom_call_target="tpu_custom_call" | custom-call | tf_op jit(solution)/shard_map/backward_product/pallas_call | solution.py:72
  125.6 2.2 collective-permute-start.10
  130.3 13.5 %all-to-all-start.4 = ((f32[16,8,128]{2,1,0:T(8,128)}), f32[16,8,128]{2,1,0:T(8,128)}, u32[]{:S(2)}, u32[]{:S(2)}) async-start(f32[16,8,128]{2,1,0:T(8,128)} %copy-done.34), calls=%async_computation.4 | async-start | bytes 131072 | tf_op jit(solution)/shard_map/all_to_all | solution.py:42
  144.9 2.1 forward_core_sum.3.refs_5_
  146.9 8.7 %all-to-all-done.4.refs_4_ = f32[16,8,128]{2,1,0:T(8,128)} async-done(((f32[16,8,128]{2,1,0:T(8,128)}), f32[16,8,128]{2,1,0:T(8,128)}, u32[]{:S(2)}, u32[]{:S(2)}) %all-to-all-start.4) | async-done | bytes 65568 | tf_op jit(solution)/shard_map/all_to_all | solution.py:42
  155.6 4.2 %all-to-all-start.5 = ((bf16[8,144,256]{2,1,0:T(8,128)(2,1)}), bf16[8,144,256]{2,1,0:T(8,128)(2,1)}, u32[]{:S(2)}, u32[]{:S(2)}) async-start(bf16[8,144,256]{2,1,0:T(8,128)(2,1)} %forward_core_sum.3.refs_5_), calls=%async_computation.5 | async-start | bytes 1179648 | tf_op jit(solution)/shard_map/all_to_all | solution.py:42
  163.9 2.4 collective-permute-start.11
  166.3 5.1 %collective-permute-done.11.refs_3_ = bf16[128,256]{1,0:T(8,128)(2,1)S(1)} collective-permute-done((bf16[128,256]{1,0:T(8,128)(2,1)S(1)}, bf16[128,256]{1,0:T(8,128)(2,1)S(1)}, u32[]{:S(2)}, u32[]{:S(2)}) %collective-permute-start.11) | collective-permute-done | bytes 65568 | tf_op jit(solution)/shard_map/ppermute | solution.py:52
  175.1 4.2 %collective-permute-start.12 = (bf16[8,128,256]{2,1,0:T(8,128)(2,1)S(1)}, bf16[8,128,256]{2,1,0:T(8,128)(2,1)S(1)}, u32[]{:S(2)}, u32[]{:S(2)}) collective-permute-start(bf16[8,128,256]{2,1,0:T(8,128)(2,1)S(1)} %get-tuple-element.72), channel_id=1, source_target_pairs={{0,1},{1,0},{2,3},{3,2},{4,5},{5,4},{6,7},{7,6},{8,9},{9,8},{10,11... | collective-permute-start | bytes 1572872 | tf_op jit(solution)/shard_map/ppermute | solution.py:286
  181.8 6.8 %all-to-all-start.6 = ((bf16[8,128,256]{2,1,0:T(8,128)(2,1)}), bf16[8,128,256]{2,1,0:T(8,128)(2,1)}, u32[]{:S(2)}, u32[]{:S(2)}) async-start(bf16[8,128,256]{2,1,0:T(8,128)(2,1)} %backward_core_sum.3.refs_1_), calls=%async_computation.6 | async-start | bytes 1048576 | tf_op jit(solution)/shard_map/all_to_all | solution.py:42
  189.7 2.3 collective-permute-start.13
  192.0 7.0 %collective-permute-done.13.refs_2_ = bf16[144,256]{1,0:T(8,128)(2,1)S(1)} collective-permute-done((bf16[144,256]{1,0:T(8,128)(2,1)S(1)}, bf16[144,256]{1,0:T(8,128)(2,1)S(1)}, u32[]{:S(2)}, u32[]{:S(2)}) %collective-permute-start.13) | collective-permute-done | bytes 73760 | tf_op jit(solution)/shard_map/ppermute | solution.py:286
  200.5 6.2 %all-to-all-done.6.refs_0_ = bf16[8,128,256]{2,1,0:T(8,128)(2,1)} async-done(((bf16[8,128,256]{2,1,0:T(8,128)(2,1)}), bf16[8,128,256]{2,1,0:T(8,128)(2,1)}, u32[]{:S(2)}, u32[]{:S(2)}) %all-to-all-start.6) | async-done | bytes 524320 | tf_op jit(solution)/shard_map/all_to_all | solution.py:42
  206.6 4.1 %all-to-all-start.7 = ((bf16[8,128,256]{2,1,0:T(8,128)(2,1)}), bf16[8,128,256]{2,1,0:T(8,128)(2,1)}, u32[]{:S(2)}, u32[]{:S(2)}) async-start(bf16[8,128,256]{2,1,0:T(8,128)(2,1)} %forward_share.3.refs_1_), calls=%async_computation.7 | async-start | bytes 1048576 | tf_op jit(solution)/shard_map/all_to_all | solution.py:42
  211.9 2.3 collective-permute-start.14
  214.2 6.9 %collective-permute-done.14.refs_2_ = bf16[128,256]{1,0:T(8,128)(2,1)S(1)} collective-permute-done((bf16[128,256]{1,0:T(8,128)(2,1)S(1)}, bf16[128,256]{1,0:T(8,128)(2,1)S(1)}, u32[]{:S(2)}, u32[]{:S(2)}) %collective-permute-start.14) | collective-permute-done | bytes 65568 | tf_op jit(solution)/shard_map/ppermute | solution.py:286
  222.5 6.3 %all-to-all-done.7.refs_1_ = bf16[8,128,256]{2,1,0:T(8,128)(2,1)} async-done(((bf16[8,128,256]{2,1,0:T(8,128)(2,1)}), bf16[8,128,256]{2,1,0:T(8,128)(2,1)}, u32[]{:S(2)}, u32[]{:S(2)}) %all-to-all-start.7) | async-done | bytes 524320 | tf_op jit(solution)/shard_map/all_to_all | solution.py:42
  228.7 4.1 %all-to-all-start.8 = ((bf16[8,128,256]{2,1,0:T(8,128)(2,1)}), bf16[8,128,256]{2,1,0:T(8,128)(2,1)}, u32[]{:S(2)}, u32[]{:S(2)}) async-start(bf16[8,128,256]{2,1,0:T(8,128)(2,1)} %backward_share.3.refs_4_), calls=%async_computation.8 | async-start | bytes 1048576 | tf_op jit(solution)/shard_map/all_to_all | solution.py:42
  232.9 2.5 forward_product.3
  235.4 2.4 collective-permute-start.15
  239.4 11.4 %all-to-all-done.8.refs_1_ = bf16[8,128,256]{2,1,0:T(8,128)(2,1)} async-done(((bf16[8,128,256]{2,1,0:T(8,128)(2,1)}), bf16[8,128,256]{2,1,0:T(8,128)(2,1)}, u32[]{:S(2)}, u32[]{:S(2)}) %all-to-all-start.8) | async-done | bytes 524320 | tf_op jit(solution)/shard_map/all_to_all | solution.py:42
  254.9 3.7 %backward_product.3 = (f32[136,256]{1,0:T(8,128)S(1)}, f32[136,256]{1,0:T(8,128)S(1)}) custom-call(s32[4]{0:T(128)S(1)} %pad_add_fusion.refs_1_.refs_0_, bf16[8,128,256]{2,1,0:T(8,128)(2,1)} %all-to-all-done.8.refs_1_, bf16[256,4096]{1,0:T(8,128)(2,1)S(1)} %bitcast.24, bf16[256,2048]{1,0:T(8,128)(2,1)} %collective-permute-done.8.refs_3_, ...), custom_call_target="tpu_custom_call" | custom-call | tf_op jit(solution)/shard_map/backward_product/pallas_call | solution.py:72
  258.6 2.4 collective-permute-start.16
  262.0 14.4 %all_to_all.50.refs_4_ = f32[16,8,128]{2,1,0:T(8,128)S(1)} all-to-all(f32[16,8,128]{2,1,0:T(8,128)S(1)} %get-tuple-element.82), channel_id=1, replica_groups={{0,2,4,6,8,10,12,14,16,18,20,22,24,26,28,30},{1,3,5,7,9,11,13,15,17,19,..., dimensions={0} | all-to-all | bytes 131072 | tf_op jit(solution)/shard_map/all_to_all | solution.py:42
  (143 shorter events, 54.6 us)
Async XLA Ops:
  7.5 12.2 %copy-start = (bf16[1,4096,256]{2,1,0:T(8,128)(2,1)S(1)}, bf16[1,4096,256]{2,1,0:T(8,128)(2,1)}, u32[]{:S(2)}) copy-start(bf16[1,4096,256]{2,1,0:T(8,128)(2,1)} %param.14) | copy-start | bytes 6291460
  7.5 12.2 %copy-start.8 = (bf16[1,8,64,256]{3,2,1,0:T(8,128)(2,1)S(1)}, bf16[1,8,64,256]{3,2,1,0:T(8,128)(2,1)}, u32[]{:S(2)}) copy-start(bf16[1,8,64,256]{3,2,1,0:T(8,128)(2,1)} %param.22) | copy-start | bytes 786436
  7.5 12.2 %copy-start.13 = (bf16[1,2,128,256]{3,2,1,0:T(8,128)(2,1)S(1)}, bf16[1,2,128,256]{3,2,1,0:T(8,128)(2,1)}, u32[]{:S(2)}) copy-start(bf16[1,2,128,256]{3,2,1,0:T(8,128)(2,1)} %param.20) | copy-start | bytes 393220
  7.6 12.2 %copy-start.28 = (bf16[1,128,256]{2,1,0:T(8,128)(2,1)S(1)}, bf16[1,128,256]{2,1,0:T(8,128)(2,1)}, u32[]{:S(2)}) copy-start(bf16[1,128,256]{2,1,0:T(8,128)(2,1)} %param.18) | copy-start | bytes 196612
  7.6 12.2 %copy-start.39 = (f32[1,256]{1,0:T(1,128)S(1)}, f32[1,256]{1,0:T(1,128)}, u32[]{:S(2)}) copy-start(f32[1,256]{1,0:T(1,128)} %refs_3_.3) | copy-start | bytes 3076
  7.6 12.2 %copy-start.48 = (s32[1,2,2]{2,1,0:T(2,128)S(1)}, s32[1,2,2]{2,1,0:T(2,128)}, u32[]{:S(2)}) copy-start(s32[1,2,2]{2,1,0:T(2,128)} %param.25) | copy-start | bytes 52
  7.6 4.3 %collective-permute-start = (bf16[8,144,256]{2,1,0:T(8,128)(2,1)S(1)}, bf16[8,144,256]{2,1,0:T(8,128)(2,1)S(1)}, u32[]{:S(2)}, u32[]{:S(2)}) collective-permute-start(bf16[8,144,256]{2,1,0:T(8,128)(2,1)S(1)} %get-tuple-element.47), channel_id=1, source_target_pairs={{0,1},{1,0},{2,3},{3,2},{4,5},{5,4},{6,7},{7,6},{8,9},{9,8},{10,11... | collective-permute-start | bytes 1769480 | tf_op jit(solution)/shard_map/ppermute | solution.py:286
  12.9 26.2 %all-to-all-start = ((bf16[8,144,256]{2,1,0:T(8,128)(2,1)}), bf16[8,144,256]{2,1,0:T(8,128)(2,1)S(1)}, u32[]{:S(2)}, u32[]{:S(2)}) async-start(bf16[8,144,256]{2,1,0:T(8,128)(2,1)} %forward_core_sum.2.refs_9_), calls=%async_computation | async-start | bytes 1179648 | tf_op jit(solution)/shard_map/all_to_all | solution.py:42
  23.3 4.1 %collective-permute-start.1 = (bf16[8,128,256]{2,1,0:T(8,128)(2,1)S(1)}, bf16[8,128,256]{2,1,0:T(8,128)(2,1)S(1)}, u32[]{:S(2)}, u32[]{:S(2)}) collective-permute-start(bf16[8,128,256]{2,1,0:T(8,128)(2,1)S(1)} %get-tuple-element.49), channel_id=1, source_target_pairs={{0,1},{1,0},{2,3},{3,2},{4,5},{5,4},{6,7},{7,6},{8,9},{9,8},{10,11... | collective-permute-start | bytes 1572872 | tf_op jit(solution)/shard_map/ppermute | solution.py:286
  39.1 21.4 %all-to-all-start.1 = ((bf16[8,128,256]{2,1,0:T(8,128)(2,1)}), bf16[8,128,256]{2,1,0:T(8,128)(2,1)S(1)}, u32[]{:S(2)}, u32[]{:S(2)}) async-start(bf16[8,128,256]{2,1,0:T(8,128)(2,1)} %backward_core_sum.2.refs_1_), calls=%async_computation.1 | async-start | bytes 1048576 | tf_op jit(solution)/shard_map/all_to_all | solution.py:42
  42.6 12.8 %collective-permute-start.2 = (bf16[144,256]{1,0:T(8,128)(2,1)S(1)}, bf16[144,256]{1,0:T(8,128)(2,1)S(1)}, u32[]{:S(2)}, u32[]{:S(2)}) collective-permute-start(bf16[144,256]{1,0:T(8,128)(2,1)S(1)} %forward_ring_sum.2.refs_1_), channel_id=1, source_target_pairs={{0,2},{1,3},{2,0},{3,1},{4,6},{5,7},{6,4},{7,5},{8,10},{9,11},{10,... | collective-permute-start | bytes 221192 | tf_op jit(solution)/shard_map/ppermute | solution.py:286
  60.4 4.2 %copy-start.11 = (bf16[8,128,256]{2,1,0:T(8,128)(2,1)}, bf16[8,128,256]{2,1,0:T(8,128)(2,1)S(1)}, u32[]{:S(2)}) copy-start(bf16[8,128,256]{2,1,0:T(8,128)(2,1)S(1)} %all-to-all-done.1.refs_0_) | copy-start | bytes 1572868
  60.4 27.4 %all-to-all-start.2 = ((bf16[8,128,256]{2,1,0:T(8,128)(2,1)}), bf16[8,128,256]{2,1,0:T(8,128)(2,1)}, u32[]{:S(2)}, u32[]{:S(2)}) async-start(bf16[8,128,256]{2,1,0:T(8,128)(2,1)} %get-tuple-element.52.refs_1_), calls=%async_computation.2 | async-start | bytes 1048576 | tf_op jit(solution)/shard_map/all_to_all | solution.py:42
  64.6 30.1 %collective-permute-start.3 = (bf16[2048,256]{1,0:T(8,128)(2,1)}, bf16[2048,256]{1,0:T(8,128)(2,1)S(1)}, u32[]{:S(2)}, u32[]{:S(2)}) collective-permute-start(bf16[2048,256]{1,0:T(8,128)(2,1)} %copy-done.54), channel_id=1, source_target_pairs={{0,1},{1,0},{2,3},{3,2},{4,5},{5,4},{6,7},{7,6},{8,9},{9,8},{10,11... | collective-permute-start | bytes 3145736 | tf_op jit(solution)/shard_map/ppermute | solution.py:286
  70.0 11.3 %collective-permute-start.4 = (bf16[128,256]{1,0:T(8,128)(2,1)S(1)}, bf16[128,256]{1,0:T(8,128)(2,1)S(1)}, u32[]{:S(2)}, u32[]{:S(2)}) collective-permute-start(bf16[128,256]{1,0:T(8,128)(2,1)S(1)} %backward_ring_sum.2.refs_1_), channel_id=1, source_target_pairs={{0,2},{1,3},{2,0},{3,1},{4,6},{5,7},{6,4},{7,5},{8,10},{9,11},{10,... | collective-permute-start | bytes 196616 | tf_op jit(solution)/shard_map/ppermute | solution.py:286
  85.4 32.5 %collective-permute-start.8 = (bf16[256,2048]{1,0:T(8,128)(2,1)}, bf16[256,2048]{1,0:T(8,128)(2,1)}, u32[]{:S(2)}, u32[]{:S(2)}) collective-permute-start(bf16[256,2048]{1,0:T(8,128)(2,1)} %get-tuple-element.61), channel_id=1, source_target_pairs={{0,1},{1,0},{2,3},{3,2},{4,5},{5,4},{6,7},{7,6},{8,9},{9,8},{10,11... | collective-permute-start | bytes 3145736 | tf_op jit(solution)/shard_map/ppermute | solution.py:286
  87.9 30.0 %all-to-all-start.3 = ((bf16[8,128,256]{2,1,0:T(8,128)(2,1)}), bf16[8,128,256]{2,1,0:T(8,128)(2,1)}, u32[]{:S(2)}, u32[]{:S(2)}) async-start(bf16[8,128,256]{2,1,0:T(8,128)(2,1)} %copy-done.9), calls=%async_computation.3 | async-start | bytes 1048576 | tf_op jit(solution)/shard_map/all_to_all | solution.py:42
  94.7 12.6 %copy-start.3 = (bf16[1,256,4096]{2,1,0:T(8,128)(2,1)S(1)}, bf16[1,256,4096]{2,1,0:T(8,128)(2,1)}, u32[]{:S(2)}) copy-start(bf16[1,256,4096]{2,1,0:T(8,128)(2,1)} %param.13) | copy-start | bytes 6291460
  94.7 12.6 %copy-start.7 = (bf16[1,8,64,256]{3,2,1,0:T(8,128)(2,1)S(1)}, bf16[1,8,64,256]{3,2,1,0:T(8,128)(2,1)}, u32[]{:S(2)}) copy-start(bf16[1,8,64,256]{3,2,1,0:T(8,128)(2,1)} %param.21) | copy-start | bytes 786436
  95.9 11.3 %copy-start.37 = (bf16[1,128,256]{2,1,0:T(8,128)(2,1)S(1)}, bf16[1,128,256]{2,1,0:T(8,128)(2,1)}, u32[]{:S(2)}) copy-start(bf16[1,128,256]{2,1,0:T(8,128)(2,1)} %refs_4_.2) | copy-start | bytes 196612
  95.9 11.3 %copy-start.40 = (f32[1,256]{1,0:T(1,128)S(1)}, f32[1,256]{1,0:T(1,128)}, u32[]{:S(2)}) copy-start(f32[1,256]{1,0:T(1,128)} %refs_3_.3) | copy-start | bytes 3076
  95.9 11.3 %copy-start.47 = (s32[1,2,2]{2,1,0:T(2,128)S(1)}, s32[1,2,2]{2,1,0:T(2,128)}, u32[]{:S(2)}) copy-start(s32[1,2,2]{2,1,0:T(2,128)} %param.24) | copy-start | bytes 52
  98.4 15.3 %copy-start.16 = (f32[2,128,256]{2,1,0:T(8,128)S(1)}, f32[2,128,256]{2,1,0:T(8,128)}, u32[]{:S(2)}) copy-start(f32[2,128,256]{2,1,0:T(8,128)} %copy-done.15) | copy-start | bytes 786436
  98.4 3.4 %collective-permute-start.5 = (f32[128,256]{1,0:T(8,128)S(1)}, f32[128,256]{1,0:T(8,128)S(1)}, u32[]{:S(2)}, u32[]{:S(2)}) collective-permute-start(f32[128,256]{1,0:T(8,128)S(1)} %get-tuple-element.57), channel_id=1, source_target_pairs={{0,1},{1,0},{2,3},{3,2},{4,5},{5,4},{6,7},{7,6},{8,9},{9,8},{10,11... | collective-permute-start | bytes 393224 | tf_op jit(solution)/shard_map/ppermute | solution.py:286
  101.8 5.4 %collective-permute-start.6 = (bf16[128,256]{1,0:T(8,128)(2,1)S(1)}, bf16[128,256]{1,0:T(8,128)(2,1)S(1)}, u32[]{:S(2)}, u32[]{:S(2)}) collective-permute-start(bf16[128,256]{1,0:T(8,128)(2,1)S(1)} %forward_end.2), channel_id=1, source_target_pairs={{0,32},{32,64},{64,96},{96,128},{128,160},{160,192},{192,224},{224... | collective-permute-start | bytes 196616 | tf_op jit(solution)/shard_map/ppermute | solution.py:52
  110.7 33.0 %collective-permute-start.7 = (bf16[8,144,256]{2,1,0:T(8,128)(2,1)}, bf16[8,144,256]{2,1,0:T(8,128)(2,1)}, u32[]{:S(2)}, u32[]{:S(2)}) collective-permute-start(bf16[8,144,256]{2,1,0:T(8,128)(2,1)} %get-tuple-element.60), channel_id=1, source_target_pairs={{0,1},{1,0},{2,3},{3,2},{4,5},{5,4},{6,7},{7,6},{8,9},{9,8},{10,11... | collective-permute-start | bytes 1769480 | tf_op jit(solution)/shard_map/ppermute | solution.py:286
  113.7 3.4 %collective-permute-start.9 = (f32[2,128,256]{2,1,0:T(8,128)S(1)}, f32[2,128,256]{2,1,0:T(8,128)S(1)}, u32[]{:S(2)}, u32[]{:S(2)}) collective-permute-start(f32[2,128,256]{2,1,0:T(8,128)S(1)} %copy-done.16), channel_id=1, source_target_pairs={{0,1},{1,0},{2,3},{3,2},{4,5},{5,4},{6,7},{7,6},{8,9},{9,8},{10,11... | collective-permute-start | bytes 786440 | tf_op jit(solution)/shard_map/ppermute | solution.py:286
  117.8 1.6 copy-start.4
  125.6 34.2 %copy-start.14 = (bf16[1,2,128,256]{3,2,1,0:T(8,128)(2,1)S(1)}, bf16[1,2,128,256]{3,2,1,0:T(8,128)(2,1)}, u32[]{:S(2)}) copy-start(bf16[1,2,128,256]{3,2,1,0:T(8,128)(2,1)} %param.20) | copy-start | bytes 393220
  125.6 3.4 %collective-permute-start.10 = (f32[136,256]{1,0:T(8,128)S(1)}, f32[136,256]{1,0:T(8,128)S(1)}, u32[]{:S(2)}, u32[]{:S(2)}) collective-permute-start(f32[136,256]{1,0:T(8,128)S(1)} %get-tuple-element.65), channel_id=1, source_target_pairs={{0,1},{1,0},{2,3},{3,2},{4,5},{5,4},{6,7},{7,6},{8,9},{9,8},{10,11... | collective-permute-start | bytes 417800 | tf_op jit(solution)/shard_map/ppermute | solution.py:286
  130.3 25.3 %all-to-all-start.4 = ((f32[16,8,128]{2,1,0:T(8,128)}), f32[16,8,128]{2,1,0:T(8,128)}, u32[]{:S(2)}, u32[]{:S(2)}) async-start(f32[16,8,128]{2,1,0:T(8,128)} %copy-done.34), calls=%async_computation.4 | async-start | bytes 131072 | tf_op jit(solution)/shard_map/all_to_all | solution.py:42
  155.6 26.1 %all-to-all-start.5 = ((bf16[8,144,256]{2,1,0:T(8,128)(2,1)}), bf16[8,144,256]{2,1,0:T(8,128)(2,1)}, u32[]{:S(2)}, u32[]{:S(2)}) async-start(bf16[8,144,256]{2,1,0:T(8,128)(2,1)} %forward_core_sum.3.refs_5_), calls=%async_computation.5 | async-start | bytes 1179648 | tf_op jit(solution)/shard_map/all_to_all | solution.py:42
  163.9 2.4 copy-start.52
  163.9 7.5 %collective-permute-start.11 = (bf16[128,256]{1,0:T(8,128)(2,1)S(1)}, bf16[128,256]{1,0:T(8,128)(2,1)S(1)}, u32[]{:S(2)}, u32[]{:S(2)}) collective-permute-start(bf16[128,256]{1,0:T(8,128)(2,1)S(1)} %get-tuple-element.70), channel_id=1, source_target_pairs={{32,0},{64,32},{96,64},{128,96},{160,128},{192,160},{224,192},{256... | collective-permute-start | bytes 196616 | tf_op jit(solution)/shard_map/ppermute | solution.py:52
  175.1 5.8 %collective-permute-start.12 = (bf16[8,128,256]{2,1,0:T(8,128)(2,1)S(1)}, bf16[8,128,256]{2,1,0:T(8,128)(2,1)S(1)}, u32[]{:S(2)}, u32[]{:S(2)}) collective-permute-start(bf16[8,128,256]{2,1,0:T(8,128)(2,1)S(1)} %get-tuple-element.72), channel_id=1, source_target_pairs={{0,1},{1,0},{2,3},{3,2},{4,5},{5,4},{6,7},{7,6},{8,9},{9,8},{10,11... | collective-permute-start | bytes 1572872 | tf_op jit(solution)/shard_map/ppermute | solution.py:286
  181.8 24.9 %all-to-all-start.6 = ((bf16[8,128,256]{2,1,0:T(8,128)(2,1)}), bf16[8,128,256]{2,1,0:T(8,128)(2,1)}, u32[]{:S(2)}, u32[]{:S(2)}) async-start(bf16[8,128,256]{2,1,0:T(8,128)(2,1)} %backward_core_sum.3.refs_1_), calls=%async_computation.6 | async-start | bytes 1048576 | tf_op jit(solution)/shard_map/all_to_all | solution.py:42
  189.7 9.3 %collective-permute-start.13 = (bf16[144,256]{1,0:T(8,128)(2,1)S(1)}, bf16[144,256]{1,0:T(8,128)(2,1)S(1)}, u32[]{:S(2)}, u32[]{:S(2)}) collective-permute-start(bf16[144,256]{1,0:T(8,128)(2,1)S(1)} %forward_ring_sum.3.refs_1_), channel_id=1, source_target_pairs={{0,2},{1,3},{2,0},{3,1},{4,6},{5,7},{6,4},{7,5},{8,10},{9,11},{10,... | collective-permute-start | bytes 221192 | tf_op jit(solution)/shard_map/ppermute | solution.py:286
  206.6 22.1 %all-to-all-start.7 = ((bf16[8,128,256]{2,1,0:T(8,128)(2,1)}), bf16[8,128,256]{2,1,0:T(8,128)(2,1)}, u32[]{:S(2)}, u32[]{:S(2)}) async-start(bf16[8,128,256]{2,1,0:T(8,128)(2,1)} %forward_share.3.refs_1_), calls=%async_computation.7 | async-start | bytes 1048576 | tf_op jit(solution)/shard_map/all_to_all | solution.py:42
  211.9 9.2 %collective-permute-start.14 = (bf16[128,256]{1,0:T(8,128)(2,1)S(1)}, bf16[128,256]{1,0:T(8,128)(2,1)S(1)}, u32[]{:S(2)}, u32[]{:S(2)}) collective-permute-start(bf16[128,256]{1,0:T(8,128)(2,1)S(1)} %backward_ring_sum.3.refs_1_), channel_id=1, source_target_pairs={{0,2},{1,3},{2,0},{3,1},{4,6},{5,7},{6,4},{7,5},{8,10},{9,11},{10,... | collective-permute-start | bytes 196616 | tf_op jit(solution)/shard_map/ppermute | solution.py:286
  228.7 22.1 %all-to-all-start.8 = ((bf16[8,128,256]{2,1,0:T(8,128)(2,1)}), bf16[8,128,256]{2,1,0:T(8,128)(2,1)}, u32[]{:S(2)}, u32[]{:S(2)}) async-start(bf16[8,128,256]{2,1,0:T(8,128)(2,1)} %backward_share.3.refs_4_), calls=%async_computation.8 | async-start | bytes 1048576 | tf_op jit(solution)/shard_map/all_to_all | solution.py:42
  232.9 5.9 %copy-start.36 = (bf16[128,256]{1,0:T(8,128)(2,1)S(1)}, bf16[128,256]{1,0:T(8,128)(2,1)}, u32[]{:S(2)}) copy-start(bf16[128,256]{1,0:T(8,128)(2,1)} %copy-done.35) | copy-start | bytes 196612
  232.9 17.9 %copy-start.18 = (f32[2,128,256]{2,1,0:T(8,128)S(1)}, f32[2,128,256]{2,1,0:T(8,128)}, u32[]{:S(2)}) copy-start(f32[2,128,256]{2,1,0:T(8,128)} %copy-done.15) | copy-start | bytes 786436
  235.4 3.4 %collective-permute-start.15 = (f32[128,256]{1,0:T(8,128)S(1)}, f32[128,256]{1,0:T(8,128)S(1)}, u32[]{:S(2)}, u32[]{:S(2)}) collective-permute-start(f32[128,256]{1,0:T(8,128)S(1)} %get-tuple-element.77), channel_id=1, source_target_pairs={{0,1},{1,0},{2,3},{3,2},{4,5},{5,4},{6,7},{7,6},{8,9},{9,8},{10,11... | collective-permute-start | bytes 393224 | tf_op jit(solution)/shard_map/ppermute | solution.py:286
  254.9 21.5 %copy-start.33 = (bf16[128,256]{1,0:T(8,128)(2,1)S(1)}, bf16[128,256]{1,0:T(8,128)(2,1)}, u32[]{:S(2)}) copy-start(bf16[128,256]{1,0:T(8,128)(2,1)} %copy-done.32) | copy-start | bytes 196612
  254.9 21.5 %copy-start.42 = (f32[1,256]{1,0:T(1,128)S(1)}, f32[1,256]{1,0:T(1,128)}, u32[]{:S(2)}) copy-start(f32[1,256]{1,0:T(1,128)} %refs_3_.3) | copy-start | bytes 3076
  254.9 21.5 %copy-start.51 = (f32[8,128]{1,0:T(8,128)S(1)}, f32[8,128]{1,0:T(8,128)}, u32[]{:S(2)}) copy-start(f32[8,128]{1,0:T(8,128)} %copy-done.50) | copy-start | bytes 12292
  254.9 21.5 %copy-start.53 = (f32[1,256]{1,0:T(1,128)S(1)}, f32[1,256]{1,0:T(1,128)}, u32[]{:S(2)}) copy-start(f32[1,256]{1,0:T(1,128)} %copy-done.52) | copy-start | bytes 3076
  258.6 3.4 %collective-permute-start.16 = (f32[136,256]{1,0:T(8,128)S(1)}, f32[136,256]{1,0:T(8,128)S(1)}, u32[]{:S(2)}, u32[]{:S(2)}) collective-permute-start(f32[136,256]{1,0:T(8,128)S(1)} %get-tuple-element.80), channel_id=1, source_target_pairs={{0,1},{1,0},{2,3},{3,2},{4,5},{5,4},{6,7},{7,6},{8,9},{9,8},{10,11... | collective-permute-start | bytes 417800 | tf_op jit(solution)/shard_map/ppermute | solution.py:286
  (33 other events, 28.6 us)

commit v7 on v5

--- a/solution.py
+++ b/solution.py
@@ -182,20 +182,23 @@
         out[ROWS:] = split_stats(stats)
 
 
-def forward_share(own, other, out):
+def forward_share(own, other, *refs):
     total = joined_stats(own[ROWS:]) + joined_stats(other[ROWS:])
     factor = lax.rsqrt(total[0:1] / D + EPSILON)
     value = own[:ROWS].astype(F32) + other[:ROWS].astype(F32)
-    out[...] = jnp.broadcast_to((down(factor) * value).astype(BF16)[None], out.shape)
-
-
-def backward_share(own, other, out):
+    value = (down(factor) * value).astype(BF16)
+    out, *half = refs[len(refs) // 2 :]
+    out[...] = jnp.broadcast_to(value[None], out.shape)
+    if half:
+        half[0][...] = refs[0][...]
+
+
+def backward_share(own, other, *refs):
     value = (own[...].astype(F32) + other[...].astype(F32)).astype(BF16)
+    out, *half = refs[len(refs) // 2 :]
     out[...] = jnp.broadcast_to(value[None], out.shape)
-
-
-def half(weight, out):
-    out[...] = weight[...]
+    if half:
+        half[0][...] = refs[0][...]
 
 
 def forward_product(blocks, own_weight, other_weight, mine, others):
@@ -325,28 +328,16 @@
         operands = (keep, over(send, core_pairs()))
         return g, *call(core_sum, "backward_core_sum", [eight], operands=operands)
 
-    def forward_turn(pieces, *after):
-        (own,) = call(ring_sum, "forward_ring_sum", [tall], operands=(pieces,), after=after)
-        return own, *call(forward_share, "forward_share", [eight], operands=(own, over(own, z_pairs())))
-
-    def backward_turn(pieces, *after):
-        (own,) = call(ring_sum, "backward_ring_sum", [low], operands=(pieces,), after=after)
-        return own, *call(backward_share, "backward_share", [eight], operands=(own, over(own, z_pairs())))
+    def turn(kernel, name, block, pieces, half, *after):
+        (own,) = call(ring_sum, name + "_ring_sum", [block], operands=(pieces,), after=after)
+        operands, outs, blocks = (own, over(own, z_pairs())), [eight], {}
+        if half:
+            weight, shape, index_map = half
+            operands, outs, blocks = (*operands, weight), [eight, shape_of(*shape)], {2: (shape, index_map)}
+        return call(with_meta(kernel), name + "_share", outs, prefetch=(meta,), operands=operands, blocks=blocks)
 
     def with_meta(kernel):
         return lambda _, *refs: kernel(*refs)
-
-    def exchanged_half(weight, block, index_map, *after):
-        (own,) = call(
-            with_meta(half),
-            "half",
-            [shape_of(*block)],
-            prefetch=(meta,),
-            operands=(weight,),
-            blocks={0: (block, index_map)},
-            after=after,
-        )
-        return over(own, core_pairs())
 
     def forward_finish(x, gathered, *after):
         mine, others = call(
@@ -387,48 +378,52 @@
             after=after,
         )
 
-    x, pieces = forward_begin(0, [arriving[0]])
-    gated = gate(pieces)
+    g, back_pieces = backward_begin(0, [returning[0]])
+    gated = gate(back_pieces)
+    back_landed = swapped(gated, rings())
+
+    x, pieces = forward_begin(0, [arriving[0]], gated)
+    gated = gate(pieces, back_landed)
     landed = swapped(gated, rings())
 
-    g, back_pieces = backward_begin(0, [returning[0]], gated)
-    gated = gate(back_pieces, landed)
+    half = (value_local, (WIDTH, HALF), lambda i, meta: (0, 1 - meta[3]))
+    back_copies, half = turn(backward_share, "backward", low, back_landed, half, gated)
+    value_other = over(half, core_pairs())
+    gated = gate(back_copies, landed)
+    back_gathered = swapped(gated, rings())
+
+    half = (output_local, (HALF, WIDTH), lambda i, meta: (1 - meta[3], 0))
+    copies, half = turn(forward_share, "forward", tall, landed, half, gated)
+    output_other = over(half, core_pairs())
+    scaled_grad, dots = backward_dots(0, back_gathered, copies)
+    all_dots = swapped(dots)
+
+    gated = gate(copies, all_dots)
+    gathered = swapped(gated, rings())
+
+    input_grad, gain_total, squares = backward_finish(0, g, scaled_grad, all_dots, (), gated)
+    g, back_pieces = backward_begin(1, [shifted(input_grad, "segment", -1), cotangents])
+    gated = gate(back_pieces, gathered)
     back_landed = swapped(gated, rings())
-
-    own, copies = forward_turn(landed, gated)
-    output_other = exchanged_half(output_local, (HALF, WIDTH), lambda i, meta: (1 - meta[3], 0), own)
-    gated = gate(copies, back_landed, output_other)
-    gathered = swapped(gated, rings())
-
-    own, copies = backward_turn(back_landed, gated)
-    value_other = exchanged_half(value_local, (WIDTH, HALF), lambda i, meta: (0, 1 - meta[3]), own)
-    gated = gate(copies, gathered, value_other)
-    back_gathered = swapped(gated, rings())
 
     segment_out = forward_finish(x, gathered, gated)
     x, pieces = forward_begin(1, [shifted(segment_out, "segment", 1), fresh_inputs])
-    scaled_grad, dots = backward_dots(0, back_gathered)
-    all_dots = swapped(dots)
-
-    gated = gate(pieces, all_dots)
+    gated = gate(pieces, back_landed)
     landed = swapped(gated, rings())
 
-    input_grad, gain_total, squares = backward_finish(0, g, scaled_grad, all_dots, (), gated)
-    g, back_pieces = backward_begin(1, [shifted(input_grad, "segment", -1), cotangents])
-    gated = gate(back_pieces, landed)
-    back_landed = swapped(gated, rings())
-
-    _, copies = forward_turn(landed, gated)
-    gated = gate(copies, back_landed)
+    (back_copies,) = turn(backward_share, "backward", low, back_landed, None, gated)
+    gated = gate(back_copies, landed)
+    back_gathered = swapped(gated, rings())
+
+    (copies,) = turn(forward_share, "forward", tall, landed, None, gated)
+    gated = gate(copies, back_gathered)
     gathered = swapped(gated, rings())
 
-    _, copies = backward_turn(back_landed, gated)
-    gated = gate(copies, gathered)
-    back_gathered = swapped(gated, rings())
+    scaled_grad, dots = backward_dots(1, back_gathered, gated)
+    gated = gate(dots, gathered)
+    all_dots = swapped(gated)
 
     segment_out = forward_finish(x, gathered, gated)
-    scaled_grad, dots = backward_dots(1, back_gathered, segment_out)
-    all_dots = swapped(dots)
     input_grad, gain_total = backward_finish(1, g, scaled_grad, all_dots, (squares, gain_total))
     return (segment_out[None], input_grad[None], gain_total)
 

time: 278 us -> 265 us (0.953)
  blocking collectives: 16.6 us -> 0 us
  starting transfers between devices: 114 us -> 118 us
    all_to_all x1 -> x0, blocking collectives: 16.6 us -> none  [swapped(): lax.all_to_all(value, 'shard', 0, 0, axis_index_groups=groups, tiled=True)]
    all_to_all x9 -> x10, starting transfers between devices: 54 us -> 60.8 us  [swapped(): lax.all_to_all(value, 'shard', 0, 0, axis_index_groups=groups, tiled=True)]
    all_to_all x9 -> x10, waiting for transfers between devices: 57 us -> 52.9 us  [swapped(): lax.all_to_all(value, 'shard', 0, 0, axis_index_groups=groups, tiled=True)]
    ppermute x14, waiting for transfers between devices: 24.7 us -> 27.7 us  [over(): return lax.ppermute(value, 'shard', pairs)]
    pallas_call x28 -> x26, Pallas kernels: 34.1 us -> 31.9 us  [call(): pl.pallas_call(body, out_shape=outs, grid_spec=pltpu.PrefetchScalarGridSp...]
  transfers between devices with their start and end apart: 25 -> 26, of which waited for: 21 -> 22; matrix products, arithmetic and copies ran while one was open for 0% -> 0% of each run, Pallas kernels for 9% -> 10%
where the time goes in v7:
time: 265 us; the launch traced here: 263 us
  starting transfers between devices  118 us (45%)
  waiting for transfers between devices  89.2 us (34%)
  Pallas kernels  31.9 us (12%)
  local copies, waits for them, and re-layouts  22.1 us (8%)
    all_to_all x10, starting transfers between devices, swapped(): lax.all_to_all(value, 'shard', 0, 0, axis_index_groups=groups, tiled=True)  60.8 us
    ppermute x14, starting transfers between devices, over(): return lax.ppermute(value, 'shard', pairs)  53.1 us
    all_to_all x10, waiting for transfers between devices, swapped(): lax.all_to_all(value, 'shard', 0, 0, axis_index_groups=groups, tiled=True)  52.9 us
    pallas_call x26, Pallas kernels, call(): pl.pallas_call(body, out_shape=outs, grid_spec=pltpu.PrefetchScalarGridSp...  31.9 us
    ppermute x14, waiting for transfers between devices, over(): return lax.ppermute(value, 'shard', pairs)  27.7 us
    unnamed x83, local copies, waits for them, and re-layouts  22.1 us
    ppermute x2, waiting for transfers between devices, shifted(): lax.ppermute(value, axis, [(source, source + steps) for source in range(l...  8.58 us
  transfers between devices with their start and end apart: 26, of which 22 were waited for; matrix products, arithmetic and copies ran while one was open for 0% of the time, Pallas kernels for 10%

profile of v7, /device:TPU:7, one launch (start us, length us, event | category | flops | bytes accessed | tf_op | source)
XLA Modules:
  0.0 262.8 jit_solution(517411041390854481)
XLA Ops:
  1.5 1.6 copy-done.1
  7.2 2.6 collective-permute-start
  12.3 6.8 %all-to-all-start = ((bf16[8,128,256]{2,1,0:T(8,128)(2,1)}), bf16[8,128,256]{2,1,0:T(8,128)(2,1)S(1)}, u32[]{:S(2)}, u32[]{:S(2)}) async-start(bf16[8,128,256]{2,1,0:T(8,128)(2,1)} %backward_core_sum.2.refs_8_), calls=%async_computation | async-start | bytes 1048576 | tf_op jit(solution)/shard_map/all_to_all | solution.py:38
  20.4 2.6 collective-permute-start.1
  23.0 1.6 collective-permute-done.1.refs_1_
  25.5 11.5 %all-to-all-done.refs_0_ = bf16[8,128,256]{2,1,0:T(8,128)(2,1)S(1)} async-done(((bf16[8,128,256]{2,1,0:T(8,128)(2,1)}), bf16[8,128,256]{2,1,0:T(8,128)(2,1)S(1)}, u32[]{:S(2)}, u32[]{:S(2)}) %all-to-all-start) | async-done | bytes 524320 | tf_op jit(solution)/shard_map/all_to_all | solution.py:38
  37.0 4.2 %all-to-all-start.1 = ((bf16[8,144,256]{2,1,0:T(8,128)(2,1)}), bf16[8,144,256]{2,1,0:T(8,128)(2,1)}, u32[]{:S(2)}, u32[]{:S(2)}) async-start(bf16[8,144,256]{2,1,0:T(8,128)(2,1)} %forward_core_sum.2.refs_1_), calls=%async_computation.1 | async-start | bytes 1179648 | tf_op jit(solution)/shard_map/all_to_all | solution.py:38
  41.3 10.6 %collective-permute-start.2 = (bf16[128,256]{1,0:T(8,128)(2,1)S(1)}, bf16[128,256]{1,0:T(8,128)(2,1)S(1)}, u32[]{:S(2)}, u32[]{:S(2)}) collective-permute-start(bf16[128,256]{1,0:T(8,128)(2,1)S(1)} %backward_ring_sum.2.refs_1_), channel_id=1, source_target_pairs={{0,2},{1,3},{2,0},{3,1},{4,6},{5,7},{6,4},{7,5},{8,10},{9,11},{10,... | collective-permute-start | bytes 196616 | tf_op jit(solution)/shard_map/ppermute | solution.py:260
  52.0 2.0 collective-permute-done.2.refs_2_
  54.0 1.6 backward_share.2
  56.4 3.8 %collective-permute-start.4 = (bf16[256,2048]{1,0:T(8,128)(2,1)}, bf16[256,2048]{1,0:T(8,128)(2,1)S(1)}, u32[]{:S(2)}, u32[]{:S(2)}) collective-permute-start(bf16[256,2048]{1,0:T(8,128)(2,1)} %get-tuple-element.53), channel_id=1, source_target_pairs={{0,1},{1,0},{2,3},{3,2},{4,5},{5,4},{6,7},{7,6},{8,9},{9,8},{10,11... | collective-permute-start | bytes 3145736 | tf_op jit(solution)/shard_map/ppermute | solution.py:260
  60.6 6.2 %all-to-all-start.2 = ((bf16[8,128,256]{2,1,0:T(8,128)(2,1)}), bf16[8,128,256]{2,1,0:T(8,128)(2,1)}, u32[]{:S(2)}, u32[]{:S(2)}) async-start(bf16[8,128,256]{2,1,0:T(8,128)(2,1)} %copy-done.10), calls=%async_computation.2 | async-start | bytes 1048576 | tf_op jit(solution)/shard_map/all_to_all | solution.py:38
  69.0 8.6 %collective-permute-start.3 = (bf16[144,256]{1,0:T(8,128)(2,1)S(1)}, bf16[144,256]{1,0:T(8,128)(2,1)S(1)}, u32[]{:S(2)}, u32[]{:S(2)}) collective-permute-start(bf16[144,256]{1,0:T(8,128)(2,1)S(1)} %forward_ring_sum.2.refs_1_), channel_id=1, source_target_pairs={{0,2},{1,3},{2,0},{3,1},{4,6},{5,7},{6,4},{7,5},{8,10},{9,11},{10,... | collective-permute-start | bytes 221192 | tf_op jit(solution)/shard_map/ppermute | solution.py:260
  77.7 2.2 collective-permute-done.3.refs_2_
  79.9 1.6 copy-done.2
  85.0 2.4 backward_product.2
  87.4 2.8 %collective-permute-start.5 = (f32[128,256]{1,0:T(8,128)S(1)}, f32[128,256]{1,0:T(8,128)S(1)}, u32[]{:S(2)}, u32[]{:S(2)}) collective-permute-start(f32[128,256]{1,0:T(8,128)S(1)} %get-tuple-element.55), channel_id=1, source_target_pairs={{0,1},{1,0},{2,3},{3,2},{4,5},{5,4},{6,7},{7,6},{8,9},{9,8},{10,11... | collective-permute-start | bytes 393224 | tf_op jit(solution)/shard_map/ppermute | solution.py:260
  92.8 13.4 %all-to-all-start.3 = ((f32[32,8,128]{2,1,0:T(8,128)}), f32[32,8,128]{2,1,0:T(8,128)}, u32[]{:S(2)}, u32[]{:S(2)}) async-start(f32[32,8,128]{2,1,0:T(8,128)} %copy-done.14), calls=%async_computation.3 | async-start | bytes 262144 | tf_op jit(solution)/shard_map/all_to_all | solution.py:38
  106.2 2.2 collective-permute-start.6
  108.4 11.0 %all-to-all-done.3.refs_4_ = f32[32,8,128]{2,1,0:T(8,128)} async-done(((f32[32,8,128]{2,1,0:T(8,128)}), f32[32,8,128]{2,1,0:T(8,128)}, u32[]{:S(2)}, u32[]{:S(2)}) %all-to-all-start.3) | async-done | bytes 131104 | tf_op jit(solution)/shard_map/all_to_all | solution.py:38
  119.4 4.2 %all-to-all-start.4 = ((bf16[8,128,256]{2,1,0:T(8,128)(2,1)}), bf16[8,128,256]{2,1,0:T(8,128)(2,1)}, u32[]{:S(2)}, u32[]{:S(2)}) async-start(bf16[8,128,256]{2,1,0:T(8,128)(2,1)} %get-tuple-element.57.refs_4_.refs_5_), calls=%async_computation.4 | async-start | bytes 1048576 | tf_op jit(solution)/shard_map/all_to_all | solution.py:38
  127.6 2.4 collective-permute-start.7
  130.1 5.1 %collective-permute-done.7.refs_3_ = bf16[128,256]{1,0:T(8,128)(2,1)S(1)} collective-permute-done((bf16[128,256]{1,0:T(8,128)(2,1)S(1)}, bf16[128,256]{1,0:T(8,128)(2,1)S(1)}, u32[]{:S(2)}, u32[]{:S(2)}) %collective-permute-start.7) | collective-permute-done | bytes 65568 | tf_op jit(solution)/shard_map/ppermute | solution.py:48
  135.2 1.6 copy-done.3
  141.5 2.8 %collective-permute-start.8 = (bf16[8,128,256]{2,1,0:T(8,128)(2,1)S(1)}, bf16[8,128,256]{2,1,0:T(8,128)(2,1)S(1)}, u32[]{:S(2)}, u32[]{:S(2)}) collective-permute-start(bf16[8,128,256]{2,1,0:T(8,128)(2,1)S(1)} %get-tuple-element.63), channel_id=1, source_target_pairs={{0,1},{1,0},{2,3},{3,2},{4,5},{5,4},{6,7},{7,6},{8,9},{9,8},{10,11... | collective-permute-start | bytes 1572872 | tf_op jit(solution)/shard_map/ppermute | solution.py:260
  146.8 6.8 %all-to-all-start.5 = ((bf16[8,128,256]{2,1,0:T(8,128)(2,1)}), bf16[8,128,256]{2,1,0:T(8,128)(2,1)}, u32[]{:S(2)}, u32[]{:S(2)}) async-start(bf16[8,128,256]{2,1,0:T(8,128)(2,1)} %backward_core_sum.3.refs_4_), calls=%async_computation.5 | async-start | bytes 1048576 | tf_op jit(solution)/shard_map/all_to_all | solution.py:38
  155.2 2.4 forward_product.2
  157.6 2.6 collective-permute-start.9
  161.1 1.9 collective-permute-start.10
  163.0 3.5 %collective-permute-done.10.refs_3_ = bf16[128,256]{1,0:T(8,128)(2,1)S(1)} collective-permute-done((bf16[128,256]{1,0:T(8,128)(2,1)S(1)}, bf16[128,256]{1,0:T(8,128)(2,1)S(1)}, u32[]{:S(2)}, u32[]{:S(2)}) %collective-permute-start.10) | collective-permute-done | bytes 65568 | tf_op jit(solution)/shard_map/ppermute | solution.py:48
  168.4 3.0 %collective-permute-start.11 = (bf16[8,144,256]{2,1,0:T(8,128)(2,1)S(1)}, bf16[8,144,256]{2,1,0:T(8,128)(2,1)S(1)}, u32[]{:S(2)}, u32[]{:S(2)}) collective-permute-start(bf16[8,144,256]{2,1,0:T(8,128)(2,1)S(1)} %get-tuple-element.69), channel_id=1, source_target_pairs={{0,1},{1,0},{2,3},{3,2},{4,5},{5,4},{6,7},{7,6},{8,9},{9,8},{10,11... | collective-permute-start | bytes 1769480 | tf_op jit(solution)/shard_map/ppermute | solution.py:260
  171.4 1.6 collective-permute-done.11.refs_1_
  174.0 6.9 %all-to-all-start.6 = ((bf16[8,144,256]{2,1,0:T(8,128)(2,1)}), bf16[8,144,256]{2,1,0:T(8,128)(2,1)}, u32[]{:S(2)}, u32[]{:S(2)}) async-start(bf16[8,144,256]{2,1,0:T(8,128)(2,1)} %forward_core_sum.3.refs_1_), calls=%async_computation.6 | async-start | bytes 1179648 | tf_op jit(solution)/shard_map/all_to_all | solution.py:38
  182.0 3.4 %collective-permute-start.12 = (bf16[128,256]{1,0:T(8,128)(2,1)S(1)}, bf16[128,256]{1,0:T(8,128)(2,1)S(1)}, u32[]{:S(2)}, u32[]{:S(2)}) collective-permute-start(bf16[128,256]{1,0:T(8,128)(2,1)S(1)} %backward_ring_sum.3.refs_1_), channel_id=1, source_target_pairs={{0,2},{1,3},{2,0},{3,1},{4,6},{5,7},{6,4},{7,5},{8,10},{9,11},{10,... | collective-permute-start | bytes 196616 | tf_op jit(solution)/shard_map/ppermute | solution.py:260
  185.5 6.5 %collective-permute-done.12.refs_2_ = bf16[128,256]{1,0:T(8,128)(2,1)S(1)} collective-permute-done((bf16[128,256]{1,0:T(8,128)(2,1)S(1)}, bf16[128,256]{1,0:T(8,128)(2,1)S(1)}, u32[]{:S(2)}, u32[]{:S(2)}) %collective-permute-start.12) | collective-permute-done | bytes 65568 | tf_op jit(solution)/shard_map/ppermute | solution.py:260
  193.4 7.0 %all-to-all-done.6.refs_0_ = bf16[8,144,256]{2,1,0:T(8,128)(2,1)} async-done(((bf16[8,144,256]{2,1,0:T(8,128)(2,1)}), bf16[8,144,256]{2,1,0:T(8,128)(2,1)}, u32[]{:S(2)}, u32[]{:S(2)}) %all-to-all-start.6) | async-done | bytes 589856 | tf_op jit(solution)/shard_map/all_to_all | solution.py:38
  200.4 4.1 %all-to-all-start.7 = ((bf16[8,128,256]{2,1,0:T(8,128)(2,1)}), bf16[8,128,256]{2,1,0:T(8,128)(2,1)}, u32[]{:S(2)}, u32[]{:S(2)}) async-start(bf16[8,128,256]{2,1,0:T(8,128)(2,1)} %backward_share.3.refs_1_), calls=%async_computation.7 | async-start | bytes 1048576 | tf_op jit(solution)/shard_map/all_to_all | solution.py:38
  205.7 3.4 %collective-permute-start.13 = (bf16[144,256]{1,0:T(8,128)(2,1)S(1)}, bf16[144,256]{1,0:T(8,128)(2,1)S(1)}, u32[]{:S(2)}, u32[]{:S(2)}) collective-permute-start(bf16[144,256]{1,0:T(8,128)(2,1)S(1)} %forward_ring_sum.3.refs_1_), channel_id=1, source_target_pairs={{0,2},{1,3},{2,0},{3,1},{4,6},{5,7},{6,4},{7,5},{8,10},{9,11},{10,... | collective-permute-start | bytes 221192 | tf_op jit(solution)/shard_map/ppermute | solution.py:260
  209.1 6.8 %collective-permute-done.13.refs_2_ = bf16[144,256]{1,0:T(8,128)(2,1)S(1)} collective-permute-done((bf16[144,256]{1,0:T(8,128)(2,1)S(1)}, bf16[144,256]{1,0:T(8,128)(2,1)S(1)}, u32[]{:S(2)}, u32[]{:S(2)}) %collective-permute-start.13) | collective-permute-done | bytes 73760 | tf_op jit(solution)/shard_map/ppermute | solution.py:260
  217.4 5.1 %all-to-all-done.7.refs_1_ = bf16[8,128,256]{2,1,0:T(8,128)(2,1)} async-done(((bf16[8,128,256]{2,1,0:T(8,128)(2,1)}), bf16[8,128,256]{2,1,0:T(8,128)(2,1)}, u32[]{:S(2)}, u32[]{:S(2)}) %all-to-all-start.7) | async-done | bytes 524320 | tf_op jit(solution)/shard_map/all_to_all | solution.py:38
  222.5 4.2 %all-to-all-start.8 = ((bf16[8,128,256]{2,1,0:T(8,128)(2,1)}), bf16[8,128,256]{2,1,0:T(8,128)(2,1)}, u32[]{:S(2)}, u32[]{:S(2)}) async-start(bf16[8,128,256]{2,1,0:T(8,128)(2,1)} %forward_share.3.refs_4_), calls=%async_computation.8 | async-start | bytes 1048576 | tf_op jit(solution)/shard_map/all_to_all | solution.py:38
  226.7 2.4 backward_product.3
  229.1 2.4 collective-permute-start.14
  233.3 11.3 %all-to-all-done.8.refs_1_ = bf16[8,128,256]{2,1,0:T(8,128)(2,1)} async-done(((bf16[8,128,256]{2,1,0:T(8,128)(2,1)}), bf16[8,128,256]{2,1,0:T(8,128)(2,1)}, u32[]{:S(2)}, u32[]{:S(2)}) %all-to-all-start.8) | async-done | bytes 524320 | tf_op jit(solution)/shard_map/all_to_all | solution.py:38
  244.6 4.0 %all-to-all-start.9 = ((f32[32,8,128]{2,1,0:T(8,128)}), f32[32,8,128]{2,1,0:T(8,128)S(1)}, u32[]{:S(2)}, u32[]{:S(2)}) async-start(f32[32,8,128]{2,1,0:T(8,128)} %get-tuple-element.76.refs_4_), calls=%async_computation.9 | async-start | bytes 262144 | tf_op jit(solution)/shard_map/all_to_all | solution.py:38
  250.2 2.4 forward_product.3
  252.6 2.3 collective-permute-start.15
  256.5 5.5 %all-to-all-done.9.refs_4_ = f32[32,8,128]{2,1,0:T(8,128)S(1)} async-done(((f32[32,8,128]{2,1,0:T(8,128)}), f32[32,8,128]{2,1,0:T(8,128)S(1)}, u32[]{:S(2)}, u32[]{:S(2)}) %all-to-all-start.9) | async-done | bytes 131104 | tf_op jit(solution)/shard_map/all_to_all | solution.py:38
  (114 shorter events, 46.7 us)
Async XLA Ops:
  1.5 1.6 copy-start.1
  5.6 13.5 %copy-start = (bf16[1,256,4096]{2,1,0:T(8,128)(2,1)S(1)}, bf16[1,256,4096]{2,1,0:T(8,128)(2,1)}, u32[]{:S(2)}) copy-start(bf16[1,256,4096]{2,1,0:T(8,128)(2,1)} %param.13) | copy-start | bytes 6291460
  5.6 13.5 %copy-start.6 = (bf16[1,8,64,256]{3,2,1,0:T(8,128)(2,1)S(1)}, bf16[1,8,64,256]{3,2,1,0:T(8,128)(2,1)}, u32[]{:S(2)}) copy-start(bf16[1,8,64,256]{3,2,1,0:T(8,128)(2,1)} %param.21) | copy-start | bytes 786436
  5.6 13.5 %copy-start.16 = (bf16[1,128,256]{2,1,0:T(8,128)(2,1)S(1)}, bf16[1,128,256]{2,1,0:T(8,128)(2,1)}, u32[]{:S(2)}) copy-start(bf16[1,128,256]{2,1,0:T(8,128)(2,1)} %param.16) | copy-start | bytes 196612
  5.6 13.5 %copy-start.27 = (f32[1,256]{1,0:T(1,128)S(1)}, f32[1,256]{1,0:T(1,128)}, u32[]{:S(2)}) copy-start(f32[1,256]{1,0:T(1,128)} %refs_3_.7) | copy-start | bytes 3076
  5.6 13.5 %copy-start.36 = (s32[1,2,2]{2,1,0:T(2,128)S(1)}, s32[1,2,2]{2,1,0:T(2,128)}, u32[]{:S(2)}) copy-start(s32[1,2,2]{2,1,0:T(2,128)} %param.24) | copy-start | bytes 52
  7.2 11.9 %copy-start.20 = (bf16[128,256]{1,0:T(8,128)(2,1)}, bf16[128,256]{1,0:T(8,128)(2,1)S(1)}, u32[]{:S(2)}) copy-start(bf16[128,256]{1,0:T(8,128)(2,1)S(1)} %get-tuple-element.59.refs_0_) | copy-start | bytes 196612
  7.2 4.1 %collective-permute-start = (bf16[8,128,256]{2,1,0:T(8,128)(2,1)S(1)}, bf16[8,128,256]{2,1,0:T(8,128)(2,1)S(1)}, u32[]{:S(2)}, u32[]{:S(2)}) collective-permute-start(bf16[8,128,256]{2,1,0:T(8,128)(2,1)S(1)} %get-tuple-element.45), channel_id=1, source_target_pairs={{0,1},{1,0},{2,3},{3,2},{4,5},{5,4},{6,7},{7,6},{8,9},{9,8},{10,11... | collective-permute-start | bytes 1572872 | tf_op jit(solution)/shard_map/ppermute | solution.py:260
  12.3 24.8 %all-to-all-start = ((bf16[8,128,256]{2,1,0:T(8,128)(2,1)}), bf16[8,128,256]{2,1,0:T(8,128)(2,1)S(1)}, u32[]{:S(2)}, u32[]{:S(2)}) async-start(bf16[8,128,256]{2,1,0:T(8,128)(2,1)} %backward_core_sum.2.refs_8_), calls=%async_computation | async-start | bytes 1048576 | tf_op jit(solution)/shard_map/all_to_all | solution.py:38
  20.4 16.6 %copy-start.22 = (bf16[128,256]{1,0:T(8,128)(2,1)}, bf16[128,256]{1,0:T(8,128)(2,1)S(1)}, u32[]{:S(2)}) copy-start(bf16[128,256]{1,0:T(8,128)(2,1)S(1)} %get-tuple-element.46.refs_0_) | copy-start | bytes 196612
  20.4 4.2 %collective-permute-start.1 = (bf16[8,144,256]{2,1,0:T(8,128)(2,1)S(1)}, bf16[8,144,256]{2,1,0:T(8,128)(2,1)S(1)}, u32[]{:S(2)}, u32[]{:S(2)}) collective-permute-start(bf16[8,144,256]{2,1,0:T(8,128)(2,1)S(1)} %get-tuple-element.48), channel_id=1, source_target_pairs={{0,1},{1,0},{2,3},{3,2},{4,5},{5,4},{6,7},{7,6},{8,9},{9,8},{10,11... | collective-permute-start | bytes 1769480 | tf_op jit(solution)/shard_map/ppermute | solution.py:260
  37.0 23.6 %all-to-all-start.1 = ((bf16[8,144,256]{2,1,0:T(8,128)(2,1)}), bf16[8,144,256]{2,1,0:T(8,128)(2,1)}, u32[]{:S(2)}, u32[]{:S(2)}) async-start(bf16[8,144,256]{2,1,0:T(8,128)(2,1)} %forward_core_sum.2.refs_1_), calls=%async_computation.1 | async-start | bytes 1179648 | tf_op jit(solution)/shard_map/all_to_all | solution.py:38
  41.3 12.7 %collective-permute-start.2 = (bf16[128,256]{1,0:T(8,128)(2,1)S(1)}, bf16[128,256]{1,0:T(8,128)(2,1)S(1)}, u32[]{:S(2)}, u32[]{:S(2)}) collective-permute-start(bf16[128,256]{1,0:T(8,128)(2,1)S(1)} %backward_ring_sum.2.refs_1_), channel_id=1, source_target_pairs={{0,2},{1,3},{2,0},{3,1},{4,6},{5,7},{6,4},{7,5},{8,10},{9,11},{10,... | collective-permute-start | bytes 196616 | tf_op jit(solution)/shard_map/ppermute | solution.py:260
  56.4 27.5 %collective-permute-start.4 = (bf16[256,2048]{1,0:T(8,128)(2,1)}, bf16[256,2048]{1,0:T(8,128)(2,1)S(1)}, u32[]{:S(2)}, u32[]{:S(2)}) collective-permute-start(bf16[256,2048]{1,0:T(8,128)(2,1)} %get-tuple-element.53), channel_id=1, source_target_pairs={{0,1},{1,0},{2,3},{3,2},{4,5},{5,4},{6,7},{7,6},{8,9},{9,8},{10,11... | collective-permute-start | bytes 3145736 | tf_op jit(solution)/shard_map/ppermute | solution.py:260
  60.6 24.3 %all-to-all-start.2 = ((bf16[8,128,256]{2,1,0:T(8,128)(2,1)}), bf16[8,128,256]{2,1,0:T(8,128)(2,1)}, u32[]{:S(2)}, u32[]{:S(2)}) async-start(bf16[8,128,256]{2,1,0:T(8,128)(2,1)} %copy-done.10), calls=%async_computation.2 | async-start | bytes 1048576 | tf_op jit(solution)/shard_map/all_to_all | solution.py:38
  69.0 10.8 %collective-permute-start.3 = (bf16[144,256]{1,0:T(8,128)(2,1)S(1)}, bf16[144,256]{1,0:T(8,128)(2,1)S(1)}, u32[]{:S(2)}, u32[]{:S(2)}) collective-permute-start(bf16[144,256]{1,0:T(8,128)(2,1)S(1)} %forward_ring_sum.2.refs_1_), channel_id=1, source_target_pairs={{0,2},{1,3},{2,0},{3,1},{4,6},{5,7},{6,4},{7,5},{8,10},{9,11},{10,... | collective-permute-start | bytes 221192 | tf_op jit(solution)/shard_map/ppermute | solution.py:260
  85.0 6.2 %copy-start.9 = (bf16[1,2,128,256]{3,2,1,0:T(8,128)(2,1)S(1)}, bf16[1,2,128,256]{3,2,1,0:T(8,128)(2,1)}, u32[]{:S(2)}) copy-start(bf16[1,2,128,256]{3,2,1,0:T(8,128)(2,1)} %param.20) | copy-start | bytes 393220
  85.0 6.2 %copy-start.28 = (f32[1,256]{1,0:T(1,128)S(1)}, f32[1,256]{1,0:T(1,128)}, u32[]{:S(2)}) copy-start(f32[1,256]{1,0:T(1,128)} %refs_3_.7) | copy-start | bytes 3076
  87.4 3.8 %collective-permute-start.5 = (f32[128,256]{1,0:T(8,128)S(1)}, f32[128,256]{1,0:T(8,128)S(1)}, u32[]{:S(2)}, u32[]{:S(2)}) collective-permute-start(f32[128,256]{1,0:T(8,128)S(1)} %get-tuple-element.55), channel_id=1, source_target_pairs={{0,1},{1,0},{2,3},{3,2},{4,5},{5,4},{6,7},{7,6},{8,9},{9,8},{10,11... | collective-permute-start | bytes 393224 | tf_op jit(solution)/shard_map/ppermute | solution.py:260
  92.8 26.6 %all-to-all-start.3 = ((f32[32,8,128]{2,1,0:T(8,128)}), f32[32,8,128]{2,1,0:T(8,128)}, u32[]{:S(2)}, u32[]{:S(2)}) async-start(f32[32,8,128]{2,1,0:T(8,128)} %copy-done.14), calls=%async_computation.3 | async-start | bytes 262144 | tf_op jit(solution)/shard_map/all_to_all | solution.py:38
  106.2 47.4 %collective-permute-start.6 = (bf16[2048,256]{1,0:T(8,128)(2,1)}, bf16[2048,256]{1,0:T(8,128)(2,1)}, u32[]{:S(2)}, u32[]{:S(2)}) collective-permute-start(bf16[2048,256]{1,0:T(8,128)(2,1)} %copy-done.40), channel_id=1, source_target_pairs={{0,1},{1,0},{2,3},{3,2},{4,5},{5,4},{6,7},{7,6},{8,9},{9,8},{10,11... | collective-permute-start | bytes 3145736 | tf_op jit(solution)/shard_map/ppermute | solution.py:260
  119.4 27.4 %all-to-all-start.4 = ((bf16[8,128,256]{2,1,0:T(8,128)(2,1)}), bf16[8,128,256]{2,1,0:T(8,128)(2,1)}, u32[]{:S(2)}, u32[]{:S(2)}) async-start(bf16[8,128,256]{2,1,0:T(8,128)(2,1)} %get-tuple-element.57.refs_4_.refs_5_), calls=%async_computation.4 | async-start | bytes 1048576 | tf_op jit(solution)/shard_map/all_to_all | solution.py:38
  127.6 2.5 copy-start.38
  127.6 7.6 %collective-permute-start.7 = (bf16[128,256]{1,0:T(8,128)(2,1)S(1)}, bf16[128,256]{1,0:T(8,128)(2,1)S(1)}, u32[]{:S(2)}, u32[]{:S(2)}) collective-permute-start(bf16[128,256]{1,0:T(8,128)(2,1)S(1)} %get-tuple-element.61), channel_id=1, source_target_pairs={{32,0},{64,32},{96,64},{128,96},{160,128},{192,160},{224,192},{256... | collective-permute-start | bytes 196616 | tf_op jit(solution)/shard_map/ppermute | solution.py:48
  141.5 4.4 %collective-permute-start.8 = (bf16[8,128,256]{2,1,0:T(8,128)(2,1)S(1)}, bf16[8,128,256]{2,1,0:T(8,128)(2,1)S(1)}, u32[]{:S(2)}, u32[]{:S(2)}) collective-permute-start(bf16[8,128,256]{2,1,0:T(8,128)(2,1)S(1)} %get-tuple-element.63), channel_id=1, source_target_pairs={{0,1},{1,0},{2,3},{3,2},{4,5},{5,4},{6,7},{7,6},{8,9},{9,8},{10,11... | collective-permute-start | bytes 1572872 | tf_op jit(solution)/shard_map/ppermute | solution.py:260
  146.8 27.2 %all-to-all-start.5 = ((bf16[8,128,256]{2,1,0:T(8,128)(2,1)}), bf16[8,128,256]{2,1,0:T(8,128)(2,1)}, u32[]{:S(2)}, u32[]{:S(2)}) async-start(bf16[8,128,256]{2,1,0:T(8,128)(2,1)} %backward_core_sum.3.refs_4_), calls=%async_computation.5 | async-start | bytes 1048576 | tf_op jit(solution)/shard_map/all_to_all | solution.py:38
  153.6 1.6 copy-start.4
  155.2 5.9 %copy-start.23 = (bf16[128,256]{1,0:T(8,128)(2,1)S(1)}, bf16[128,256]{1,0:T(8,128)(2,1)}, u32[]{:S(2)}) copy-start(bf16[128,256]{1,0:T(8,128)(2,1)} %copy-done.22) | copy-start | bytes 196612
  155.2 11.4 %copy-start.26 = (bf16[1,128,256]{2,1,0:T(8,128)(2,1)S(1)}, bf16[1,128,256]{2,1,0:T(8,128)(2,1)}, u32[]{:S(2)}) copy-start(bf16[1,128,256]{2,1,0:T(8,128)(2,1)} %refs_4_.3) | copy-start | bytes 196612
  155.2 11.4 %copy-start.30 = (f32[1,256]{1,0:T(1,128)S(1)}, f32[1,256]{1,0:T(1,128)}, u32[]{:S(2)}) copy-start(f32[1,256]{1,0:T(1,128)} %refs_3_.7) | copy-start | bytes 3076
  155.2 11.4 %copy-start.37 = (s32[1,2,2]{2,1,0:T(2,128)S(1)}, s32[1,2,2]{2,1,0:T(2,128)}, u32[]{:S(2)}) copy-start(s32[1,2,2]{2,1,0:T(2,128)} %param.24) | copy-start | bytes 52
  157.6 3.5 %collective-permute-start.9 = (f32[128,256]{1,0:T(8,128)S(1)}, f32[128,256]{1,0:T(8,128)S(1)}, u32[]{:S(2)}, u32[]{:S(2)}) collective-permute-start(f32[128,256]{1,0:T(8,128)S(1)} %get-tuple-element.66), channel_id=1, source_target_pairs={{0,1},{1,0},{2,3},{3,2},{4,5},{5,4},{6,7},{7,6},{8,9},{9,8},{10,11... | collective-permute-start | bytes 393224 | tf_op jit(solution)/shard_map/ppermute | solution.py:260
  161.1 5.4 %collective-permute-start.10 = (bf16[128,256]{1,0:T(8,128)(2,1)S(1)}, bf16[128,256]{1,0:T(8,128)(2,1)S(1)}, u32[]{:S(2)}, u32[]{:S(2)}) collective-permute-start(bf16[128,256]{1,0:T(8,128)(2,1)S(1)} %forward_end.2), channel_id=1, source_target_pairs={{0,32},{32,64},{64,96},{96,128},{128,160},{160,192},{192,224},{224... | collective-permute-start | bytes 196616 | tf_op jit(solution)/shard_map/ppermute | solution.py:48
  168.4 4.6 %collective-permute-start.11 = (bf16[8,144,256]{2,1,0:T(8,128)(2,1)S(1)}, bf16[8,144,256]{2,1,0:T(8,128)(2,1)S(1)}, u32[]{:S(2)}, u32[]{:S(2)}) collective-permute-start(bf16[8,144,256]{2,1,0:T(8,128)(2,1)S(1)} %get-tuple-element.69), channel_id=1, source_target_pairs={{0,1},{1,0},{2,3},{3,2},{4,5},{5,4},{6,7},{7,6},{8,9},{9,8},{10,11... | collective-permute-start | bytes 1769480 | tf_op jit(solution)/shard_map/ppermute | solution.py:260
  174.0 26.4 %all-to-all-start.6 = ((bf16[8,144,256]{2,1,0:T(8,128)(2,1)}), bf16[8,144,256]{2,1,0:T(8,128)(2,1)}, u32[]{:S(2)}, u32[]{:S(2)}) async-start(bf16[8,144,256]{2,1,0:T(8,128)(2,1)} %forward_core_sum.3.refs_1_), calls=%async_computation.6 | async-start | bytes 1179648 | tf_op jit(solution)/shard_map/all_to_all | solution.py:38
  182.0 10.0 %collective-permute-start.12 = (bf16[128,256]{1,0:T(8,128)(2,1)S(1)}, bf16[128,256]{1,0:T(8,128)(2,1)S(1)}, u32[]{:S(2)}, u32[]{:S(2)}) collective-permute-start(bf16[128,256]{1,0:T(8,128)(2,1)S(1)} %backward_ring_sum.3.refs_1_), channel_id=1, source_target_pairs={{0,2},{1,3},{2,0},{3,1},{4,6},{5,7},{6,4},{7,5},{8,10},{9,11},{10,... | collective-permute-start | bytes 196616 | tf_op jit(solution)/shard_map/ppermute | solution.py:260
  200.4 22.1 %all-to-all-start.7 = ((bf16[8,128,256]{2,1,0:T(8,128)(2,1)}), bf16[8,128,256]{2,1,0:T(8,128)(2,1)}, u32[]{:S(2)}, u32[]{:S(2)}) async-start(bf16[8,128,256]{2,1,0:T(8,128)(2,1)} %backward_share.3.refs_1_), calls=%async_computation.7 | async-start | bytes 1048576 | tf_op jit(solution)/shard_map/all_to_all | solution.py:38
  205.7 10.3 %collective-permute-start.13 = (bf16[144,256]{1,0:T(8,128)(2,1)S(1)}, bf16[144,256]{1,0:T(8,128)(2,1)S(1)}, u32[]{:S(2)}, u32[]{:S(2)}) collective-permute-start(bf16[144,256]{1,0:T(8,128)(2,1)S(1)} %forward_ring_sum.3.refs_1_), channel_id=1, source_target_pairs={{0,2},{1,3},{2,0},{3,1},{4,6},{5,7},{6,4},{7,5},{8,10},{9,11},{10,... | collective-permute-start | bytes 221192 | tf_op jit(solution)/shard_map/ppermute | solution.py:260
  222.5 22.1 %all-to-all-start.8 = ((bf16[8,128,256]{2,1,0:T(8,128)(2,1)}), bf16[8,128,256]{2,1,0:T(8,128)(2,1)}, u32[]{:S(2)}, u32[]{:S(2)}) async-start(bf16[8,128,256]{2,1,0:T(8,128)(2,1)} %forward_share.3.refs_4_), calls=%async_computation.8 | async-start | bytes 1048576 | tf_op jit(solution)/shard_map/all_to_all | solution.py:38
  226.7 5.8 %copy-start.31 = (f32[1,256]{1,0:T(1,128)S(1)}, f32[1,256]{1,0:T(1,128)}, u32[]{:S(2)}) copy-start(f32[1,256]{1,0:T(1,128)} %refs_3_.7) | copy-start | bytes 3076
  229.1 3.4 %collective-permute-start.14 = (f32[128,256]{1,0:T(8,128)S(1)}, f32[128,256]{1,0:T(8,128)S(1)}, u32[]{:S(2)}, u32[]{:S(2)}) collective-permute-start(f32[128,256]{1,0:T(8,128)S(1)} %get-tuple-element.74), channel_id=1, source_target_pairs={{0,1},{1,0},{2,3},{3,2},{4,5},{5,4},{6,7},{7,6},{8,9},{9,8},{10,11... | collective-permute-start | bytes 393224 | tf_op jit(solution)/shard_map/ppermute | solution.py:260
  233.3 22.6 %copy-start.25 = (bf16[128,256]{1,0:T(8,128)(2,1)S(1)}, bf16[128,256]{1,0:T(8,128)(2,1)}, u32[]{:S(2)}) copy-start(bf16[128,256]{1,0:T(8,128)(2,1)} %copy-done.24) | copy-start | bytes 196612
  244.6 17.4 %all-to-all-start.9 = ((f32[32,8,128]{2,1,0:T(8,128)}), f32[32,8,128]{2,1,0:T(8,128)S(1)}, u32[]{:S(2)}, u32[]{:S(2)}) async-start(f32[32,8,128]{2,1,0:T(8,128)} %get-tuple-element.76.refs_4_), calls=%async_computation.9 | async-start | bytes 262144 | tf_op jit(solution)/shard_map/all_to_all | solution.py:38
  248.6 1.6 copy-start.5
  250.2 11.8 %copy-start.19 = (bf16[128,256]{1,0:T(8,128)(2,1)S(1)}, bf16[128,256]{1,0:T(8,128)(2,1)}, u32[]{:S(2)}) copy-start(bf16[128,256]{1,0:T(8,128)(2,1)} %copy-done.18) | copy-start | bytes 196612
  250.2 11.8 %copy-start.33 = (f32[8,128]{1,0:T(8,128)S(1)}, f32[8,128]{1,0:T(8,128)}, u32[]{:S(2)}) copy-start(f32[8,128]{1,0:T(8,128)} %copy-done.32) | copy-start | bytes 12292
  250.2 11.8 %copy-start.39 = (f32[1,256]{1,0:T(1,128)S(1)}, f32[1,256]{1,0:T(1,128)}, u32[]{:S(2)}) copy-start(f32[1,256]{1,0:T(1,128)} %copy-done.38) | copy-start | bytes 3076
  252.6 3.2 %collective-permute-start.15 = (f32[128,256]{1,0:T(8,128)S(1)}, f32[128,256]{1,0:T(8,128)S(1)}, u32[]{:S(2)}, u32[]{:S(2)}) collective-permute-start(f32[128,256]{1,0:T(8,128)S(1)} %get-tuple-element.78), channel_id=1, source_target_pairs={{0,1},{1,0},{2,3},{3,2},{4,5},{5,4},{6,7},{7,6},{8,9},{9,8},{10,11... | collective-permute-start | bytes 393224 | tf_op jit(solution)/shard_map/ppermute | solution.py:260
  (19 other events, 16.5 us)

commit v8 on v7

v8 whole, which is shorter than its diff:
```python
import functools

import jax
import jax.numpy as jnp
from jax import lax
from jax.experimental import pallas as pl
from jax.experimental.pallas import tpu as pltpu
from jax.sharding import PartitionSpec as P

D = 8192
BLOCK = 128
ROWS = 128
WIDTH = 256
SEQ = 64
RING = 8
HALF = RING * WIDTH
EPSILON = 1e-05
F32 = jnp.float32
BF16 = jnp.bfloat16
VMEM_LIMIT = 20 * 1024 * 1024
DOT_ROWS = 8
SEGMENT_AT, CORE_AT, FORWARD_AT, BACKWARD_AT = 34, 35, 36, 40


def core_pairs():
    return [(index, index ^ 1) for index in range(4 * RING)]


def z_pairs():
    return [(index, index ^ 2) for index in range(4 * RING)]


def rings():
    return [[4 * y + rest for y in range(RING)] for rest in range(4)]


def swapped(value, groups=None):
    return lax.all_to_all(value, "shard", 0, 0, axis_index_groups=groups, tiled=True)


def gate(value, *after):
    return lax.optimization_barrier((value, *after))[0]


def shifted(value, axis, steps):
    count = lax.axis_size(axis)
    leading, last = (max(0, -steps), min(count, count - steps))
    return lax.ppermute(value, axis, [(source, source + steps) for source in range(leading, last)])


def call(kernel, name, outs, *, prefetch=(), blocks=None, operands=(), after=()):
    blocks = blocks or {}
    first, last = len(prefetch) + len(operands), len(prefetch) + len(operands) + len(after)

    def body(*refs):
        kernel(*refs[:first], *refs[last:])

    def spec(position, operand):
        if position in blocks:
            shape, index_map = blocks[position]
            return pl.BlockSpec(shape, index_map)
        rank = len(operand.shape)
        return pl.BlockSpec(operand.shape, lambda *_: (0,) * rank)

    in_specs = [spec(position, operand) for position, operand in enumerate(operands)]
    return pl.pallas_call(
        body,
        out_shape=outs,
        grid_spec=pltpu.PrefetchScalarGridSpec(
            num_scalar_prefetch=len(prefetch),
            grid=(1,),
            in_specs=in_specs + [pl.BlockSpec(memory_space=pl.ANY)] * len(after),
            out_specs=[pl.BlockSpec(out.shape, lambda *_, rank=len(out.shape): (0,) * rank) for out in outs],
        ),
        compiler_params=pltpu.CompilerParams(vmem_limit_bytes=VMEM_LIMIT),
        cost_estimate=pl.CostEstimate(flops=0, bytes_accessed=0, transcendentals=0),
        name=name,
    )(*prefetch, *operands, *after)


def shape_of(*dims, dtype=BF16):
    return jax.ShapeDtypeStruct(dims, dtype)


def across(column):
    return jnp.broadcast_to(column, (ROWS, ROWS)).T[0:1]


def down(row):
    square = jnp.broadcast_to(row, (ROWS, ROWS)).T
    return jnp.concatenate([square, square], axis=1)


def power_row(low, high, sign):
    lane = lax.broadcasted_iota(jnp.int32, (1, WIDTH), 1)
    exponent = sign * jnp.where(lane < BLOCK, low, high)
    magnitude = jnp.abs(exponent)
    grown = jnp.ones((1, WIDTH), F32)
    shrunk = jnp.ones((1, WIDTH), F32)
    for bit in range(4):
        bit_set = (magnitude >> bit) & 1 == 1
        grown = jnp.where(bit_set, grown * 2.0 ** (2**bit), grown)
        shrunk = jnp.where(bit_set, shrunk * 0.5 ** (2**bit), shrunk)
    return jnp.where(exponent < 0, shrunk, grown)


def decoded(message, first_ref, second_ref, scalars, at):
    low, high = scalars[at], scalars[at + 1]
    scale = power_row(low, high, 1)
    inverse = power_row(low, high, -1)
    base = jnp.concatenate([first_ref[0], second_ref[0]], axis=0).astype(F32)
    delta = jnp.clip((message.astype(F32) - base) * inverse, -127.0, 127.0).astype(BF16)
    return (base + delta.astype(F32) * scale).astype(BF16)


def chosen(scalars, edge, refs):
    if len(refs) == 1:
        return refs[0][...]
    return jnp.where(scalars[SEGMENT_AT] == edge, refs[1][0].astype(F32), refs[0][...].astype(F32))


def forward_start(tick, messages, scalars, *refs):
    given, (first, second, gain, weight, x_out, keep, send, squares) = refs[:messages], refs[messages:]
    x = decoded(chosen(scalars, 0, given), first, second, scalars, FORWARD_AT + 2 * tick)
    x_out[...] = x
    x = x.astype(F32)
    scaled = (x * gain[...]).astype(BF16)
    squares[...] = jnp.broadcast_to(across(jnp.sum(x * x, axis=1, keepdims=True)), squares.shape)
    core = scalars[CORE_AT]
    for out, half in ((send, 1 - core), (keep, core)):
        for j in range(RING):
            at = pl.multiple_of((half * RING + j) * WIDTH, WIDTH)
            part = jnp.dot(scaled, weight[:, pl.ds(at, WIDTH)], preferred_element_type=F32)
            out[j] = part.astype(BF16)


def backward_start(tick, messages, last, scalars, *refs):
    given, (first, second, weight, g_out, keep, send) = refs[:messages], refs[messages:]
    g = decoded(chosen(scalars, last, given), first, second, scalars, BACKWARD_AT + 2 * tick)
    g_out[...] = g
    core = scalars[CORE_AT]
    for out, half in ((send, 1 - core), (keep, core)):
        for j in range(RING):
            at = pl.multiple_of((half * RING + j) * WIDTH, WIDTH)
            part = lax.dot_general(
                g, weight[pl.ds(at, WIDTH), :], (((1,), (1,)), ((), ())), preferred_element_type=F32
            )
            out[j] = part.astype(BF16)


def core_sum(mine, other, out):
    for j in range(RING):
        out[j] = (mine[j].astype(F32) + other[j].astype(F32)).astype(BF16)


def ring_sum(pieces, out):
    total = pieces[0].astype(F32)
    for j in range(1, RING):
        total = total + pieces[j].astype(F32)
    out[...] = total.astype(BF16)


def share(own, other, *refs):
    value = (own[...].astype(F32) + other[...].astype(F32)).astype(BF16)
    out, *half = refs[len(refs) // 2 :]
    out[...] = jnp.broadcast_to(value[None], out.shape)
    if half:
        half[0][...] = refs[0][...]


def forward_product(blocks, own_weight, other_weight, mine, others):
    for weight, out in ((other_weight, others), (own_weight, mine)):
        total = jnp.zeros((ROWS, WIDTH), F32)
        for j in range(RING):
            rows = weight[j * WIDTH : (j + 1) * WIDTH, :]
            total = total + jnp.dot(blocks[j], rows, preferred_element_type=F32)
        out[...] = total


def backward_product(blocks, own_weight, other_weight, mine, others):
    for weight, out in ((other_weight, others), (own_weight, mine)):
        total = jnp.zeros((ROWS, WIDTH), F32)
        for j in range(RING):
            columns = weight[:, j * WIDTH : (j + 1) * WIDTH]
            total = total + lax.dot_general(
                blocks[j], columns, (((1,), (1,)), ((), ())), preferred_element_type=F32
            )
        out[...] = total


def row_factor(squares):
    return down(lax.rsqrt(squares / D + EPSILON))


def forward_sum(x, mine, other, squares):
    return (x[...].astype(F32) + row_factor(squares) * (mine[...] + other[...])).astype(BF16)


def forward_end(x, mine, other, totals, out):
    out[...] = forward_sum(x, mine, other, totals[3:4])


def backward_middle(tick, mine, other, saved, gain, g, squares, packed, dots):
    value = mine[...] + other[...]
    packed[:ROWS] = value
    packed[ROWS : 2 * ROWS] = g[...].astype(F32)
    packed[2 * ROWS :] = jnp.broadcast_to(gain[...], (8, WIDTH))
    terms = [saved[tick].astype(F32) * gain[...] * value]
    if tick == 0:
        for k in range(2):
            kept = saved[k].astype(F32)
            terms.append(kept * kept)
    rows = [across(jnp.sum(term, axis=1, keepdims=True)) for term in terms]
    rows += [jnp.zeros((1, ROWS), F32)] * (3 - len(rows))
    rows += [squares[:1], jnp.zeros((DOT_ROWS - 4, ROWS), F32)]
    dots[...] = jnp.broadcast_to(jnp.concatenate(rows, axis=0)[None], dots.shape)


def backward_end(tick, packed, saved, dots, *refs):
    total = dots[0]
    for j in range(1, dots.shape[0]):
        total = total + dots[j]
    if tick == 0:
        out, gain_out, totals = refs
        totals[...] = total
        squares = total[1:2]
    else:
        before, gain_before, x, mine, other, out, gain_out, segment_out = refs
        segment_out[...] = forward_sum(x, mine, other, total[3:4])
        squares = before[2:3]
    factor = row_factor(squares)
    kept = saved[tick].astype(F32)
    scaled_grad, g, gain = packed[:ROWS], packed[ROWS : 2 * ROWS], packed[2 * ROWS : 2 * ROWS + 1]
    sums = jnp.sum(scaled_grad * kept * factor, axis=0, keepdims=True)
    gain_out[...] = sums + gain_before[...] if tick else sums
    value = g + factor * gain * scaled_grad
    out[...] = (value - kept * (factor * factor * factor) * down(total[0:1]) / D).astype(BF16)


def over(value, pairs):
    return lax.ppermute(value, "shard", pairs)


def shards(
    value_weight,
    output_weight,
    norm_gain,
    arriving,
    fresh_inputs,
    returning,
    cotangents,
    saved_inputs,
    forward_base,
    backward_base,
    sample_ids,
    forward_exponents,
    backward_exponents,
):
    segment = lax.axis_index("segment")
    segments = lax.axis_size("segment")
    position = lax.axis_index("shard")
    core = position % 2
    numbers = (sample_ids, jnp.stack([segment, core]), forward_exponents, backward_exponents)
    scalars = jnp.concatenate([number.astype(jnp.int32).reshape(-1) for number in numbers])
    value_local, output_local = value_weight[0], output_weight[0]
    saved = saved_inputs[0]
    low = shape_of(ROWS, WIDTH)
    wide = shape_of(ROWS, WIDTH, dtype=F32)
    eight = shape_of(RING, ROWS, WIDTH)
    row = shape_of(1, WIDTH, dtype=F32)
    small = shape_of(DOT_ROWS, ROWS, dtype=F32)
    own_half = {1: ((HALF, WIDTH), lambda i, scalars: (scalars[CORE_AT], 0))}
    own_columns = {1: ((WIDTH, HALF), lambda i, scalars: (0, scalars[CORE_AT]))}

    def base_blocks(first, micro):
        return {
            first + sample: (
                (1, SEQ, WIDTH),
                lambda i, scalars, sample=sample: (scalars[2 * micro(scalars[SEGMENT_AT]) + sample], 0, 0),
            )
            for sample in range(2)
        }

    def run(kernel, name, outs, operands, blocks=None, after=()):
        return call(kernel, name, outs, prefetch=(scalars,), operands=operands, blocks=blocks, after=after)

    def plain(kernel):
        return lambda _, *refs: kernel(*refs)

    def forward_begin(tick, messages, *after):
        count = len(messages)
        x, keep, send, squares = run(
            functools.partial(forward_start, tick, count),
            "forward_start",
            [low, eight, eight, small],
            (*messages, forward_base[0], forward_base[0], norm_gain, value_local),
            base_blocks(count, lambda segment: tick - segment + segments - 1),
            after,
        )
        operands = (keep, over(send, core_pairs()))
        return x, squares, *call(core_sum, "forward_core_sum", [eight], operands=operands)

    def backward_begin(tick, messages, *after):
        count = len(messages)
        g, keep, send = run(
            functools.partial(backward_start, tick, count, segments - 1),
            "backward_start",
            [low, eight, eight],
            (*messages, backward_base[0], backward_base[0], output_local),
            base_blocks(count, lambda segment: tick + segment),
            after,
        )
        operands = (keep, over(send, core_pairs()))
        return g, *call(core_sum, "backward_core_sum", [eight], operands=operands)

    def turn(name, pieces, half, *after):
        (own,) = call(ring_sum, name + "_ring_sum", [low], operands=(pieces,), after=after)
        operands, outs, blocks = (own, over(own, z_pairs())), [eight], {}
        if half:
            weight, shape, index_map = half
            operands, outs, blocks = (*operands, weight), [eight, shape_of(*shape)], {2: (shape, index_map)}
        return run(plain(share), name + "_share", outs, operands, blocks)

    def forward_product_of(gathered, *after):
        operands = (gathered, output_local, output_other)
        mine, others = run(plain(forward_product), "forward_product", [wide, wide], operands, own_half, after)
        return mine, over(others, core_pairs())

    def backward_dots(tick, gathered, g, squares, *after):
        operands = (gathered, value_local, value_other)
        mine, others = run(plain(backward_product), "backward_product", [wide, wide], operands, own_columns, after)
        return call(
            functools.partial(backward_middle, tick),
            "backward_middle",
            [shape_of(2 * ROWS + 8, WIDTH, dtype=F32), shape_of(4 * RING, DOT_ROWS, ROWS, dtype=F32)],
            operands=(mine, over(others, core_pairs()), saved, norm_gain, g, squares),
        )

    def backward_finish(tick, packed, dots, left, outs, *after):
        operands = (packed, saved, dots, *left)
        return call(
            functools.partial(backward_end, tick), "backward_end", [low, row, *outs], operands=operands, after=after
        )

    g, back_pieces = backward_begin(0, [returning[0]])
    gated = gate(back_pieces)
    back_landed = swapped(gated, rings())

    x, squares, pieces = forward_begin(0, [arriving[0]], gated)
    gated = gate(pieces, back_landed)
    landed = swapped(gated, rings())

    half = (value_local, (WIDTH, HALF), lambda i, scalars: (0, 1 - scalars[CORE_AT]))
    back_copies, half = turn("backward", back_landed, half, gated)
    value_other = over(half, core_pairs())
    gated = gate(back_copies, landed)
    back_gathered = swapped(gated, rings())

    half = (output_local, (HALF, WIDTH), lambda i, scalars: (1 - scalars[CORE_AT], 0))
    copies, half = turn("forward", landed, half, gated)
    output_other = over(half, core_pairs())
    packed, dots = backward_dots(0, back_gathered, g, squares, copies)
    all_dots = swapped(dots)

    gated = gate(copies, all_dots)
    gathered = swapped(gated, rings())

    input_grad, gain_total, totals = backward_finish(0, packed, all_dots, (), [small], gated)
    g, back_pieces = backward_begin(1, [shifted(input_grad, "segment", -1), cotangents])
    gated = gate(back_pieces, gathered)
    back_landed = swapped(gated, rings())

    operands = (x, *forward_product_of(gathered, gated), totals)
    (segment_out,) = call(forward_end, "forward_end", [low], operands=operands)
    x, squares, pieces = forward_begin(1, [shifted(segment_out, "segment", 1), fresh_inputs])
    gated = gate(pieces, back_landed)
    landed = swapped(gated, rings())

    (back_copies,) = turn("backward", back_landed, None, gated)
    gated = gate(back_copies, landed)
    back_gathered = swapped(gated, rings())

    (copies,) = turn("forward", landed, None, gated)
    gated = gate(copies, back_gathered)
    gathered = swapped(gated, rings())

    packed, dots = backward_dots(1, back_gathered, g, squares, gated)
    gated = gate(dots, gathered)
    all_dots = swapped(gated)

    left = (totals, gain_total, x, *forward_product_of(gathered, gated))
    input_grad, gain_total, segment_out = backward_finish(1, packed, all_dots, left, [low])
    return (segment_out[None], input_grad[None], gain_total)


def solution(mesh):
    return jax.shard_map(
        shards,
        mesh=mesh,
        in_specs=(
            P("segment", "shard", None),
            P("segment", None, "shard"),
            P("segment", "shard"),
            P("segment", None, "shard"),
            P(None, None, "shard"),
            P("segment", None, "shard"),
            P(None, None, "shard"),
            P("segment", None, None, "shard"),
            P("segment", None, None, "shard"),
            P("segment", None, None, "shard"),
            P(),
            P("segment", None, "shard"),
            P("segment", None, "shard"),
        ),
        out_specs=(P("segment", None, "shard"), P("segment", None, "shard"), P("segment", "shard")),
        check_vma=False,
    )
```

time: 265 us -> 263 us (level)
  blocking collectives: 0 us -> 25.7 us
  starting transfers between devices: 118 us -> 104 us
  waiting for transfers between devices: 89.2 us -> 77.2 us
    all_to_all x0 -> x1, blocking collectives: none -> 25.7 us  [swapped(): lax.all_to_all(value, 'shard', 0, 0, axis_index_groups=groups, tiled=True)]
    all_to_all x10 -> x9, starting transfers between devices: 60.8 us -> 47.7 us  [swapped(): lax.all_to_all(value, 'shard', 0, 0, axis_index_groups=groups, tiled=True)]
    all_to_all x10 -> x9, waiting for transfers between devices: 52.9 us -> 40.4 us  [swapped(): lax.all_to_all(value, 'shard', 0, 0, axis_index_groups=groups, tiled=True)]
    unnamed x83 -> x65, local copies, waits for them, and re-layouts: 22.1 us -> 20.5 us
    pallas_call x26 -> x25, Pallas kernels: 31.9 us -> 30.6 us  [call(): pl.pallas_call(body, out_shape=outs, grid_spec=pltpu.PrefetchScalarGridSp...]
  transfers between devices with their start and end apart: 26 -> 25, of which waited for: 22 -> 20; matrix products, arithmetic and copies ran while one was open for 0% -> 0% of each run, Pallas kernels for 10% -> 9%
where the time goes in v8:
time: 263 us; the launch traced here: 261 us
  starting transfers between devices  104 us (40%)
  waiting for transfers between devices  77.2 us (29%)
  Pallas kernels  30.6 us (12%)
  blocking collectives  25.7 us (10%)
  local copies, waits for them, and re-layouts  22.2 us (8%)
    ppermute x14, starting transfers between devices, over(): return lax.ppermute(value, 'shard', pairs)  52.2 us
    all_to_all x9, starting transfers between devices, swapped(): lax.all_to_all(value, 'shard', 0, 0, axis_index_groups=groups, tiled=True)  47.7 us
    all_to_all x9, waiting for transfers between devices, swapped(): lax.all_to_all(value, 'shard', 0, 0, axis_index_groups=groups, tiled=True)  40.4 us
    pallas_call x25, Pallas kernels, call(): pl.pallas_call(body, out_shape=outs, grid_spec=pltpu.PrefetchScalarGridSp...  30.6 us
    ppermute x14, waiting for transfers between devices, over(): return lax.ppermute(value, 'shard', pairs)  28.3 us
    all_to_all x1, blocking collectives, swapped(): lax.all_to_all(value, 'shard', 0, 0, axis_index_groups=groups, tiled=True)  25.7 us
    unnamed x65, local copies, waits for them, and re-layouts  20.5 us
    ppermute x2, waiting for transfers between devices, shifted(): lax.ppermute(value, axis, [(source, source + steps) for source in range(l...  8.54 us
  transfers between devices with their start and end apart: 25, of which 20 were waited for; matrix products, arithmetic and copies ran while one was open for 0% of the time, Pallas kernels for 9%

profile of v8, /device:TPU:7, one launch (start us, length us, event | category | flops | bytes accessed | tf_op | source)
XLA Modules:
  0.0 261.1 jit_solution(6605764868135302188)
XLA Ops:
  3.1 1.6 copy-done.1
  7.9 2.6 collective-permute-start
  12.9 6.8 %all-to-all-start = ((bf16[8,128,256]{2,1,0:T(8,128)(2,1)}), bf16[8,128,256]{2,1,0:T(8,128)(2,1)}, u32[]{:S(2)}, u32[]{:S(2)}) async-start(bf16[8,128,256]{2,1,0:T(8,128)(2,1)} %backward_core_sum.2.refs_6_), calls=%async_computation | async-start | bytes 1048576 | tf_op jit(solution)/shard_map/all_to_all | solution.py:38
  20.8 2.6 collective-permute-start.1
  25.9 11.9 %all-to-all-done.refs_0_ = bf16[8,128,256]{2,1,0:T(8,128)(2,1)} async-done(((bf16[8,128,256]{2,1,0:T(8,128)(2,1)}), bf16[8,128,256]{2,1,0:T(8,128)(2,1)}, u32[]{:S(2)}, u32[]{:S(2)}) %all-to-all-start) | async-done | bytes 524320 | tf_op jit(solution)/shard_map/all_to_all | solution.py:38
  37.8 4.1 %all-to-all-start.1 = ((bf16[8,128,256]{2,1,0:T(8,128)(2,1)}), bf16[8,128,256]{2,1,0:T(8,128)(2,1)}, u32[]{:S(2)}, u32[]{:S(2)}) async-start(bf16[8,128,256]{2,1,0:T(8,128)(2,1)} %forward_core_sum.2.refs_1_), calls=%async_computation.1 | async-start | bytes 1048576 | tf_op jit(solution)/shard_map/all_to_all | solution.py:38
  43.1 10.6 %collective-permute-start.2 = (bf16[128,256]{1,0:T(8,128)(2,1)S(1)}, bf16[128,256]{1,0:T(8,128)(2,1)S(1)}, u32[]{:S(2)}, u32[]{:S(2)}) collective-permute-start(bf16[128,256]{1,0:T(8,128)(2,1)S(1)} %backward_ring_sum.2.refs_1_), channel_id=1, source_target_pairs={{0,2},{1,3},{2,0},{3,1},{4,6},{5,7},{6,4},{7,5},{8,10},{9,11},{10,... | collective-permute-start | bytes 196616 | tf_op jit(solution)/shard_map/ppermute | solution.py:241
  53.7 2.0 collective-permute-done.2.refs_2_
  55.7 1.6 backward_share.2
  58.2 3.8 %collective-permute-start.3 = (bf16[256,2048]{1,0:T(8,128)(2,1)}, bf16[256,2048]{1,0:T(8,128)(2,1)S(1)}, u32[]{:S(2)}, u32[]{:S(2)}) collective-permute-start(bf16[256,2048]{1,0:T(8,128)(2,1)} %get-tuple-element.54), channel_id=1, source_target_pairs={{0,1},{1,0},{2,3},{3,2},{4,5},{5,4},{6,7},{7,6},{8,9},{9,8},{10,11... | collective-permute-start | bytes 3145736 | tf_op jit(solution)/shard_map/ppermute | solution.py:241
  61.9 6.7 %all-to-all-start.2 = ((bf16[8,128,256]{2,1,0:T(8,128)(2,1)}), bf16[8,128,256]{2,1,0:T(8,128)(2,1)}, u32[]{:S(2)}, u32[]{:S(2)}) async-start(bf16[8,128,256]{2,1,0:T(8,128)(2,1)} %copy-done.10), calls=%async_computation.2 | async-start | bytes 1048576 | tf_op jit(solution)/shard_map/all_to_all | solution.py:38
  70.8 8.0 %collective-permute-start.4 = (bf16[128,256]{1,0:T(8,128)(2,1)S(1)}, bf16[128,256]{1,0:T(8,128)(2,1)S(1)}, u32[]{:S(2)}, u32[]{:S(2)}) collective-permute-start(bf16[128,256]{1,0:T(8,128)(2,1)S(1)} %forward_ring_sum.2.refs_1_), channel_id=1, source_target_pairs={{0,2},{1,3},{2,0},{3,1},{4,6},{5,7},{6,4},{7,5},{8,10},{9,11},{10,... | collective-permute-start | bytes 196616 | tf_op jit(solution)/shard_map/ppermute | solution.py:241
  78.8 2.2 collective-permute-done.4.refs_2_
  81.0 1.6 copy-done.2
  85.1 1.7 all-to-all-done.2.refs_1_
  86.8 2.4 backward_product.2
  89.2 2.5 collective-permute-start.5
  93.7 25.7 %all_to_all.50.refs_2_ = f32[32,8,128]{2,1,0:T(8,128)} all-to-all(f32[32,8,128]{2,1,0:T(8,128)S(1)} %get-tuple-element.61), channel_id=1, replica_groups=mesh['segment'=16,'shard'=32] {'shard'}, dimensions={0} | all-to-all | bytes 262144 | tf_op jit(solution)/shard_map/all_to_all | solution.py:38
  119.3 4.1 %all-to-all-start.4 = ((bf16[8,128,256]{2,1,0:T(8,128)(2,1)}), bf16[8,128,256]{2,1,0:T(8,128)(2,1)}, u32[]{:S(2)}, u32[]{:S(2)}) async-start(bf16[8,128,256]{2,1,0:T(8,128)(2,1)} %get-tuple-element.62.refs_4_.refs_3_), calls=%async_computation.4 | async-start | bytes 1048576 | tf_op jit(solution)/shard_map/all_to_all | solution.py:38
  123.5 2.1 collective-permute-start.8
  127.7 2.5 collective-permute-start.6
  130.1 5.1 %collective-permute-done.6.refs_1_ = bf16[128,256]{1,0:T(8,128)(2,1)S(1)} collective-permute-done((bf16[128,256]{1,0:T(8,128)(2,1)S(1)}, bf16[128,256]{1,0:T(8,128)(2,1)S(1)}, u32[]{:S(2)}, u32[]{:S(2)}) %collective-permute-start.6) | collective-permute-done | bytes 65568 | tf_op jit(solution)/shard_map/ppermute | solution.py:48
  135.2 1.6 copy-done.3
  139.6 2.9 %collective-permute-start.7 = (bf16[8,128,256]{2,1,0:T(8,128)(2,1)S(1)}, bf16[8,128,256]{2,1,0:T(8,128)(2,1)S(1)}, u32[]{:S(2)}, u32[]{:S(2)}) collective-permute-start(bf16[8,128,256]{2,1,0:T(8,128)(2,1)S(1)} %get-tuple-element.65), channel_id=1, source_target_pairs={{0,1},{1,0},{2,3},{3,2},{4,5},{5,4},{6,7},{7,6},{8,9},{9,8},{10,11... | collective-permute-start | bytes 1572872 | tf_op jit(solution)/shard_map/ppermute | solution.py:241
  145.0 6.8 %all-to-all-start.5 = ((bf16[8,128,256]{2,1,0:T(8,128)(2,1)}), bf16[8,128,256]{2,1,0:T(8,128)(2,1)}, u32[]{:S(2)}, u32[]{:S(2)}) async-start(bf16[8,128,256]{2,1,0:T(8,128)(2,1)} %backward_core_sum.3.refs_4_), calls=%async_computation.5 | async-start | bytes 1048576 | tf_op jit(solution)/shard_map/all_to_all | solution.py:38
  151.8 1.6 copy-done.4
  153.4 2.4 forward_product.2
  155.7 2.6 collective-permute-start.9
  159.4 1.9 collective-permute-start.10
  161.3 3.5 %collective-permute-done.10.refs_1_ = bf16[128,256]{1,0:T(8,128)(2,1)S(1)} collective-permute-done((bf16[128,256]{1,0:T(8,128)(2,1)S(1)}, bf16[128,256]{1,0:T(8,128)(2,1)S(1)}, u32[]{:S(2)}, u32[]{:S(2)}) %collective-permute-start.10) | collective-permute-done | bytes 65568 | tf_op jit(solution)/shard_map/ppermute | solution.py:48
  166.5 3.0 %collective-permute-start.11 = (bf16[8,128,256]{2,1,0:T(8,128)(2,1)S(1)}, bf16[8,128,256]{2,1,0:T(8,128)(2,1)S(1)}, u32[]{:S(2)}, u32[]{:S(2)}) collective-permute-start(bf16[8,128,256]{2,1,0:T(8,128)(2,1)S(1)} %get-tuple-element.73), channel_id=1, source_target_pairs={{0,1},{1,0},{2,3},{3,2},{4,5},{5,4},{6,7},{7,6},{8,9},{9,8},{10,11... | collective-permute-start | bytes 1572872 | tf_op jit(solution)/shard_map/ppermute | solution.py:241
  171.9 6.9 %all-to-all-start.6 = ((bf16[8,128,256]{2,1,0:T(8,128)(2,1)}), bf16[8,128,256]{2,1,0:T(8,128)(2,1)}, u32[]{:S(2)}, u32[]{:S(2)}) async-start(bf16[8,128,256]{2,1,0:T(8,128)(2,1)} %forward_core_sum.3.refs_1_), calls=%async_computation.6 | async-start | bytes 1048576 | tf_op jit(solution)/shard_map/all_to_all | solution.py:38
  180.0 3.4 %collective-permute-start.12 = (bf16[128,256]{1,0:T(8,128)(2,1)S(1)}, bf16[128,256]{1,0:T(8,128)(2,1)S(1)}, u32[]{:S(2)}, u32[]{:S(2)}) collective-permute-start(bf16[128,256]{1,0:T(8,128)(2,1)S(1)} %backward_ring_sum.3.refs_1_), channel_id=1, source_target_pairs={{0,2},{1,3},{2,0},{3,1},{4,6},{5,7},{6,4},{7,5},{8,10},{9,11},{10,... | collective-permute-start | bytes 196616 | tf_op jit(solution)/shard_map/ppermute | solution.py:241
  183.4 6.9 %collective-permute-done.12.refs_2_ = bf16[128,256]{1,0:T(8,128)(2,1)S(1)} collective-permute-done((bf16[128,256]{1,0:T(8,128)(2,1)S(1)}, bf16[128,256]{1,0:T(8,128)(2,1)S(1)}, u32[]{:S(2)}, u32[]{:S(2)}) %collective-permute-start.12) | collective-permute-done | bytes 65568 | tf_op jit(solution)/shard_map/ppermute | solution.py:241
  191.7 5.2 %all-to-all-done.6.refs_0_ = bf16[8,128,256]{2,1,0:T(8,128)(2,1)} async-done(((bf16[8,128,256]{2,1,0:T(8,128)(2,1)}), bf16[8,128,256]{2,1,0:T(8,128)(2,1)}, u32[]{:S(2)}, u32[]{:S(2)}) %all-to-all-start.6) | async-done | bytes 524320 | tf_op jit(solution)/shard_map/all_to_all | solution.py:38
  196.9 4.1 %all-to-all-start.7 = ((bf16[8,128,256]{2,1,0:T(8,128)(2,1)}), bf16[8,128,256]{2,1,0:T(8,128)(2,1)}, u32[]{:S(2)}, u32[]{:S(2)}) async-start(bf16[8,128,256]{2,1,0:T(8,128)(2,1)} %backward_share.3.refs_1_), calls=%async_computation.7 | async-start | bytes 1048576 | tf_op jit(solution)/shard_map/all_to_all | solution.py:38
  202.2 3.4 %collective-permute-start.13 = (bf16[128,256]{1,0:T(8,128)(2,1)S(1)}, bf16[128,256]{1,0:T(8,128)(2,1)S(1)}, u32[]{:S(2)}, u32[]{:S(2)}) collective-permute-start(bf16[128,256]{1,0:T(8,128)(2,1)S(1)} %forward_ring_sum.3.refs_1_), channel_id=1, source_target_pairs={{0,2},{1,3},{2,0},{3,1},{4,6},{5,7},{6,4},{7,5},{8,10},{9,11},{10,... | collective-permute-start | bytes 196616 | tf_op jit(solution)/shard_map/ppermute | solution.py:241
  205.6 7.2 %collective-permute-done.13.refs_2_ = bf16[128,256]{1,0:T(8,128)(2,1)S(1)} collective-permute-done((bf16[128,256]{1,0:T(8,128)(2,1)S(1)}, bf16[128,256]{1,0:T(8,128)(2,1)S(1)}, u32[]{:S(2)}, u32[]{:S(2)}) %collective-permute-start.13) | collective-permute-done | bytes 65568 | tf_op jit(solution)/shard_map/ppermute | solution.py:241
  214.3 4.8 %all-to-all-done.7.refs_1_ = bf16[8,128,256]{2,1,0:T(8,128)(2,1)} async-done(((bf16[8,128,256]{2,1,0:T(8,128)(2,1)}), bf16[8,128,256]{2,1,0:T(8,128)(2,1)}, u32[]{:S(2)}, u32[]{:S(2)}) %all-to-all-start.7) | async-done | bytes 524320 | tf_op jit(solution)/shard_map/all_to_all | solution.py:38
  219.0 4.1 %all-to-all-start.8 = ((bf16[8,128,256]{2,1,0:T(8,128)(2,1)}), bf16[8,128,256]{2,1,0:T(8,128)(2,1)}, u32[]{:S(2)}, u32[]{:S(2)}) async-start(bf16[8,128,256]{2,1,0:T(8,128)(2,1)} %forward_share.3.refs_4_), calls=%async_computation.8 | async-start | bytes 1048576 | tf_op jit(solution)/shard_map/all_to_all | solution.py:38
  223.2 2.4 backward_product.3
  225.6 2.4 collective-permute-start.14
  230.5 10.6 %all-to-all-done.8.refs_1_ = bf16[8,128,256]{2,1,0:T(8,128)(2,1)} async-done(((bf16[8,128,256]{2,1,0:T(8,128)(2,1)}), bf16[8,128,256]{2,1,0:T(8,128)(2,1)}, u32[]{:S(2)}, u32[]{:S(2)}) %all-to-all-start.8) | async-done | bytes 524320 | tf_op jit(solution)/shard_map/all_to_all | solution.py:38
  241.1 4.0 %all-to-all-start.9 = ((f32[32,8,128]{2,1,0:T(8,128)}), f32[32,8,128]{2,1,0:T(8,128)S(1)}, u32[]{:S(2)}, u32[]{:S(2)}) async-start(f32[32,8,128]{2,1,0:T(8,128)} %get-tuple-element.83.refs_4_), calls=%async_computation.9 | async-start | bytes 262144 | tf_op jit(solution)/shard_map/all_to_all | solution.py:38
  245.1 1.6 copy-done.5
  246.7 2.4 forward_product.3
  249.1 2.3 collective-permute-start.15
  252.4 6.1 %all-to-all-done.9.refs_2_ = f32[32,8,128]{2,1,0:T(8,128)S(1)} async-done(((f32[32,8,128]{2,1,0:T(8,128)}), f32[32,8,128]{2,1,0:T(8,128)S(1)}, u32[]{:S(2)}, u32[]{:S(2)}) %all-to-all-start.9) | async-done | bytes 131104 | tf_op jit(solution)/shard_map/all_to_all | solution.py:38
  (97 shorter events, 43.6 us)
Async XLA Ops:
  3.1 1.6 copy-start.1
  4.7 0.9 copy-start.6
  6.5 13.3 %copy-start = (bf16[1,256,4096]{2,1,0:T(8,128)(2,1)S(1)}, bf16[1,256,4096]{2,1,0:T(8,128)(2,1)}, u32[]{:S(2)}) copy-start(bf16[1,256,4096]{2,1,0:T(8,128)(2,1)} %param.13) | copy-start | bytes 6291460
  6.5 13.3 %copy-start.8 = (bf16[1,8,64,256]{3,2,1,0:T(8,128)(2,1)S(1)}, bf16[1,8,64,256]{3,2,1,0:T(8,128)(2,1)}, u32[]{:S(2)}) copy-start(bf16[1,8,64,256]{3,2,1,0:T(8,128)(2,1)} %param.21) | copy-start | bytes 786436
  6.5 13.3 %copy-start.19 = (bf16[1,128,256]{2,1,0:T(8,128)(2,1)S(1)}, bf16[1,128,256]{2,1,0:T(8,128)(2,1)}, u32[]{:S(2)}) copy-start(bf16[1,128,256]{2,1,0:T(8,128)(2,1)} %param.16) | copy-start | bytes 196612
  6.5 13.3 %copy-start.30 = (f32[1,256]{1,0:T(1,128)S(1)}, f32[1,256]{1,0:T(1,128)}, u32[]{:S(2)}) copy-start(f32[1,256]{1,0:T(1,128)} %refs_3_.3) | copy-start | bytes 3076
  7.9 13.0 %copy-start.26 = (bf16[128,256]{1,0:T(8,128)(2,1)}, bf16[128,256]{1,0:T(8,128)(2,1)S(1)}, u32[]{:S(2)}) copy-start(bf16[128,256]{1,0:T(8,128)(2,1)S(1)} %get-tuple-element.58.refs_4_) | copy-start | bytes 196612
  7.9 4.1 %collective-permute-start = (bf16[8,128,256]{2,1,0:T(8,128)(2,1)S(1)}, bf16[8,128,256]{2,1,0:T(8,128)(2,1)S(1)}, u32[]{:S(2)}, u32[]{:S(2)}) collective-permute-start(bf16[8,128,256]{2,1,0:T(8,128)(2,1)S(1)} %get-tuple-element.48), channel_id=1, source_target_pairs={{0,1},{1,0},{2,3},{3,2},{4,5},{5,4},{6,7},{7,6},{8,9},{9,8},{10,11... | collective-permute-start | bytes 1572872 | tf_op jit(solution)/shard_map/ppermute | solution.py:241
  12.9 24.9 %all-to-all-start = ((bf16[8,128,256]{2,1,0:T(8,128)(2,1)}), bf16[8,128,256]{2,1,0:T(8,128)(2,1)}, u32[]{:S(2)}, u32[]{:S(2)}) async-start(bf16[8,128,256]{2,1,0:T(8,128)(2,1)} %backward_core_sum.2.refs_6_), calls=%async_computation | async-start | bytes 1048576 | tf_op jit(solution)/shard_map/all_to_all | solution.py:38
  20.8 17.0 %copy-start.22 = (bf16[128,256]{1,0:T(8,128)(2,1)}, bf16[128,256]{1,0:T(8,128)(2,1)S(1)}, u32[]{:S(2)}) copy-start(bf16[128,256]{1,0:T(8,128)(2,1)S(1)} %get-tuple-element.67.refs_0_) | copy-start | bytes 196612
  20.8 4.1 %collective-permute-start.1 = (bf16[8,128,256]{2,1,0:T(8,128)(2,1)S(1)}, bf16[8,128,256]{2,1,0:T(8,128)(2,1)S(1)}, u32[]{:S(2)}, u32[]{:S(2)}) collective-permute-start(bf16[8,128,256]{2,1,0:T(8,128)(2,1)S(1)} %get-tuple-element.50), channel_id=1, source_target_pairs={{0,1},{1,0},{2,3},{3,2},{4,5},{5,4},{6,7},{7,6},{8,9},{9,8},{10,11... | collective-permute-start | bytes 1572872 | tf_op jit(solution)/shard_map/ppermute | solution.py:241
  37.8 24.1 %all-to-all-start.1 = ((bf16[8,128,256]{2,1,0:T(8,128)(2,1)}), bf16[8,128,256]{2,1,0:T(8,128)(2,1)}, u32[]{:S(2)}, u32[]{:S(2)}) async-start(bf16[8,128,256]{2,1,0:T(8,128)(2,1)} %forward_core_sum.2.refs_1_), calls=%async_computation.1 | async-start | bytes 1048576 | tf_op jit(solution)/shard_map/all_to_all | solution.py:38
  43.1 12.7 %collective-permute-start.2 = (bf16[128,256]{1,0:T(8,128)(2,1)S(1)}, bf16[128,256]{1,0:T(8,128)(2,1)S(1)}, u32[]{:S(2)}, u32[]{:S(2)}) collective-permute-start(bf16[128,256]{1,0:T(8,128)(2,1)S(1)} %backward_ring_sum.2.refs_1_), channel_id=1, source_target_pairs={{0,2},{1,3},{2,0},{3,1},{4,6},{5,7},{6,4},{7,5},{8,10},{9,11},{10,... | collective-permute-start | bytes 196616 | tf_op jit(solution)/shard_map/ppermute | solution.py:241
  58.2 26.9 %collective-permute-start.3 = (bf16[256,2048]{1,0:T(8,128)(2,1)}, bf16[256,2048]{1,0:T(8,128)(2,1)S(1)}, u32[]{:S(2)}, u32[]{:S(2)}) collective-permute-start(bf16[256,2048]{1,0:T(8,128)(2,1)} %get-tuple-element.54), channel_id=1, source_target_pairs={{0,1},{1,0},{2,3},{3,2},{4,5},{5,4},{6,7},{7,6},{8,9},{9,8},{10,11... | collective-permute-start | bytes 3145736 | tf_op jit(solution)/shard_map/ppermute | solution.py:241
  61.9 24.8 %all-to-all-start.2 = ((bf16[8,128,256]{2,1,0:T(8,128)(2,1)}), bf16[8,128,256]{2,1,0:T(8,128)(2,1)}, u32[]{:S(2)}, u32[]{:S(2)}) async-start(bf16[8,128,256]{2,1,0:T(8,128)(2,1)} %copy-done.10), calls=%async_computation.2 | async-start | bytes 1048576 | tf_op jit(solution)/shard_map/all_to_all | solution.py:38
  68.6 1.1 copy-start.11
  70.8 10.2 %collective-permute-start.4 = (bf16[128,256]{1,0:T(8,128)(2,1)S(1)}, bf16[128,256]{1,0:T(8,128)(2,1)S(1)}, u32[]{:S(2)}, u32[]{:S(2)}) collective-permute-start(bf16[128,256]{1,0:T(8,128)(2,1)S(1)} %forward_ring_sum.2.refs_1_), channel_id=1, source_target_pairs={{0,2},{1,3},{2,0},{3,1},{4,6},{5,7},{6,4},{7,5},{8,10},{9,11},{10,... | collective-permute-start | bytes 196616 | tf_op jit(solution)/shard_map/ppermute | solution.py:241
  81.0 1.6 copy-start.2
  84.1 1.0 copy-start.31
  86.8 5.9 %copy-start.12 = (bf16[1,2,128,256]{3,2,1,0:T(8,128)(2,1)S(1)}, bf16[1,2,128,256]{3,2,1,0:T(8,128)(2,1)}, u32[]{:S(2)}) copy-start(bf16[1,2,128,256]{3,2,1,0:T(8,128)(2,1)} %param.20) | copy-start | bytes 393220
  86.8 5.9 %copy-start.27 = (bf16[128,256]{1,0:T(8,128)(2,1)S(1)}, bf16[128,256]{1,0:T(8,128)(2,1)}, u32[]{:S(2)}) copy-start(bf16[128,256]{1,0:T(8,128)(2,1)} %copy-done.26) | copy-start | bytes 196612
  89.2 46.0 %copy-start.7 = (bf16[1,8,64,256]{3,2,1,0:T(8,128)(2,1)S(1)}, bf16[1,8,64,256]{3,2,1,0:T(8,128)(2,1)}, u32[]{:S(2)}) copy-start(bf16[1,8,64,256]{3,2,1,0:T(8,128)(2,1)} %param.22) | copy-start | bytes 786436
  89.2 3.5 %collective-permute-start.5 = (f32[128,256]{1,0:T(8,128)S(1)}, f32[128,256]{1,0:T(8,128)S(1)}, u32[]{:S(2)}, u32[]{:S(2)}) collective-permute-start(f32[128,256]{1,0:T(8,128)S(1)} %get-tuple-element.57), channel_id=1, source_target_pairs={{0,1},{1,0},{2,3},{3,2},{4,5},{5,4},{6,7},{7,6},{8,9},{9,8},{10,11... | collective-permute-start | bytes 393224 | tf_op jit(solution)/shard_map/ppermute | solution.py:241
  119.3 25.6 %all-to-all-start.4 = ((bf16[8,128,256]{2,1,0:T(8,128)(2,1)}), bf16[8,128,256]{2,1,0:T(8,128)(2,1)}, u32[]{:S(2)}, u32[]{:S(2)}) async-start(bf16[8,128,256]{2,1,0:T(8,128)(2,1)} %get-tuple-element.62.refs_4_.refs_3_), calls=%async_computation.4 | async-start | bytes 1048576 | tf_op jit(solution)/shard_map/all_to_all | solution.py:38
  123.5 28.3 %collective-permute-start.8 = (bf16[2048,256]{1,0:T(8,128)(2,1)}, bf16[2048,256]{1,0:T(8,128)(2,1)}, u32[]{:S(2)}, u32[]{:S(2)}) collective-permute-start(bf16[2048,256]{1,0:T(8,128)(2,1)} %copy-done.31), channel_id=1, source_target_pairs={{0,1},{1,0},{2,3},{3,2},{4,5},{5,4},{6,7},{7,6},{8,9},{9,8},{10,11... | collective-permute-start | bytes 3145736 | tf_op jit(solution)/shard_map/ppermute | solution.py:241
  126.5 1.0 copy-start.17
  127.7 7.5 %collective-permute-start.6 = (bf16[128,256]{1,0:T(8,128)(2,1)S(1)}, bf16[128,256]{1,0:T(8,128)(2,1)S(1)}, u32[]{:S(2)}, u32[]{:S(2)}) collective-permute-start(bf16[128,256]{1,0:T(8,128)(2,1)S(1)} %get-tuple-element.63), channel_id=1, source_target_pairs={{32,0},{64,32},{96,64},{128,96},{160,128},{192,160},{224,192},{256... | collective-permute-start | bytes 196616 | tf_op jit(solution)/shard_map/ppermute | solution.py:48
  135.2 1.6 copy-start.3
  139.6 4.4 %collective-permute-start.7 = (bf16[8,128,256]{2,1,0:T(8,128)(2,1)S(1)}, bf16[8,128,256]{2,1,0:T(8,128)(2,1)S(1)}, u32[]{:S(2)}, u32[]{:S(2)}) collective-permute-start(bf16[8,128,256]{2,1,0:T(8,128)(2,1)S(1)} %get-tuple-element.65), channel_id=1, source_target_pairs={{0,1},{1,0},{2,3},{3,2},{4,5},{5,4},{6,7},{7,6},{8,9},{9,8},{10,11... | collective-permute-start | bytes 1572872 | tf_op jit(solution)/shard_map/ppermute | solution.py:241
  145.0 27.0 %all-to-all-start.5 = ((bf16[8,128,256]{2,1,0:T(8,128)(2,1)}), bf16[8,128,256]{2,1,0:T(8,128)(2,1)}, u32[]{:S(2)}, u32[]{:S(2)}) async-start(bf16[8,128,256]{2,1,0:T(8,128)(2,1)} %backward_core_sum.3.refs_4_), calls=%async_computation.5 | async-start | bytes 1048576 | tf_op jit(solution)/shard_map/all_to_all | solution.py:38
  151.8 1.6 copy-start.4
  153.3 5.9 %copy-start.23 = (bf16[128,256]{1,0:T(8,128)(2,1)S(1)}, bf16[128,256]{1,0:T(8,128)(2,1)}, u32[]{:S(2)}) copy-start(bf16[128,256]{1,0:T(8,128)(2,1)} %copy-done.22) | copy-start | bytes 196612
  153.3 11.4 %copy-start.9 = (bf16[1,8,64,256]{3,2,1,0:T(8,128)(2,1)S(1)}, bf16[1,8,64,256]{3,2,1,0:T(8,128)(2,1)}, u32[]{:S(2)}) copy-start(bf16[1,8,64,256]{3,2,1,0:T(8,128)(2,1)} %param.21) | copy-start | bytes 786436
  153.4 11.4 %copy-start.21 = (bf16[1,128,256]{2,1,0:T(8,128)(2,1)S(1)}, bf16[1,128,256]{2,1,0:T(8,128)(2,1)}, u32[]{:S(2)}) copy-start(bf16[1,128,256]{2,1,0:T(8,128)(2,1)} %refs_2_.3) | copy-start | bytes 196612
  155.7 3.5 %collective-permute-start.9 = (f32[128,256]{1,0:T(8,128)S(1)}, f32[128,256]{1,0:T(8,128)S(1)}, u32[]{:S(2)}, u32[]{:S(2)}) collective-permute-start(f32[128,256]{1,0:T(8,128)S(1)} %get-tuple-element.70), channel_id=1, source_target_pairs={{0,1},{1,0},{2,3},{3,2},{4,5},{5,4},{6,7},{7,6},{8,9},{9,8},{10,11... | collective-permute-start | bytes 393224 | tf_op jit(solution)/shard_map/ppermute | solution.py:241
  159.4 5.4 %collective-permute-start.10 = (bf16[128,256]{1,0:T(8,128)(2,1)S(1)}, bf16[128,256]{1,0:T(8,128)(2,1)S(1)}, u32[]{:S(2)}, u32[]{:S(2)}) collective-permute-start(bf16[128,256]{1,0:T(8,128)(2,1)S(1)} %forward_end.1), channel_id=1, source_target_pairs={{0,32},{32,64},{64,96},{96,128},{128,160},{160,192},{192,224},{224... | collective-permute-start | bytes 196616 | tf_op jit(solution)/shard_map/ppermute | solution.py:48
  166.5 4.5 %collective-permute-start.11 = (bf16[8,128,256]{2,1,0:T(8,128)(2,1)S(1)}, bf16[8,128,256]{2,1,0:T(8,128)(2,1)S(1)}, u32[]{:S(2)}, u32[]{:S(2)}) collective-permute-start(bf16[8,128,256]{2,1,0:T(8,128)(2,1)S(1)} %get-tuple-element.73), channel_id=1, source_target_pairs={{0,1},{1,0},{2,3},{3,2},{4,5},{5,4},{6,7},{7,6},{8,9},{9,8},{10,11... | collective-permute-start | bytes 1572872 | tf_op jit(solution)/shard_map/ppermute | solution.py:241
  171.9 25.0 %all-to-all-start.6 = ((bf16[8,128,256]{2,1,0:T(8,128)(2,1)}), bf16[8,128,256]{2,1,0:T(8,128)(2,1)}, u32[]{:S(2)}, u32[]{:S(2)}) async-start(bf16[8,128,256]{2,1,0:T(8,128)(2,1)} %forward_core_sum.3.refs_1_), calls=%async_computation.6 | async-start | bytes 1048576 | tf_op jit(solution)/shard_map/all_to_all | solution.py:38
  180.0 10.3 %collective-permute-start.12 = (bf16[128,256]{1,0:T(8,128)(2,1)S(1)}, bf16[128,256]{1,0:T(8,128)(2,1)S(1)}, u32[]{:S(2)}, u32[]{:S(2)}) collective-permute-start(bf16[128,256]{1,0:T(8,128)(2,1)S(1)} %backward_ring_sum.3.refs_1_), channel_id=1, source_target_pairs={{0,2},{1,3},{2,0},{3,1},{4,6},{5,7},{6,4},{7,5},{8,10},{9,11},{10,... | collective-permute-start | bytes 196616 | tf_op jit(solution)/shard_map/ppermute | solution.py:241
  196.9 22.1 %all-to-all-start.7 = ((bf16[8,128,256]{2,1,0:T(8,128)(2,1)}), bf16[8,128,256]{2,1,0:T(8,128)(2,1)}, u32[]{:S(2)}, u32[]{:S(2)}) async-start(bf16[8,128,256]{2,1,0:T(8,128)(2,1)} %backward_share.3.refs_1_), calls=%async_computation.7 | async-start | bytes 1048576 | tf_op jit(solution)/shard_map/all_to_all | solution.py:38
  202.2 10.7 %collective-permute-start.13 = (bf16[128,256]{1,0:T(8,128)(2,1)S(1)}, bf16[128,256]{1,0:T(8,128)(2,1)S(1)}, u32[]{:S(2)}, u32[]{:S(2)}) collective-permute-start(bf16[128,256]{1,0:T(8,128)(2,1)S(1)} %forward_ring_sum.3.refs_1_), channel_id=1, source_target_pairs={{0,2},{1,3},{2,0},{3,1},{4,6},{5,7},{6,4},{7,5},{8,10},{9,11},{10,... | collective-permute-start | bytes 196616 | tf_op jit(solution)/shard_map/ppermute | solution.py:241
  219.0 22.1 %all-to-all-start.8 = ((bf16[8,128,256]{2,1,0:T(8,128)(2,1)}), bf16[8,128,256]{2,1,0:T(8,128)(2,1)}, u32[]{:S(2)}, u32[]{:S(2)}) async-start(bf16[8,128,256]{2,1,0:T(8,128)(2,1)} %forward_share.3.refs_4_), calls=%async_computation.8 | async-start | bytes 1048576 | tf_op jit(solution)/shard_map/all_to_all | solution.py:38
  223.2 5.8 %copy-start.25 = (bf16[128,256]{1,0:T(8,128)(2,1)S(1)}, bf16[128,256]{1,0:T(8,128)(2,1)}, u32[]{:S(2)}) copy-start(bf16[128,256]{1,0:T(8,128)(2,1)} %copy-done.24) | copy-start | bytes 196612
  225.6 3.4 %collective-permute-start.14 = (f32[128,256]{1,0:T(8,128)S(1)}, f32[128,256]{1,0:T(8,128)S(1)}, u32[]{:S(2)}, u32[]{:S(2)}) collective-permute-start(f32[128,256]{1,0:T(8,128)S(1)} %get-tuple-element.78), channel_id=1, source_target_pairs={{0,1},{1,0},{2,3},{3,2},{4,5},{5,4},{6,7},{7,6},{8,9},{9,8},{10,11... | collective-permute-start | bytes 393224 | tf_op jit(solution)/shard_map/ppermute | solution.py:241
  241.1 17.4 %all-to-all-start.9 = ((f32[32,8,128]{2,1,0:T(8,128)}), f32[32,8,128]{2,1,0:T(8,128)S(1)}, u32[]{:S(2)}, u32[]{:S(2)}) async-start(f32[32,8,128]{2,1,0:T(8,128)} %get-tuple-element.83.refs_4_), calls=%async_computation.9 | async-start | bytes 262144 | tf_op jit(solution)/shard_map/all_to_all | solution.py:38
  245.1 1.6 copy-start.5
  249.1 3.2 %collective-permute-start.15 = (f32[128,256]{1,0:T(8,128)S(1)}, f32[128,256]{1,0:T(8,128)S(1)}, u32[]{:S(2)}, u32[]{:S(2)}) collective-permute-start(f32[128,256]{1,0:T(8,128)S(1)} %get-tuple-element.87), channel_id=1, source_target_pairs={{0,1},{1,0},{2,3},{3,2},{4,5},{5,4},{6,7},{7,6},{8,9},{9,8},{10,11... | collective-permute-start | bytes 393224 | tf_op jit(solution)/shard_map/ppermute | solution.py:241
  258.5 1.0 copy-start.15
  (9 other events, 6.9 us)

commit v9 on v8

--- a/solution.py
+++ b/solution.py
@@ -237,6 +237,13 @@
     out[...] = (value - kept * (factor * factor * factor) * down(total[0:1]) / D).astype(BF16)
 
 
+def flat(values):
+    rows, columns = values.shape
+    position = jnp.arange(rows)[:, None] * columns + jnp.arange(columns)[None, :]
+    chosen_one = jnp.arange(rows * columns)[:, None, None] == position[None]
+    return jnp.sum(jnp.where(chosen_one, values[None], 0), axis=(1, 2)).astype(jnp.int32)
+
+
 def over(value, pairs):
     return lax.ppermute(value, "shard", pairs)
 
@@ -260,8 +267,9 @@
     segments = lax.axis_size("segment")
     position = lax.axis_index("shard")
     core = position % 2
-    numbers = (sample_ids, jnp.stack([segment, core]), forward_exponents, backward_exponents)
-    scalars = jnp.concatenate([number.astype(jnp.int32).reshape(-1) for number in numbers])
+    place = jnp.stack([segment, core]).astype(jnp.int32)
+    exponents = flat(forward_exponents[0]), flat(backward_exponents[0])
+    scalars = jnp.concatenate([flat(sample_ids), place, *exponents])
     value_local, output_local = value_weight[0], output_weight[0]
     saved = saved_inputs[0]
     low = shape_of(ROWS, WIDTH)

time: 263 us -> 259 us (0.985)
  local copies, waits for them, and re-layouts: 22.2 us -> 18.1 us
    unnamed x65 -> x57, local copies, waits for them, and re-layouts: 20.5 us -> 18 us
where the time goes in v9:
time: 259 us; the launch traced here: 257 us
  starting transfers between devices  104 us (40%)
  waiting for transfers between devices  77.3 us (30%)
  Pallas kernels  29.5 us (11%)
  blocking collectives  25.7 us (10%)
  local copies, waits for them, and re-layouts  18.1 us (7%)
    ppermute x14, starting transfers between devices, over(): return lax.ppermute(value, 'shard', pairs)  52.2 us
    all_to_all x9, starting transfers between devices, swapped(): lax.all_to_all(value, 'shard', 0, 0, axis_index_groups=groups, tiled=True)  47.8 us
    all_to_all x9, waiting for transfers between devices, swapped(): lax.all_to_all(value, 'shard', 0, 0, axis_index_groups=groups, tiled=True)  40.5 us
    pallas_call x25, Pallas kernels, call(): pl.pallas_call(body, out_shape=outs, grid_spec=pltpu.PrefetchScalarGridSp...  29.5 us
    ppermute x14, waiting for transfers between devices, over(): return lax.ppermute(value, 'shard', pairs)  28.3 us
    all_to_all x1, blocking collectives, swapped(): lax.all_to_all(value, 'shard', 0, 0, axis_index_groups=groups, tiled=True)  25.7 us
    unnamed x57, local copies, waits for them, and re-layouts  18 us
    ppermute x2, waiting for transfers between devices, shifted(): lax.ppermute(value, axis, [(source, source + steps) for source in range(l...  8.53 us
  transfers between devices with their start and end apart: 25, of which 20 were waited for; matrix products, arithmetic and copies ran while one was open for 0% of the time, Pallas kernels for 9%

profile of v9, /device:TPU:7, one launch (start us, length us, event | category | flops | bytes accessed | tf_op | source)
XLA Modules:
  0.0 257.1 jit_solution(7712625596021454742)
XLA Ops:
  2.6 1.6 copy-done.1
  7.3 2.6 %collective-permute-start = (bf16[8,128,256]{2,1,0:T(8,128)(2,1)S(1)}, bf16[8,128,256]{2,1,0:T(8,128)(2,1)S(1)}, u32[]{:S(2)}, u32[]{:S(2)}) collective-permute-start(bf16[8,128,256]{2,1,0:T(8,128)(2,1)S(1)} %get-tuple-element.48), channel_id=1, source_target_pairs={{0,1},{1,0},{2,3},{3,2},{4,5},{5,4},{6,7},{7,6},{8,9},{9,8},{10,11... | collective-permute-start | bytes 1572872 | tf_op jit(solution)/shard_map/ppermute | solution.py:248
  12.4 6.8 %all-to-all-start = ((bf16[8,128,256]{2,1,0:T(8,128)(2,1)}), bf16[8,128,256]{2,1,0:T(8,128)(2,1)S(1)}, u32[]{:S(2)}, u32[]{:S(2)}) async-start(bf16[8,128,256]{2,1,0:T(8,128)(2,1)} %backward_core_sum.2.refs_6_), calls=%async_computation | async-start | bytes 1048576 | tf_op jit(solution)/shard_map/all_to_all | solution.py:38
  20.9 2.6 collective-permute-start.1
  25.9 11.2 %all-to-all-done.refs_0_ = bf16[8,128,256]{2,1,0:T(8,128)(2,1)S(1)} async-done(((bf16[8,128,256]{2,1,0:T(8,128)(2,1)}), bf16[8,128,256]{2,1,0:T(8,128)(2,1)S(1)}, u32[]{:S(2)}, u32[]{:S(2)}) %all-to-all-start) | async-done | bytes 524320 | tf_op jit(solution)/shard_map/all_to_all | solution.py:38
  37.2 4.2 %all-to-all-start.1 = ((bf16[8,128,256]{2,1,0:T(8,128)(2,1)}), bf16[8,128,256]{2,1,0:T(8,128)(2,1)}, u32[]{:S(2)}, u32[]{:S(2)}) async-start(bf16[8,128,256]{2,1,0:T(8,128)(2,1)} %forward_core_sum.2.refs_1_), calls=%async_computation.1 | async-start | bytes 1048576 | tf_op jit(solution)/shard_map/all_to_all | solution.py:38
  41.4 10.6 %collective-permute-start.2 = (bf16[128,256]{1,0:T(8,128)(2,1)S(1)}, bf16[128,256]{1,0:T(8,128)(2,1)S(1)}, u32[]{:S(2)}, u32[]{:S(2)}) collective-permute-start(bf16[128,256]{1,0:T(8,128)(2,1)S(1)} %backward_ring_sum.2.refs_1_), channel_id=1, source_target_pairs={{0,2},{1,3},{2,0},{3,1},{4,6},{5,7},{6,4},{7,5},{8,10},{9,11},{10,... | collective-permute-start | bytes 196616 | tf_op jit(solution)/shard_map/ppermute | solution.py:248
  52.0 2.0 collective-permute-done.2.refs_2_
  54.0 1.7 backward_share.2
  56.5 3.8 %collective-permute-start.3 = (bf16[256,2048]{1,0:T(8,128)(2,1)}, bf16[256,2048]{1,0:T(8,128)(2,1)S(1)}, u32[]{:S(2)}, u32[]{:S(2)}) collective-permute-start(bf16[256,2048]{1,0:T(8,128)(2,1)} %get-tuple-element.54), channel_id=1, source_target_pairs={{0,1},{1,0},{2,3},{3,2},{4,5},{5,4},{6,7},{7,6},{8,9},{9,8},{10,11... | collective-permute-start | bytes 3145736 | tf_op jit(solution)/shard_map/ppermute | solution.py:248
  60.3 6.7 %all-to-all-start.2 = ((bf16[8,128,256]{2,1,0:T(8,128)(2,1)}), bf16[8,128,256]{2,1,0:T(8,128)(2,1)}, u32[]{:S(2)}, u32[]{:S(2)}) async-start(bf16[8,128,256]{2,1,0:T(8,128)(2,1)} %copy-done.10), calls=%async_computation.2 | async-start | bytes 1048576 | tf_op jit(solution)/shard_map/all_to_all | solution.py:38
  69.1 8.0 %collective-permute-start.4 = (bf16[128,256]{1,0:T(8,128)(2,1)S(1)}, bf16[128,256]{1,0:T(8,128)(2,1)S(1)}, u32[]{:S(2)}, u32[]{:S(2)}) collective-permute-start(bf16[128,256]{1,0:T(8,128)(2,1)S(1)} %forward_ring_sum.2.refs_1_), channel_id=1, source_target_pairs={{0,2},{1,3},{2,0},{3,1},{4,6},{5,7},{6,4},{7,5},{8,10},{9,11},{10,... | collective-permute-start | bytes 196616 | tf_op jit(solution)/shard_map/ppermute | solution.py:248
  77.1 2.2 collective-permute-done.4.refs_2_
  79.4 1.6 copy-done.2
  83.4 1.7 all-to-all-done.2.refs_1_
  85.1 2.4 backward_product.2
  87.5 2.5 collective-permute-start.5
  92.0 25.7 %all_to_all.50.refs_2_ = f32[32,8,128]{2,1,0:T(8,128)} all-to-all(f32[32,8,128]{2,1,0:T(8,128)S(1)} %get-tuple-element.61), channel_id=1, replica_groups=mesh['segment'=16,'shard'=32] {'shard'}, dimensions={0} | all-to-all | bytes 262144 | tf_op jit(solution)/shard_map/all_to_all | solution.py:38
  117.7 4.1 %all-to-all-start.4 = ((bf16[8,128,256]{2,1,0:T(8,128)(2,1)}), bf16[8,128,256]{2,1,0:T(8,128)(2,1)}, u32[]{:S(2)}, u32[]{:S(2)}) async-start(bf16[8,128,256]{2,1,0:T(8,128)(2,1)} %get-tuple-element.62.refs_4_.refs_3_), calls=%async_computation.4 | async-start | bytes 1048576 | tf_op jit(solution)/shard_map/all_to_all | solution.py:38
  121.8 2.1 collective-permute-start.8
  126.0 2.5 collective-permute-start.6
  128.5 5.1 %collective-permute-done.6.refs_1_ = bf16[128,256]{1,0:T(8,128)(2,1)S(1)} collective-permute-done((bf16[128,256]{1,0:T(8,128)(2,1)S(1)}, bf16[128,256]{1,0:T(8,128)(2,1)S(1)}, u32[]{:S(2)}, u32[]{:S(2)}) %collective-permute-start.6) | collective-permute-done | bytes 65568 | tf_op jit(solution)/shard_map/ppermute | solution.py:48
  133.5 1.6 copy-done.3
  137.9 2.9 %collective-permute-start.7 = (bf16[8,128,256]{2,1,0:T(8,128)(2,1)S(1)}, bf16[8,128,256]{2,1,0:T(8,128)(2,1)S(1)}, u32[]{:S(2)}, u32[]{:S(2)}) collective-permute-start(bf16[8,128,256]{2,1,0:T(8,128)(2,1)S(1)} %get-tuple-element.65), channel_id=1, source_target_pairs={{0,1},{1,0},{2,3},{3,2},{4,5},{5,4},{6,7},{7,6},{8,9},{9,8},{10,11... | collective-permute-start | bytes 1572872 | tf_op jit(solution)/shard_map/ppermute | solution.py:248
  143.3 6.8 %all-to-all-start.5 = ((bf16[8,128,256]{2,1,0:T(8,128)(2,1)}), bf16[8,128,256]{2,1,0:T(8,128)(2,1)}, u32[]{:S(2)}, u32[]{:S(2)}) async-start(bf16[8,128,256]{2,1,0:T(8,128)(2,1)} %backward_core_sum.3.refs_4_), calls=%async_computation.5 | async-start | bytes 1048576 | tf_op jit(solution)/shard_map/all_to_all | solution.py:38
  150.1 1.6 copy-done.4
  151.7 2.4 forward_product.2
  154.1 2.6 collective-permute-start.9
  157.7 1.9 collective-permute-start.10
  159.7 3.5 %collective-permute-done.10.refs_1_ = bf16[128,256]{1,0:T(8,128)(2,1)S(1)} collective-permute-done((bf16[128,256]{1,0:T(8,128)(2,1)S(1)}, bf16[128,256]{1,0:T(8,128)(2,1)S(1)}, u32[]{:S(2)}, u32[]{:S(2)}) %collective-permute-start.10) | collective-permute-done | bytes 65568 | tf_op jit(solution)/shard_map/ppermute | solution.py:48
  164.2 3.0 %collective-permute-start.11 = (bf16[8,128,256]{2,1,0:T(8,128)(2,1)S(1)}, bf16[8,128,256]{2,1,0:T(8,128)(2,1)S(1)}, u32[]{:S(2)}, u32[]{:S(2)}) collective-permute-start(bf16[8,128,256]{2,1,0:T(8,128)(2,1)S(1)} %get-tuple-element.73), channel_id=1, source_target_pairs={{0,1},{1,0},{2,3},{3,2},{4,5},{5,4},{6,7},{7,6},{8,9},{9,8},{10,11... | collective-permute-start | bytes 1572872 | tf_op jit(solution)/shard_map/ppermute | solution.py:248
  169.7 6.9 %all-to-all-start.6 = ((bf16[8,128,256]{2,1,0:T(8,128)(2,1)}), bf16[8,128,256]{2,1,0:T(8,128)(2,1)}, u32[]{:S(2)}, u32[]{:S(2)}) async-start(bf16[8,128,256]{2,1,0:T(8,128)(2,1)} %forward_core_sum.3.refs_1_), calls=%async_computation.6 | async-start | bytes 1048576 | tf_op jit(solution)/shard_map/all_to_all | solution.py:38
  177.7 3.4 %collective-permute-start.12 = (bf16[128,256]{1,0:T(8,128)(2,1)S(1)}, bf16[128,256]{1,0:T(8,128)(2,1)S(1)}, u32[]{:S(2)}, u32[]{:S(2)}) collective-permute-start(bf16[128,256]{1,0:T(8,128)(2,1)S(1)} %backward_ring_sum.3.refs_1_), channel_id=1, source_target_pairs={{0,2},{1,3},{2,0},{3,1},{4,6},{5,7},{6,4},{7,5},{8,10},{9,11},{10,... | collective-permute-start | bytes 196616 | tf_op jit(solution)/shard_map/ppermute | solution.py:248
  181.2 6.9 %collective-permute-done.12.refs_2_ = bf16[128,256]{1,0:T(8,128)(2,1)S(1)} collective-permute-done((bf16[128,256]{1,0:T(8,128)(2,1)S(1)}, bf16[128,256]{1,0:T(8,128)(2,1)S(1)}, u32[]{:S(2)}, u32[]{:S(2)}) %collective-permute-start.12) | collective-permute-done | bytes 65568 | tf_op jit(solution)/shard_map/ppermute | solution.py:248
  189.4 5.3 %all-to-all-done.6.refs_0_ = bf16[8,128,256]{2,1,0:T(8,128)(2,1)} async-done(((bf16[8,128,256]{2,1,0:T(8,128)(2,1)}), bf16[8,128,256]{2,1,0:T(8,128)(2,1)}, u32[]{:S(2)}, u32[]{:S(2)}) %all-to-all-start.6) | async-done | bytes 524320 | tf_op jit(solution)/shard_map/all_to_all | solution.py:38
  194.7 4.1 %all-to-all-start.7 = ((bf16[8,128,256]{2,1,0:T(8,128)(2,1)}), bf16[8,128,256]{2,1,0:T(8,128)(2,1)}, u32[]{:S(2)}, u32[]{:S(2)}) async-start(bf16[8,128,256]{2,1,0:T(8,128)(2,1)} %backward_share.3.refs_1_), calls=%async_computation.7 | async-start | bytes 1048576 | tf_op jit(solution)/shard_map/all_to_all | solution.py:38
  199.9 3.4 %collective-permute-start.13 = (bf16[128,256]{1,0:T(8,128)(2,1)S(1)}, bf16[128,256]{1,0:T(8,128)(2,1)S(1)}, u32[]{:S(2)}, u32[]{:S(2)}) collective-permute-start(bf16[128,256]{1,0:T(8,128)(2,1)S(1)} %forward_ring_sum.3.refs_1_), channel_id=1, source_target_pairs={{0,2},{1,3},{2,0},{3,1},{4,6},{5,7},{6,4},{7,5},{8,10},{9,11},{10,... | collective-permute-start | bytes 196616 | tf_op jit(solution)/shard_map/ppermute | solution.py:248
  203.4 7.2 %collective-permute-done.13.refs_2_ = bf16[128,256]{1,0:T(8,128)(2,1)S(1)} collective-permute-done((bf16[128,256]{1,0:T(8,128)(2,1)S(1)}, bf16[128,256]{1,0:T(8,128)(2,1)S(1)}, u32[]{:S(2)}, u32[]{:S(2)}) %collective-permute-start.13) | collective-permute-done | bytes 65568 | tf_op jit(solution)/shard_map/ppermute | solution.py:248
  212.0 4.8 %all-to-all-done.7.refs_1_ = bf16[8,128,256]{2,1,0:T(8,128)(2,1)} async-done(((bf16[8,128,256]{2,1,0:T(8,128)(2,1)}), bf16[8,128,256]{2,1,0:T(8,128)(2,1)}, u32[]{:S(2)}, u32[]{:S(2)}) %all-to-all-start.7) | async-done | bytes 524320 | tf_op jit(solution)/shard_map/all_to_all | solution.py:38
  216.8 4.2 %all-to-all-start.8 = ((bf16[8,128,256]{2,1,0:T(8,128)(2,1)}), bf16[8,128,256]{2,1,0:T(8,128)(2,1)}, u32[]{:S(2)}, u32[]{:S(2)}) async-start(bf16[8,128,256]{2,1,0:T(8,128)(2,1)} %forward_share.3.refs_4_), calls=%async_computation.8 | async-start | bytes 1048576 | tf_op jit(solution)/shard_map/all_to_all | solution.py:38
  220.9 2.4 backward_product.3
  223.3 2.4 collective-permute-start.14
  227.5 11.3 %all-to-all-done.8.refs_1_ = bf16[8,128,256]{2,1,0:T(8,128)(2,1)} async-done(((bf16[8,128,256]{2,1,0:T(8,128)(2,1)}), bf16[8,128,256]{2,1,0:T(8,128)(2,1)}, u32[]{:S(2)}, u32[]{:S(2)}) %all-to-all-start.8) | async-done | bytes 524320 | tf_op jit(solution)/shard_map/all_to_all | solution.py:38
  238.9 4.0 %all-to-all-start.9 = ((f32[32,8,128]{2,1,0:T(8,128)}), f32[32,8,128]{2,1,0:T(8,128)S(1)}, u32[]{:S(2)}, u32[]{:S(2)}) async-start(f32[32,8,128]{2,1,0:T(8,128)} %get-tuple-element.83.refs_4_), calls=%async_computation.9 | async-start | bytes 262144 | tf_op jit(solution)/shard_map/all_to_all | solution.py:38
  242.9 1.6 copy-done.5
  244.5 2.4 forward_product.3
  246.9 2.3 collective-permute-start.15
  250.1 6.2 %all-to-all-done.9.refs_2_ = f32[32,8,128]{2,1,0:T(8,128)S(1)} async-done(((f32[32,8,128]{2,1,0:T(8,128)}), f32[32,8,128]{2,1,0:T(8,128)S(1)}, u32[]{:S(2)}, u32[]{:S(2)}) %all-to-all-start.9) | async-done | bytes 131104 | tf_op jit(solution)/shard_map/all_to_all | solution.py:38
  (92 shorter events, 39.5 us)
Async XLA Ops:
  2.6 1.6 copy-start.1
  4.2 0.9 copy-start.6
  5.1 0.8 copy-start.16
  5.9 13.3 %copy-start = (bf16[1,256,4096]{2,1,0:T(8,128)(2,1)S(1)}, bf16[1,256,4096]{2,1,0:T(8,128)(2,1)}, u32[]{:S(2)}) copy-start(bf16[1,256,4096]{2,1,0:T(8,128)(2,1)} %param.13) | copy-start | bytes 6291460
  5.9 13.3 %copy-start.8 = (bf16[1,8,64,256]{3,2,1,0:T(8,128)(2,1)S(1)}, bf16[1,8,64,256]{3,2,1,0:T(8,128)(2,1)}, u32[]{:S(2)}) copy-start(bf16[1,8,64,256]{3,2,1,0:T(8,128)(2,1)} %param.21) | copy-start | bytes 786436
  6.0 13.3 %copy-start.17 = (bf16[1,128,256]{2,1,0:T(8,128)(2,1)S(1)}, bf16[1,128,256]{2,1,0:T(8,128)(2,1)}, u32[]{:S(2)}) copy-start(bf16[1,128,256]{2,1,0:T(8,128)(2,1)} %param.16) | copy-start | bytes 196612
  6.0 13.3 %copy-start.26 = (f32[1,256]{1,0:T(1,128)S(1)}, f32[1,256]{1,0:T(1,128)}, u32[]{:S(2)}) copy-start(f32[1,256]{1,0:T(1,128)} %refs_3_.3) | copy-start | bytes 3076
  7.3 5.1 %copy-start.24 = (bf16[128,256]{1,0:T(8,128)(2,1)}, bf16[128,256]{1,0:T(8,128)(2,1)S(1)}, u32[]{:S(2)}) copy-start(bf16[128,256]{1,0:T(8,128)(2,1)S(1)} %get-tuple-element.58.refs_4_) | copy-start | bytes 196612
  7.3 4.1 %collective-permute-start = (bf16[8,128,256]{2,1,0:T(8,128)(2,1)S(1)}, bf16[8,128,256]{2,1,0:T(8,128)(2,1)S(1)}, u32[]{:S(2)}, u32[]{:S(2)}) collective-permute-start(bf16[8,128,256]{2,1,0:T(8,128)(2,1)S(1)} %get-tuple-element.48), channel_id=1, source_target_pairs={{0,1},{1,0},{2,3},{3,2},{4,5},{5,4},{6,7},{7,6},{8,9},{9,8},{10,11... | collective-permute-start | bytes 1572872 | tf_op jit(solution)/shard_map/ppermute | solution.py:248
  12.4 24.8 %all-to-all-start = ((bf16[8,128,256]{2,1,0:T(8,128)(2,1)}), bf16[8,128,256]{2,1,0:T(8,128)(2,1)S(1)}, u32[]{:S(2)}, u32[]{:S(2)}) async-start(bf16[8,128,256]{2,1,0:T(8,128)(2,1)} %backward_core_sum.2.refs_6_), calls=%async_computation | async-start | bytes 1048576 | tf_op jit(solution)/shard_map/all_to_all | solution.py:38
  20.9 4.1 %collective-permute-start.1 = (bf16[8,128,256]{2,1,0:T(8,128)(2,1)S(1)}, bf16[8,128,256]{2,1,0:T(8,128)(2,1)S(1)}, u32[]{:S(2)}, u32[]{:S(2)}) collective-permute-start(bf16[8,128,256]{2,1,0:T(8,128)(2,1)S(1)} %get-tuple-element.50), channel_id=1, source_target_pairs={{0,1},{1,0},{2,3},{3,2},{4,5},{5,4},{6,7},{7,6},{8,9},{9,8},{10,11... | collective-permute-start | bytes 1572872 | tf_op jit(solution)/shard_map/ppermute | solution.py:248
  37.2 23.1 %all-to-all-start.1 = ((bf16[8,128,256]{2,1,0:T(8,128)(2,1)}), bf16[8,128,256]{2,1,0:T(8,128)(2,1)}, u32[]{:S(2)}, u32[]{:S(2)}) async-start(bf16[8,128,256]{2,1,0:T(8,128)(2,1)} %forward_core_sum.2.refs_1_), calls=%async_computation.1 | async-start | bytes 1048576 | tf_op jit(solution)/shard_map/all_to_all | solution.py:38
  41.4 12.7 %collective-permute-start.2 = (bf16[128,256]{1,0:T(8,128)(2,1)S(1)}, bf16[128,256]{1,0:T(8,128)(2,1)S(1)}, u32[]{:S(2)}, u32[]{:S(2)}) collective-permute-start(bf16[128,256]{1,0:T(8,128)(2,1)S(1)} %backward_ring_sum.2.refs_1_), channel_id=1, source_target_pairs={{0,2},{1,3},{2,0},{3,1},{4,6},{5,7},{6,4},{7,5},{8,10},{9,11},{10,... | collective-permute-start | bytes 196616 | tf_op jit(solution)/shard_map/ppermute | solution.py:248
  56.5 26.9 %collective-permute-start.3 = (bf16[256,2048]{1,0:T(8,128)(2,1)}, bf16[256,2048]{1,0:T(8,128)(2,1)S(1)}, u32[]{:S(2)}, u32[]{:S(2)}) collective-permute-start(bf16[256,2048]{1,0:T(8,128)(2,1)} %get-tuple-element.54), channel_id=1, source_target_pairs={{0,1},{1,0},{2,3},{3,2},{4,5},{5,4},{6,7},{7,6},{8,9},{9,8},{10,11... | collective-permute-start | bytes 3145736 | tf_op jit(solution)/shard_map/ppermute | solution.py:248
  60.3 24.8 %all-to-all-start.2 = ((bf16[8,128,256]{2,1,0:T(8,128)(2,1)}), bf16[8,128,256]{2,1,0:T(8,128)(2,1)}, u32[]{:S(2)}, u32[]{:S(2)}) async-start(bf16[8,128,256]{2,1,0:T(8,128)(2,1)} %copy-done.10), calls=%async_computation.2 | async-start | bytes 1048576 | tf_op jit(solution)/shard_map/all_to_all | solution.py:38
  66.9 1.1 copy-start.11
  69.1 10.2 %collective-permute-start.4 = (bf16[128,256]{1,0:T(8,128)(2,1)S(1)}, bf16[128,256]{1,0:T(8,128)(2,1)S(1)}, u32[]{:S(2)}, u32[]{:S(2)}) collective-permute-start(bf16[128,256]{1,0:T(8,128)(2,1)S(1)} %forward_ring_sum.2.refs_1_), channel_id=1, source_target_pairs={{0,2},{1,3},{2,0},{3,1},{4,6},{5,7},{6,4},{7,5},{8,10},{9,11},{10,... | collective-permute-start | bytes 196616 | tf_op jit(solution)/shard_map/ppermute | solution.py:248
  79.4 1.6 copy-start.2
  82.4 1.0 copy-start.27
  85.1 5.9 %copy-start.12 = (bf16[1,2,128,256]{3,2,1,0:T(8,128)(2,1)S(1)}, bf16[1,2,128,256]{3,2,1,0:T(8,128)(2,1)}, u32[]{:S(2)}) copy-start(bf16[1,2,128,256]{3,2,1,0:T(8,128)(2,1)} %param.20) | copy-start | bytes 393220
  85.1 5.9 %copy-start.25 = (bf16[128,256]{1,0:T(8,128)(2,1)S(1)}, bf16[128,256]{1,0:T(8,128)(2,1)}, u32[]{:S(2)}) copy-start(bf16[128,256]{1,0:T(8,128)(2,1)} %copy-done.24) | copy-start | bytes 196612
  87.5 46.0 %copy-start.7 = (bf16[1,8,64,256]{3,2,1,0:T(8,128)(2,1)S(1)}, bf16[1,8,64,256]{3,2,1,0:T(8,128)(2,1)}, u32[]{:S(2)}) copy-start(bf16[1,8,64,256]{3,2,1,0:T(8,128)(2,1)} %param.22) | copy-start | bytes 786436
  87.5 3.5 %collective-permute-start.5 = (f32[128,256]{1,0:T(8,128)S(1)}, f32[128,256]{1,0:T(8,128)S(1)}, u32[]{:S(2)}, u32[]{:S(2)}) collective-permute-start(f32[128,256]{1,0:T(8,128)S(1)} %get-tuple-element.57), channel_id=1, source_target_pairs={{0,1},{1,0},{2,3},{3,2},{4,5},{5,4},{6,7},{7,6},{8,9},{9,8},{10,11... | collective-permute-start | bytes 393224 | tf_op jit(solution)/shard_map/ppermute | solution.py:248
  117.7 25.7 %all-to-all-start.4 = ((bf16[8,128,256]{2,1,0:T(8,128)(2,1)}), bf16[8,128,256]{2,1,0:T(8,128)(2,1)}, u32[]{:S(2)}, u32[]{:S(2)}) async-start(bf16[8,128,256]{2,1,0:T(8,128)(2,1)} %get-tuple-element.62.refs_4_.refs_3_), calls=%async_computation.4 | async-start | bytes 1048576 | tf_op jit(solution)/shard_map/all_to_all | solution.py:38
  121.8 28.3 %collective-permute-start.8 = (bf16[2048,256]{1,0:T(8,128)(2,1)}, bf16[2048,256]{1,0:T(8,128)(2,1)}, u32[]{:S(2)}, u32[]{:S(2)}) collective-permute-start(bf16[2048,256]{1,0:T(8,128)(2,1)} %copy-done.27), channel_id=1, source_target_pairs={{0,1},{1,0},{2,3},{3,2},{4,5},{5,4},{6,7},{7,6},{8,9},{9,8},{10,11... | collective-permute-start | bytes 3145736 | tf_op jit(solution)/shard_map/ppermute | solution.py:248
  124.0 0.9 copy-start.13
  124.9 1.0 copy-start.15
  126.0 7.5 %collective-permute-start.6 = (bf16[128,256]{1,0:T(8,128)(2,1)S(1)}, bf16[128,256]{1,0:T(8,128)(2,1)S(1)}, u32[]{:S(2)}, u32[]{:S(2)}) collective-permute-start(bf16[128,256]{1,0:T(8,128)(2,1)S(1)} %get-tuple-element.63), channel_id=1, source_target_pairs={{32,0},{64,32},{96,64},{128,96},{160,128},{192,160},{224,192},{256... | collective-permute-start | bytes 196616 | tf_op jit(solution)/shard_map/ppermute | solution.py:48
  133.5 1.6 copy-start.3
  137.9 4.4 %collective-permute-start.7 = (bf16[8,128,256]{2,1,0:T(8,128)(2,1)S(1)}, bf16[8,128,256]{2,1,0:T(8,128)(2,1)S(1)}, u32[]{:S(2)}, u32[]{:S(2)}) collective-permute-start(bf16[8,128,256]{2,1,0:T(8,128)(2,1)S(1)} %get-tuple-element.65), channel_id=1, source_target_pairs={{0,1},{1,0},{2,3},{3,2},{4,5},{5,4},{6,7},{7,6},{8,9},{9,8},{10,11... | collective-permute-start | bytes 1572872 | tf_op jit(solution)/shard_map/ppermute | solution.py:248
  143.3 26.3 %all-to-all-start.5 = ((bf16[8,128,256]{2,1,0:T(8,128)(2,1)}), bf16[8,128,256]{2,1,0:T(8,128)(2,1)}, u32[]{:S(2)}, u32[]{:S(2)}) async-start(bf16[8,128,256]{2,1,0:T(8,128)(2,1)} %backward_core_sum.3.refs_4_), calls=%async_computation.5 | async-start | bytes 1048576 | tf_op jit(solution)/shard_map/all_to_all | solution.py:38
  150.1 1.6 copy-start.4
  151.7 5.9 %copy-start.21 = (bf16[128,256]{1,0:T(8,128)(2,1)S(1)}, bf16[128,256]{1,0:T(8,128)(2,1)}, u32[]{:S(2)}) copy-start(bf16[128,256]{1,0:T(8,128)(2,1)} %copy-done.20) | copy-start | bytes 196612
  151.7 11.5 %copy-start.9 = (bf16[1,8,64,256]{3,2,1,0:T(8,128)(2,1)S(1)}, bf16[1,8,64,256]{3,2,1,0:T(8,128)(2,1)}, u32[]{:S(2)}) copy-start(bf16[1,8,64,256]{3,2,1,0:T(8,128)(2,1)} %param.21) | copy-start | bytes 786436
  151.7 11.5 %copy-start.19 = (bf16[1,128,256]{2,1,0:T(8,128)(2,1)S(1)}, bf16[1,128,256]{2,1,0:T(8,128)(2,1)}, u32[]{:S(2)}) copy-start(bf16[1,128,256]{2,1,0:T(8,128)(2,1)} %refs_2_.3) | copy-start | bytes 196612
  154.1 3.5 %collective-permute-start.9 = (f32[128,256]{1,0:T(8,128)S(1)}, f32[128,256]{1,0:T(8,128)S(1)}, u32[]{:S(2)}, u32[]{:S(2)}) collective-permute-start(f32[128,256]{1,0:T(8,128)S(1)} %get-tuple-element.70), channel_id=1, source_target_pairs={{0,1},{1,0},{2,3},{3,2},{4,5},{5,4},{6,7},{7,6},{8,9},{9,8},{10,11... | collective-permute-start | bytes 393224 | tf_op jit(solution)/shard_map/ppermute | solution.py:248
  157.7 5.4 %collective-permute-start.10 = (bf16[128,256]{1,0:T(8,128)(2,1)S(1)}, bf16[128,256]{1,0:T(8,128)(2,1)S(1)}, u32[]{:S(2)}, u32[]{:S(2)}) collective-permute-start(bf16[128,256]{1,0:T(8,128)(2,1)S(1)} %forward_end.1), channel_id=1, source_target_pairs={{0,32},{32,64},{64,96},{96,128},{128,160},{160,192},{192,224},{224... | collective-permute-start | bytes 196616 | tf_op jit(solution)/shard_map/ppermute | solution.py:48
  164.2 4.5 %collective-permute-start.11 = (bf16[8,128,256]{2,1,0:T(8,128)(2,1)S(1)}, bf16[8,128,256]{2,1,0:T(8,128)(2,1)S(1)}, u32[]{:S(2)}, u32[]{:S(2)}) collective-permute-start(bf16[8,128,256]{2,1,0:T(8,128)(2,1)S(1)} %get-tuple-element.73), channel_id=1, source_target_pairs={{0,1},{1,0},{2,3},{3,2},{4,5},{5,4},{6,7},{7,6},{8,9},{9,8},{10,11... | collective-permute-start | bytes 1572872 | tf_op jit(solution)/shard_map/ppermute | solution.py:248
  169.7 25.0 %all-to-all-start.6 = ((bf16[8,128,256]{2,1,0:T(8,128)(2,1)}), bf16[8,128,256]{2,1,0:T(8,128)(2,1)}, u32[]{:S(2)}, u32[]{:S(2)}) async-start(bf16[8,128,256]{2,1,0:T(8,128)(2,1)} %forward_core_sum.3.refs_1_), calls=%async_computation.6 | async-start | bytes 1048576 | tf_op jit(solution)/shard_map/all_to_all | solution.py:38
  177.7 10.3 %collective-permute-start.12 = (bf16[128,256]{1,0:T(8,128)(2,1)S(1)}, bf16[128,256]{1,0:T(8,128)(2,1)S(1)}, u32[]{:S(2)}, u32[]{:S(2)}) collective-permute-start(bf16[128,256]{1,0:T(8,128)(2,1)S(1)} %backward_ring_sum.3.refs_1_), channel_id=1, source_target_pairs={{0,2},{1,3},{2,0},{3,1},{4,6},{5,7},{6,4},{7,5},{8,10},{9,11},{10,... | collective-permute-start | bytes 196616 | tf_op jit(solution)/shard_map/ppermute | solution.py:248
  194.7 22.1 %all-to-all-start.7 = ((bf16[8,128,256]{2,1,0:T(8,128)(2,1)}), bf16[8,128,256]{2,1,0:T(8,128)(2,1)}, u32[]{:S(2)}, u32[]{:S(2)}) async-start(bf16[8,128,256]{2,1,0:T(8,128)(2,1)} %backward_share.3.refs_1_), calls=%async_computation.7 | async-start | bytes 1048576 | tf_op jit(solution)/shard_map/all_to_all | solution.py:38
  199.9 10.7 %collective-permute-start.13 = (bf16[128,256]{1,0:T(8,128)(2,1)S(1)}, bf16[128,256]{1,0:T(8,128)(2,1)S(1)}, u32[]{:S(2)}, u32[]{:S(2)}) collective-permute-start(bf16[128,256]{1,0:T(8,128)(2,1)S(1)} %forward_ring_sum.3.refs_1_), channel_id=1, source_target_pairs={{0,2},{1,3},{2,0},{3,1},{4,6},{5,7},{6,4},{7,5},{8,10},{9,11},{10,... | collective-permute-start | bytes 196616 | tf_op jit(solution)/shard_map/ppermute | solution.py:248
  216.8 22.1 %all-to-all-start.8 = ((bf16[8,128,256]{2,1,0:T(8,128)(2,1)}), bf16[8,128,256]{2,1,0:T(8,128)(2,1)}, u32[]{:S(2)}, u32[]{:S(2)}) async-start(bf16[8,128,256]{2,1,0:T(8,128)(2,1)} %forward_share.3.refs_4_), calls=%async_computation.8 | async-start | bytes 1048576 | tf_op jit(solution)/shard_map/all_to_all | solution.py:38
  220.9 5.8 %copy-start.23 = (bf16[128,256]{1,0:T(8,128)(2,1)S(1)}, bf16[128,256]{1,0:T(8,128)(2,1)}, u32[]{:S(2)}) copy-start(bf16[128,256]{1,0:T(8,128)(2,1)} %copy-done.22) | copy-start | bytes 196612
  223.3 3.4 %collective-permute-start.14 = (f32[128,256]{1,0:T(8,128)S(1)}, f32[128,256]{1,0:T(8,128)S(1)}, u32[]{:S(2)}, u32[]{:S(2)}) collective-permute-start(f32[128,256]{1,0:T(8,128)S(1)} %get-tuple-element.78), channel_id=1, source_target_pairs={{0,1},{1,0},{2,3},{3,2},{4,5},{5,4},{6,7},{7,6},{8,9},{9,8},{10,11... | collective-permute-start | bytes 393224 | tf_op jit(solution)/shard_map/ppermute | solution.py:248
  238.9 17.4 %all-to-all-start.9 = ((f32[32,8,128]{2,1,0:T(8,128)}), f32[32,8,128]{2,1,0:T(8,128)S(1)}, u32[]{:S(2)}, u32[]{:S(2)}) async-start(f32[32,8,128]{2,1,0:T(8,128)} %get-tuple-element.83.refs_4_), calls=%async_computation.9 | async-start | bytes 262144 | tf_op jit(solution)/shard_map/all_to_all | solution.py:38
  242.9 1.6 copy-start.5
  246.9 3.2 %collective-permute-start.15 = (f32[128,256]{1,0:T(8,128)S(1)}, f32[128,256]{1,0:T(8,128)S(1)}, u32[]{:S(2)}, u32[]{:S(2)}) collective-permute-start(f32[128,256]{1,0:T(8,128)S(1)} %get-tuple-element.87), channel_id=1, source_target_pairs={{0,1},{1,0},{2,3},{3,2},{4,5},{5,4},{6,7},{7,6},{8,9},{9,8},{10,11... | collective-permute-start | bytes 393224 | tf_op jit(solution)/shard_map/ppermute | solution.py:248
  (5 other events, 3.6 us)

commit v10 on v9

--- a/solution.py
+++ b/solution.py
@@ -166,6 +166,10 @@
     out[...] = jnp.broadcast_to(value[None], out.shape)
     if half:
         half[0][...] = refs[0][...]
+
+
+def copied(weight, out):
+    out[...] = weight[...]
 
 
 def forward_product(blocks, own_weight, other_weight, mine, others):
@@ -355,7 +359,10 @@
     back_landed = swapped(gated, rings())
 
     x, squares, pieces = forward_begin(0, [arriving[0]], gated)
-    gated = gate(pieces, back_landed)
+    own_rows = {0: ((HALF, WIDTH), lambda i, scalars: (1 - scalars[CORE_AT], 0))}
+    (half,) = run(plain(copied), "half", [shape_of(HALF, WIDTH)], (output_local,), own_rows, (pieces,))
+    output_other = over(half, core_pairs())
+    gated = gate(pieces, back_landed, half)
     landed = swapped(gated, rings())
 
     half = (value_local, (WIDTH, HALF), lambda i, scalars: (0, 1 - scalars[CORE_AT]))
@@ -364,9 +371,7 @@
     gated = gate(back_copies, landed)
     back_gathered = swapped(gated, rings())
 
-    half = (output_local, (HALF, WIDTH), lambda i, scalars: (1 - scalars[CORE_AT], 0))
-    copies, half = turn("forward", landed, half, gated)
-    output_other = over(half, core_pairs())
+    (copies,) = turn("forward", landed, None, gated)
     packed, dots = backward_dots(0, back_gathered, g, squares, copies)
     all_dots = swapped(dots)
 

time: 259 us -> 261 us (level)
  blocking collectives: 25.7 us -> 23 us
    all_to_all x1, blocking collectives: 25.7 us -> 23 us  [swapped(): lax.all_to_all(value, 'shard', 0, 0, axis_index_groups=groups, tiled=True)]
    unnamed x57 -> x65, local copies, waits for them, and re-layouts: 18 us -> 19.8 us
    pallas_call x25 -> x26, Pallas kernels: 29.5 us -> 31.1 us  [call(): pl.pallas_call(body, out_shape=outs, grid_spec=pltpu.PrefetchScalarGridSp...]
  transfers between devices with their start and end apart: 25 -> 25, of which waited for: 20 -> 20; matrix products, arithmetic and copies ran while one was open for 0% -> 0% of each run, Pallas kernels for 9% -> 10%
where the time goes in v10:
time: 261 us; the launch traced here: 259 us
  starting transfers between devices  104 us (40%)
  waiting for transfers between devices  78.3 us (30%)
  Pallas kernels  31.1 us (12%)
  blocking collectives  23 us (9%)
  local copies, waits for them, and re-layouts  19.9 us (8%)
    ppermute x14, starting transfers between devices, over(): return lax.ppermute(value, 'shard', pairs)  52.2 us
    all_to_all x9, starting transfers between devices, swapped(): lax.all_to_all(value, 'shard', 0, 0, axis_index_groups=groups, tiled=True)  47.8 us
    all_to_all x9, waiting for transfers between devices, swapped(): lax.all_to_all(value, 'shard', 0, 0, axis_index_groups=groups, tiled=True)  41.5 us
    pallas_call x26, Pallas kernels, call(): pl.pallas_call(body, out_shape=outs, grid_spec=pltpu.PrefetchScalarGridSp...  31.1 us
    ppermute x14, waiting for transfers between devices, over(): return lax.ppermute(value, 'shard', pairs)  28.3 us
    all_to_all x1, blocking collectives, swapped(): lax.all_to_all(value, 'shard', 0, 0, axis_index_groups=groups, tiled=True)  23 us
    unnamed x65, local copies, waits for them, and re-layouts  19.8 us
    ppermute x2, waiting for transfers between devices, shifted(): lax.ppermute(value, axis, [(source, source + steps) for source in range(l...  8.54 us
  transfers between devices with their start and end apart: 25, of which 20 were waited for; matrix products, arithmetic and copies ran while one was open for 0% of the time, Pallas kernels for 10%

profile of v10, /device:TPU:7, one launch (start us, length us, event | category | flops | bytes accessed | tf_op | source)
XLA Modules:
  0.0 258.8 jit_solution(1180161580275738810)
XLA Ops:
  2.6 1.6 copy-done.1
  7.3 2.6 collective-permute-start
  12.4 6.8 %all-to-all-start = ((bf16[8,128,256]{2,1,0:T(8,128)(2,1)}), bf16[8,128,256]{2,1,0:T(8,128)(2,1)}, u32[]{:S(2)}, u32[]{:S(2)}) async-start(bf16[8,128,256]{2,1,0:T(8,128)(2,1)} %backward_core_sum.2.refs_6_), calls=%async_computation | async-start | bytes 1048576 | tf_op jit(solution)/shard_map/all_to_all | solution.py:38
  20.3 2.6 collective-permute-start.1
  22.9 1.5 collective-permute-done.1.refs_1_
  26.9 10.3 %all-to-all-done.refs_0_ = bf16[8,128,256]{2,1,0:T(8,128)(2,1)} async-done(((bf16[8,128,256]{2,1,0:T(8,128)(2,1)}), bf16[8,128,256]{2,1,0:T(8,128)(2,1)}, u32[]{:S(2)}, u32[]{:S(2)}) %all-to-all-start) | async-done | bytes 524320 | tf_op jit(solution)/shard_map/all_to_all | solution.py:38
  37.2 4.2 %all-to-all-start.1 = ((bf16[8,128,256]{2,1,0:T(8,128)(2,1)}), bf16[8,128,256]{2,1,0:T(8,128)(2,1)}, u32[]{:S(2)}, u32[]{:S(2)}) async-start(bf16[8,128,256]{2,1,0:T(8,128)(2,1)} %forward_core_sum.2.refs_2_.refs_1_), calls=%async_computation.1 | async-start | bytes 1048576 | tf_op jit(solution)/shard_map/all_to_all | solution.py:38
  42.5 10.6 %collective-permute-start.2 = (bf16[128,256]{1,0:T(8,128)(2,1)S(1)}, bf16[128,256]{1,0:T(8,128)(2,1)S(1)}, u32[]{:S(2)}, u32[]{:S(2)}) collective-permute-start(bf16[128,256]{1,0:T(8,128)(2,1)S(1)} %backward_ring_sum.2.refs_1_), channel_id=1, source_target_pairs={{0,2},{1,3},{2,0},{3,1},{4,6},{5,7},{6,4},{7,5},{8,10},{9,11},{10,... | collective-permute-start | bytes 196616 | tf_op jit(solution)/shard_map/ppermute | solution.py:252
  53.2 2.0 collective-permute-done.2.refs_2_
  55.2 1.7 backward_share.2
  57.7 3.8 %collective-permute-start.3 = (bf16[256,2048]{1,0:T(8,128)(2,1)}, bf16[256,2048]{1,0:T(8,128)(2,1)S(1)}, u32[]{:S(2)}, u32[]{:S(2)}) collective-permute-start(bf16[256,2048]{1,0:T(8,128)(2,1)} %get-tuple-element.52), channel_id=1, source_target_pairs={{0,1},{1,0},{2,3},{3,2},{4,5},{5,4},{6,7},{7,6},{8,9},{9,8},{10,11... | collective-permute-start | bytes 3145736 | tf_op jit(solution)/shard_map/ppermute | solution.py:252
  61.4 6.7 %all-to-all-start.2 = ((bf16[8,128,256]{2,1,0:T(8,128)(2,1)}), bf16[8,128,256]{2,1,0:T(8,128)(2,1)}, u32[]{:S(2)}, u32[]{:S(2)}) async-start(bf16[8,128,256]{2,1,0:T(8,128)(2,1)} %copy-done.10), calls=%async_computation.2 | async-start | bytes 1048576 | tf_op jit(solution)/shard_map/all_to_all | solution.py:38
  70.3 8.0 %collective-permute-start.4 = (bf16[128,256]{1,0:T(8,128)(2,1)S(1)}, bf16[128,256]{1,0:T(8,128)(2,1)S(1)}, u32[]{:S(2)}, u32[]{:S(2)}) collective-permute-start(bf16[128,256]{1,0:T(8,128)(2,1)S(1)} %forward_ring_sum.2.refs_1_), channel_id=1, source_target_pairs={{0,2},{1,3},{2,0},{3,1},{4,6},{5,7},{6,4},{7,5},{8,10},{9,11},{10,... | collective-permute-start | bytes 196616 | tf_op jit(solution)/shard_map/ppermute | solution.py:252
  78.3 2.2 collective-permute-done.4.refs_2_
  81.9 4.3 %all-to-all-done.2.refs_1_ = bf16[8,128,256]{2,1,0:T(8,128)(2,1)} async-done(((bf16[8,128,256]{2,1,0:T(8,128)(2,1)}), bf16[8,128,256]{2,1,0:T(8,128)(2,1)}, u32[]{:S(2)}, u32[]{:S(2)}) %all-to-all-start.2) | async-done | bytes 524320 | tf_op jit(solution)/shard_map/all_to_all | solution.py:38
  86.2 2.4 backward_product.2
  88.7 2.5 collective-permute-start.5
  94.0 23.0 %all_to_all.50.refs_2_ = f32[32,8,128]{2,1,0:T(8,128)} all-to-all(f32[32,8,128]{2,1,0:T(8,128)S(1)} %get-tuple-element.58), channel_id=1, replica_groups=mesh['segment'=16,'shard'=32] {'shard'}, dimensions={0} | all-to-all | bytes 262144 | tf_op jit(solution)/shard_map/all_to_all | solution.py:38
  117.0 4.2 %all-to-all-start.4 = ((bf16[8,128,256]{2,1,0:T(8,128)(2,1)}), bf16[8,128,256]{2,1,0:T(8,128)(2,1)}, u32[]{:S(2)}, u32[]{:S(2)}) async-start(bf16[8,128,256]{2,1,0:T(8,128)(2,1)} %forward_share.2.refs_4_.refs_3_), calls=%async_computation.4 | async-start | bytes 1048576 | tf_op jit(solution)/shard_map/all_to_all | solution.py:38
  121.2 2.1 collective-permute-start.8
  125.3 2.5 collective-permute-start.6
  127.8 5.1 %collective-permute-done.6.refs_1_ = bf16[128,256]{1,0:T(8,128)(2,1)S(1)} collective-permute-done((bf16[128,256]{1,0:T(8,128)(2,1)S(1)}, bf16[128,256]{1,0:T(8,128)(2,1)S(1)}, u32[]{:S(2)}, u32[]{:S(2)}) %collective-permute-start.6) | collective-permute-done | bytes 65568 | tf_op jit(solution)/shard_map/ppermute | solution.py:48
  132.9 1.6 copy-done.3
  137.3 2.9 %collective-permute-start.7 = (bf16[8,128,256]{2,1,0:T(8,128)(2,1)S(1)}, bf16[8,128,256]{2,1,0:T(8,128)(2,1)S(1)}, u32[]{:S(2)}, u32[]{:S(2)}) collective-permute-start(bf16[8,128,256]{2,1,0:T(8,128)(2,1)S(1)} %get-tuple-element.62), channel_id=1, source_target_pairs={{0,1},{1,0},{2,3},{3,2},{4,5},{5,4},{6,7},{7,6},{8,9},{9,8},{10,11... | collective-permute-start | bytes 1572872 | tf_op jit(solution)/shard_map/ppermute | solution.py:252
  142.7 6.8 %all-to-all-start.5 = ((bf16[8,128,256]{2,1,0:T(8,128)(2,1)}), bf16[8,128,256]{2,1,0:T(8,128)(2,1)}, u32[]{:S(2)}, u32[]{:S(2)}) async-start(bf16[8,128,256]{2,1,0:T(8,128)(2,1)} %backward_core_sum.3.refs_4_), calls=%async_computation.5 | async-start | bytes 1048576 | tf_op jit(solution)/shard_map/all_to_all | solution.py:38
  149.5 1.6 copy-done.4
  151.0 2.4 forward_product.2
  153.4 2.6 collective-permute-start.9
  157.1 1.9 collective-permute-start.10
  159.0 3.5 %collective-permute-done.10.refs_1_ = bf16[128,256]{1,0:T(8,128)(2,1)S(1)} collective-permute-done((bf16[128,256]{1,0:T(8,128)(2,1)S(1)}, bf16[128,256]{1,0:T(8,128)(2,1)S(1)}, u32[]{:S(2)}, u32[]{:S(2)}) %collective-permute-start.10) | collective-permute-done | bytes 65568 | tf_op jit(solution)/shard_map/ppermute | solution.py:48
  164.2 3.0 %collective-permute-start.11 = (bf16[8,128,256]{2,1,0:T(8,128)(2,1)S(1)}, bf16[8,128,256]{2,1,0:T(8,128)(2,1)S(1)}, u32[]{:S(2)}, u32[]{:S(2)}) collective-permute-start(bf16[8,128,256]{2,1,0:T(8,128)(2,1)S(1)} %get-tuple-element.69), channel_id=1, source_target_pairs={{0,1},{1,0},{2,3},{3,2},{4,5},{5,4},{6,7},{7,6},{8,9},{9,8},{10,11... | collective-permute-start | bytes 1572872 | tf_op jit(solution)/shard_map/ppermute | solution.py:252
  169.6 6.9 %all-to-all-start.6 = ((bf16[8,128,256]{2,1,0:T(8,128)(2,1)}), bf16[8,128,256]{2,1,0:T(8,128)(2,1)}, u32[]{:S(2)}, u32[]{:S(2)}) async-start(bf16[8,128,256]{2,1,0:T(8,128)(2,1)} %forward_core_sum.3.refs_1_), calls=%async_computation.6 | async-start | bytes 1048576 | tf_op jit(solution)/shard_map/all_to_all | solution.py:38
  177.7 3.4 %collective-permute-start.12 = (bf16[128,256]{1,0:T(8,128)(2,1)S(1)}, bf16[128,256]{1,0:T(8,128)(2,1)S(1)}, u32[]{:S(2)}, u32[]{:S(2)}) collective-permute-start(bf16[128,256]{1,0:T(8,128)(2,1)S(1)} %backward_ring_sum.3.refs_1_), channel_id=1, source_target_pairs={{0,2},{1,3},{2,0},{3,1},{4,6},{5,7},{6,4},{7,5},{8,10},{9,11},{10,... | collective-permute-start | bytes 196616 | tf_op jit(solution)/shard_map/ppermute | solution.py:252
  181.1 6.9 %collective-permute-done.12.refs_2_ = bf16[128,256]{1,0:T(8,128)(2,1)S(1)} collective-permute-done((bf16[128,256]{1,0:T(8,128)(2,1)S(1)}, bf16[128,256]{1,0:T(8,128)(2,1)S(1)}, u32[]{:S(2)}, u32[]{:S(2)}) %collective-permute-start.12) | collective-permute-done | bytes 65568 | tf_op jit(solution)/shard_map/ppermute | solution.py:252
  189.4 5.2 %all-to-all-done.6.refs_0_ = bf16[8,128,256]{2,1,0:T(8,128)(2,1)} async-done(((bf16[8,128,256]{2,1,0:T(8,128)(2,1)}), bf16[8,128,256]{2,1,0:T(8,128)(2,1)}, u32[]{:S(2)}, u32[]{:S(2)}) %all-to-all-start.6) | async-done | bytes 524320 | tf_op jit(solution)/shard_map/all_to_all | solution.py:38
  194.6 4.1 %all-to-all-start.7 = ((bf16[8,128,256]{2,1,0:T(8,128)(2,1)}), bf16[8,128,256]{2,1,0:T(8,128)(2,1)}, u32[]{:S(2)}, u32[]{:S(2)}) async-start(bf16[8,128,256]{2,1,0:T(8,128)(2,1)} %backward_share.3.refs_1_), calls=%async_computation.7 | async-start | bytes 1048576 | tf_op jit(solution)/shard_map/all_to_all | solution.py:38
  199.9 3.4 %collective-permute-start.13 = (bf16[128,256]{1,0:T(8,128)(2,1)S(1)}, bf16[128,256]{1,0:T(8,128)(2,1)S(1)}, u32[]{:S(2)}, u32[]{:S(2)}) collective-permute-start(bf16[128,256]{1,0:T(8,128)(2,1)S(1)} %forward_ring_sum.3.refs_1_), channel_id=1, source_target_pairs={{0,2},{1,3},{2,0},{3,1},{4,6},{5,7},{6,4},{7,5},{8,10},{9,11},{10,... | collective-permute-start | bytes 196616 | tf_op jit(solution)/shard_map/ppermute | solution.py:252
  203.3 7.2 %collective-permute-done.13.refs_2_ = bf16[128,256]{1,0:T(8,128)(2,1)S(1)} collective-permute-done((bf16[128,256]{1,0:T(8,128)(2,1)S(1)}, bf16[128,256]{1,0:T(8,128)(2,1)S(1)}, u32[]{:S(2)}, u32[]{:S(2)}) %collective-permute-start.13) | collective-permute-done | bytes 65568 | tf_op jit(solution)/shard_map/ppermute | solution.py:252
  211.9 4.8 %all-to-all-done.7.refs_1_ = bf16[8,128,256]{2,1,0:T(8,128)(2,1)} async-done(((bf16[8,128,256]{2,1,0:T(8,128)(2,1)}), bf16[8,128,256]{2,1,0:T(8,128)(2,1)}, u32[]{:S(2)}, u32[]{:S(2)}) %all-to-all-start.7) | async-done | bytes 524320 | tf_op jit(solution)/shard_map/all_to_all | solution.py:38
  216.7 4.1 %all-to-all-start.8 = ((bf16[8,128,256]{2,1,0:T(8,128)(2,1)}), bf16[8,128,256]{2,1,0:T(8,128)(2,1)}, u32[]{:S(2)}, u32[]{:S(2)}) async-start(bf16[8,128,256]{2,1,0:T(8,128)(2,1)} %forward_share.3.refs_4_), calls=%async_computation.8 | async-start | bytes 1048576 | tf_op jit(solution)/shard_map/all_to_all | solution.py:38
  220.9 2.4 backward_product.3
  223.3 2.4 collective-permute-start.14
  228.2 10.6 %all-to-all-done.8.refs_1_ = bf16[8,128,256]{2,1,0:T(8,128)(2,1)} async-done(((bf16[8,128,256]{2,1,0:T(8,128)(2,1)}), bf16[8,128,256]{2,1,0:T(8,128)(2,1)}, u32[]{:S(2)}, u32[]{:S(2)}) %all-to-all-start.8) | async-done | bytes 524320 | tf_op jit(solution)/shard_map/all_to_all | solution.py:38
  238.8 4.0 %all-to-all-start.9 = ((f32[32,8,128]{2,1,0:T(8,128)}), f32[32,8,128]{2,1,0:T(8,128)S(1)}, u32[]{:S(2)}, u32[]{:S(2)}) async-start(f32[32,8,128]{2,1,0:T(8,128)} %get-tuple-element.79.refs_4_), calls=%async_computation.9 | async-start | bytes 262144 | tf_op jit(solution)/shard_map/all_to_all | solution.py:38
  242.8 1.6 copy-done.5
  244.4 2.4 forward_product.3
  246.8 2.3 collective-permute-start.15
  250.0 6.2 %all-to-all-done.9.refs_2_ = f32[32,8,128]{2,1,0:T(8,128)S(1)} async-done(((f32[32,8,128]{2,1,0:T(8,128)}), f32[32,8,128]{2,1,0:T(8,128)S(1)}, u32[]{:S(2)}, u32[]{:S(2)}) %all-to-all-start.9) | async-done | bytes 131104 | tf_op jit(solution)/shard_map/all_to_all | solution.py:38
  (101 shorter events, 42.9 us)
Async XLA Ops:
  2.6 1.6 copy-start.1
  4.2 0.9 copy-start.6
  6.0 13.2 %copy-start = (bf16[1,256,4096]{2,1,0:T(8,128)(2,1)S(1)}, bf16[1,256,4096]{2,1,0:T(8,128)(2,1)}, u32[]{:S(2)}) copy-start(bf16[1,256,4096]{2,1,0:T(8,128)(2,1)} %param.13) | copy-start | bytes 6291460
  6.0 13.2 %copy-start.8 = (bf16[1,8,64,256]{3,2,1,0:T(8,128)(2,1)S(1)}, bf16[1,8,64,256]{3,2,1,0:T(8,128)(2,1)}, u32[]{:S(2)}) copy-start(bf16[1,8,64,256]{3,2,1,0:T(8,128)(2,1)} %param.21) | copy-start | bytes 786436
  6.0 13.2 %copy-start.20 = (bf16[1,128,256]{2,1,0:T(8,128)(2,1)S(1)}, bf16[1,128,256]{2,1,0:T(8,128)(2,1)}, u32[]{:S(2)}) copy-start(bf16[1,128,256]{2,1,0:T(8,128)(2,1)} %param.16) | copy-start | bytes 196612
  6.0 13.3 %copy-start.31 = (f32[1,256]{1,0:T(1,128)S(1)}, f32[1,256]{1,0:T(1,128)}, u32[]{:S(2)}) copy-start(f32[1,256]{1,0:T(1,128)} %refs_3_.3) | copy-start | bytes 3076
  7.3 13.0 %copy-start.27 = (bf16[128,256]{1,0:T(8,128)(2,1)}, bf16[128,256]{1,0:T(8,128)(2,1)S(1)}, u32[]{:S(2)}) copy-start(bf16[128,256]{1,0:T(8,128)(2,1)S(1)} %get-tuple-element.55.refs_4_) | copy-start | bytes 196612
  7.3 4.1 %collective-permute-start = (bf16[8,128,256]{2,1,0:T(8,128)(2,1)S(1)}, bf16[8,128,256]{2,1,0:T(8,128)(2,1)S(1)}, u32[]{:S(2)}, u32[]{:S(2)}) collective-permute-start(bf16[8,128,256]{2,1,0:T(8,128)(2,1)S(1)} %get-tuple-element.46), channel_id=1, source_target_pairs={{0,1},{1,0},{2,3},{3,2},{4,5},{5,4},{6,7},{7,6},{8,9},{9,8},{10,11... | collective-permute-start | bytes 1572872 | tf_op jit(solution)/shard_map/ppermute | solution.py:252
  12.4 24.9 %all-to-all-start = ((bf16[8,128,256]{2,1,0:T(8,128)(2,1)}), bf16[8,128,256]{2,1,0:T(8,128)(2,1)}, u32[]{:S(2)}, u32[]{:S(2)}) async-start(bf16[8,128,256]{2,1,0:T(8,128)(2,1)} %backward_core_sum.2.refs_6_), calls=%async_computation | async-start | bytes 1048576 | tf_op jit(solution)/shard_map/all_to_all | solution.py:38
  19.2 6.1 %copy-start.2 = (bf16[1,4096,256]{2,1,0:T(8,128)(2,1)S(1)}, bf16[1,4096,256]{2,1,0:T(8,128)(2,1)}, u32[]{:S(2)}) copy-start(bf16[1,4096,256]{2,1,0:T(8,128)(2,1)} %param.14) | copy-start | bytes 6291460
  20.3 5.6 %copy-start.23 = (bf16[128,256]{1,0:T(8,128)(2,1)}, bf16[128,256]{1,0:T(8,128)(2,1)S(1)}, u32[]{:S(2)}) copy-start(bf16[128,256]{1,0:T(8,128)(2,1)S(1)} %get-tuple-element.64.refs_0_) | copy-start | bytes 196612
  20.3 4.1 %collective-permute-start.1 = (bf16[8,128,256]{2,1,0:T(8,128)(2,1)S(1)}, bf16[8,128,256]{2,1,0:T(8,128)(2,1)S(1)}, u32[]{:S(2)}, u32[]{:S(2)}) collective-permute-start(bf16[8,128,256]{2,1,0:T(8,128)(2,1)S(1)} %get-tuple-element.48), channel_id=1, source_target_pairs={{0,1},{1,0},{2,3},{3,2},{4,5},{5,4},{6,7},{7,6},{8,9},{9,8},{10,11... | collective-permute-start | bytes 1572872 | tf_op jit(solution)/shard_map/ppermute | solution.py:252
  25.9 1.0 copy-start.13
  37.2 24.2 %all-to-all-start.1 = ((bf16[8,128,256]{2,1,0:T(8,128)(2,1)}), bf16[8,128,256]{2,1,0:T(8,128)(2,1)}, u32[]{:S(2)}, u32[]{:S(2)}) async-start(bf16[8,128,256]{2,1,0:T(8,128)(2,1)} %forward_core_sum.2.refs_2_.refs_1_), calls=%async_computation.1 | async-start | bytes 1048576 | tf_op jit(solution)/shard_map/all_to_all | solution.py:38
  42.5 12.7 %collective-permute-start.2 = (bf16[128,256]{1,0:T(8,128)(2,1)S(1)}, bf16[128,256]{1,0:T(8,128)(2,1)S(1)}, u32[]{:S(2)}, u32[]{:S(2)}) collective-permute-start(bf16[128,256]{1,0:T(8,128)(2,1)S(1)} %backward_ring_sum.2.refs_1_), channel_id=1, source_target_pairs={{0,2},{1,3},{2,0},{3,1},{4,6},{5,7},{6,4},{7,5},{8,10},{9,11},{10,... | collective-permute-start | bytes 196616 | tf_op jit(solution)/shard_map/ppermute | solution.py:252
  57.7 24.2 %collective-permute-start.3 = (bf16[256,2048]{1,0:T(8,128)(2,1)}, bf16[256,2048]{1,0:T(8,128)(2,1)S(1)}, u32[]{:S(2)}, u32[]{:S(2)}) collective-permute-start(bf16[256,2048]{1,0:T(8,128)(2,1)} %get-tuple-element.52), channel_id=1, source_target_pairs={{0,1},{1,0},{2,3},{3,2},{4,5},{5,4},{6,7},{7,6},{8,9},{9,8},{10,11... | collective-permute-start | bytes 3145736 | tf_op jit(solution)/shard_map/ppermute | solution.py:252
  61.4 24.8 %all-to-all-start.2 = ((bf16[8,128,256]{2,1,0:T(8,128)(2,1)}), bf16[8,128,256]{2,1,0:T(8,128)(2,1)}, u32[]{:S(2)}, u32[]{:S(2)}) async-start(bf16[8,128,256]{2,1,0:T(8,128)(2,1)} %copy-done.10), calls=%async_computation.2 | async-start | bytes 1048576 | tf_op jit(solution)/shard_map/all_to_all | solution.py:38
  68.1 1.1 copy-start.11
  70.3 10.2 %collective-permute-start.4 = (bf16[128,256]{1,0:T(8,128)(2,1)S(1)}, bf16[128,256]{1,0:T(8,128)(2,1)S(1)}, u32[]{:S(2)}, u32[]{:S(2)}) collective-permute-start(bf16[128,256]{1,0:T(8,128)(2,1)S(1)} %forward_ring_sum.2.refs_1_), channel_id=1, source_target_pairs={{0,2},{1,3},{2,0},{3,1},{4,6},{5,7},{6,4},{7,5},{8,10},{9,11},{10,... | collective-permute-start | bytes 196616 | tf_op jit(solution)/shard_map/ppermute | solution.py:252
  81.9 10.2 %copy-start.12 = (bf16[1,2,128,256]{3,2,1,0:T(8,128)(2,1)S(1)}, bf16[1,2,128,256]{3,2,1,0:T(8,128)(2,1)}, u32[]{:S(2)}) copy-start(bf16[1,2,128,256]{3,2,1,0:T(8,128)(2,1)} %param.20) | copy-start | bytes 393220
  88.6 44.2 %copy-start.7 = (bf16[1,8,64,256]{3,2,1,0:T(8,128)(2,1)S(1)}, bf16[1,8,64,256]{3,2,1,0:T(8,128)(2,1)}, u32[]{:S(2)}) copy-start(bf16[1,8,64,256]{3,2,1,0:T(8,128)(2,1)} %param.22) | copy-start | bytes 786436
  88.7 3.5 %collective-permute-start.5 = (f32[128,256]{1,0:T(8,128)S(1)}, f32[128,256]{1,0:T(8,128)S(1)}, u32[]{:S(2)}, u32[]{:S(2)}) collective-permute-start(f32[128,256]{1,0:T(8,128)S(1)} %get-tuple-element.54), channel_id=1, source_target_pairs={{0,1},{1,0},{2,3},{3,2},{4,5},{5,4},{6,7},{7,6},{8,9},{9,8},{10,11... | collective-permute-start | bytes 393224 | tf_op jit(solution)/shard_map/ppermute | solution.py:252
  117.0 25.7 %all-to-all-start.4 = ((bf16[8,128,256]{2,1,0:T(8,128)(2,1)}), bf16[8,128,256]{2,1,0:T(8,128)(2,1)}, u32[]{:S(2)}, u32[]{:S(2)}) async-start(bf16[8,128,256]{2,1,0:T(8,128)(2,1)} %forward_share.2.refs_4_.refs_3_), calls=%async_computation.4 | async-start | bytes 1048576 | tf_op jit(solution)/shard_map/all_to_all | solution.py:38
  121.2 28.3 %collective-permute-start.8 = (bf16[2048,256]{1,0:T(8,128)(2,1)}, bf16[2048,256]{1,0:T(8,128)(2,1)}, u32[]{:S(2)}, u32[]{:S(2)}) collective-permute-start(bf16[2048,256]{1,0:T(8,128)(2,1)} %copy-done.13), channel_id=1, source_target_pairs={{0,1},{1,0},{2,3},{3,2},{4,5},{5,4},{6,7},{7,6},{8,9},{9,8},{10,11... | collective-permute-start | bytes 3145736 | tf_op jit(solution)/shard_map/ppermute | solution.py:252
  123.3 0.9 copy-start.14
  124.2 1.0 copy-start.18
  125.3 7.5 %collective-permute-start.6 = (bf16[128,256]{1,0:T(8,128)(2,1)S(1)}, bf16[128,256]{1,0:T(8,128)(2,1)S(1)}, u32[]{:S(2)}, u32[]{:S(2)}) collective-permute-start(bf16[128,256]{1,0:T(8,128)(2,1)S(1)} %get-tuple-element.60), channel_id=1, source_target_pairs={{32,0},{64,32},{96,64},{128,96},{160,128},{192,160},{224,192},{256... | collective-permute-start | bytes 196616 | tf_op jit(solution)/shard_map/ppermute | solution.py:48
  132.9 1.6 copy-start.3
  137.3 4.4 %collective-permute-start.7 = (bf16[8,128,256]{2,1,0:T(8,128)(2,1)S(1)}, bf16[8,128,256]{2,1,0:T(8,128)(2,1)S(1)}, u32[]{:S(2)}, u32[]{:S(2)}) collective-permute-start(bf16[8,128,256]{2,1,0:T(8,128)(2,1)S(1)} %get-tuple-element.62), channel_id=1, source_target_pairs={{0,1},{1,0},{2,3},{3,2},{4,5},{5,4},{6,7},{7,6},{8,9},{9,8},{10,11... | collective-permute-start | bytes 1572872 | tf_op jit(solution)/shard_map/ppermute | solution.py:252
  142.7 27.0 %all-to-all-start.5 = ((bf16[8,128,256]{2,1,0:T(8,128)(2,1)}), bf16[8,128,256]{2,1,0:T(8,128)(2,1)}, u32[]{:S(2)}, u32[]{:S(2)}) async-start(bf16[8,128,256]{2,1,0:T(8,128)(2,1)} %backward_core_sum.3.refs_4_), calls=%async_computation.5 | async-start | bytes 1048576 | tf_op jit(solution)/shard_map/all_to_all | solution.py:38
  149.4 1.6 copy-start.4
  151.0 5.9 %copy-start.24 = (bf16[128,256]{1,0:T(8,128)(2,1)S(1)}, bf16[128,256]{1,0:T(8,128)(2,1)}, u32[]{:S(2)}) copy-start(bf16[128,256]{1,0:T(8,128)(2,1)} %copy-done.23) | copy-start | bytes 196612
  151.0 11.5 %copy-start.9 = (bf16[1,8,64,256]{3,2,1,0:T(8,128)(2,1)S(1)}, bf16[1,8,64,256]{3,2,1,0:T(8,128)(2,1)}, u32[]{:S(2)}) copy-start(bf16[1,8,64,256]{3,2,1,0:T(8,128)(2,1)} %param.21) | copy-start | bytes 786436
  151.0 11.5 %copy-start.22 = (bf16[1,128,256]{2,1,0:T(8,128)(2,1)S(1)}, bf16[1,128,256]{2,1,0:T(8,128)(2,1)}, u32[]{:S(2)}) copy-start(bf16[1,128,256]{2,1,0:T(8,128)(2,1)} %refs_2_.3) | copy-start | bytes 196612
  153.4 3.5 %collective-permute-start.9 = (f32[128,256]{1,0:T(8,128)S(1)}, f32[128,256]{1,0:T(8,128)S(1)}, u32[]{:S(2)}, u32[]{:S(2)}) collective-permute-start(f32[128,256]{1,0:T(8,128)S(1)} %get-tuple-element.66), channel_id=1, source_target_pairs={{0,1},{1,0},{2,3},{3,2},{4,5},{5,4},{6,7},{7,6},{8,9},{9,8},{10,11... | collective-permute-start | bytes 393224 | tf_op jit(solution)/shard_map/ppermute | solution.py:252
  157.1 5.4 %collective-permute-start.10 = (bf16[128,256]{1,0:T(8,128)(2,1)S(1)}, bf16[128,256]{1,0:T(8,128)(2,1)S(1)}, u32[]{:S(2)}, u32[]{:S(2)}) collective-permute-start(bf16[128,256]{1,0:T(8,128)(2,1)S(1)} %forward_end.1), channel_id=1, source_target_pairs={{0,32},{32,64},{64,96},{96,128},{128,160},{160,192},{192,224},{224... | collective-permute-start | bytes 196616 | tf_op jit(solution)/shard_map/ppermute | solution.py:48
  164.2 4.5 %collective-permute-start.11 = (bf16[8,128,256]{2,1,0:T(8,128)(2,1)S(1)}, bf16[8,128,256]{2,1,0:T(8,128)(2,1)S(1)}, u32[]{:S(2)}, u32[]{:S(2)}) collective-permute-start(bf16[8,128,256]{2,1,0:T(8,128)(2,1)S(1)} %get-tuple-element.69), channel_id=1, source_target_pairs={{0,1},{1,0},{2,3},{3,2},{4,5},{5,4},{6,7},{7,6},{8,9},{9,8},{10,11... | collective-permute-start | bytes 1572872 | tf_op jit(solution)/shard_map/ppermute | solution.py:252
  169.6 25.0 %all-to-all-start.6 = ((bf16[8,128,256]{2,1,0:T(8,128)(2,1)}), bf16[8,128,256]{2,1,0:T(8,128)(2,1)}, u32[]{:S(2)}, u32[]{:S(2)}) async-start(bf16[8,128,256]{2,1,0:T(8,128)(2,1)} %forward_core_sum.3.refs_1_), calls=%async_computation.6 | async-start | bytes 1048576 | tf_op jit(solution)/shard_map/all_to_all | solution.py:38
  177.7 10.3 %collective-permute-start.12 = (bf16[128,256]{1,0:T(8,128)(2,1)S(1)}, bf16[128,256]{1,0:T(8,128)(2,1)S(1)}, u32[]{:S(2)}, u32[]{:S(2)}) collective-permute-start(bf16[128,256]{1,0:T(8,128)(2,1)S(1)} %backward_ring_sum.3.refs_1_), channel_id=1, source_target_pairs={{0,2},{1,3},{2,0},{3,1},{4,6},{5,7},{6,4},{7,5},{8,10},{9,11},{10,... | collective-permute-start | bytes 196616 | tf_op jit(solution)/shard_map/ppermute | solution.py:252
  194.6 22.1 %all-to-all-start.7 = ((bf16[8,128,256]{2,1,0:T(8,128)(2,1)}), bf16[8,128,256]{2,1,0:T(8,128)(2,1)}, u32[]{:S(2)}, u32[]{:S(2)}) async-start(bf16[8,128,256]{2,1,0:T(8,128)(2,1)} %backward_share.3.refs_1_), calls=%async_computation.7 | async-start | bytes 1048576 | tf_op jit(solution)/shard_map/all_to_all | solution.py:38
  199.9 10.7 %collective-permute-start.13 = (bf16[128,256]{1,0:T(8,128)(2,1)S(1)}, bf16[128,256]{1,0:T(8,128)(2,1)S(1)}, u32[]{:S(2)}, u32[]{:S(2)}) collective-permute-start(bf16[128,256]{1,0:T(8,128)(2,1)S(1)} %forward_ring_sum.3.refs_1_), channel_id=1, source_target_pairs={{0,2},{1,3},{2,0},{3,1},{4,6},{5,7},{6,4},{7,5},{8,10},{9,11},{10,... | collective-permute-start | bytes 196616 | tf_op jit(solution)/shard_map/ppermute | solution.py:252
  216.7 22.1 %all-to-all-start.8 = ((bf16[8,128,256]{2,1,0:T(8,128)(2,1)}), bf16[8,128,256]{2,1,0:T(8,128)(2,1)}, u32[]{:S(2)}, u32[]{:S(2)}) async-start(bf16[8,128,256]{2,1,0:T(8,128)(2,1)} %forward_share.3.refs_4_), calls=%async_computation.8 | async-start | bytes 1048576 | tf_op jit(solution)/shard_map/all_to_all | solution.py:38
  220.9 5.8 %copy-start.26 = (bf16[128,256]{1,0:T(8,128)(2,1)S(1)}, bf16[128,256]{1,0:T(8,128)(2,1)}, u32[]{:S(2)}) copy-start(bf16[128,256]{1,0:T(8,128)(2,1)} %copy-done.25) | copy-start | bytes 196612
  223.3 3.4 %collective-permute-start.14 = (f32[128,256]{1,0:T(8,128)S(1)}, f32[128,256]{1,0:T(8,128)S(1)}, u32[]{:S(2)}, u32[]{:S(2)}) collective-permute-start(f32[128,256]{1,0:T(8,128)S(1)} %get-tuple-element.74), channel_id=1, source_target_pairs={{0,1},{1,0},{2,3},{3,2},{4,5},{5,4},{6,7},{7,6},{8,9},{9,8},{10,11... | collective-permute-start | bytes 393224 | tf_op jit(solution)/shard_map/ppermute | solution.py:252
  238.8 17.4 %all-to-all-start.9 = ((f32[32,8,128]{2,1,0:T(8,128)}), f32[32,8,128]{2,1,0:T(8,128)S(1)}, u32[]{:S(2)}, u32[]{:S(2)}) async-start(f32[32,8,128]{2,1,0:T(8,128)} %get-tuple-element.79.refs_4_), calls=%async_computation.9 | async-start | bytes 262144 | tf_op jit(solution)/shard_map/all_to_all | solution.py:38
  242.8 1.6 copy-start.5
  246.8 3.2 %collective-permute-start.15 = (f32[128,256]{1,0:T(8,128)S(1)}, f32[128,256]{1,0:T(8,128)S(1)}, u32[]{:S(2)}, u32[]{:S(2)}) collective-permute-start(f32[128,256]{1,0:T(8,128)S(1)} %get-tuple-element.83), channel_id=1, source_target_pairs={{0,1},{1,0},{2,3},{3,2},{4,5},{5,4},{6,7},{7,6},{8,9},{9,8},{10,11... | collective-permute-start | bytes 393224 | tf_op jit(solution)/shard_map/ppermute | solution.py:252
  256.2 1.0 copy-start.16
  (9 other events, 6.8 us)
